TPU v7x, 128 devices: a whole 4x4x4 slice. The times are simulated.
128 devices in a mesh: rows: 16 (over x_hi, z, core), chan: 8 (over y, x_lo).
Axes of the slice: x: 4 (x_hi: 2, x_lo: 2; x = x_hi * 2 + x_lo), y: 4, z: 4, core: 2. Of those that a mesh axis runs over, the one named last changes fastest.
Arguments:
- coarse_input: bfloat16 [2, 256, 256, 256], P(None, 'rows', None, 'chan'), may hold values from -6 to 6
- coarse_pre: bfloat16 [2, 256, 256, 256], P(None, 'rows', None, 'chan'), may hold values from -8 to 8
- skip_feats: bfloat16 [2, 512, 512, 128], P(None, ('rows', 'chan')), may hold values from -6 to 6
- fine_pre: bfloat16 [2, 512, 512, 128], P(None, ('rows', 'chan')), may hold values from -8 to 8
- fine_cotangent: bfloat16 [2, 512, 512, 128], P(None, ('rows', 'chan')), may hold values from -6 to 6
- fine_weight: bfloat16 [3, 3, 384, 128], replicated, may hold values from -0.109375 to 0.109375
- coarse_weight: bfloat16 [3, 3, 256, 256], replicated, may hold values from -0.125 to 0.125
Outputs:
- grad_skip: bfloat16 [2, 512, 512, 128], P(None, ('rows', 'chan'))
- grad_input: bfloat16 [2, 256, 256, 256], P(None, 'rows', None, 'chan')
- grad_fine_weight: float32 [3, 3, 384, 128], replicated
- grad_coarse_weight: float32 [3, 3, 256, 256], replicated
All inputs are finite; a program needn't handle non-finite values.
Results may differ from a plain program's by a relative error of at most 0.0058.
Values may be sent and summed in bfloat16 or wider, within the bound.
No kernel may reach another device: no remote copies, remote signals or barrier semaphores. Data moves between devices by JAX's collectives and lax.ppermute only.
A program may use at most 192 MiB of HBM per device.

v0:
```python
import math

import jax
import jax.numpy as jnp
from jax import lax
from jax.sharding import PartitionSpec as P


def extended(block, sides, width):
    for axis, dim in sides:
        count = lax.axis_size(axis)
        forward = [(i, i + 1) for i in range(count - 1)]
        backward = [(target, source) for source, target in forward]
        low = lax.ppermute(
            lax.slice_in_dim(block, block.shape[dim] - width, None, axis=dim), axis, forward
        )
        high = lax.ppermute(lax.slice_in_dim(block, 0, width, axis=dim), axis, backward)
        block = jnp.concatenate([low, block, high], axis=dim)
    return block


def silu_grad(value):
    sigma = jax.nn.sigmoid(value)
    return sigma * (1.0 + value * (1.0 - sigma))


def upsample(field):
    return jnp.repeat(jnp.repeat(field, 2, axis=-3), 2, axis=-2)


def pooling(field):
    shape = field.shape
    return field.reshape(shape[:-3] + (shape[-3] // 2, 2, shape[-2] // 2, 2, shape[-1])).sum(
        axis=(-4, -2)
    )


def widen(field):
    return jnp.pad(field, ((0, 0), (0, 0), (1, 1), (0, 0)))


def tap_grads(inputs, padded):
    height, breadth = (inputs.shape[-3], inputs.shape[-2])
    kernel_rows = []
    for vertical in range(3):
        row_taps = []
        for lateral in range(3):
            window = padded[
                ..., 2 - vertical : 2 - vertical + height, 2 - lateral : 2 - lateral + breadth, :
            ]
            row_taps.append(
                jnp.einsum("...hwi,...hwo->io", inputs, window, preferred_element_type=jnp.float32)
            )
        kernel_rows.append(jnp.stack(row_taps))
    return jnp.stack(kernel_rows)


def tap_back(padded, kernel):
    height, breadth = (padded.shape[-3] - 2, padded.shape[-2] - 2)
    total = None
    for vertical in range(3):
        for lateral in range(3):
            window = padded[
                ..., 2 - vertical : 2 - vertical + height, 2 - lateral : 2 - lateral + breadth, :
            ]
            term = jnp.einsum(
                "...hwo,io->...hwi",
                window,
                kernel[vertical, lateral],
                preferred_element_type=jnp.float32,
            )
            total = term if total is None else total + term
    return total


def shards(
    coarse_input, coarse_pre, skip_feats, fine_pre, fine_cotangent, fine_weight, coarse_weight
):
    channels = coarse_weight.shape[2]
    pieces = lax.axis_size("chan")
    devices = lax.axis_size("rows") * pieces
    strip_input, strip_pre = (
        lax.all_to_all(coarse_input, "chan", split_axis=1, concat_axis=3, tiled=True),
        lax.all_to_all(coarse_pre, "chan", split_axis=1, concat_axis=3, tiled=True),
    )
    pre_value = strip_pre.astype(jnp.float32)
    upsampled = upsample(jax.nn.silu(pre_value)).astype(jnp.bfloat16)
    stacked = jnp.concatenate([upsampled, skip_feats], axis=-1)
    fine_grad = (
        fine_cotangent.astype(jnp.float32) * silu_grad(fine_pre.astype(jnp.float32))
    ).astype(jnp.bfloat16)
    fine_pad = widen(extended(fine_grad, ((("rows", "chan"), 1),), 1))
    fine_cells = fine_grad.shape[0] * fine_grad.shape[1] * fine_grad.shape[2] * devices
    grad_fine_weight = lax.psum(
        tap_grads(stacked, fine_pad) * (1.0 / math.sqrt(fine_cells)), ("rows", "chan")
    )
    back = tap_back(fine_pad, fine_weight)
    grad_skip = back[..., channels:].astype(jnp.bfloat16)
    coarse_grad = (pooling(back[..., :channels]) * silu_grad(pre_value)).astype(jnp.bfloat16)
    coarse_cells = coarse_grad.shape[0] * coarse_grad.shape[1] * coarse_grad.shape[2] * devices
    factor = 1.0 / math.sqrt(coarse_cells)
    coarse_pad = widen(extended(coarse_grad, ((("rows", "chan"), 1),), 1))
    grad_coarse_weight = lax.psum(tap_grads(strip_input, coarse_pad) * factor, ("rows", "chan"))
    strip_back = tap_back(coarse_pad, coarse_weight).astype(jnp.bfloat16)
    grad_input = lax.all_to_all(strip_back, "chan", split_axis=3, concat_axis=1, tiled=True)
    return (grad_skip, grad_input, grad_fine_weight, grad_coarse_weight)


def solution(mesh):
    return jax.shard_map(
        shards,
        mesh=mesh,
        in_specs=(
            P(None, "rows", None, "chan"),
            P(None, "rows", None, "chan"),
            P(None, ("rows", "chan"), None, None),
            P(None, ("rows", "chan"), None, None),
            P(None, ("rows", "chan"), None, None),
            P(),
            P(),
        ),
        out_specs=(P(None, ("rows", "chan"), None, None), P(None, "rows", None, "chan"), P(), P()),
        check_vma=False,
    )
```

profile of v0, /device:TPU:1, one launch (start us, length us, event | category | flops | bytes accessed | tf_op | source)
XLA Modules:
  0.0 336.8 jit_solution(12021980148239901610)
XLA Ops:
  10.4 3.9 %collective-permute-start = (bf16[2,1,512,128]{3,2,1,0:T(8,128)(2,1)}, bf16[2,1,512,128]{3,2,1,0:T(8,128)(2,1)S(1)}, u32[]{:S(2)}, u32[]{:S(2)}) collective-permute-start(bf16[2,1,512,128]{3,2,1,0:T(8,128)(2,1)} %get-tuple-element.29), channel_id=1, source_target_pairs={{0,1},{1,2},{2,3},{3,4},{4,5},{5,6},{6,7},{7,8},{8,9},{9,10},{10,1... | collective-permute-start | bytes 786440 | tf_op jit(solution)/shard_map/ppermute | solution.py:14
  14.4 4.9 %collective-permute-start.1 = (bf16[2,1,512,128]{3,2,1,0:T(8,128)(2,1)}, bf16[2,1,512,128]{3,2,1,0:T(8,128)(2,1)S(1)}, u32[]{:S(2)}, u32[]{:S(2)}) collective-permute-start(bf16[2,1,512,128]{3,2,1,0:T(8,128)(2,1)} %get-tuple-element.28), channel_id=1, source_target_pairs={{1,0},{2,1},{3,2},{4,3},{5,4},{6,5},{7,6},{8,7},{9,8},{10,9},{11,1... | collective-permute-start | bytes 786440 | tf_op jit(solution)/shard_map/ppermute | solution.py:17
  20.2 3.5 %all-to-all-start = ((bf16[2,16,256,32]{2,3,0,1:T(8,128)(2,1)}), bf16[2,16,256,32]{2,3,0,1:T(8,128)(2,1)S(1)}, u32[]{:S(2)}, u32[]{:S(2)}) async-start(bf16[2,16,256,32]{2,3,0,1:T(8,128)(2,1)} %copy.117), calls=%async_computation | async-start | bytes 1048576 | tf_op jit(solution)/shard_map/all_to_all | solution.py:84
  26.9 4.5 %fusion.92 = f32[2,4,512,384]{3,2,1,0:T(8,128)} fusion(bf16[2,4,512,128]{3,2,1,0:T(8,128)(2,1)S(1)} %fusion.8, bf16[3,3,384,128]{3,2,1,0:T(8,128)(2,1)} %param.12), kind=kOutput, calls=%fused_computation.139 | convolution fusion | flops 402653184 | bytes 7438336 | tf_op jit(solution)/shard_map/...hwo,io->...hwi/dot_general | solution.py:66
  33.6 3.6 %fusion.42 = f32[2,4,512,384]{3,2,1,0:T(8,128)} fusion(bf16[2,6,514,128]{3,2,1,0:T(8,128)(2,1)S(1)} %fusion.13, bf16[3,3,384,128]{3,2,1,0:T(8,128)(2,1)S(1)} %copy-done.13), kind=kOutput, calls=%fused_computation.81 | convolution fusion | flops 402653184 | bytes 7438336 | tf_op jit(solution)/shard_map/...hwo,io->...hwi/dot_general | solution.py:66
  37.2 3.6 %fusion.45 = f32[2,4,512,384]{3,2,1,0:T(8,128)} fusion(bf16[2,6,514,128]{3,2,1,0:T(8,128)(2,1)S(1)} %fusion.13, bf16[3,3,384,128]{3,2,1,0:T(8,128)(2,1)S(1)} %copy-done.13), kind=kOutput, calls=%fused_computation.84 | convolution fusion | flops 402653184 | bytes 7438336 | tf_op jit(solution)/shard_map/...hwo,io->...hwi/dot_general | solution.py:66
  40.8 3.6 %fusion.48 = f32[2,4,512,384]{3,2,1,0:T(8,128)} fusion(bf16[2,6,514,128]{3,2,1,0:T(8,128)(2,1)S(1)} %fusion.13, bf16[3,3,384,128]{3,2,1,0:T(8,128)(2,1)S(1)} %copy-done.13), kind=kOutput, calls=%fused_computation.87 | convolution fusion | flops 402653184 | bytes 7438336 | tf_op jit(solution)/shard_map/...hwo,io->...hwi/dot_general | solution.py:66
  44.4 3.7 %fusion.51 = f32[2,4,512,384]{3,2,1,0:T(8,128)} fusion(bf16[2,6,514,128]{3,2,1,0:T(8,128)(2,1)S(1)} %fusion.13, bf16[3,3,384,128]{3,2,1,0:T(8,128)(2,1)S(1)} %copy-done.13), kind=kOutput, calls=%fused_computation.90 | convolution fusion | flops 402653184 | bytes 7438336 | tf_op jit(solution)/shard_map/...hwo,io->...hwi/dot_general | solution.py:66
  48.1 3.7 %fusion.54 = f32[2,4,512,384]{3,2,1,0:T(8,128)} fusion(bf16[2,6,514,128]{3,2,1,0:T(8,128)(2,1)S(1)} %fusion.13, bf16[3,3,384,128]{3,2,1,0:T(8,128)(2,1)S(1)} %copy-done.13), kind=kOutput, calls=%fused_computation.93 | convolution fusion | flops 402653184 | bytes 7438336 | tf_op jit(solution)/shard_map/...hwo,io->...hwi/dot_general | solution.py:66
  51.8 3.6 %fusion.15 = f32[2,4,512,384]{3,2,1,0:T(8,128)} fusion(bf16[2,1,512,128]{3,2,1,0:T(8,128)(2,1)S(1)} %collective-permute-done.1, bf16[2,4,512,128]{3,2,1,0:T(8,128)(2,1)S(1)} %fusion.8, bf16[3,3,384,128]{3,2,1,0:T(8,128)(2,1)S(1)} %copy-done.13), kind=kOutput, calls=%fused_computation.33 | convolution fusion | flops 405274624 | bytes 7700480 | tf_op jit(solution)/shard_map/...hwo,io->...hwi/dot_general | solution.py:66
  55.3 3.6 %fusion.19 = f32[2,4,512,384]{3,2,1,0:T(8,128)} fusion(bf16[2,4,512,128]{3,2,1,0:T(8,128)(2,1)S(1)} %fusion.8, bf16[2,1,512,128]{3,2,1,0:T(8,128)(2,1)S(1)} %copy-done.11, bf16[3,3,384,128]{3,2,1,0:T(8,128)(2,1)S(1)} %copy-done.13), kind=kOutput, calls=%fused_computation.37 | convolution fusion | flops 405274624 | bytes 7700480 | tf_op jit(solution)/shard_map/...hwo,io->...hwi/dot_general | solution.py:66
  58.9 19.6 %add_add_fusion = f32[2,4,512,384]{3,2,1,0:T(8,128)} fusion(f32[2,4,512,384]{3,2,1,0:T(8,128)} %fusion.19, f32[2,4,512,384]{3,2,1,0:T(8,128)} %fusion.42, f32[2,4,512,384]{3,2,1,0:T(8,128)} %fusion.45, f32[2,4,512,384]{3,2,1,0:T(8,128)} %fusion.92, f32[2,4,512,384]{3,2,1,0:T(8,128)} %fusion.48, f32[2,4,512,384]{3,2,1,0:T(8,128)} %fusion.51, ...), kind=kOutput, calls=%fused_computation | convolution fusion | flops 415236096 | bytes 57769984 | tf_op jit(solution)/shard_map/...hwo,io->...hwi/dot_general | solution.py:66
  78.5 4.4 %slice.200 = f32[2,4,512,256]{3,2,1,0:T(8,128)} slice(f32[2,4,512,384]{3,2,1,0:T(8,128)} %add_add_fusion), slice={[0:2], [0:4], [0:512], [0:256]} | slice | bytes 8388608 | tf_op jit(solution)/shard_map/slice | solution.py:99
  83.0 5.9 %reshape.25 = f32[2,2,2,256,2,256]{5,4,3,2,1,0:T(2,128)} reshape(f32[2,4,512,256]{3,2,1,0:T(8,128)} %slice.200) | data formatting | bytes 8388608 | tf_op jit(solution)/shard_map/reshape | solution.py:33
  88.9 6.2 %reduce_sum.11 = f32[2,2,256,256]{3,2,1,0:T(8,128)} reduce(f32[2,2,2,256,2,256]{5,4,3,2,1,0:T(2,128)} %reshape.25, f32[]{:T(128)} %constant.2.clone.1), dimensions={2,4}, to_apply=%region_0.1 | reduce | flops 786432 | bytes 5242884 | tf_op jit(solution)/shard_map/reduce_sum | solution.py:33
  97.6 5.1 %all-to-all-start.2 = ((bf16[2,16,256,32]{2,3,0,1:T(8,128)(2,1)}), bf16[2,16,256,32]{2,3,0,1:T(8,128)(2,1)}, u32[]{:S(2)}, u32[]{:S(2)}) async-start(bf16[2,16,256,32]{2,3,0,1:T(8,128)(2,1)} %copy.133), calls=%async_computation.2 | async-start | bytes 1048576 | tf_op jit(solution)/shard_map/all_to_all | solution.py:83
  111.5 3.7 %convert_element_type.68 = bf16[2,4,256,256]{3,1,2,0:T(4,128)(2,1)} reshape(bf16[2,2,2,256,256]{4,2,1,3,0:T(2,128)(2,1)} %broadcast_in_dim.6) | data formatting | bytes 2097152 | tf_op jit(solution)/shard_map/convert_element_type | solution.py:87
  118.3 4.3 %copy.131 = bf16[2,4,512,256]{2,3,1,0:T(8,128)(2,1)} copy(bf16[2,4,512,256]{3,1,2,0:T(4,128)(2,1)} %bitcast.308) | data formatting | bytes 4194304 | tf_op jit(solution)/shard_map/convert_element_type | solution.py:87
  122.6 3.7 %convolution_bitcast_fusion.12 = f32[1,384,128]{2,1,0:T(8,128)} fusion(bf16[2,6,514,128]{3,2,1,0:T(8,128)(2,1)S(1)} %fusion.13, bf16[2,4,512,128]{2,3,1,0:T(8,128)(2,1)} %copy.132, bf16[2,4,512,256]{2,3,1,0:T(8,128)(2,1)} %copy.131), kind=kOutput, calls=%fused_computation.57 | convolution fusion | flops 408944640 | bytes 4390912 | tf_op jit(solution)/shard_map/...hwi,...hwo->io/dot_general | solution.py:52
  135.4 6.6 %collective-permute-start.3 = (bf16[2,1,256,256]{3,2,1,0:T(8,128)(2,1)}, bf16[2,1,256,256]{3,2,1,0:T(8,128)(2,1)}, u32[]{:S(2)}, u32[]{:S(2)}) collective-permute-start(bf16[2,1,256,256]{3,2,1,0:T(8,128)(2,1)} %get-tuple-element.31), channel_id=1, source_target_pairs={{1,0},{2,1},{3,2},{4,3},{5,4},{6,5},{7,6},{8,7},{9,8},{10,9},{11,1... | collective-permute-start | bytes 786440 | tf_op jit(solution)/shard_map/ppermute | solution.py:17
  153.2 4.0 %collective-permute-done.2 = bf16[2,1,256,256]{3,2,1,0:T(8,128)(2,1)S(1)} collective-permute-done((bf16[2,1,256,256]{3,2,1,0:T(8,128)(2,1)}, bf16[2,1,256,256]{3,2,1,0:T(8,128)(2,1)S(1)}, u32[]{:S(2)}, u32[]{:S(2)}) %collective-permute-start.2) | collective-permute-done | bytes 262176 | tf_op jit(solution)/shard_map/ppermute | solution.py:14
  177.7 3.5 %all-to-all-start.1 = ((bf16[2,2,256,256]{2,1,0,3:T(2,128)(2,1)}), bf16[2,2,256,256]{2,1,0,3:T(2,128)(2,1)S(1)}, u32[]{:S(2)}, u32[]{:S(2)}) async-start(bf16[2,2,256,256]{2,1,0,3:T(2,128)(2,1)} %copy.126), calls=%async_computation.1 | async-start | bytes 1048576 | tf_op jit(solution)/shard_map/all_to_all | solution.py:105
  184.0 7.8 %all-to-all-done.1 = bf16[2,2,256,256]{2,1,0,3:T(2,128)(2,1)S(1)} async-done(((bf16[2,2,256,256]{2,1,0,3:T(2,128)(2,1)}), bf16[2,2,256,256]{2,1,0,3:T(2,128)(2,1)S(1)}, u32[]{:S(2)}, u32[]{:S(2)}) %all-to-all-start.1) | async-done | bytes 524320 | tf_op jit(solution)/shard_map/all_to_all | solution.py:105
  192.6 132.9 %all-reduce.5.cloned.1.call-done = (f32[3,3,384,128]{3,2,1,0:T(8,128)}, f32[3,3,256,256]{2,3,1,0:T(8,128)}) async-done(((f32[3,3,384,128]{3,2,1,0:T(8,128)}, f32[3,3,256,256]{2,3,1,0:T(8,128)}), (f32[3,3,384,128]{3,2,1,0:T(8,128)}, f32[3,3,256,256]{2,3,1,0:T(8,128)})) %all-reduce.5.cloned.1.call-update) | async-done | bytes 4128784 | tf_op jit(solution)/shard_map/psum | solution.py:94
  (110 shorter events, 72.4 us)
Async XLA Ops:
  7.2 12.2 %copy-start.14 = (bf16[2,16,256,32]{2,3,1,0:T(8,128)(2,1)S(1)}, bf16[2,16,256,32]{2,3,1,0:T(8,128)(2,1)}, u32[]{:S(2)}) copy-start(bf16[2,16,256,32]{2,3,1,0:T(8,128)(2,1)} %param.8) | copy-start | bytes 1572868
  9.6 16.0 %copy-start.5 = (bf16[2,4,512,128]{3,2,1,0:T(8,128)(2,1)S(1)}, bf16[2,4,512,128]{3,2,1,0:T(8,128)(2,1)}, u32[]{:S(2)}) copy-start(bf16[2,4,512,128]{3,2,1,0:T(8,128)(2,1)} %param.9) | copy-start | bytes 3145732
  10.4 20.9 %collective-permute-start = (bf16[2,1,512,128]{3,2,1,0:T(8,128)(2,1)}, bf16[2,1,512,128]{3,2,1,0:T(8,128)(2,1)S(1)}, u32[]{:S(2)}, u32[]{:S(2)}) collective-permute-start(bf16[2,1,512,128]{3,2,1,0:T(8,128)(2,1)} %get-tuple-element.29), channel_id=1, source_target_pairs={{0,1},{1,2},{2,3},{3,4},{4,5},{5,6},{6,7},{7,8},{8,9},{9,10},{10,1... | collective-permute-start | bytes 786440 | tf_op jit(solution)/shard_map/ppermute | solution.py:14
  14.4 17.7 %collective-permute-start.1 = (bf16[2,1,512,128]{3,2,1,0:T(8,128)(2,1)}, bf16[2,1,512,128]{3,2,1,0:T(8,128)(2,1)S(1)}, u32[]{:S(2)}, u32[]{:S(2)}) collective-permute-start(bf16[2,1,512,128]{3,2,1,0:T(8,128)(2,1)} %get-tuple-element.28), channel_id=1, source_target_pairs={{1,0},{2,1},{3,2},{4,3},{5,4},{6,5},{7,6},{8,7},{9,8},{10,9},{11,1... | collective-permute-start | bytes 786440 | tf_op jit(solution)/shard_map/ppermute | solution.py:17
  20.2 77.5 %all-to-all-start = ((bf16[2,16,256,32]{2,3,0,1:T(8,128)(2,1)}), bf16[2,16,256,32]{2,3,0,1:T(8,128)(2,1)S(1)}, u32[]{:S(2)}, u32[]{:S(2)}) async-start(bf16[2,16,256,32]{2,3,0,1:T(8,128)(2,1)} %copy.117), calls=%async_computation | async-start | bytes 1048576 | tf_op jit(solution)/shard_map/all_to_all | solution.py:84
  31.4 2.2 copy-start.13
  32.1 19.7 %copy-start.8 = (bf16[2,1,512,128]{3,2,1,0:T(8,128)(2,1)}, bf16[2,1,512,128]{3,2,1,0:T(8,128)(2,1)S(1)}, u32[]{:S(2)}) copy-start(bf16[2,1,512,128]{3,2,1,0:T(8,128)(2,1)S(1)} %collective-permute-done.1) | copy-start | bytes 786436
  51.8 3.6 %copy-start.11 = (bf16[2,1,512,128]{3,2,1,0:T(8,128)(2,1)S(1)}, bf16[2,1,512,128]{3,2,1,0:T(8,128)(2,1)}, u32[]{:S(2)}) copy-start(bf16[2,1,512,128]{3,2,1,0:T(8,128)(2,1)} %copy-done.10) | copy-start | bytes 786436
  97.6 46.1 %all-to-all-start.2 = ((bf16[2,16,256,32]{2,3,0,1:T(8,128)(2,1)}), bf16[2,16,256,32]{2,3,0,1:T(8,128)(2,1)}, u32[]{:S(2)}, u32[]{:S(2)}) async-start(bf16[2,16,256,32]{2,3,0,1:T(8,128)(2,1)} %copy.133), calls=%async_computation.2 | async-start | bytes 1048576 | tf_op jit(solution)/shard_map/all_to_all | solution.py:83
  102.7 222.9 %all-reduce.5.cloned.1.call-start = ((), (), s32[]{:S(2)}) async-start(), calls=%async_computation.3 | async-start | bytes 8257536 | tf_op jit(solution)/shard_map/psum | solution.py:94
  122.6 3.7 %copy-start.2 = (bf16[2,4,512,256]{2,3,1,0:T(8,128)(2,1)S(1)}, bf16[2,4,512,256]{2,3,1,0:T(8,128)(2,1)}, u32[]{:S(2)}) copy-start(bf16[2,4,512,256]{2,3,1,0:T(8,128)(2,1)} %copy.131) | copy-start | bytes 6291460
  122.6 3.7 %copy-start.6 = (bf16[2,4,512,128]{2,3,1,0:T(8,128)(2,1)S(1)}, bf16[2,4,512,128]{2,3,1,0:T(8,128)(2,1)}, u32[]{:S(2)}) copy-start(bf16[2,4,512,128]{2,3,1,0:T(8,128)(2,1)} %copy.132) | copy-start | bytes 3145732
  135.4 17.7 %collective-permute-start.3 = (bf16[2,1,256,256]{3,2,1,0:T(8,128)(2,1)}, bf16[2,1,256,256]{3,2,1,0:T(8,128)(2,1)}, u32[]{:S(2)}, u32[]{:S(2)}) collective-permute-start(bf16[2,1,256,256]{3,2,1,0:T(8,128)(2,1)} %get-tuple-element.31), channel_id=1, source_target_pairs={{1,0},{2,1},{3,2},{4,3},{5,4},{6,5},{7,6},{8,7},{9,8},{10,9},{11,1... | collective-permute-start | bytes 786440 | tf_op jit(solution)/shard_map/ppermute | solution.py:17
  143.7 5.2 %copy-start.3 = (bf16[2,4,512,256]{2,3,1,0:T(8,128)(2,1)S(1)}, bf16[2,4,512,256]{2,3,1,0:T(8,128)(2,1)}, u32[]{:S(2)}) copy-start(bf16[2,4,512,256]{2,3,1,0:T(8,128)(2,1)} %copy.131) | copy-start | bytes 6291460
  143.7 5.2 %copy-start.7 = (bf16[2,4,512,128]{2,3,1,0:T(8,128)(2,1)S(1)}, bf16[2,4,512,128]{2,3,1,0:T(8,128)(2,1)}, u32[]{:S(2)}) copy-start(bf16[2,4,512,128]{2,3,1,0:T(8,128)(2,1)} %copy.132) | copy-start | bytes 3145732
  143.7 5.2 %copy-start.12 = (bf16[2,1,512,128]{3,2,1,0:T(8,128)(2,1)S(1)}, bf16[2,1,512,128]{3,2,1,0:T(8,128)(2,1)}, u32[]{:S(2)}) copy-start(bf16[2,1,512,128]{3,2,1,0:T(8,128)(2,1)} %copy-done.10) | copy-start | bytes 786436
  144.9 12.3 %collective-permute-start.2 = (bf16[2,1,256,256]{3,2,1,0:T(8,128)(2,1)}, bf16[2,1,256,256]{3,2,1,0:T(8,128)(2,1)S(1)}, u32[]{:S(2)}, u32[]{:S(2)}) collective-permute-start(bf16[2,1,256,256]{3,2,1,0:T(8,128)(2,1)} %get-tuple-element.30), channel_id=1, source_target_pairs={{0,1},{1,2},{2,3},{3,4},{4,5},{5,6},{6,7},{7,8},{8,9},{9,10},{10,1... | collective-permute-start | bytes 786440 | tf_op jit(solution)/shard_map/ppermute | solution.py:14
  148.9 1.1 copy-start.9
  150.1 1.1 copy-start.17
  150.1 1.2 copy-start.18
  150.1 1.3 copy-start.19
  168.9 1.3 copy-start.1
  177.7 14.1 %all-to-all-start.1 = ((bf16[2,2,256,256]{2,1,0,3:T(2,128)(2,1)}), bf16[2,2,256,256]{2,1,0,3:T(2,128)(2,1)S(1)}, u32[]{:S(2)}, u32[]{:S(2)}) async-start(bf16[2,2,256,256]{2,1,0,3:T(2,128)(2,1)} %copy.126), calls=%async_computation.1 | async-start | bytes 1048576 | tf_op jit(solution)/shard_map/all_to_all | solution.py:105
  325.6 3.2 copy-start.4
  (6 other events, 5.6 us)
Sparse Core Ops, SparseCore 0:
  169.0 156.5 all-reduce.4
where the time goes:
time: 338 us; the launch traced here: 337 us
  waiting for transfers between devices  145 us (43%)
  matrix products  81.5 us (24%)
  local copies, waits for them, and re-layouts  47.9 us (14%)
  starting transfers between devices  29.7 us (9%)
  other arithmetic  18.4 us (5%)
  between operations  14.5 us (4%)
    psum x1, waiting for transfers between devices, shards(): lax.psum(tap_grads(stacked, fine_pad) * (1.0 / math.sqrt(fine_cells)), ('...  133 us
    dot_general x18, matrix products, tap_back(): jnp.einsum('...hwo,io->...hwi', window, kernel[vertical, lateral], prefer...  61.8 us
    dot_general x18, matrix products, tap_grads(): jnp.einsum('...hwi,...hwo->io', inputs, window, preferred_element_type=jn...  19.7 us
    ppermute x2, starting transfers between devices, extended(): lax.ppermute(lax.slice_in_dim(block, 0, width, axis=dim), axis, backward)  11.5 us
    unnamed x49, local copies, waits for them, and re-layouts  10.3 us
    convert_element_type x3, local copies, waits for them, and re-layouts, shards(): upsampled = upsample(jax.nn.silu(pre_value)).astype(jnp.bfloat16)  8.49 us
    all_to_all x1, waiting for transfers between devices, shards(): lax.all_to_all(strip_back, 'chan', split_axis=3, concat_axis=1, tiled=True)  7.77 us
  transfers between devices with their start and end apart: 8, of which 3 were waited for; matrix products, arithmetic and copies ran while one was open for 38% of the time, Pallas kernels for 0%

commit v1 on v0

v1 whole, which is shorter than its diff:
```python
import functools
import math

import jax
import jax.numpy as jnp
from jax import lax
from jax.experimental import pallas as pl
from jax.experimental.pallas import tpu as pltpu
from jax.sharding import Mesh
from jax.sharding import PartitionSpec as P

F32 = jnp.float32
BF16 = jnp.bfloat16
MIB = 1 << 20
VMEM = 28

SPLIT = (("xh", 2), ("z", 4), ("core", 2), ("y", 4), ("xl", 2))
ROWS = ("xh", "z", "core")
CHAN = ("y", "xl")
ALL = ROWS + CHAN
CHIPS = ("xh", "xl", "z", "y")


def params(limit):
    return pltpu.CompilerParams(vmem_limit_bytes=limit * MIB)


def cost(flops, nbytes):
    return pl.CostEstimate(flops=int(flops), bytes_accessed=int(nbytes), transcendentals=0)


def silu_grad(value):
    sigma = jax.nn.sigmoid(value)
    return sigma * (1.0 + value * (1.0 - sigma))


def shifted(field):
    extent = field.shape[0]
    index = lax.broadcasted_iota(jnp.int32, field.shape, 0)
    before = jnp.where(index == 0, 0.0, pltpu.roll(field, 1, 0))
    after = jnp.where(index == extent - 1, 0.0, pltpu.roll(field, extent - 1, 0))
    return before, after


def tdot(left, right):
    return lax.dot_general(left, right, (((0,), (0,)), ((), ())), preferred_element_type=F32)


def dott(left, right):
    return lax.dot_general(left, right, (((1,), (1,)), ((), ())), preferred_element_type=F32)


def tiles(block):
    return block.astype(BF16).reshape(block.shape[0] // 16, 16, block.shape[1])


def box_kernel(
    cot_ref, pre_ref, low_ref, high_ref, weight_ref, grad_ref, pooled_ref, box_ref, rows32, up_weight
):
    sample = pl.program_id(0)
    c3 = cot_ref.shape[-1]
    c4 = pooled_ref.shape[-1]
    half = pooled_ref.shape[-2]

    @pl.when(sample == 0)
    def _():
        for dy in range(3):
            for d in range(3):
                at = (dy * 3 + d) * c3
                up_weight[at : at + c3, :] = weight_ref[2 - dy, 2 - d, :c4, :].astype(F32).T.astype(BF16)

    for v in range(6):
        if v == 0:
            grad = low_ref[0]
        elif v == 5:
            grad = high_ref[0]
        else:
            grad = cot_ref[0, v - 1].astype(F32) * silu_grad(pre_ref[0, v - 1].astype(F32))
            grad = grad.astype(BF16)
        grad_ref[0, v] = grad
        rows32[v] = grad.astype(F32)

    for v in range(5):
        even = rows32[v, pl.ds(0, half, 2), :] + rows32[v + 1, pl.ds(0, half, 2), :]
        odd = rows32[v, pl.ds(1, half, 2), :] + rows32[v + 1, pl.ds(1, half, 2), :]
        before, _ = shifted(odd)
        _, after = shifted(even)
        sums = ((before + even).astype(BF16), (even + odd).astype(BF16), (odd + after).astype(BF16))
        for i in range(2):
            dy = v - 2 * i
            if 0 <= dy <= 2:
                for d in range(3):
                    at = (dy * 3 + d) * c3
                    box_ref[0, i * half : (i + 1) * half, at : at + c3] = sums[d]

    pooled = jnp.dot(box_ref[0], up_weight[...], preferred_element_type=F32)
    pooled_ref[0] = pooled.reshape(pooled_ref.shape[1:])


def box_level(cot, pre, low, high, weight, cs):
    samples, height, wide, c3 = cot.shape
    c4 = weight.shape[2] - cs
    half = wide // 2
    block = pl.BlockSpec((1, height, wide, c3), lambda s: (s, 0, 0, 0))
    edge = pl.BlockSpec((1, wide, c3), lambda s: (s, 0, 0))
    return pl.pallas_call(
        box_kernel,
        grid=(samples,),
        in_specs=[block, block, edge, edge, pl.BlockSpec(weight.shape, lambda s: (0, 0, 0, 0))],
        out_specs=[
            pl.BlockSpec((1, height + 2, wide, c3), lambda s: (s, 0, 0, 0)),
            pl.BlockSpec((1, 2, half, c4), lambda s: (s, 0, 0, 0)),
            pl.BlockSpec((1, 2 * half, 9 * c3), lambda s: (s, 0, 0)),
        ],
        out_shape=[
            jax.ShapeDtypeStruct((samples, height + 2, wide, c3), BF16),
            jax.ShapeDtypeStruct((samples, 2, half, c4), F32),
            jax.ShapeDtypeStruct((samples, 2 * half, 9 * c3), BF16),
        ],
        scratch_shapes=[pltpu.VMEM((6, wide, c3), F32), pltpu.VMEM((9 * c3, c4), BF16)],
        compiler_params=params(VMEM),
        cost_estimate=cost(1.5e9, 8e6),
        name="box_level",
    )(cot, pre, low, high, weight)


def fine_kernel(
    core_ref, grad_ref, skip_ref, weight_ref, pre_ref, box_ref,
    grad_skip_ref, keep_ref, send_ref,
    taps, skip_weight, total, up_total, *, scale,
):
    sample = pl.program_id(0)
    c3 = grad_ref.shape[-1]
    cs = skip_ref.shape[-1]
    c4 = weight_ref.shape[2] - cs
    half = pre_ref.shape[-1]

    @pl.when(sample == 0)
    def _():
        total[...] = jnp.zeros_like(total)
        up_total[...] = jnp.zeros_like(up_total)
        for u in range(4):
            for d in range(3):
                at = (u * 3 + d) * c3
                for t in range(2):
                    dy = u - t
                    if 0 <= dy <= 2:
                        block = weight_ref[2 - dy, 2 - d, c4:, :].astype(F32).T.astype(BF16)
                    else:
                        block = jnp.zeros((c3, cs), BF16)
                    skip_weight[at : at + c3, t * cs : (t + 1) * cs] = block

    for i in range(2):
        value = pre_ref[:, 0, 0, i].reshape(c4, half).astype(F32)
        value = (value * jax.nn.sigmoid(value)).astype(BF16)
        up_total[...] += jnp.dot(value, box_ref[0, i * half : (i + 1) * half, :], preferred_element_type=F32)

    for v in range(6):
        grad = grad_ref[0, v]
        before, after = shifted(grad.astype(F32))
        at = v * 3 * c3
        taps[:, at : at + c3] = before.astype(BF16)
        taps[:, at + c3 : at + 2 * c3] = grad
        taps[:, at + 2 * c3 : at + 3 * c3] = after.astype(BF16)

    for pair in range(2):
        window = taps[:, 2 * pair * 3 * c3 : (2 * pair + 4) * 3 * c3]
        back = jnp.dot(window, skip_weight[...], preferred_element_type=F32)
        grad_skip_ref[0, 2 * pair] = back[:, :cs].astype(BF16)
        grad_skip_ref[0, 2 * pair + 1] = back[:, cs:].astype(BF16)
        feats = jnp.concatenate([skip_ref[0, 2 * pair], skip_ref[0, 2 * pair + 1]], axis=1)
        total[...] += tdot(feats, window)

    @pl.when(sample == pl.num_programs(0) - 1)
    def _():
        core = core_ref[0]

        def put(tap, at, value):
            part = value.shape[0] // 2
            low, high = value[:part], value[part:]
            keep_ref[tap, at : at + part // 16] = tiles(jnp.where(core == 0, low, high))
            send_ref[tap, at : at + part // 16] = tiles(jnp.where(core == 0, high, low))

        for dy in range(3):
            for d in range(3):
                first = (dy * 3 + d) * c3
                second = ((dy + 1) * 3 + d) * c3
                tap = (2 - dy) * 3 + 2 - d
                put(tap, 0, up_total[:, first : first + c3] * scale)
                value = total[:cs, first : first + c3] + total[cs:, second : second + c3]
                put(tap, c4 // 32, value * scale)


def fine_level(core, grad, skip, weight, received, box, fine_cells):
    samples, height, wide, cs = skip.shape
    c3 = grad.shape[-1]
    c4 = weight.shape[2] - cs
    half = wide // 2
    peers, own = received.shape[0], received.shape[-2]
    part = jax.ShapeDtypeStruct((9, (c4 + cs) // 32, 16, c3), BF16)
    whole = pl.BlockSpec(part.shape, lambda s: (0, 0, 0, 0))
    return pl.pallas_call(
        functools.partial(fine_kernel, scale=1.0 / math.sqrt(fine_cells)),
        grid=(samples,),
        in_specs=[
            pl.BlockSpec(memory_space=pltpu.SMEM),
            pl.BlockSpec((1, height + 2, wide, c3), lambda s: (s, 0, 0, 0)),
            pl.BlockSpec((1, height, wide, cs), lambda s: (s, 0, 0, 0)),
            pl.BlockSpec(weight.shape, lambda s: (0, 0, 0, 0)),
            pl.BlockSpec((peers, 1, 1, 2, own, half), lambda s: (0, 0, s, 0, 0, 0)),
            pl.BlockSpec((1, 2 * half, 9 * c3), lambda s: (s, 0, 0)),
        ],
        out_specs=[pl.BlockSpec((1, height, wide, cs), lambda s: (s, 0, 0, 0)), whole, whole],
        out_shape=[jax.ShapeDtypeStruct((samples, height, wide, cs), BF16), part, part],
        scratch_shapes=[
            pltpu.VMEM((wide, 18 * c3), BF16),
            pltpu.VMEM((12 * c3, 2 * cs), BF16),
            pltpu.VMEM((2 * cs, 12 * c3), F32),
            pltpu.VMEM((c4, 9 * c3), F32),
        ],
        compiler_params=params(VMEM),
        cost_estimate=cost(6e9, 12e6),
        name="fine_level",
    )(core, grad, skip, weight, received, box)


def coarse_grad_kernel(pooled_ref, pre_ref, first_ref, second_ref):
    channels, wide = pooled_ref.shape[-1], pooled_ref.shape[-2]
    for i, out_ref in enumerate((first_ref, second_ref)):
        value = pre_ref[:, 0, 0, i].reshape(channels, wide).astype(F32).T
        out_ref[0] = (pooled_ref[0, i] * silu_grad(value)).astype(BF16)


def coarse_grad(pooled, received):
    samples, _, wide, c4 = pooled.shape
    peers, _, _, _, own, _ = received.shape
    out = jax.ShapeDtypeStruct((samples, wide, c4), BF16)
    spec = pl.BlockSpec((1, wide, c4), lambda s: (s, 0, 0))
    return pl.pallas_call(
        coarse_grad_kernel,
        grid=(samples,),
        in_specs=[
            pl.BlockSpec((1, 2, wide, c4), lambda s: (s, 0, 0, 0)),
            pl.BlockSpec((peers, 1, 1, 2, own, wide), lambda s: (0, 0, s, 0, 0, 0)),
        ],
        out_specs=[spec, spec],
        out_shape=[out, out],
        compiler_params=params(VMEM),
        cost_estimate=cost(2e7, 2e6),
        name="coarse_grad",
    )(pooled, received)


def fill_coarse_taps(rows, taps):
    wide, c4 = rows[0].shape
    for v, row in enumerate(rows):
        value = row.astype(F32)
        before, after = shifted(value)
        taps[v * wide : (v + 1) * wide, :c4] = before.astype(BF16)
        taps[v * wide : (v + 1) * wide, c4 : 2 * c4] = row
        taps[v * wide : (v + 1) * wide, 2 * c4 :] = after.astype(BF16)


def coarse_weight_kernel(
    core_ref, input_ref, low_ref, first_ref, second_ref, high_ref, keep_ref, send_ref, taps, total, *, scale
):
    sample = pl.program_id(0)
    wide = input_ref.shape[-1]
    c4 = input_ref.shape[0] * input_ref.shape[-2]

    @pl.when(sample == 0)
    def _():
        total[...] = jnp.zeros_like(total)

    fill_coarse_taps((low_ref[0], first_ref[0], second_ref[0], high_ref[0]), taps)
    values = jnp.concatenate([input_ref[:, 0, 0, i].reshape(c4, wide) for i in range(2)], axis=1)
    for dy in range(3):
        total[dy] += jnp.dot(values, taps[dy * wide : (dy + 2) * wide, :], preferred_element_type=F32)

    @pl.when(sample == pl.num_programs(0) - 1)
    def _():
        core = core_ref[0]
        part = c4 // 2
        count = part // 16
        for dy in range(3):
            for d in range(3):
                for side in range(c4 // 128):
                    at = d * c4 + side * 128
                    value = total[dy, :, at : at + 128] * scale
                    low, high = value[:part], value[part:]
                    tap = ((2 - dy) * 3 + 2 - d) * (c4 // 128) + side
                    keep_ref[tap * count : (tap + 1) * count] = tiles(jnp.where(core == 0, low, high))
                    send_ref[tap * count : (tap + 1) * count] = tiles(jnp.where(core == 0, high, low))


def coarse_specs(samples, wide, c4):
    return [pl.BlockSpec((1, wide, c4), lambda s: (s, 0, 0))] * 4


def coarse_weight_level(core, received, rows, coarse_cells):
    peers, _, samples, _, own, wide = received.shape
    c4 = peers * own
    part = jax.ShapeDtypeStruct((9 * (c4 // 128) * (c4 // 32), 16, 128), BF16)
    whole = pl.BlockSpec(part.shape, lambda s: (0, 0, 0))
    return pl.pallas_call(
        functools.partial(coarse_weight_kernel, scale=1.0 / math.sqrt(coarse_cells)),
        grid=(samples,),
        in_specs=[
            pl.BlockSpec(memory_space=pltpu.SMEM),
            pl.BlockSpec((peers, 1, 1, 2, own, wide), lambda s: (0, 1, s, 0, 0, 0)),
        ] + coarse_specs(samples, wide, c4),
        out_specs=[whole, whole],
        out_shape=[part, part],
        scratch_shapes=[pltpu.VMEM((4 * wide, 3 * c4), BF16), pltpu.VMEM((3, c4, 3 * c4), F32)],
        compiler_params=params(VMEM),
        cost_estimate=cost(1.3e9, 3e6),
        name="coarse_weight_level",
    )(core, received, *rows)


def coarse_input_kernel(weight_ref, low_ref, first_ref, second_ref, high_ref, out_ref, taps):
    wide, c4 = low_ref.shape[1:]
    peers, own = out_ref.shape[0], out_ref.shape[-2]
    fill_coarse_taps((low_ref[0], first_ref[0], second_ref[0], high_ref[0]), taps)
    total = None
    for dy in range(3):
        for d in range(3):
            window = taps[dy * wide : (dy + 2) * wide, d * c4 : (d + 1) * c4]
            term = dott(weight_ref[2 - dy, 2 - d], window)
            total = term if total is None else total + term
    total = total.astype(BF16)
    for i in range(2):
        out_ref[:, 0, i] = total[:, i * wide : (i + 1) * wide].reshape(peers, own, wide)


def coarse_input_level(weight, rows, peers):
    samples, wide, c4 = rows[0].shape
    own = c4 // peers
    return pl.pallas_call(
        coarse_input_kernel,
        grid=(samples,),
        in_specs=[pl.BlockSpec(weight.shape, lambda s: (0, 0, 0, 0))] + coarse_specs(samples, wide, c4),
        out_specs=pl.BlockSpec((peers, 1, 2, own, wide), lambda s: (0, s, 0, 0, 0)),
        out_shape=jax.ShapeDtypeStruct((peers, samples, 2, own, wide), BF16),
        scratch_shapes=[pltpu.VMEM((4 * wide, 3 * c4), BF16)],
        compiler_params=params(VMEM),
        cost_estimate=cost(1.3e9, 3e6),
        name="coarse_input_level",
    )(weight, *rows)


def join_kernel(coarse_ref, coarse_more_ref, fine_ref, fine_more_ref, out_ref):
    count = coarse_ref.shape[0]
    out_ref[:count] = (coarse_ref[...].astype(F32) + coarse_more_ref[...].astype(F32)).astype(BF16)
    fines = fine_ref.shape[0]
    out_ref[count : count + fines] = (fine_ref[...].astype(F32) + fine_more_ref[...].astype(F32)).astype(BF16)
    rest = out_ref.shape[0] - count - fines
    if rest:
        out_ref[count + fines :] = jnp.zeros((rest,) + out_ref.shape[1:], BF16)


def sum_kernel(parts_ref, out_ref):
    total = parts_ref[0].astype(F32)
    for k in range(1, parts_ref.shape[0]):
        total = total + parts_ref[k].astype(F32)
    total = total.astype(BF16)
    for k in range(out_ref.shape[0]):
        out_ref[k] = total


def unpack_kernel(core_ref, mine_ref, other_ref, fine_ref, coarse_ref):
    c4 = coarse_ref.shape[-1]
    cs = fine_ref.shape[-2] - c4
    sides = c4 // 128
    lines = c4 // 32
    skips = cs // 32
    mine = core_ref[0]
    for core in range(2):

        def take(at, count):
            block = jnp.where(mine == core, mine_ref[at : at + count].astype(F32), other_ref[at : at + count].astype(F32))
            return block.reshape(count * 16, 128)

        for tap in range(9):
            for side in range(sides):
                block = take((tap * sides + side) * lines, lines)
                coarse_ref[tap, core * lines * 16 : (core + 1) * lines * 16, side * 128 : (side + 1) * 128] = block
            at = 9 * sides * lines + tap * (lines + skips)
            fine_ref[tap, core * lines * 16 : (core + 1) * lines * 16, :] = take(at, lines)
            fine_ref[tap, c4 + core * skips * 16 : c4 + (core + 1) * skips * 16, :] = take(at + lines, skips)


SWAP = ((0, 1), (1, 0))


def grad_sums(fine_keep, fine_more, coarse_keep, coarse_more):
    chips = 1
    for axis in CHIPS:
        chips *= lax.axis_size(axis)
    fine_keep, fine_more = (a.reshape((-1, 16, 128)) for a in (fine_keep, fine_more))
    count = coarse_keep.shape[0] + fine_keep.shape[0]
    each = -(-count // chips)
    joined = pl.pallas_call(
        join_kernel,
        out_shape=jax.ShapeDtypeStruct((chips * each, 16, 128), BF16),
        compiler_params=params(VMEM),
        cost_estimate=cost(1e6, 3e6),
        name="join",
    )(coarse_keep, coarse_more, fine_keep, fine_more)
    parts = lax.all_to_all(joined.reshape(chips, each, 16, 128), CHIPS, 0, 0, tiled=True)
    summed = pl.pallas_call(
        sum_kernel,
        out_shape=jax.ShapeDtypeStruct((chips, each, 16, 128), BF16),
        compiler_params=params(VMEM),
        cost_estimate=cost(1e6, 1.3e6),
        name="sum_parts",
    )(parts)
    return lax.all_to_all(summed, CHIPS, 0, 0, tiled=True).reshape(chips * each, 16, 128)


def unpacked(core, mine, other, fine_shape, coarse_shape):
    fine_flat = (9,) + fine_shape[2:]
    coarse_flat = (9,) + coarse_shape[2:]
    vmem = pl.BlockSpec(memory_space=pltpu.VMEM)
    fine, coarse = pl.pallas_call(
        unpack_kernel,
        in_specs=[pl.BlockSpec(memory_space=pltpu.SMEM), vmem, vmem],
        out_shape=[jax.ShapeDtypeStruct(fine_flat, F32), jax.ShapeDtypeStruct(coarse_flat, F32)],
        compiler_params=params(VMEM),
        cost_estimate=cost(1e6, 6e6),
        name="unpack",
    )(core, mine, other)
    return fine.reshape(fine_shape), coarse.reshape(coarse_shape)


def edges(low, high):
    count = 1
    for axis in ALL:
        count *= lax.axis_size(axis)
    forward = [(i, i + 1) for i in range(count - 1)]
    backward = [(target, source) for source, target in forward]
    return lax.ppermute(high, ALL, forward), lax.ppermute(low, ALL, backward)


def shards(coarse_input, coarse_pre, skip_feats, fine_pre, fine_cotangent, fine_weight, coarse_weight):
    peers = 1
    for axis in CHAN:
        peers *= lax.axis_size(axis)
    devices = peers
    for axis in ROWS:
        devices *= lax.axis_size(axis)
    samples, lines, wide, own = coarse_input.shape
    core = lax.axis_index("core").astype(jnp.int32).reshape(1)

    def grad_row(line):
        return (
            fine_cotangent[:, line].astype(F32) * silu_grad(fine_pre[:, line].astype(F32))
        ).astype(BF16)

    top, bottom = grad_row(0), grad_row(-1)
    low, high = edges(top, bottom)
    both = jnp.stack([coarse_pre, coarse_input]).reshape(2, samples, peers, lines // peers, wide, own)
    both = both.transpose(2, 0, 1, 3, 5, 4)
    both, top, bottom = lax.optimization_barrier((both, top, bottom))
    received = lax.all_to_all(both, CHAN, 0, 0, tiled=True)

    cs = skip_feats.shape[-1]
    fine_cells = fine_pre.shape[0] * fine_pre.shape[1] * fine_pre.shape[2] * devices
    fine_grad, pooled, box = box_level(fine_cotangent, fine_pre, low, high, fine_weight, cs)
    first, second = coarse_grad(pooled, received)
    coarse_low, coarse_high = edges(first, second)
    grad_skip, fine_keep, fine_send = fine_level(
        core, fine_grad, skip_feats, fine_weight, received, box, fine_cells
    )
    fine_more = lax.ppermute(fine_send, "core", SWAP)
    rows = (coarse_low, first, second, coarse_high)
    coarse_cells = samples * (lines // peers) * wide * devices
    coarse_keep, coarse_send = coarse_weight_level(core, received, rows, coarse_cells)
    coarse_more = lax.ppermute(coarse_send, "core", SWAP)
    back = coarse_input_level(coarse_weight, rows, peers)
    mine = grad_sums(fine_keep, fine_more, coarse_keep, coarse_more)
    back, mine = lax.optimization_barrier((back, mine))
    other = lax.ppermute(mine, "core", SWAP)
    back = lax.all_to_all(back, CHAN, 0, 0, tiled=True)
    grad_input = back.transpose(1, 0, 2, 4, 3).reshape(coarse_input.shape)
    grad_fine, grad_coarse = unpacked(core, mine, other, fine_weight.shape, coarse_weight.shape)
    return grad_skip, grad_input, grad_fine, grad_coarse


def solution(mesh):
    split = Mesh(mesh.devices.reshape([size for _, size in SPLIT]), tuple(name for name, _ in SPLIT))
    coarse = P(None, ROWS, None, CHAN)
    fine = P(None, ALL, None, None)
    return jax.shard_map(
        shards,
        mesh=split,
        in_specs=(coarse, coarse, fine, fine, fine, P(), P()),
        out_specs=(fine, coarse, P(), P()),
        check_vma=False,
    )
```

time: 338 us -> 142 us (0.42)
  waiting for transfers between devices: 145 us -> 38.9 us
  matrix products: 81.5 us -> 0 us
  blocking collectives: 0 us -> 42 us
  local copies, waits for them, and re-layouts: 47.9 us -> 8.15 us
  Pallas kernels: 0 us -> 16.5 us
  other arithmetic: 18.4 us -> 2.75 us
  between operations: 14.5 us -> 0.81 us
    psum x1 -> x0, waiting for transfers between devices: 133 us -> none  [shards(): lax.psum(tap_grads(stacked, fine_pad) * (1.0 / math.sqrt(fine_cells)), ('...]
    dot_general x36 -> x0, matrix products: 81.5 us -> none  [the longest x18 61.8 us: tap_back(): jnp.einsum('...hwo,io->...hwi', window, kernel[vertical, lateral], prefer...]
    all_to_all x0 -> x2, blocking collectives: none -> 42 us  [the longest x1 29.6 us: grad_sums(): lax.all_to_all(joined.reshape(chips, each, 16, 128), CHIPS, 0, 0, tiled=T...]
    ppermute x4 -> x7, waiting for transfers between devices: 4.04 us -> 25.4 us  [the longest x4 23.8 us: edges(): return (lax.ppermute(high, ALL, forward), lax.ppermute(low, ALL, backward))]
    pallas_call x0 -> x8, Pallas kernels: none -> 16.5 us  [the longest x1 5.81 us: fine_level(): pl.pallas_call(functools.partial(fine_kernel, scale=1.0 / math.sqrt(fine_...]
    convert_element_type x7 -> x0, local copies, waits for them, and re-layouts: 13.3 us -> none  [the longest x3 8.49 us: shards(): upsampled = upsample(jax.nn.silu(pre_value)).astype(jnp.bfloat16)]
    slice x4 -> x0, local copies, waits for them, and re-layouts: 8.89 us -> none  [the longest x1 4.44 us: shards(): back[..., :channels]]
    reduce_sum x1 -> x0, other arithmetic: 6.19 us -> none  [pooling(): field.reshape(shape[:-3] + (shape[-3] // 2, 2, shape[-2] // 2, 2, shape[-...]
  transfers between devices with their start and end apart: 8 -> 9, of which waited for: 3 -> 6; matrix products, arithmetic and copies ran while one was open for 38% -> 1% of each run, Pallas kernels for 0% -> 7%
where the time goes in v1:
time: 142 us; the launch traced here: 141 us
  blocking collectives  42 us (30%)
  waiting for transfers between devices  38.9 us (27%)
  starting transfers between devices  32.1 us (23%)
  Pallas kernels  16.5 us (12%)
  local copies, waits for them, and re-layouts  8.15 us (6%)
  other arithmetic  2.75 us (2%)
    all_to_all x1, blocking collectives, grad_sums(): lax.all_to_all(joined.reshape(chips, each, 16, 128), CHIPS, 0, 0, tiled=T...  29.6 us
    ppermute x4, waiting for transfers between devices, edges(): return (lax.ppermute(high, ALL, forward), lax.ppermute(low, ALL, backward))  23.8 us
    ppermute x4, starting transfers between devices, edges(): return (lax.ppermute(high, ALL, forward), lax.ppermute(low, ALL, backward))  16.2 us
    all_to_all x1, waiting for transfers between devices, grad_sums(): lax.all_to_all(summed, CHIPS, 0, 0, tiled=True)  13.5 us
    all_to_all x1, blocking collectives, shards(): back = lax.all_to_all(back, CHAN, 0, 0, tiled=True)  12.4 us
    unnamed x28, local copies, waits for them, and re-layouts  7.32 us
    all_to_all x1, starting transfers between devices, shards(): received = lax.all_to_all(both, CHAN, 0, 0, tiled=True)  5.95 us
    pallas_call x1, Pallas kernels, fine_level(): pl.pallas_call(functools.partial(fine_kernel, scale=1.0 / math.sqrt(fine_...  5.81 us
  transfers between devices with their start and end apart: 9, of which 6 were waited for; matrix products, arithmetic and copies ran while one was open for 1% of the time, Pallas kernels for 7%

profile of v1, /device:TPU:1, one launch (start us, length us, event | category | flops | bytes accessed | tf_op | source)
XLA Modules:
  0.0 141.3 jit_solution(17587172377419254672)
XLA Ops:
  0.7 1.7 %fusion.13 = (bf16[2,512,128]{2,1,0:T(8,128)(2,1)S(1)}, bf16[2,512,128]{2,1,0:T(8,128)(2,1)S(1)}) fusion(bf16[2,4,512,128]{3,2,1,0:T(8,128)(2,1)} %pre_ref.1, bf16[2,4,512,128]{3,2,1,0:T(8,128)(2,1)} %cot_ref.1), kind=kLoop, calls=%fused_computation.19 | loop fusion | flops 2883584 | bytes 1572864 | tf_op jit(solution)/shard_map/convert_element_type | solution.py:458
  3.4 5.9 %all-to-all-start = ((bf16[8,2,2,2,32,256]{5,4,3,2,1,0:T(8,128)(2,1)}), bf16[8,2,2,2,32,256]{5,4,3,2,1,0:T(8,128)(2,1)S(1)}, u32[]{:S(2)}, u32[]{:S(2)}) async-start(bf16[8,2,2,2,32,256]{5,4,3,2,1,0:T(8,128)(2,1)} %copy_bitcast_fusion), calls=%async_computation | async-start | bytes 2097152 | tf_op jit(solution)/shard_map/all_to_all | solution.py:465
  9.4 6.6 %collective-permute-start.1 = (bf16[2,512,128]{2,1,0:T(8,128)(2,1)S(1)}, bf16[2,512,128]{2,1,0:T(8,128)(2,1)S(1)}, u32[]{:S(2)}, u32[]{:S(2)}) collective-permute-start(bf16[2,512,128]{2,1,0:T(8,128)(2,1)S(1)} %get-tuple-element.34), channel_id=1, source_target_pairs={{1,0},{2,1},{3,2},{4,3},{5,4},{6,5},{7,6},{8,7},{9,8},{10,9},{11,1... | collective-permute-start | bytes 786440 | tf_op jit(solution)/shard_map/ppermute | solution.py:442
  16.0 1.9 %collective-permute-start = (bf16[2,512,128]{2,1,0:T(8,128)(2,1)S(1)}, bf16[2,512,128]{2,1,0:T(8,128)(2,1)S(1)}, u32[]{:S(2)}, u32[]{:S(2)}) collective-permute-start(bf16[2,512,128]{2,1,0:T(8,128)(2,1)S(1)} %get-tuple-element.35), channel_id=1, source_target_pairs={{0,1},{1,2},{2,3},{3,4},{4,5},{5,6},{6,7},{7,8},{8,9},{9,10},{10,1... | collective-permute-start | bytes 786440 | tf_op jit(solution)/shard_map/ppermute | solution.py:442
  17.9 9.8 %collective-permute-done.1.high_ref = bf16[2,512,128]{2,1,0:T(8,128)(2,1)S(1)} collective-permute-done((bf16[2,512,128]{2,1,0:T(8,128)(2,1)S(1)}, bf16[2,512,128]{2,1,0:T(8,128)(2,1)S(1)}, u32[]{:S(2)}, u32[]{:S(2)}) %collective-permute-start.1) | collective-permute-done | bytes 262176 | tf_op jit(solution)/shard_map/ppermute | solution.py:442
  27.7 8.9 %collective-permute-done.low_ref = bf16[2,512,128]{2,1,0:T(8,128)(2,1)S(1)} collective-permute-done((bf16[2,512,128]{2,1,0:T(8,128)(2,1)S(1)}, bf16[2,512,128]{2,1,0:T(8,128)(2,1)S(1)}, u32[]{:S(2)}, u32[]{:S(2)}) %collective-permute-start) | collective-permute-done | bytes 262176 | tf_op jit(solution)/shard_map/ppermute | solution.py:442
  36.6 1.2 copy-done.1
  39.0 2.5 %box_level.1 = (bf16[2,6,512,128]{3,2,1,0:T(8,128)(2,1)S(1)}, f32[2,2,256,256]{3,2,1,0:T(8,128)S(1)}, bf16[2,512,1152]{2,1,0:T(8,128)(2,1)S(1)}) custom-call(bf16[2,4,512,128]{3,2,1,0:T(8,128)(2,1)S(1)} %copy-done, bf16[2,4,512,128]{3,2,1,0:T(8,128)(2,1)S(1)} %copy-done.1, bf16[2,512,128]{2,1,0:T(8,128)(2,1)S(1)} %collective-permute-done.low_ref, ...), custom_call_target="tpu_custom_call" | custom-call | flops 1500000000 | bytes 8000000 | tf_op jit(solution)/shard_map/box_level/pallas_call | solution.py:106
  41.5 1.4 copy-done.8
  44.6 1.9 %collective-permute-start.2 = (bf16[2,256,256]{2,1,0:T(8,128)(2,1)S(1)}, bf16[2,256,256]{2,1,0:T(8,128)(2,1)S(1)}, u32[]{:S(2)}, u32[]{:S(2)}) collective-permute-start(bf16[2,256,256]{2,1,0:T(8,128)(2,1)S(1)} %get-tuple-element.24.second_ref), channel_id=1, source_target_pairs={{0,1},{1,2},{2,3},{3,4},{4,5},{5,6},{6,7},{7,8},{8,9},{9,10},{10,1... | collective-permute-start | bytes 786440 | tf_op jit(solution)/shard_map/ppermute | solution.py:442
  46.5 5.8 %collective-permute-start.3 = (bf16[2,256,256]{2,1,0:T(8,128)(2,1)S(1)}, bf16[2,256,256]{2,1,0:T(8,128)(2,1)S(1)}, u32[]{:S(2)}, u32[]{:S(2)}) collective-permute-start(bf16[2,256,256]{2,1,0:T(8,128)(2,1)S(1)} %get-tuple-element.25.first_ref), channel_id=1, source_target_pairs={{1,0},{2,1},{3,2},{4,3},{5,4},{6,5},{7,6},{8,7},{9,8},{10,9},{11,1... | collective-permute-start | bytes 786440 | tf_op jit(solution)/shard_map/ppermute | solution.py:442
  52.3 4.9 %collective-permute-done.2.low_ref = bf16[2,256,256]{2,1,0:T(8,128)(2,1)S(1)} collective-permute-done((bf16[2,256,256]{2,1,0:T(8,128)(2,1)S(1)}, bf16[2,256,256]{2,1,0:T(8,128)(2,1)S(1)}, u32[]{:S(2)}, u32[]{:S(2)}) %collective-permute-start.2) | collective-permute-done | bytes 262176 | tf_op jit(solution)/shard_map/ppermute | solution.py:442
  57.4 2.1 %coarse_weight_level.1 = (bf16[144,16,128]{2,1,0:T(8,128)(2,1)S(1)}, bf16[144,16,128]{2,1,0:T(8,128)(2,1)S(1)}) custom-call(s32[1]{0:T(128)} %bitcast.core_ref, bf16[8,2,2,2,32,256]{5,4,3,2,1,0:T(8,128)(2,1)S(1)} %all-to-all-done.pre_ref.input_ref, bf16[2,256,256]{2,1,0:T(8,128)(2,1)S(1)} %collective-permute-done.2.low_ref, ...), custom_call_target="tpu_custom_call" | custom-call | flops 1300000000 | bytes 3000000 | tf_op jit(solution)/shard_map/coarse_weight_level/pallas_call | solution.py:305
  60.7 1.4 copy-done.11
  62.1 5.8 %fine_level.1 = (bf16[2,4,512,128]{3,2,1,0:T(8,128)(2,1)}, bf16[9,12,16,128]{3,2,1,0:T(8,128)(2,1)S(1)}, bf16[9,12,16,128]{3,2,1,0:T(8,128)(2,1)S(1)}) custom-call(s32[1]{0:T(128)} %bitcast.core_ref, bf16[2,6,512,128]{3,2,1,0:T(8,128)(2,1)S(1)} %copy-done.11, bf16[2,4,512,128]{3,2,1,0:T(8,128)(2,1)S(1)} %copy-done.3, bf16[3,3,384,128]{3,2,1,0:T(8,128)(2,1)S(1)} %copy-done.5, ...), custom_call_target="tpu_custom_call" | custom-call | flops 6000000000 | bytes 12000000 | tf_op jit(solution)/shard_map/fine_level/pallas_call | solution.py:202
  68.0 1.7 %collective-permute-done.5 = bf16[9,12,16,128]{3,2,1,0:T(8,128)(2,1)S(1)} collective-permute-done((bf16[9,12,16,128]{3,2,1,0:T(8,128)(2,1)S(1)}, bf16[9,12,16,128]{3,2,1,0:T(8,128)(2,1)S(1)}, u32[]{:S(2)}, u32[]{:S(2)}) %collective-permute-start.5) | collective-permute-done | bytes 442400 | tf_op jit(solution)/shard_map/ppermute | solution.py:475
  69.9 29.6 %all_to_all.20.parts_ref = bf16[64,4,16,128]{3,2,1,0:T(8,128)(2,1)S(1)} all-to-all(bf16[64,4,16,128]{3,2,1,0:T(8,128)(2,1)S(1)} %bitcast.33), channel_id=1, replica_groups=mesh['xh'=2,'z'=4,'core'=2,'y'=4,'xl'=2] {'xh','xl','z','y'}, dimensions={0} | all-to-all | bytes 2097152 | tf_op jit(solution)/shard_map/all_to_all | solution.py:410
  99.6 1.2 sum_parts.1
  100.8 5.4 %all-to-all-start.2 = ((bf16[64,4,16,128]{3,2,1,0:T(8,128)(2,1)}), bf16[64,4,16,128]{3,2,1,0:T(8,128)(2,1)S(1)}, u32[]{:S(2)}, u32[]{:S(2)}) async-start(bf16[64,4,16,128]{3,2,1,0:T(8,128)(2,1)} %sum_parts.1), calls=%async_computation.2 | async-start | bytes 2097152 | tf_op jit(solution)/shard_map/all_to_all | solution.py:418
  107.1 1.7 %coarse_input_level.1 = bf16[8,2,2,32,256]{4,3,2,1,0:T(8,128)(2,1)S(1)} custom-call(bf16[3,3,256,256]{3,2,1,0:T(8,128)(2,1)S(1)} %copy-done.2, bf16[2,256,256]{2,1,0:T(8,128)(2,1)S(1)} %collective-permute-done.2.low_ref, bf16[2,256,256]{2,1,0:T(8,128)(2,1)S(1)} %get-tuple-element.25.first_ref, bf16[2,256,256]{2,1,0:T(8,128)(2,1)S(1)} %get-tuple-element.24.second_ref, ...), custom_call_target="tpu_custom_call" | custom-call | flops 1300000000 | bytes 3000000 | tf_op jit(solution)/shard_map/coarse_input_level/pallas_call | solution.py:339
  108.8 13.5 %all-to-all-done.2 = bf16[64,4,16,128]{3,2,1,0:T(8,128)(2,1)S(1)} async-done(((bf16[64,4,16,128]{3,2,1,0:T(8,128)(2,1)}), bf16[64,4,16,128]{3,2,1,0:T(8,128)(2,1)S(1)}, u32[]{:S(2)}, u32[]{:S(2)}) %all-to-all-start.2) | async-done | bytes 1048608 | tf_op jit(solution)/shard_map/all_to_all | solution.py:418
  122.3 3.3 %collective-permute-start.6 = (bf16[256,16,128]{2,1,0:T(8,128)(2,1)S(1)}, bf16[256,16,128]{2,1,0:T(8,128)(2,1)S(1)}, u32[]{:S(2)}, u32[]{:S(2)}) collective-permute-start(bf16[256,16,128]{2,1,0:T(8,128)(2,1)S(1)} %bitcast.34), channel_id=1, source_target_pairs={{0,8},{8,0},{1,9},{9,1},{2,10},{10,2},{3,11},{11,3},{4,12},{12,4},... | collective-permute-start | bytes 3145736 | tf_op jit(solution)/shard_map/ppermute | solution.py:483
  125.7 12.4 %all_to_all.21 = bf16[8,2,2,32,256]{4,3,2,1,0:T(8,128)(2,1)S(1)} all-to-all(bf16[8,2,2,32,256]{4,3,2,1,0:T(8,128)(2,1)S(1)} %coarse_input_level.1), channel_id=1, replica_groups=mesh['xh'=2,'z'=4,'core'=2,'y'=4,'xl'=2] {'y','xl'}, dimensions={0} | all-to-all | bytes 1048576 | tf_op jit(solution)/shard_map/all_to_all | solution.py:484
  138.9 2.4 %unpack.1 = (f32[9,384,128]{2,1,0:T(8,128)}, f32[9,256,256]{2,1,0:T(8,128)}) custom-call(s32[1]{0:T(128)} %bitcast.core_ref, bf16[256,16,128]{2,1,0:T(8,128)(2,1)S(1)} %bitcast.35, bf16[256,16,128]{2,1,0:T(8,128)(2,1)S(1)} %collective-permute-done.6.other_ref), custom_call_target="tpu_custom_call" | custom-call | flops 1000000 | bytes 6000000 | tf_op jit(solution)/shard_map/unpack/pallas_call | solution.py:425
  (35 shorter events, 7.5 us)
Async XLA Ops:
  0.6 1.7 %copy-start.13 = (bf16[2,16,256,32]{2,3,1,0:T(8,128)(2,1)S(1)}, bf16[2,16,256,32]{2,3,1,0:T(8,128)(2,1)}, u32[]{:S(2)}) copy-start(bf16[2,16,256,32]{2,3,1,0:T(8,128)(2,1)} %param.8) | copy-start | bytes 1572868
  0.6 1.7 %copy-start.12 = (bf16[2,16,256,32]{2,3,1,0:T(8,128)(2,1)S(1)}, bf16[2,16,256,32]{2,3,1,0:T(8,128)(2,1)}, u32[]{:S(2)}) copy-start(bf16[2,16,256,32]{2,3,1,0:T(8,128)(2,1)} %param.7) | copy-start | bytes 1572868
  2.4 34.2 %copy-start = (bf16[2,4,512,128]{3,2,1,0:T(8,128)(2,1)S(1)}, bf16[2,4,512,128]{3,2,1,0:T(8,128)(2,1)}, u32[]{:S(2)}) copy-start(bf16[2,4,512,128]{3,2,1,0:T(8,128)(2,1)} %cot_ref.1) | copy-start | bytes 3145732
  3.4 40.6 %all-to-all-start = ((bf16[8,2,2,2,32,256]{5,4,3,2,1,0:T(8,128)(2,1)}), bf16[8,2,2,2,32,256]{5,4,3,2,1,0:T(8,128)(2,1)S(1)}, u32[]{:S(2)}, u32[]{:S(2)}) async-start(bf16[8,2,2,2,32,256]{5,4,3,2,1,0:T(8,128)(2,1)} %copy_bitcast_fusion), calls=%async_computation | async-start | bytes 2097152 | tf_op jit(solution)/shard_map/all_to_all | solution.py:465
  9.4 18.3 %collective-permute-start.1 = (bf16[2,512,128]{2,1,0:T(8,128)(2,1)S(1)}, bf16[2,512,128]{2,1,0:T(8,128)(2,1)S(1)}, u32[]{:S(2)}, u32[]{:S(2)}) collective-permute-start(bf16[2,512,128]{2,1,0:T(8,128)(2,1)S(1)} %get-tuple-element.34), channel_id=1, source_target_pairs={{1,0},{2,1},{3,2},{4,3},{5,4},{6,5},{7,6},{8,7},{9,8},{10,9},{11,1... | collective-permute-start | bytes 786440 | tf_op jit(solution)/shard_map/ppermute | solution.py:442
  16.0 20.6 %collective-permute-start = (bf16[2,512,128]{2,1,0:T(8,128)(2,1)S(1)}, bf16[2,512,128]{2,1,0:T(8,128)(2,1)S(1)}, u32[]{:S(2)}, u32[]{:S(2)}) collective-permute-start(bf16[2,512,128]{2,1,0:T(8,128)(2,1)S(1)} %get-tuple-element.35), channel_id=1, source_target_pairs={{0,1},{1,2},{2,3},{3,4},{4,5},{5,6},{6,7},{7,8},{8,9},{9,10},{10,1... | collective-permute-start | bytes 786440 | tf_op jit(solution)/shard_map/ppermute | solution.py:442
  36.6 1.2 copy-start.1
  37.8 1.2 copy-start.4
  41.5 1.4 copy-start.8
  42.9 1.1 copy-start.10
  44.6 12.5 %collective-permute-start.2 = (bf16[2,256,256]{2,1,0:T(8,128)(2,1)S(1)}, bf16[2,256,256]{2,1,0:T(8,128)(2,1)S(1)}, u32[]{:S(2)}, u32[]{:S(2)}) collective-permute-start(bf16[2,256,256]{2,1,0:T(8,128)(2,1)S(1)} %get-tuple-element.24.second_ref), channel_id=1, source_target_pairs={{0,1},{1,2},{2,3},{3,4},{4,5},{5,6},{6,7},{7,8},{8,9},{9,10},{10,1... | collective-permute-start | bytes 786440 | tf_op jit(solution)/shard_map/ppermute | solution.py:442
  46.5 10.9 %collective-permute-start.3 = (bf16[2,256,256]{2,1,0:T(8,128)(2,1)S(1)}, bf16[2,256,256]{2,1,0:T(8,128)(2,1)S(1)}, u32[]{:S(2)}, u32[]{:S(2)}) collective-permute-start(bf16[2,256,256]{2,1,0:T(8,128)(2,1)S(1)} %get-tuple-element.25.first_ref), channel_id=1, source_target_pairs={{1,0},{2,1},{3,2},{4,3},{5,4},{6,5},{7,6},{8,7},{9,8},{10,9},{11,1... | collective-permute-start | bytes 786440 | tf_op jit(solution)/shard_map/ppermute | solution.py:442
  57.4 2.1 %copy-start.6 = (bf16[2,256,256]{2,1,0:T(8,128)(2,1)}, bf16[2,256,256]{2,1,0:T(8,128)(2,1)S(1)}, u32[]{:S(2)}) copy-start(bf16[2,256,256]{2,1,0:T(8,128)(2,1)S(1)} %collective-permute-done.3.high_ref) | copy-start | bytes 786436
  57.4 3.3 %copy-start.3 = (bf16[2,4,512,128]{3,2,1,0:T(8,128)(2,1)S(1)}, bf16[2,4,512,128]{3,2,1,0:T(8,128)(2,1)}, u32[]{:S(2)}) copy-start(bf16[2,4,512,128]{3,2,1,0:T(8,128)(2,1)} %skip_ref.1) | copy-start | bytes 3145732
  57.4 3.3 %copy-start.5 = (bf16[3,3,384,128]{3,2,1,0:T(8,128)(2,1)S(1)}, bf16[3,3,384,128]{3,2,1,0:T(8,128)(2,1)}, u32[]{:S(2)}) copy-start(bf16[3,3,384,128]{3,2,1,0:T(8,128)(2,1)} %weight_ref.4) | copy-start | bytes 2654212
  57.4 3.3 %copy-start.9 = (bf16[2,512,1152]{2,1,0:T(8,128)(2,1)S(1)}, bf16[2,512,1152]{2,1,0:T(8,128)(2,1)}, u32[]{:S(2)}) copy-start(bf16[2,512,1152]{2,1,0:T(8,128)(2,1)} %copy-done.8) | copy-start | bytes 7077892
  59.5 10.2 %collective-permute-start.4 = (bf16[144,16,128]{2,1,0:T(8,128)(2,1)S(1)}, bf16[144,16,128]{2,1,0:T(8,128)(2,1)S(1)}, u32[]{:S(2)}, u32[]{:S(2)}) collective-permute-start(bf16[144,16,128]{2,1,0:T(8,128)(2,1)S(1)} %get-tuple-element.27), channel_id=1, source_target_pairs={{0,8},{8,0},{1,9},{9,1},{2,10},{10,2},{3,11},{11,3},{4,12},{12,4},... | collective-permute-start | bytes 1769480 | tf_op jit(solution)/shard_map/ppermute | solution.py:479
  60.7 1.4 copy-start.11
  67.9 1.8 %collective-permute-start.5 = (bf16[9,12,16,128]{3,2,1,0:T(8,128)(2,1)S(1)}, bf16[9,12,16,128]{3,2,1,0:T(8,128)(2,1)S(1)}, u32[]{:S(2)}, u32[]{:S(2)}) collective-permute-start(bf16[9,12,16,128]{3,2,1,0:T(8,128)(2,1)S(1)} %get-tuple-element.29), channel_id=1, source_target_pairs={{0,8},{8,0},{1,9},{9,1},{2,10},{10,2},{3,11},{11,3},{4,12},{12,4},... | collective-permute-start | bytes 1327112 | tf_op jit(solution)/shard_map/ppermute | solution.py:475
  99.5 6.6 %copy-start.2 = (bf16[3,3,256,256]{3,2,1,0:T(8,128)(2,1)S(1)}, bf16[3,3,256,256]{3,2,1,0:T(8,128)(2,1)}, u32[]{:S(2)}) copy-start(bf16[3,3,256,256]{3,2,1,0:T(8,128)(2,1)} %weight_ref.5) | copy-start | bytes 3538948
  100.8 21.5 %all-to-all-start.2 = ((bf16[64,4,16,128]{3,2,1,0:T(8,128)(2,1)}), bf16[64,4,16,128]{3,2,1,0:T(8,128)(2,1)S(1)}, u32[]{:S(2)}, u32[]{:S(2)}) async-start(bf16[64,4,16,128]{3,2,1,0:T(8,128)(2,1)} %sum_parts.1), calls=%async_computation.2 | async-start | bytes 2097152 | tf_op jit(solution)/shard_map/all_to_all | solution.py:418
  106.2 1.0 copy-start.7
  122.3 16.6 %collective-permute-start.6 = (bf16[256,16,128]{2,1,0:T(8,128)(2,1)S(1)}, bf16[256,16,128]{2,1,0:T(8,128)(2,1)S(1)}, u32[]{:S(2)}, u32[]{:S(2)}) collective-permute-start(bf16[256,16,128]{2,1,0:T(8,128)(2,1)S(1)} %bitcast.34), channel_id=1, source_target_pairs={{0,8},{8,0},{1,9},{9,1},{2,10},{10,2},{3,11},{11,3},{4,12},{12,4},... | collective-permute-start | bytes 3145736 | tf_op jit(solution)/shard_map/ppermute | solution.py:483

commit v2 on v1

--- a/solution.py
+++ b/solution.py
@@ -12,7 +12,7 @@
 F32 = jnp.float32
 BF16 = jnp.bfloat16
 MIB = 1 << 20
-VMEM = 28
+VMEM = 18
 
 SPLIT = (("xh", 2), ("z", 4), ("core", 2), ("y", 4), ("xl", 2))
 ROWS = ("xh", "z", "core")
@@ -54,91 +54,78 @@
     return block.astype(BF16).reshape(block.shape[0] // 16, 16, block.shape[1])
 
 
-def box_kernel(
-    cot_ref, pre_ref, low_ref, high_ref, weight_ref, grad_ref, pooled_ref, box_ref, rows32, up_weight
-):
-    sample = pl.program_id(0)
+def box_sums(upper, lower, half):
+    even = upper[pl.ds(0, half, 2), :] + lower[pl.ds(0, half, 2), :]
+    odd = upper[pl.ds(1, half, 2), :] + lower[pl.ds(1, half, 2), :]
+    before, _ = shifted(odd)
+    _, after = shifted(even)
+    return (before + even).astype(BF16), (even + odd).astype(BF16), (odd + after).astype(BF16)
+
+
+def box_kernel(cot_ref, pre_ref, weight_ref, grad_ref, pooled_ref, box_ref, up_weight, rows32):
     c3 = cot_ref.shape[-1]
     c4 = pooled_ref.shape[-1]
     half = pooled_ref.shape[-2]
-
-    @pl.when(sample == 0)
+    reach = 3 * c3
+
+    @pl.when(pl.program_id(0) == 0)
     def _():
         for dy in range(3):
             for d in range(3):
                 at = (dy * 3 + d) * c3
                 up_weight[at : at + c3, :] = weight_ref[2 - dy, 2 - d, :c4, :].astype(F32).T.astype(BF16)
 
-    for v in range(6):
-        if v == 0:
-            grad = low_ref[0]
-        elif v == 5:
-            grad = high_ref[0]
-        else:
-            grad = cot_ref[0, v - 1].astype(F32) * silu_grad(pre_ref[0, v - 1].astype(F32))
-            grad = grad.astype(BF16)
+    for v in range(4):
+        grad = (cot_ref[0, v].astype(F32) * silu_grad(pre_ref[0, v].astype(F32))).astype(BF16)
         grad_ref[0, v] = grad
         rows32[v] = grad.astype(F32)
-
-    for v in range(5):
-        even = rows32[v, pl.ds(0, half, 2), :] + rows32[v + 1, pl.ds(0, half, 2), :]
-        odd = rows32[v, pl.ds(1, half, 2), :] + rows32[v + 1, pl.ds(1, half, 2), :]
-        before, _ = shifted(odd)
-        _, after = shifted(even)
-        sums = ((before + even).astype(BF16), (even + odd).astype(BF16), (odd + after).astype(BF16))
-        for i in range(2):
-            dy = v - 2 * i
-            if 0 <= dy <= 2:
-                for d in range(3):
-                    at = (dy * 3 + d) * c3
-                    box_ref[0, i * half : (i + 1) * half, at : at + c3] = sums[d]
-
-    pooled = jnp.dot(box_ref[0], up_weight[...], preferred_element_type=F32)
-    pooled_ref[0] = pooled.reshape(pooled_ref.shape[1:])
-
-
-def box_level(cot, pre, low, high, weight, cs):
+    for v in range(3):
+        for d, value in enumerate(box_sums(rows32.at[v], rows32.at[v + 1], half)):
+            at = v * reach + d * c3
+            box_ref[0, :, at : at + c3] = value
+    pooled_ref[0, 0] = jnp.dot(box_ref[0, :, : 2 * reach], up_weight[reach:, :], preferred_element_type=F32)
+    pooled_ref[0, 1] = jnp.dot(box_ref[0, :, reach:], up_weight[: 2 * reach, :], preferred_element_type=F32)
+
+
+def box_level(cot, pre, weight, cs):
     samples, height, wide, c3 = cot.shape
     c4 = weight.shape[2] - cs
     half = wide // 2
     block = pl.BlockSpec((1, height, wide, c3), lambda s: (s, 0, 0, 0))
-    edge = pl.BlockSpec((1, wide, c3), lambda s: (s, 0, 0))
     return pl.pallas_call(
         box_kernel,
         grid=(samples,),
-        in_specs=[block, block, edge, edge, pl.BlockSpec(weight.shape, lambda s: (0, 0, 0, 0))],
+        in_specs=[block, block, pl.BlockSpec(weight.shape, lambda s: (0, 0, 0, 0))],
         out_specs=[
-            pl.BlockSpec((1, height + 2, wide, c3), lambda s: (s, 0, 0, 0)),
+            block,
             pl.BlockSpec((1, 2, half, c4), lambda s: (s, 0, 0, 0)),
-            pl.BlockSpec((1, 2 * half, 9 * c3), lambda s: (s, 0, 0)),
+            pl.BlockSpec((1, half, 9 * c3), lambda s: (s, 0, 0)),
+            pl.BlockSpec((9 * c3, c4), lambda s: (0, 0)),
         ],
         out_shape=[
-            jax.ShapeDtypeStruct((samples, height + 2, wide, c3), BF16),
+            jax.ShapeDtypeStruct((samples, height, wide, c3), BF16),
             jax.ShapeDtypeStruct((samples, 2, half, c4), F32),
-            jax.ShapeDtypeStruct((samples, 2 * half, 9 * c3), BF16),
+            jax.ShapeDtypeStruct((samples, half, 9 * c3), BF16),
+            jax.ShapeDtypeStruct((9 * c3, c4), BF16),
         ],
-        scratch_shapes=[pltpu.VMEM((6, wide, c3), F32), pltpu.VMEM((9 * c3, c4), BF16)],
-        compiler_params=params(VMEM),
-        cost_estimate=cost(1.5e9, 8e6),
+        scratch_shapes=[pltpu.VMEM((height, wide, c3), F32)],
+        compiler_params=params(VMEM),
+        cost_estimate=cost(1.2e9, 8e6),
         name="box_level",
-    )(cot, pre, low, high, weight)
+    )(cot, pre, weight)
 
 
 def fine_kernel(
-    core_ref, grad_ref, skip_ref, weight_ref, pre_ref, box_ref,
-    grad_skip_ref, keep_ref, send_ref,
-    taps, skip_weight, total, up_total, *, scale,
+    core_ref, grad_ref, low_ref, high_ref, skip_ref, weight_ref, grad_skip_ref, keep_ref, send_ref, taps, skip_weight, total, *, scale
 ):
     sample = pl.program_id(0)
     c3 = grad_ref.shape[-1]
     cs = skip_ref.shape[-1]
     c4 = weight_ref.shape[2] - cs
-    half = pre_ref.shape[-1]
 
     @pl.when(sample == 0)
     def _():
         total[...] = jnp.zeros_like(total)
-        up_total[...] = jnp.zeros_like(up_total)
         for u in range(4):
             for d in range(3):
                 at = (u * 3 + d) * c3
@@ -150,13 +137,8 @@
                         block = jnp.zeros((c3, cs), BF16)
                     skip_weight[at : at + c3, t * cs : (t + 1) * cs] = block
 
-    for i in range(2):
-        value = pre_ref[:, 0, 0, i].reshape(c4, half).astype(F32)
-        value = (value * jax.nn.sigmoid(value)).astype(BF16)
-        up_total[...] += jnp.dot(value, box_ref[0, i * half : (i + 1) * half, :], preferred_element_type=F32)
-
     for v in range(6):
-        grad = grad_ref[0, v]
+        grad = low_ref[0] if v == 0 else high_ref[0] if v == 5 else grad_ref[0, v - 1]
         before, after = shifted(grad.astype(F32))
         at = v * 3 * c3
         taps[:, at : at + c3] = before.astype(BF16)
@@ -175,40 +157,33 @@
     def _():
         core = core_ref[0]
 
-        def put(tap, at, value):
-            part = value.shape[0] // 2
-            low, high = value[:part], value[part:]
-            keep_ref[tap, at : at + part // 16] = tiles(jnp.where(core == 0, low, high))
-            send_ref[tap, at : at + part // 16] = tiles(jnp.where(core == 0, high, low))
-
+        part = cs // 2
         for dy in range(3):
             for d in range(3):
                 first = (dy * 3 + d) * c3
                 second = ((dy + 1) * 3 + d) * c3
+                value = (total[:cs, first : first + c3] + total[cs:, second : second + c3]) * scale
+                low, high = value[:part], value[part:]
                 tap = (2 - dy) * 3 + 2 - d
-                put(tap, 0, up_total[:, first : first + c3] * scale)
-                value = total[:cs, first : first + c3] + total[cs:, second : second + c3]
-                put(tap, c4 // 32, value * scale)
-
-
-def fine_level(core, grad, skip, weight, received, box, fine_cells):
+                keep_ref[tap] = tiles(jnp.where(core == 0, low, high))
+                send_ref[tap] = tiles(jnp.where(core == 0, high, low))
+
+
+def fine_level(core, grad, low, high, skip, weight, fine_cells):
     samples, height, wide, cs = skip.shape
     c3 = grad.shape[-1]
-    c4 = weight.shape[2] - cs
-    half = wide // 2
-    peers, own = received.shape[0], received.shape[-2]
-    part = jax.ShapeDtypeStruct((9, (c4 + cs) // 32, 16, c3), BF16)
+    part = jax.ShapeDtypeStruct((9, cs // 32, 16, c3), BF16)
     whole = pl.BlockSpec(part.shape, lambda s: (0, 0, 0, 0))
     return pl.pallas_call(
         functools.partial(fine_kernel, scale=1.0 / math.sqrt(fine_cells)),
         grid=(samples,),
         in_specs=[
             pl.BlockSpec(memory_space=pltpu.SMEM),
-            pl.BlockSpec((1, height + 2, wide, c3), lambda s: (s, 0, 0, 0)),
+            pl.BlockSpec((1, height, wide, c3), lambda s: (s, 0, 0, 0)),
+            pl.BlockSpec((1, wide, c3), lambda s: (s, 0, 0)),
+            pl.BlockSpec((1, wide, c3), lambda s: (s, 0, 0)),
             pl.BlockSpec((1, height, wide, cs), lambda s: (s, 0, 0, 0)),
             pl.BlockSpec(weight.shape, lambda s: (0, 0, 0, 0)),
-            pl.BlockSpec((peers, 1, 1, 2, own, half), lambda s: (0, 0, s, 0, 0, 0)),
-            pl.BlockSpec((1, 2 * half, 9 * c3), lambda s: (s, 0, 0)),
         ],
         out_specs=[pl.BlockSpec((1, height, wide, cs), lambda s: (s, 0, 0, 0)), whole, whole],
         out_shape=[jax.ShapeDtypeStruct((samples, height, wide, cs), BF16), part, part],
@@ -216,39 +191,129 @@
             pltpu.VMEM((wide, 18 * c3), BF16),
             pltpu.VMEM((12 * c3, 2 * cs), BF16),
             pltpu.VMEM((2 * cs, 12 * c3), F32),
-            pltpu.VMEM((c4, 9 * c3), F32),
         ],
         compiler_params=params(VMEM),
-        cost_estimate=cost(6e9, 12e6),
+        cost_estimate=cost(5e9, 8e6),
         name="fine_level",
-    )(core, grad, skip, weight, received, box)
-
-
-def coarse_grad_kernel(pooled_ref, pre_ref, first_ref, second_ref):
-    channels, wide = pooled_ref.shape[-1], pooled_ref.shape[-2]
-    for i, out_ref in enumerate((first_ref, second_ref)):
-        value = pre_ref[:, 0, 0, i].reshape(channels, wide).astype(F32).T
-        out_ref[0] = (pooled_ref[0, i] * silu_grad(value)).astype(BF16)
-
-
-def coarse_grad(pooled, received):
-    samples, _, wide, c4 = pooled.shape
+    )(core, grad, low, high, skip, weight)
+
+
+def coarse_grad_kernel(
+    low_ref, high_ref, top_ref, bottom_ref, pooled_ref, low_weight_ref, high_weight_ref, pre_ref,
+    first_ref, second_ref, box_low_ref, box_high_ref, edge32,
+):
+    channels, half = pooled_ref.shape[-1], pooled_ref.shape[-2]
+    c3 = low_ref.shape[-1]
+    sides = (
+        (low_ref, top_ref, low_weight_ref, first_ref, box_low_ref),
+        (bottom_ref, high_ref, high_weight_ref, second_ref, box_high_ref),
+    )
+    for i, (upper, lower, weight_ref, out_ref, box_ref) in enumerate(sides):
+        edge32[0] = upper[...].reshape(edge32.shape[1:]).astype(F32)
+        edge32[1] = lower[...].reshape(edge32.shape[1:]).astype(F32)
+        for d, value in enumerate(box_sums(edge32.at[0], edge32.at[1], half)):
+            box_ref[0, :, d * c3 : (d + 1) * c3] = value
+        pooled = pooled_ref[0, i] + jnp.dot(box_ref[0], weight_ref[...], preferred_element_type=F32)
+        value = pre_ref[:, 0, 0, i].reshape(channels, half).astype(F32).T
+        out_ref[0] = (pooled * silu_grad(value)).astype(BF16)
+
+
+def coarse_grad(low, high, grad, pooled, up_weight, received):
+    samples, _, half, c4 = pooled.shape
     peers, _, _, _, own, _ = received.shape
-    out = jax.ShapeDtypeStruct((samples, wide, c4), BF16)
-    spec = pl.BlockSpec((1, wide, c4), lambda s: (s, 0, 0))
+    _, height, wide, c3 = grad.shape
+    out = jax.ShapeDtypeStruct((samples, half, c4), BF16)
+    box = jax.ShapeDtypeStruct((samples, half, 3 * c3), BF16)
+    edge = pl.BlockSpec((1, wide, c3), lambda s: (s, 0, 0))
+    spec = pl.BlockSpec((1, half, c4), lambda s: (s, 0, 0))
+    box_spec = pl.BlockSpec((1, half, 3 * c3), lambda s: (s, 0, 0))
     return pl.pallas_call(
         coarse_grad_kernel,
         grid=(samples,),
         in_specs=[
-            pl.BlockSpec((1, 2, wide, c4), lambda s: (s, 0, 0, 0)),
+            edge, edge,
+            pl.BlockSpec((1, 1, wide, c3), lambda s: (s, 0, 0, 0)),
+            pl.BlockSpec((1, 1, wide, c3), lambda s: (s, height - 1, 0, 0)),
+            pl.BlockSpec((1, 2, half, c4), lambda s: (s, 0, 0, 0)),
+            pl.BlockSpec((3 * c3, c4), lambda s: (0, 0)),
+            pl.BlockSpec((3 * c3, c4), lambda s: (2, 0)),
+            pl.BlockSpec((peers, 1, 1, 2, own, half), lambda s: (0, 0, s, 0, 0, 0)),
+        ],
+        out_specs=[spec, spec, box_spec, box_spec],
+        out_shape=[out, out, box, box],
+        scratch_shapes=[pltpu.VMEM((2, wide, c3), F32)],
+        compiler_params=params(VMEM),
+        cost_estimate=cost(4e8, 4e6),
+        name="coarse_grad",
+    )(low, high, grad, grad, pooled, up_weight, up_weight, received)
+
+
+def up_kernel(
+    core_ref, pre_ref, box_ref, box_low_ref, box_high_ref, skip_keep_ref, skip_send_ref, keep_ref, send_ref, total,
+    *, scale
+):
+    sample = pl.program_id(0)
+    wide = pre_ref.shape[-1]
+    c4 = pre_ref.shape[0] * pre_ref.shape[-2]
+    c3 = keep_ref.shape[-1]
+
+    @pl.when(sample == 0)
+    def _():
+        total[...] = jnp.zeros_like(total)
+
+    reach = 3 * c3
+    windows = (
+        ((0, box_low_ref[0]), (reach, box_ref[0, :, : 2 * reach])),
+        ((0, box_ref[0, :, reach:]), (2 * reach, box_high_ref[0])),
+    )
+    for i in range(2):
+        value = pre_ref[:, 0, 0, i].reshape(c4, wide).astype(F32)
+        value = (value * jax.nn.sigmoid(value)).astype(BF16)
+        for at, window in windows[i]:
+            total[:, at : at + window.shape[1]] += jnp.dot(value, window, preferred_element_type=F32)
+
+    @pl.when(sample == pl.num_programs(0) - 1)
+    def _():
+        core = core_ref[0]
+        part = c4 // 2
+        mine = part // 16
+        for dy in range(3):
+            for d in range(3):
+                at = (dy * 3 + d) * c3
+                value = total[:, at : at + c3] * scale
+                low, high = value[:part], value[part:]
+                tap = (2 - dy) * 3 + 2 - d
+                keep_ref[tap, :mine] = tiles(jnp.where(core == 0, low, high))
+                send_ref[tap, :mine] = tiles(jnp.where(core == 0, high, low))
+                keep_ref[tap, mine:] = skip_keep_ref[tap]
+                send_ref[tap, mine:] = skip_send_ref[tap]
+
+
+def up_level(core, received, box, box_low, box_high, skip_keep, skip_send, fine_cells):
+    peers, _, samples, _, own, wide = received.shape
+    c4 = peers * own
+    c3 = box.shape[-1] // 9
+    part = jax.ShapeDtypeStruct((9, c4 // 32 + skip_keep.shape[1], 16, c3), BF16)
+    whole = pl.BlockSpec(part.shape, lambda s: (0, 0, 0, 0))
+    skips = pl.BlockSpec(skip_keep.shape, lambda s: (0, 0, 0, 0))
+    return pl.pallas_call(
+        functools.partial(up_kernel, scale=1.0 / math.sqrt(fine_cells)),
+        grid=(samples,),
+        in_specs=[
+            pl.BlockSpec(memory_space=pltpu.SMEM),
             pl.BlockSpec((peers, 1, 1, 2, own, wide), lambda s: (0, 0, s, 0, 0, 0)),
+            pl.BlockSpec((1, wide, 9 * c3), lambda s: (s, 0, 0)),
+            pl.BlockSpec((1, wide, 3 * c3), lambda s: (s, 0, 0)),
+            pl.BlockSpec((1, wide, 3 * c3), lambda s: (s, 0, 0)),
+            skips, skips,
         ],
-        out_specs=[spec, spec],
-        out_shape=[out, out],
-        compiler_params=params(VMEM),
-        cost_estimate=cost(2e7, 2e6),
-        name="coarse_grad",
-    )(pooled, received)
+        out_specs=[whole, whole],
+        out_shape=[part, part],
+        scratch_shapes=[pltpu.VMEM((c4, 9 * c3), F32)],
+        compiler_params=params(VMEM),
+        cost_estimate=cost(1e9, 5e6),
+        name="up_level",
+    )(core, received, box, box_low, box_high, skip_keep, skip_send)
 
 
 def fill_coarse_taps(rows, taps):
@@ -293,8 +358,8 @@
                     send_ref[tap * count : (tap + 1) * count] = tiles(jnp.where(core == 0, high, low))
 
 
-def coarse_specs(samples, wide, c4):
-    return [pl.BlockSpec((1, wide, c4), lambda s: (s, 0, 0))] * 4
+def coarse_specs(wide, c4, count):
+    return [pl.BlockSpec((1, wide, c4), lambda s: (s, 0, 0))] * count
 
 
 def coarse_weight_level(core, received, rows, coarse_cells):
@@ -308,7 +373,7 @@
         in_specs=[
             pl.BlockSpec(memory_space=pltpu.SMEM),
             pl.BlockSpec((peers, 1, 1, 2, own, wide), lambda s: (0, 1, s, 0, 0, 0)),
-        ] + coarse_specs(samples, wide, c4),
+        ] + coarse_specs(wide, c4, 4),
         out_specs=[whole, whole],
         out_shape=[part, part],
         scratch_shapes=[pltpu.VMEM((4 * wide, 3 * c4), BF16), pltpu.VMEM((3, c4, 3 * c4), F32)],
@@ -318,9 +383,10 @@
     )(core, received, *rows)
 
 
-def coarse_input_kernel(weight_ref, low_ref, first_ref, second_ref, high_ref, out_ref, taps):
+def coarse_input_kernel(chan_ref, weight_ref, low_ref, first_ref, second_ref, high_ref, *rest):
+    *piece_refs, taps, stage = rest
     wide, c4 = low_ref.shape[1:]
-    peers, own = out_ref.shape[0], out_ref.shape[-2]
+    own = c4 // len(piece_refs)
     fill_coarse_taps((low_ref[0], first_ref[0], second_ref[0], high_ref[0]), taps)
     total = None
     for dy in range(3):
@@ -328,25 +394,49 @@
             window = taps[dy * wide : (dy + 2) * wide, d * c4 : (d + 1) * c4]
             term = dott(weight_ref[2 - dy, 2 - d], window)
             total = term if total is None else total + term
-    total = total.astype(BF16)
-    for i in range(2):
-        out_ref[:, 0, i] = total[:, i * wide : (i + 1) * wide].reshape(peers, own, wide)
-
-
-def coarse_input_level(weight, rows, peers):
+    stage[...] = total.astype(BF16)
+    for k, ref in enumerate(piece_refs):
+        at = pl.multiple_of(jnp.bitwise_xor(chan_ref[0], k) * own, own)
+        for i in range(2):
+            ref[0, i] = stage[pl.ds(at, own), i * wide : (i + 1) * wide]
+
+
+def coarse_input_level(chan, weight, rows, peers):
     samples, wide, c4 = rows[0].shape
     own = c4 // peers
     return pl.pallas_call(
         coarse_input_kernel,
         grid=(samples,),
-        in_specs=[pl.BlockSpec(weight.shape, lambda s: (0, 0, 0, 0))] + coarse_specs(samples, wide, c4),
-        out_specs=pl.BlockSpec((peers, 1, 2, own, wide), lambda s: (0, s, 0, 0, 0)),
-        out_shape=jax.ShapeDtypeStruct((peers, samples, 2, own, wide), BF16),
-        scratch_shapes=[pltpu.VMEM((4 * wide, 3 * c4), BF16)],
+        in_specs=[
+            pl.BlockSpec(memory_space=pltpu.SMEM),
+            pl.BlockSpec(weight.shape, lambda s: (0, 0, 0, 0)),
+        ] + coarse_specs(wide, c4, 4),
+        out_specs=[pl.BlockSpec((1, 2, own, wide), lambda s: (s, 0, 0, 0))] * peers,
+        out_shape=[jax.ShapeDtypeStruct((samples, 2, own, wide), BF16)] * peers,
+        scratch_shapes=[pltpu.VMEM((4 * wide, 3 * c4), BF16), pltpu.VMEM((c4, 2 * wide), BF16)],
         compiler_params=params(VMEM),
         cost_estimate=cost(1.3e9, 3e6),
         name="coarse_input_level",
-    )(weight, *rows)
+    )(chan, weight, *rows)
+
+
+def place_kernel(chan_ref, *refs):
+    *piece_refs, out_ref = refs
+    for k, ref in enumerate(piece_refs):
+        at = jnp.bitwise_xor(chan_ref[0], k) * 2
+        out_ref[:, pl.ds(at, 2)] = ref[...]
+
+
+def placed(chan, pieces):
+    samples, rows, own, wide = pieces[0].shape
+    return pl.pallas_call(
+        place_kernel,
+        in_specs=[pl.BlockSpec(memory_space=pltpu.SMEM)] + [pl.BlockSpec(memory_space=pltpu.VMEM)] * len(pieces),
+        out_shape=jax.ShapeDtypeStruct((samples, rows * len(pieces), own, wide), BF16),
+        compiler_params=params(VMEM),
+        cost_estimate=cost(1e6, 1e6),
+        name="place",
+    )(chan, *pieces)
 
 
 def join_kernel(coarse_ref, coarse_more_ref, fine_ref, fine_more_ref, out_ref):
@@ -393,7 +483,7 @@
 SWAP = ((0, 1), (1, 0))
 
 
-def grad_sums(fine_keep, fine_more, coarse_keep, coarse_more):
+def grad_sums(fine_keep, fine_more, coarse_keep, coarse_more, back):
     chips = 1
     for axis in CHIPS:
         chips *= lax.axis_size(axis)
@@ -415,7 +505,8 @@
         cost_estimate=cost(1e6, 1.3e6),
         name="sum_parts",
     )(parts)
-    return lax.all_to_all(summed, CHIPS, 0, 0, tiled=True).reshape(chips * each, 16, 128)
+    summed, *back = lax.optimization_barrier((summed, *back))
+    return lax.all_to_all(summed, CHIPS, 0, 0, tiled=True).reshape(chips * each, 16, 128), back
 
 
 def unpacked(core, mine, other, fine_shape, coarse_shape):
@@ -433,13 +524,13 @@
     return fine.reshape(fine_shape), coarse.reshape(coarse_shape)
 
 
-def edges(low, high):
+def edges(low, high, axes):
     count = 1
-    for axis in ALL:
+    for axis in axes:
         count *= lax.axis_size(axis)
     forward = [(i, i + 1) for i in range(count - 1)]
     backward = [(target, source) for source, target in forward]
-    return lax.ppermute(high, ALL, forward), lax.ppermute(low, ALL, backward)
+    return lax.ppermute(high, axes, forward), lax.ppermute(low, axes, backward)
 
 
 def shards(coarse_input, coarse_pre, skip_feats, fine_pre, fine_cotangent, fine_weight, coarse_weight):
@@ -451,38 +542,40 @@
         devices *= lax.axis_size(axis)
     samples, lines, wide, own = coarse_input.shape
     core = lax.axis_index("core").astype(jnp.int32).reshape(1)
+    chan = lax.axis_index(CHAN).astype(jnp.int32).reshape(1)
 
     def grad_row(line):
         return (
             fine_cotangent[:, line].astype(F32) * silu_grad(fine_pre[:, line].astype(F32))
         ).astype(BF16)
 
-    top, bottom = grad_row(0), grad_row(-1)
-    low, high = edges(top, bottom)
-    both = jnp.stack([coarse_pre, coarse_input]).reshape(2, samples, peers, lines // peers, wide, own)
-    both = both.transpose(2, 0, 1, 3, 5, 4)
-    both, top, bottom = lax.optimization_barrier((both, top, bottom))
-    received = lax.all_to_all(both, CHAN, 0, 0, tiled=True)
+    pieces = jnp.stack([coarse_pre, coarse_input]).reshape(2, samples, peers, lines // peers, wide, own)
+    pieces = pieces.transpose(2, 0, 1, 3, 5, 4)
+    received = lax.all_to_all(pieces, CHAN, 0, 0, tiled=True)
+    low, high = edges(grad_row(0), grad_row(-1), ALL)
 
     cs = skip_feats.shape[-1]
     fine_cells = fine_pre.shape[0] * fine_pre.shape[1] * fine_pre.shape[2] * devices
-    fine_grad, pooled, box = box_level(fine_cotangent, fine_pre, low, high, fine_weight, cs)
-    first, second = coarse_grad(pooled, received)
-    coarse_low, coarse_high = edges(first, second)
-    grad_skip, fine_keep, fine_send = fine_level(
-        core, fine_grad, skip_feats, fine_weight, received, box, fine_cells
-    )
+    fine_grad, pooled, box, up_weight = box_level(fine_cotangent, fine_pre, fine_weight, cs)
+    pooled = pltpu.with_memory_space_constraint(pooled, pltpu.HBM)
+    first, second, box_low, box_high = coarse_grad(low, high, fine_grad, pooled, up_weight, received)
+    coarse_low, coarse_high = edges(first, second, ALL)
+    low, first = lax.optimization_barrier((low, first))
+    grad_skip, skip_keep, skip_send = fine_level(core, fine_grad, low, high, skip_feats, fine_weight, fine_cells)
+    fine_keep, fine_send = up_level(core, received, box, box_low, box_high, skip_keep, skip_send, fine_cells)
     fine_more = lax.ppermute(fine_send, "core", SWAP)
+    coarse_low, coarse_high, fine_keep = lax.optimization_barrier((coarse_low, coarse_high, fine_keep))
     rows = (coarse_low, first, second, coarse_high)
     coarse_cells = samples * (lines // peers) * wide * devices
     coarse_keep, coarse_send = coarse_weight_level(core, received, rows, coarse_cells)
     coarse_more = lax.ppermute(coarse_send, "core", SWAP)
-    back = coarse_input_level(coarse_weight, rows, peers)
-    mine = grad_sums(fine_keep, fine_more, coarse_keep, coarse_more)
-    back, mine = lax.optimization_barrier((back, mine))
+    back = coarse_input_level(chan, coarse_weight, rows, peers)
+    back = [back[0]] + [
+        lax.ppermute(back[k], CHAN, [(i, i ^ k) for i in range(peers)]) for k in range(1, peers)
+    ]
+    mine, back = grad_sums(fine_keep, fine_more, coarse_keep, coarse_more, back)
     other = lax.ppermute(mine, "core", SWAP)
-    back = lax.all_to_all(back, CHAN, 0, 0, tiled=True)
-    grad_input = back.transpose(1, 0, 2, 4, 3).reshape(coarse_input.shape)
+    grad_input = placed(chan, back).transpose(0, 1, 3, 2)
     grad_fine, grad_coarse = unpacked(core, mine, other, fine_weight.shape, coarse_weight.shape)
     return grad_skip, grad_input, grad_fine, grad_coarse
 

time: 142 us -> 123 us (0.87)
  blocking collectives: 42 us -> 24.2 us
  waiting for transfers between devices: 38.9 us -> 26 us
  starting transfers between devices: 32.1 us -> 42.7 us
  Pallas kernels: 16.5 us -> 19.6 us
  local copies, waits for them, and re-layouts: 8.15 us -> 5.64 us
    all_to_all x2 -> x1, blocking collectives: 42 us -> 24.2 us  [grad_sums(): lax.all_to_all(summed, CHIPS, 0, 0, tiled=True)]
    all_to_all x2, waiting for transfers between devices: 13.5 us -> 0.37 us  [the longest x1 0.37 us: grad_sums(): lax.all_to_all(joined.reshape(chips, each, 16, 128), CHIPS, 0, 0, tiled=T...]
    ppermute x4 -> x11, starting transfers between devices: 16.2 us -> 23.2 us  [the longest x7 9.43 us: shards(): lax.ppermute(back[k], CHAN, [(i, i ^ k) for i in range(peers)])]
    all_to_all x2, starting transfers between devices: 11.3 us -> 15.1 us  [the longest x1 9.2 us: grad_sums(): lax.all_to_all(joined.reshape(chips, each, 16, 128), CHIPS, 0, 0, tiled=T...]
    pallas_call x2 -> x4, Pallas kernels: 3.07 us -> 6.38 us  [the longest x1 2.23 us: coarse_grad(): pl.pallas_call(coarse_grad_kernel, grid=(samples,), in_specs=[edge, edge,...]
    ppermute x4 -> x11, waiting for transfers between devices: 23.8 us -> 22 us  [the longest x2 12 us: edges(): lax.ppermute(high, axes, forward)]
    unnamed x28 -> x34, local copies, waits for them, and re-layouts: 7.32 us -> 5.64 us
    ppermute x1, waiting for transfers between devices: 0.01 us -> 1.46 us  [shards(): other = lax.ppermute(mine, 'core', SWAP)]
  transfers between devices with their start and end apart: 9 -> 16, of which waited for: 6 -> 11; matrix products, arithmetic and copies ran while one was open for 1% -> 1% of each run, Pallas kernels for 7% -> 10%
where the time goes in v2:
time: 123 us
  starting transfers between devices  42.7 us (35%)
  waiting for transfers between devices  26 us (21%)
  blocking collectives  24.2 us (20%)
  Pallas kernels  19.6 us (16%)
  local copies, waits for them, and re-layouts  5.64 us (5%)
  other arithmetic  3.55 us (3%)
    all_to_all x1, blocking collectives, grad_sums(): lax.all_to_all(summed, CHIPS, 0, 0, tiled=True)  24.2 us
    ppermute x2, waiting for transfers between devices, edges(): lax.ppermute(high, axes, forward)  12 us
    ppermute x7, starting transfers between devices, shards(): lax.ppermute(back[k], CHAN, [(i, i ^ k) for i in range(peers)])  9.43 us
    ppermute x2, starting transfers between devices, edges(): lax.ppermute(low, axes, backward)  9.35 us
    all_to_all x1, starting transfers between devices, grad_sums(): lax.all_to_all(joined.reshape(chips, each, 16, 128), CHIPS, 0, 0, tiled=T...  9.2 us
    ppermute x7, waiting for transfers between devices, shards(): lax.ppermute(back[k], CHAN, [(i, i ^ k) for i in range(peers)])  9.07 us
    all_to_all x1, starting transfers between devices, shards(): received = lax.all_to_all(pieces, CHAN, 0, 0, tiled=True)  5.95 us
    unnamed x34, local copies, waits for them, and re-layouts  5.64 us
  transfers between devices with their start and end apart: 16, of which 11 were waited for; matrix products, arithmetic and copies ran while one was open for 1% of the time, Pallas kernels for 10%

profile of v2, /device:TPU:1, one launch (start us, length us, event | category | flops | bytes accessed | tf_op | source)
XLA Modules:
  0.0 122.6 jit_solution(6370544147556953961)
XLA Ops:
  0.7 2.4 %copy_bitcast_fusion = bf16[8,2,2,2,32,256]{5,4,3,2,1,0:T(8,128)(2,1)} fusion(bf16[1,2,8,2,256,32]{4,5,3,2,1,0:T(8,128)(2,1)} %bitcast.38, bf16[1,2,8,2,256,32]{4,5,3,2,1,0:T(8,128)(2,1)} %bitcast.39), kind=kLoop, calls=%fused_computation.1 | loop fusion | flops 524288 | bytes 2097152 | tf_op jit(solution)/shard_map/transpose | solution.py:553
  3.1 5.9 %all-to-all-start = ((bf16[8,2,2,2,32,256]{5,4,3,2,1,0:T(8,128)(2,1)}), bf16[8,2,2,2,32,256]{5,4,3,2,1,0:T(8,128)(2,1)S(1)}, u32[]{:S(2)}, u32[]{:S(2)}) async-start(bf16[8,2,2,2,32,256]{5,4,3,2,1,0:T(8,128)(2,1)} %copy_bitcast_fusion), calls=%async_computation | async-start | bytes 2097152 | tf_op jit(solution)/shard_map/all_to_all | solution.py:554
  10.2 6.6 %collective-permute-start.1 = (bf16[2,512,128]{2,1,0:T(8,128)(2,1)}, bf16[2,512,128]{2,1,0:T(8,128)(2,1)S(1)}, u32[]{:S(2)}, u32[]{:S(2)}) collective-permute-start(bf16[2,512,128]{2,1,0:T(8,128)(2,1)} %get-tuple-element.82), channel_id=1, source_target_pairs={{1,0},{2,1},{3,2},{4,3},{5,4},{6,5},{7,6},{8,7},{9,8},{10,9},{11,1... | collective-permute-start | bytes 786440 | tf_op jit(solution)/shard_map/ppermute | solution.py:533
  16.8 1.9 %collective-permute-start = (bf16[2,512,128]{2,1,0:T(8,128)(2,1)S(1)}, bf16[2,512,128]{2,1,0:T(8,128)(2,1)S(1)}, u32[]{:S(2)}, u32[]{:S(2)}) collective-permute-start(bf16[2,512,128]{2,1,0:T(8,128)(2,1)S(1)} %get-tuple-element.83), channel_id=1, source_target_pairs={{0,1},{1,2},{2,3},{3,4},{4,5},{5,6},{6,7},{7,8},{8,9},{9,10},{10,1... | collective-permute-start | bytes 786440 | tf_op jit(solution)/shard_map/ppermute | solution.py:533
  22.3 2.1 %box_level.1 = (bf16[2,4,512,128]{3,2,1,0:T(8,128)(2,1)S(1)}, f32[2,2,256,256]{3,2,1,0:T(8,128)S(1)}, bf16[2,256,1152]{2,1,0:T(8,128)(2,1)S(1)}, bf16[1152,256]{1,0:T(8,128)(2,1)S(1)}) custom-call(bf16[2,4,512,128]{3,2,1,0:T(8,128)(2,1)S(1)} %copy-done.2, bf16[2,4,512,128]{3,2,1,0:T(8,128)(2,1)S(1)} %copy-done.4, bf16[3,3,384,128]{3,2,1,0:T(8,128)(2,1)S(1)} %copy-done.7), custom_call_target="tpu_custom_call" | custom-call | flops 1200000000 | bytes 8000000 | tf_op jit(solution)/shard_map/box_level/pallas_call | solution.py:95
  27.3 8.9 %collective-permute-done.low_ref = bf16[2,512,128]{2,1,0:T(8,128)(2,1)S(1)} collective-permute-done((bf16[2,512,128]{2,1,0:T(8,128)(2,1)S(1)}, bf16[2,512,128]{2,1,0:T(8,128)(2,1)S(1)}, u32[]{:S(2)}, u32[]{:S(2)}) %collective-permute-start) | collective-permute-done | bytes 262176 | tf_op jit(solution)/shard_map/ppermute | solution.py:533
  36.2 2.2 %coarse_grad.1 = (bf16[2,256,256]{2,1,0:T(8,128)(2,1)S(1)}, bf16[2,256,256]{2,1,0:T(8,128)(2,1)S(1)}, bf16[2,256,384]{2,1,0:T(8,128)(2,1)S(1)}, bf16[2,256,384]{2,1,0:T(8,128)(2,1)S(1)}) custom-call(bf16[2,512,128]{2,1,0:T(8,128)(2,1)S(1)} %collective-permute-done.low_ref, bf16[2,512,128]{2,1,0:T(8,128)(2,1)S(1)} %collective-permute-done.1.high_ref, ...), custom_call_target="tpu_custom_call" | custom-call | flops 400000000 | bytes 4000000 | tf_op jit(solution)/shard_map/coarse_grad/pallas_call | solution.py:230
  38.5 2.8 %collective-permute-start.3 = (bf16[2,256,256]{2,1,0:T(8,128)(2,1)S(1)}, bf16[2,256,256]{2,1,0:T(8,128)(2,1)S(1)}, u32[]{:S(2)}, u32[]{:S(2)}) collective-permute-start(bf16[2,256,256]{2,1,0:T(8,128)(2,1)S(1)} %get-tuple-element.57.first_ref), channel_id=1, source_target_pairs={{1,0},{2,1},{3,2},{4,3},{5,4},{6,5},{7,6},{8,7},{9,8},{10,9},{11,1... | collective-permute-start | bytes 786440 | tf_op jit(solution)/shard_map/ppermute | solution.py:533
  41.3 2.5 %collective-permute-start.2 = (bf16[2,256,256]{2,1,0:T(8,128)(2,1)S(1)}, bf16[2,256,256]{2,1,0:T(8,128)(2,1)S(1)}, u32[]{:S(2)}, u32[]{:S(2)}) collective-permute-start(bf16[2,256,256]{2,1,0:T(8,128)(2,1)S(1)} %get-tuple-element.49.second_ref), channel_id=1, source_target_pairs={{0,1},{1,2},{2,3},{3,4},{4,5},{5,6},{6,7},{7,8},{8,9},{9,10},{10,1... | collective-permute-start | bytes 786440 | tf_op jit(solution)/shard_map/ppermute | solution.py:533
  43.8 4.9 %fine_level.1 = (bf16[2,4,512,128]{3,2,1,0:T(8,128)(2,1)}, bf16[9,4,16,128]{3,2,1,0:T(8,128)(2,1)S(1)}, bf16[9,4,16,128]{3,2,1,0:T(8,128)(2,1)S(1)}) custom-call(s32[1]{0:T(128)} %bitcast.core_ref, bf16[2,4,512,128]{3,2,1,0:T(8,128)(2,1)S(1)} %get-tuple-element.43.top_ref.bottom_ref.grad_ref, bf16[2,512,128]{2,1,0:T(8,128)(2,1)S(1)} %collective-permute-done.low_ref, ...), custom_call_target="tpu_custom_call" | custom-call | flops 5000000000 | bytes 8000000 | tf_op jit(solution)/shard_map/fine_level/pallas_call | solution.py:177
  48.7 1.3 %up_level.1 = (bf16[9,12,16,128]{3,2,1,0:T(8,128)(2,1)S(1)}, bf16[9,12,16,128]{3,2,1,0:T(8,128)(2,1)S(1)}) custom-call(s32[1]{0:T(128)} %bitcast.core_ref, bf16[8,2,2,2,32,256]{5,4,3,2,1,0:T(8,128)(2,1)S(1)} %all-to-all-done.pre_ref.input_ref, bf16[2,256,1152]{2,1,0:T(8,128)(2,1)S(1)} %copy-done.16, bf16[2,256,384]{2,1,0:T(8,128)(2,1)S(1)} %get-tuple-element.51.box_low_ref, ...), custom_call_target="tpu_custom_call" | custom-call | flops 1000000000 | bytes 5000000 | tf_op jit(solution)/shard_map/up_level/pallas_call | solution.py:299
  50.0 3.1 %collective-permute-done.2.low_ref = bf16[2,256,256]{2,1,0:T(8,128)(2,1)S(1)} collective-permute-done((bf16[2,256,256]{2,1,0:T(8,128)(2,1)S(1)}, bf16[2,256,256]{2,1,0:T(8,128)(2,1)S(1)}, u32[]{:S(2)}, u32[]{:S(2)}) %collective-permute-start.2) | collective-permute-done | bytes 262176 | tf_op jit(solution)/shard_map/ppermute | solution.py:533
  53.2 2.1 %coarse_weight_level.1 = (bf16[144,16,128]{2,1,0:T(8,128)(2,1)S(1)}, bf16[144,16,128]{2,1,0:T(8,128)(2,1)S(1)}) custom-call(s32[1]{0:T(128)} %bitcast.core_ref, bf16[8,2,2,2,32,256]{5,4,3,2,1,0:T(8,128)(2,1)S(1)} %all-to-all-done.pre_ref.input_ref, bf16[2,256,256]{2,1,0:T(8,128)(2,1)S(1)} %collective-permute-done.2.low_ref, ...), custom_call_target="tpu_custom_call" | custom-call | flops 1300000000 | bytes 3000000 | tf_op jit(solution)/shard_map/coarse_weight_level/pallas_call | solution.py:370
  55.8 2.1 %collective-permute-done.5 = bf16[9,12,16,128]{3,2,1,0:T(8,128)(2,1)S(1)} collective-permute-done((bf16[9,12,16,128]{3,2,1,0:T(8,128)(2,1)S(1)}, bf16[9,12,16,128]{3,2,1,0:T(8,128)(2,1)S(1)}, u32[]{:S(2)}, u32[]{:S(2)}) %collective-permute-start.5) | collective-permute-done | bytes 442400 | tf_op jit(solution)/shard_map/ppermute | solution.py:566
  59.2 9.2 %all-to-all-start.1 = ((bf16[64,4,16,128]{3,2,1,0:T(8,128)(2,1)}), bf16[64,4,16,128]{3,2,1,0:T(8,128)(2,1)S(1)}, u32[]{:S(2)}, u32[]{:S(2)}) async-start(bf16[64,4,16,128]{3,2,1,0:T(8,128)(2,1)} %bitcast.13), calls=%async_computation.1 | async-start | bytes 2097152 | tf_op jit(solution)/shard_map/all_to_all | solution.py:500
  68.4 2.4 %coarse_input_level.1 = (bf16[2,2,32,256]{3,2,1,0:T(8,128)(2,1)S(1)}, bf16[2,2,32,256]{3,2,1,0:T(8,128)(2,1)S(1)}, bf16[2,2,32,256]{3,2,1,0:T(8,128)(2,1)S(1)}, ...) custom-call(s32[1]{0:T(128)} %bitcast.10.chan_ref, ...), custom_call_target="tpu_custom_call" | custom-call | flops 1300000000 | bytes 3000000 | tf_op jit(solution)/shard_map/coarse_input_level/pallas_call | solution.py:407
  73.5 2.5 %collective-permute-start.9 = (bf16[2,2,32,256]{3,2,1,0:T(8,128)(2,1)}, bf16[2,2,32,256]{3,2,1,0:T(8,128)(2,1)S(1)}, u32[]{:S(2)}, u32[]{:S(2)}) collective-permute-start(bf16[2,2,32,256]{3,2,1,0:T(8,128)(2,1)} %get-tuple-element.67), channel_id=1, source_target_pairs={{0,4},{1,5},{2,6},{3,7},{4,0},{5,1},{6,2},{7,3},{8,12},{9,13},{10,... | collective-permute-start | bytes 196616 | tf_op jit(solution)/shard_map/ppermute | solution.py:574
  77.2 5.1 %collective-permute-done.6.refs_1_ = bf16[2,2,32,256]{3,2,1,0:T(8,128)(2,1)S(1)} collective-permute-done((bf16[2,2,32,256]{3,2,1,0:T(8,128)(2,1)S(1)}, bf16[2,2,32,256]{3,2,1,0:T(8,128)(2,1)S(1)}, u32[]{:S(2)}, u32[]{:S(2)}) %collective-permute-start.6) | collective-permute-done | bytes 65568 | tf_op jit(solution)/shard_map/ppermute | solution.py:574
  82.3 2.4 %collective-permute-start.11 = (bf16[2,2,32,256]{3,2,1,0:T(8,128)(2,1)S(1)}, bf16[2,2,32,256]{3,2,1,0:T(8,128)(2,1)S(1)}, u32[]{:S(2)}, u32[]{:S(2)}) collective-permute-start(bf16[2,2,32,256]{3,2,1,0:T(8,128)(2,1)S(1)} %get-tuple-element.69), channel_id=1, source_target_pairs={{0,6},{1,7},{2,4},{3,5},{4,2},{5,3},{6,0},{7,1},{8,14},{9,15},{10,... | collective-permute-start | bytes 196616 | tf_op jit(solution)/shard_map/ppermute | solution.py:574
  87.7 2.2 %collective-permute-done.12.refs_7_ = bf16[2,2,32,256]{3,2,1,0:T(8,128)(2,1)S(1)} collective-permute-done((bf16[2,2,32,256]{3,2,1,0:T(8,128)(2,1)S(1)}, bf16[2,2,32,256]{3,2,1,0:T(8,128)(2,1)S(1)}, u32[]{:S(2)}, u32[]{:S(2)}) %collective-permute-start.12) | collective-permute-done | bytes 65568 | tf_op jit(solution)/shard_map/ppermute | solution.py:574
  89.9 24.2 %all_to_all.15 = bf16[64,4,16,128]{3,2,1,0:T(8,128)(2,1)S(1)} all-to-all(bf16[64,4,16,128]{3,2,1,0:T(8,128)(2,1)S(1)} %sum_parts.1), channel_id=1, replica_groups=mesh['xh'=2,'z'=4,'core'=2,'y'=4,'xl'=2] {'xh','xl','z','y'}, dimensions={0} | all-to-all | bytes 2097152 | tf_op jit(solution)/shard_map/all_to_all | solution.py:509
  114.2 3.8 %collective-permute-start.13 = (bf16[256,16,128]{2,1,0:T(8,128)(2,1)S(1)}, bf16[256,16,128]{2,1,0:T(8,128)(2,1)S(1)}, u32[]{:S(2)}, u32[]{:S(2)}) collective-permute-start(bf16[256,16,128]{2,1,0:T(8,128)(2,1)S(1)} %bitcast.33), channel_id=1, source_target_pairs={{0,8},{8,0},{1,9},{9,1},{2,10},{10,2},{3,11},{11,3},{4,12},{12,4},... | collective-permute-start | bytes 3145736 | tf_op jit(solution)/shard_map/ppermute | solution.py:577
  118.8 1.5 %collective-permute-done.13.other_ref = bf16[256,16,128]{2,1,0:T(8,128)(2,1)S(1)} collective-permute-done((bf16[256,16,128]{2,1,0:T(8,128)(2,1)S(1)}, bf16[256,16,128]{2,1,0:T(8,128)(2,1)S(1)}, u32[]{:S(2)}, u32[]{:S(2)}) %collective-permute-start.13) | collective-permute-done | bytes 1048608 | tf_op jit(solution)/shard_map/ppermute | solution.py:577
  120.2 2.4 %unpack.1 = (f32[9,384,128]{2,1,0:T(8,128)}, f32[9,256,256]{2,1,0:T(8,128)}) custom-call(s32[1]{0:T(128)} %bitcast.core_ref, bf16[256,16,128]{2,1,0:T(8,128)(2,1)S(1)} %bitcast.34, bf16[256,16,128]{2,1,0:T(8,128)(2,1)S(1)} %collective-permute-done.13.other_ref), custom_call_target="tpu_custom_call" | custom-call | flops 1000000 | bytes 6000000 | tf_op jit(solution)/shard_map/unpack/pallas_call | solution.py:516
  (55 shorter events, 17.2 us)
Async XLA Ops:
  0.6 8.4 %copy-start.1 = (bf16[2,4,512,128]{3,2,1,0:T(8,128)(2,1)S(1)}, bf16[2,4,512,128]{3,2,1,0:T(8,128)(2,1)}, u32[]{:S(2)}) copy-start(bf16[2,4,512,128]{3,2,1,0:T(8,128)(2,1)} %cot_ref.1) | copy-start | bytes 3145732
  0.6 8.4 %copy-start.3 = (bf16[2,4,512,128]{3,2,1,0:T(8,128)(2,1)S(1)}, bf16[2,4,512,128]{3,2,1,0:T(8,128)(2,1)}, u32[]{:S(2)}) copy-start(bf16[2,4,512,128]{3,2,1,0:T(8,128)(2,1)} %pre_ref.1) | copy-start | bytes 3145732
  3.1 33.2 %all-to-all-start = ((bf16[8,2,2,2,32,256]{5,4,3,2,1,0:T(8,128)(2,1)}), bf16[8,2,2,2,32,256]{5,4,3,2,1,0:T(8,128)(2,1)S(1)}, u32[]{:S(2)}, u32[]{:S(2)}) async-start(bf16[8,2,2,2,32,256]{5,4,3,2,1,0:T(8,128)(2,1)} %copy_bitcast_fusion), calls=%async_computation | async-start | bytes 2097152 | tf_op jit(solution)/shard_map/all_to_all | solution.py:554
  10.2 17.2 %collective-permute-start.1 = (bf16[2,512,128]{2,1,0:T(8,128)(2,1)}, bf16[2,512,128]{2,1,0:T(8,128)(2,1)S(1)}, u32[]{:S(2)}, u32[]{:S(2)}) collective-permute-start(bf16[2,512,128]{2,1,0:T(8,128)(2,1)} %get-tuple-element.82), channel_id=1, source_target_pairs={{1,0},{2,1},{3,2},{4,3},{5,4},{6,5},{7,6},{8,7},{9,8},{10,9},{11,1... | collective-permute-start | bytes 786440 | tf_op jit(solution)/shard_map/ppermute | solution.py:533
  16.8 19.5 %collective-permute-start = (bf16[2,512,128]{2,1,0:T(8,128)(2,1)S(1)}, bf16[2,512,128]{2,1,0:T(8,128)(2,1)S(1)}, u32[]{:S(2)}, u32[]{:S(2)}) collective-permute-start(bf16[2,512,128]{2,1,0:T(8,128)(2,1)S(1)} %get-tuple-element.83), channel_id=1, source_target_pairs={{0,1},{1,2},{2,3},{3,4},{4,5},{5,6},{6,7},{7,8},{8,9},{9,10},{10,1... | collective-permute-start | bytes 786440 | tf_op jit(solution)/shard_map/ppermute | solution.py:533
  36.2 7.6 %copy-start.8 = (bf16[3,3,384,128]{3,2,1,0:T(8,128)(2,1)S(1)}, bf16[3,3,384,128]{3,2,1,0:T(8,128)(2,1)}, u32[]{:S(2)}) copy-start(bf16[3,3,384,128]{3,2,1,0:T(8,128)(2,1)} %weight_ref.4) | copy-start | bytes 2654212
  38.5 14.7 %copy-start.9 = (bf16[2,256,256]{2,1,0:T(8,128)(2,1)}, bf16[2,256,256]{2,1,0:T(8,128)(2,1)S(1)}, u32[]{:S(2)}) copy-start(bf16[2,256,256]{2,1,0:T(8,128)(2,1)S(1)} %get-tuple-element.49.second_ref) | copy-start | bytes 786436
  38.5 11.5 %collective-permute-start.3 = (bf16[2,256,256]{2,1,0:T(8,128)(2,1)S(1)}, bf16[2,256,256]{2,1,0:T(8,128)(2,1)S(1)}, u32[]{:S(2)}, u32[]{:S(2)}) collective-permute-start(bf16[2,256,256]{2,1,0:T(8,128)(2,1)S(1)} %get-tuple-element.57.first_ref), channel_id=1, source_target_pairs={{1,0},{2,1},{3,2},{4,3},{5,4},{6,5},{7,6},{8,7},{9,8},{10,9},{11,1... | collective-permute-start | bytes 786440 | tf_op jit(solution)/shard_map/ppermute | solution.py:533
  41.3 11.9 %collective-permute-start.2 = (bf16[2,256,256]{2,1,0:T(8,128)(2,1)S(1)}, bf16[2,256,256]{2,1,0:T(8,128)(2,1)S(1)}, u32[]{:S(2)}, u32[]{:S(2)}) collective-permute-start(bf16[2,256,256]{2,1,0:T(8,128)(2,1)S(1)} %get-tuple-element.49.second_ref), channel_id=1, source_target_pairs={{0,1},{1,2},{2,3},{3,4},{4,5},{5,6},{6,7},{7,8},{8,9},{9,10},{10,1... | collective-permute-start | bytes 786440 | tf_op jit(solution)/shard_map/ppermute | solution.py:533
  55.3 2.7 %collective-permute-start.4 = (bf16[144,16,128]{2,1,0:T(8,128)(2,1)S(1)}, bf16[144,16,128]{2,1,0:T(8,128)(2,1)S(1)}, u32[]{:S(2)}, u32[]{:S(2)}) collective-permute-start(bf16[144,16,128]{2,1,0:T(8,128)(2,1)S(1)} %get-tuple-element.60), channel_id=1, source_target_pairs={{0,8},{8,0},{1,9},{9,1},{2,10},{10,2},{3,11},{11,3},{4,12},{12,4},... | collective-permute-start | bytes 1769480 | tf_op jit(solution)/shard_map/ppermute | solution.py:571
  55.3 2.6 %collective-permute-start.5 = (bf16[9,12,16,128]{3,2,1,0:T(8,128)(2,1)S(1)}, bf16[9,12,16,128]{3,2,1,0:T(8,128)(2,1)S(1)}, u32[]{:S(2)}, u32[]{:S(2)}) collective-permute-start(bf16[9,12,16,128]{3,2,1,0:T(8,128)(2,1)S(1)} %get-tuple-element.62), channel_id=1, source_target_pairs={{0,8},{8,0},{1,9},{9,1},{2,10},{10,2},{3,11},{11,3},{4,12},{12,4},... | collective-permute-start | bytes 1327112 | tf_op jit(solution)/shard_map/ppermute | solution.py:566
  59.2 9.2 %copy-start.5 = (bf16[3,3,256,256]{3,2,1,0:T(8,128)(2,1)S(1)}, bf16[3,3,256,256]{3,2,1,0:T(8,128)(2,1)}, u32[]{:S(2)}) copy-start(bf16[3,3,256,256]{3,2,1,0:T(8,128)(2,1)} %weight_ref.5) | copy-start | bytes 3538948
  59.2 9.2 %copy-start.10 = (bf16[2,256,256]{2,1,0:T(8,128)(2,1)S(1)}, bf16[2,256,256]{2,1,0:T(8,128)(2,1)}, u32[]{:S(2)}) copy-start(bf16[2,256,256]{2,1,0:T(8,128)(2,1)} %copy-done.9) | copy-start | bytes 786436
  59.2 9.2 %copy-start.12 = (bf16[2,256,256]{2,1,0:T(8,128)(2,1)S(1)}, bf16[2,256,256]{2,1,0:T(8,128)(2,1)}, u32[]{:S(2)}) copy-start(bf16[2,256,256]{2,1,0:T(8,128)(2,1)} %copy-done.11) | copy-start | bytes 786436
  59.2 9.2 %copy-start.14 = (bf16[2,256,256]{2,1,0:T(8,128)(2,1)S(1)}, bf16[2,256,256]{2,1,0:T(8,128)(2,1)}, u32[]{:S(2)}) copy-start(bf16[2,256,256]{2,1,0:T(8,128)(2,1)} %copy-done.13) | copy-start | bytes 786436
  59.2 26.5 %all-to-all-start.1 = ((bf16[64,4,16,128]{3,2,1,0:T(8,128)(2,1)}), bf16[64,4,16,128]{3,2,1,0:T(8,128)(2,1)S(1)}, u32[]{:S(2)}, u32[]{:S(2)}) async-start(bf16[64,4,16,128]{3,2,1,0:T(8,128)(2,1)} %bitcast.13), calls=%async_computation.1 | async-start | bytes 2097152 | tf_op jit(solution)/shard_map/all_to_all | solution.py:500
  70.8 11.5 %collective-permute-start.6 = (bf16[2,2,32,256]{3,2,1,0:T(8,128)(2,1)S(1)}, bf16[2,2,32,256]{3,2,1,0:T(8,128)(2,1)S(1)}, u32[]{:S(2)}, u32[]{:S(2)}) collective-permute-start(bf16[2,2,32,256]{3,2,1,0:T(8,128)(2,1)S(1)} %get-tuple-element.64), channel_id=1, source_target_pairs={{0,1},{1,0},{2,3},{3,2},{4,5},{5,4},{6,7},{7,6},{8,9},{9,8},{10,11... | collective-permute-start | bytes 196616 | tf_op jit(solution)/shard_map/ppermute | solution.py:574
  71.8 12.8 %collective-permute-start.7 = (bf16[2,2,32,256]{3,2,1,0:T(8,128)(2,1)S(1)}, bf16[2,2,32,256]{3,2,1,0:T(8,128)(2,1)S(1)}, u32[]{:S(2)}, u32[]{:S(2)}) collective-permute-start(bf16[2,2,32,256]{3,2,1,0:T(8,128)(2,1)S(1)} %get-tuple-element.65), channel_id=1, source_target_pairs={{0,2},{1,3},{2,0},{3,1},{4,6},{5,7},{6,4},{7,5},{8,10},{9,11},{10,... | collective-permute-start | bytes 196616 | tf_op jit(solution)/shard_map/ppermute | solution.py:574
  73.0 13.0 %collective-permute-start.8 = (bf16[2,2,32,256]{3,2,1,0:T(8,128)(2,1)}, bf16[2,2,32,256]{3,2,1,0:T(8,128)(2,1)S(1)}, u32[]{:S(2)}, u32[]{:S(2)}) collective-permute-start(bf16[2,2,32,256]{3,2,1,0:T(8,128)(2,1)} %get-tuple-element.66), channel_id=1, source_target_pairs={{0,3},{1,2},{2,1},{3,0},{4,7},{5,6},{6,5},{7,4},{8,11},{9,10},{10,... | collective-permute-start | bytes 196616 | tf_op jit(solution)/shard_map/ppermute | solution.py:574
  73.5 12.9 %collective-permute-start.9 = (bf16[2,2,32,256]{3,2,1,0:T(8,128)(2,1)}, bf16[2,2,32,256]{3,2,1,0:T(8,128)(2,1)S(1)}, u32[]{:S(2)}, u32[]{:S(2)}) collective-permute-start(bf16[2,2,32,256]{3,2,1,0:T(8,128)(2,1)} %get-tuple-element.67), channel_id=1, source_target_pairs={{0,4},{1,5},{2,6},{3,7},{4,0},{5,1},{6,2},{7,3},{8,12},{9,13},{10,... | collective-permute-start | bytes 196616 | tf_op jit(solution)/shard_map/ppermute | solution.py:574
  76.0 11.5 %collective-permute-start.10 = (bf16[2,2,32,256]{3,2,1,0:T(8,128)(2,1)S(1)}, bf16[2,2,32,256]{3,2,1,0:T(8,128)(2,1)S(1)}, u32[]{:S(2)}, u32[]{:S(2)}) collective-permute-start(bf16[2,2,32,256]{3,2,1,0:T(8,128)(2,1)S(1)} %get-tuple-element.68), channel_id=1, source_target_pairs={{0,5},{1,4},{2,7},{3,6},{4,1},{5,0},{6,3},{7,2},{8,13},{9,12},{10,... | collective-permute-start | bytes 196616 | tf_op jit(solution)/shard_map/ppermute | solution.py:574
  82.3 5.5 %collective-permute-start.11 = (bf16[2,2,32,256]{3,2,1,0:T(8,128)(2,1)S(1)}, bf16[2,2,32,256]{3,2,1,0:T(8,128)(2,1)S(1)}, u32[]{:S(2)}, u32[]{:S(2)}) collective-permute-start(bf16[2,2,32,256]{3,2,1,0:T(8,128)(2,1)S(1)} %get-tuple-element.69), channel_id=1, source_target_pairs={{0,6},{1,7},{2,4},{3,5},{4,2},{5,3},{6,0},{7,1},{8,14},{9,15},{10,... | collective-permute-start | bytes 196616 | tf_op jit(solution)/shard_map/ppermute | solution.py:574
  84.7 5.3 %collective-permute-start.12 = (bf16[2,2,32,256]{3,2,1,0:T(8,128)(2,1)S(1)}, bf16[2,2,32,256]{3,2,1,0:T(8,128)(2,1)S(1)}, u32[]{:S(2)}, u32[]{:S(2)}) collective-permute-start(bf16[2,2,32,256]{3,2,1,0:T(8,128)(2,1)S(1)} %get-tuple-element.70), channel_id=1, source_target_pairs={{0,7},{1,6},{2,5},{3,4},{4,3},{5,2},{6,1},{7,0},{8,15},{9,14},{10,... | collective-permute-start | bytes 196616 | tf_op jit(solution)/shard_map/ppermute | solution.py:574
  114.2 6.1 %collective-permute-start.13 = (bf16[256,16,128]{2,1,0:T(8,128)(2,1)S(1)}, bf16[256,16,128]{2,1,0:T(8,128)(2,1)S(1)}, u32[]{:S(2)}, u32[]{:S(2)}) collective-permute-start(bf16[256,16,128]{2,1,0:T(8,128)(2,1)S(1)} %bitcast.33), channel_id=1, source_target_pairs={{0,8},{8,0},{1,9},{9,1},{2,10},{10,2},{3,11},{11,3},{4,12},{12,4},... | collective-permute-start | bytes 3145736 | tf_op jit(solution)/shard_map/ppermute | solution.py:577
  (9 other events, 25.4 us)

commit v3 on v2

v3 whole, which is shorter than its diff:
```python
import functools
import math

import jax
import jax.numpy as jnp
from jax import lax
from jax.experimental import pallas as pl
from jax.experimental.pallas import tpu as pltpu
from jax.sharding import Mesh
from jax.sharding import PartitionSpec as P

F32 = jnp.float32
BF16 = jnp.bfloat16
MIB = 1 << 20
VMEM = 18
EARLY = 6
LONG = 1e11

SPLIT = (("xh", 2), ("z", 4), ("core", 2), ("y", 4), ("xl", 2))
ROWS = ("xh", "z", "core")
CHAN = ("y", "xl")
ALL = ROWS + CHAN
CHIPS = ("xh", "xl", "z", "y")


def params(limit):
    return pltpu.CompilerParams(vmem_limit_bytes=limit * MIB)


def cost(flops, nbytes):
    return pl.CostEstimate(flops=int(flops), bytes_accessed=int(nbytes), transcendentals=0)


def in_hbm(array):
    return pltpu.with_memory_space_constraint(array, pltpu.HBM)


def silu_grad(value):
    sigma = jax.nn.sigmoid(value)
    return sigma * (1.0 + value * (1.0 - sigma))


def shifted(field):
    extent = field.shape[0]
    index = lax.broadcasted_iota(jnp.int32, field.shape, 0)
    before = jnp.where(index == 0, 0.0, pltpu.roll(field, 1, 0))
    after = jnp.where(index == extent - 1, 0.0, pltpu.roll(field, extent - 1, 0))
    return before, after


def tdot(left, right):
    return lax.dot_general(left, right, (((0,), (0,)), ((), ())), preferred_element_type=F32)


def dott(left, right):
    return lax.dot_general(left, right, (((1,), (1,)), ((), ())), preferred_element_type=F32)


def tiles(block):
    return block.astype(BF16).reshape(block.shape[0] // 16, 16, block.shape[1])


def box_sums(upper, lower, half):
    even = upper[pl.ds(0, half, 2), :] + lower[pl.ds(0, half, 2), :]
    odd = upper[pl.ds(1, half, 2), :] + lower[pl.ds(1, half, 2), :]
    before, _ = shifted(odd)
    _, after = shifted(even)
    return (before + even).astype(BF16), (even + odd).astype(BF16), (odd + after).astype(BF16)


def box_kernel(
    place_ref, cot_ref, pre_ref, near_ref, far_ref, weight_ref, grad_ref, pooled_ref, box_ref, rows32, up_weight
):
    c3 = cot_ref.shape[-1]
    c4 = pooled_ref.shape[-1]
    half = pooled_ref.shape[-2]
    odd = place_ref[0] >= 2

    @pl.when(pl.program_id(0) == 0)
    def _():
        for dy in range(3):
            for d in range(3):
                at = (dy * 3 + d) * c3
                up_weight[at : at + c3, :] = weight_ref[2 - dy, 2 - d, :c4, :].astype(F32).T.astype(BF16)

    for v in range(6):
        if v == 0:
            grad = jnp.where(odd, near_ref[0], far_ref[0])
        elif v == 5:
            grad = jnp.where(odd, far_ref[0], near_ref[0])
        else:
            grad = (cot_ref[0, v - 1].astype(F32) * silu_grad(pre_ref[0, v - 1].astype(F32))).astype(BF16)
        grad_ref[0, v] = grad
        rows32[v] = grad.astype(F32)
    for v in range(5):
        sums = box_sums(rows32.at[v], rows32.at[v + 1], half)
        for i in range(2):
            dy = v - 2 * i
            if 0 <= dy <= 2:
                for d in range(3):
                    at = (dy * 3 + d) * c3
                    box_ref[0, i * half : (i + 1) * half, at : at + c3] = sums[d]
    pooled = jnp.dot(box_ref[0], up_weight[...], preferred_element_type=F32)
    pooled_ref[0] = pooled.reshape(pooled_ref.shape[1:])


def box_level(place, cot, pre, near, far, weight, cs):
    samples, height, wide, c3 = cot.shape
    c4 = weight.shape[2] - cs
    half = wide // 2
    block = pl.BlockSpec((1, height, wide, c3), lambda s: (s, 0, 0, 0))
    edge = pl.BlockSpec((1, wide, c3), lambda s: (s, 0, 0))
    return pl.pallas_call(
        box_kernel,
        grid=(samples,),
        in_specs=[
            pl.BlockSpec(memory_space=pltpu.SMEM), block, block, edge, edge,
            pl.BlockSpec(weight.shape, lambda s: (0, 0, 0, 0)),
        ],
        out_specs=[
            pl.BlockSpec((1, height + 2, wide, c3), lambda s: (s, 0, 0, 0)),
            pl.BlockSpec((1, 2, half, c4), lambda s: (s, 0, 0, 0)),
            pl.BlockSpec((1, 2 * half, 9 * c3), lambda s: (s, 0, 0)),
        ],
        out_shape=[
            jax.ShapeDtypeStruct((samples, height + 2, wide, c3), BF16),
            jax.ShapeDtypeStruct((samples, 2, half, c4), F32),
            jax.ShapeDtypeStruct((samples, 2 * half, 9 * c3), BF16),
        ],
        scratch_shapes=[pltpu.VMEM((6, wide, c3), F32), pltpu.VMEM((9 * c3, c4), BF16)],
        compiler_params=params(VMEM),
        cost_estimate=cost(LONG, 8e6),
        name="box_level",
    )(place, cot, pre, near, far, weight)


def fine_kernel(
    place_ref, grad_ref, skip_ref, weight_ref, grad_skip_ref, keep_ref, send_ref, taps, skip_weight, total, *, scale
):
    sample = pl.program_id(0)
    c3 = grad_ref.shape[-1]
    cs = skip_ref.shape[-1]
    c4 = weight_ref.shape[2] - cs

    @pl.when(sample == 0)
    def _():
        total[...] = jnp.zeros_like(total)
        for u in range(4):
            for d in range(3):
                at = (u * 3 + d) * c3
                for t in range(2):
                    dy = u - t
                    if 0 <= dy <= 2:
                        block = weight_ref[2 - dy, 2 - d, c4:, :].astype(F32).T.astype(BF16)
                    else:
                        block = jnp.zeros((c3, cs), BF16)
                    skip_weight[at : at + c3, t * cs : (t + 1) * cs] = block

    for v in range(6):
        grad = grad_ref[0, v]
        before, after = shifted(grad.astype(F32))
        at = v * 3 * c3
        taps[:, at : at + c3] = before.astype(BF16)
        taps[:, at + c3 : at + 2 * c3] = grad
        taps[:, at + 2 * c3 : at + 3 * c3] = after.astype(BF16)

    for pair in range(2):
        window = taps[:, 2 * pair * 3 * c3 : (2 * pair + 4) * 3 * c3]
        back = jnp.dot(window, skip_weight[...], preferred_element_type=F32)
        grad_skip_ref[0, 2 * pair] = back[:, :cs].astype(BF16)
        grad_skip_ref[0, 2 * pair + 1] = back[:, cs:].astype(BF16)
        feats = jnp.concatenate([skip_ref[0, 2 * pair], skip_ref[0, 2 * pair + 1]], axis=1)
        total[...] += tdot(feats, window)

    @pl.when(sample == pl.num_programs(0) - 1)
    def _():
        core = place_ref[0] % 2

        part = cs // 2
        for dy in range(3):
            for d in range(3):
                first = (dy * 3 + d) * c3
                second = ((dy + 1) * 3 + d) * c3
                value = (total[:cs, first : first + c3] + total[cs:, second : second + c3]) * scale
                low, high = value[:part], value[part:]
                tap = (2 - dy) * 3 + 2 - d
                keep_ref[tap] = tiles(jnp.where(core == 0, low, high))
                send_ref[tap] = tiles(jnp.where(core == 0, high, low))


def fine_level(place, grad, skip, weight, fine_cells):
    samples, height, wide, cs = skip.shape
    c3 = grad.shape[-1]
    part = jax.ShapeDtypeStruct((9, cs // 32, 16, c3), BF16)
    whole = pl.BlockSpec(part.shape, lambda s: (0, 0, 0, 0))
    return pl.pallas_call(
        functools.partial(fine_kernel, scale=1.0 / math.sqrt(fine_cells)),
        grid=(samples,),
        in_specs=[
            pl.BlockSpec(memory_space=pltpu.SMEM),
            pl.BlockSpec((1, height + 2, wide, c3), lambda s: (s, 0, 0, 0)),
            pl.BlockSpec((1, height, wide, cs), lambda s: (s, 0, 0, 0)),
            pl.BlockSpec(weight.shape, lambda s: (0, 0, 0, 0)),
        ],
        out_specs=[pl.BlockSpec((1, height, wide, cs), lambda s: (s, 0, 0, 0)), whole, whole],
        out_shape=[jax.ShapeDtypeStruct((samples, height, wide, cs), BF16), part, part],
        scratch_shapes=[
            pltpu.VMEM((wide, 18 * c3), BF16),
            pltpu.VMEM((12 * c3, 2 * cs), BF16),
            pltpu.VMEM((2 * cs, 12 * c3), F32),
        ],
        compiler_params=params(VMEM),
        cost_estimate=cost(5e9, 8e6),
        name="fine_level",
    )(place, grad, skip, weight)


def coarse_grad_kernel(place_ref, pooled_ref, pre_ref, near_ref, far_ref):
    channels, half = pooled_ref.shape[-1], pooled_ref.shape[-2]
    odd = place_ref[0] >= 2
    rows = []
    for i in range(2):
        value = pre_ref[:, 0, 0, i].reshape(channels, half).astype(F32).T
        rows.append((pooled_ref[0, i] * silu_grad(value)).astype(BF16))
    near_ref[0] = jnp.where(odd, rows[0], rows[1])
    far_ref[0] = jnp.where(odd, rows[1], rows[0])


def coarse_grad(place, pooled, received):
    samples, _, half, c4 = pooled.shape
    peers, _, _, _, own, _ = received.shape
    out = jax.ShapeDtypeStruct((samples, half, c4), BF16)
    spec = pl.BlockSpec((1, half, c4), lambda s: (s, 0, 0))
    return pl.pallas_call(
        coarse_grad_kernel,
        grid=(samples,),
        in_specs=[
            pl.BlockSpec(memory_space=pltpu.SMEM),
            pl.BlockSpec((1, 2, half, c4), lambda s: (s, 0, 0, 0)),
            pl.BlockSpec((peers, 1, 1, 2, own, half), lambda s: (0, 0, s, 0, 0, 0)),
        ],
        out_specs=[spec, spec],
        out_shape=[out, out],
        compiler_params=params(VMEM),
        cost_estimate=cost(2e7, 2e6),
        name="coarse_grad",
    )(place, in_hbm(pooled), received)


def up_kernel(
    place_ref, pre_ref, box_ref, skip_keep_ref, skip_send_ref, keep_ref, send_ref, total, *, scale
):
    sample = pl.program_id(0)
    wide = pre_ref.shape[-1]
    c4 = pre_ref.shape[0] * pre_ref.shape[-2]
    c3 = keep_ref.shape[-1]

    @pl.when(sample == 0)
    def _():
        total[...] = jnp.zeros_like(total)

    value = jnp.concatenate([pre_ref[:, 0, 0, i].reshape(c4, wide) for i in range(2)], axis=1).astype(F32)
    value = (value * jax.nn.sigmoid(value)).astype(BF16)
    total[...] += jnp.dot(value, box_ref[0], preferred_element_type=F32)

    @pl.when(sample == pl.num_programs(0) - 1)
    def _():
        core = place_ref[0] % 2
        part = c4 // 2
        mine = part // 16
        for dy in range(3):
            for d in range(3):
                at = (dy * 3 + d) * c3
                value = total[:, at : at + c3] * scale
                low, high = value[:part], value[part:]
                tap = (2 - dy) * 3 + 2 - d
                keep_ref[tap, :mine] = tiles(jnp.where(core == 0, low, high))
                send_ref[tap, :mine] = tiles(jnp.where(core == 0, high, low))
                keep_ref[tap, mine:] = skip_keep_ref[tap]
                send_ref[tap, mine:] = skip_send_ref[tap]


def up_level(place, received, box, skip_keep, skip_send, fine_cells):
    peers, _, samples, _, own, wide = received.shape
    c4 = peers * own
    c3 = box.shape[-1] // 9
    part = jax.ShapeDtypeStruct((9, c4 // 32 + skip_keep.shape[1], 16, c3), BF16)
    whole = pl.BlockSpec(part.shape, lambda s: (0, 0, 0, 0))
    skips = pl.BlockSpec(skip_keep.shape, lambda s: (0, 0, 0, 0))
    return pl.pallas_call(
        functools.partial(up_kernel, scale=1.0 / math.sqrt(fine_cells)),
        grid=(samples,),
        in_specs=[
            pl.BlockSpec(memory_space=pltpu.SMEM),
            pl.BlockSpec((peers, 1, 1, 2, own, wide), lambda s: (0, 0, s, 0, 0, 0)),
            pl.BlockSpec((1, 2 * wide, 9 * c3), lambda s: (s, 0, 0)),
            skips, skips,
        ],
        out_specs=[whole, whole],
        out_shape=[part, part],
        scratch_shapes=[pltpu.VMEM((c4, 9 * c3), F32)],
        compiler_params=params(VMEM),
        cost_estimate=cost(1e9, 5e6),
        name="up_level",
    )(place, received, box, skip_keep, skip_send)


def fill_coarse_taps(odd, rows, taps):
    wide, c4 = rows[0].shape

    def fill(order):
        for v, row in zip(order, rows):
            before, after = shifted(row.astype(F32))
            lines = slice(v * wide, (v + 1) * wide)
            taps[lines, :c4] = before.astype(BF16)
            taps[lines, c4 : 2 * c4] = row
            taps[lines, 2 * c4 :] = after.astype(BF16)

    pl.when(odd)(lambda: fill((3, 2, 1, 0)))
    pl.when(jnp.logical_not(odd))(lambda: fill((0, 1, 2, 3)))


def coarse_weight_kernel(
    place_ref, input_ref, first_ref, second_ref, third_ref, fourth_ref, out_ref, taps, total, *, scale
):
    sample = pl.program_id(0)
    wide = input_ref.shape[-1]
    part = input_ref.shape[0] * input_ref.shape[-2]
    c4 = first_ref.shape[-1]

    @pl.when(sample == 0)
    def _():
        total[...] = jnp.zeros_like(total)

    rows = (first_ref[0], second_ref[0], third_ref[0], fourth_ref[0])
    fill_coarse_taps(place_ref[0] >= 2, rows, taps)
    values = jnp.concatenate([input_ref[:, 0, 0, i].reshape(part, wide) for i in range(2)], axis=1)
    for dy in range(3):
        total[dy] += jnp.dot(values, taps[dy * wide : (dy + 2) * wide, :], preferred_element_type=F32)

    @pl.when(sample == pl.num_programs(0) - 1)
    def _():
        count = part // 16
        for dy in range(3):
            for d in range(3):
                for side in range(c4 // 128):
                    at = d * c4 + side * 128
                    tap = ((2 - dy) * 3 + 2 - d) * (c4 // 128) + side
                    out_ref[tap * count : (tap + 1) * count] = tiles(total[dy, :, at : at + 128] * scale)


def coarse_specs(wide, c4, count):
    return [pl.BlockSpec((1, wide, c4), lambda s: (s, 0, 0))] * count


def coarse_weight_level(place, received, rows, coarse_cells):
    peers, _, samples, _, own, wide = received.shape
    c4 = peers * own
    shape = (9 * (c4 // 128) * (c4 // 32), 16, 128)
    return pl.pallas_call(
        functools.partial(coarse_weight_kernel, scale=1.0 / math.sqrt(coarse_cells)),
        grid_spec=pltpu.PrefetchScalarGridSpec(
            num_scalar_prefetch=1,
            grid=(samples,),
            in_specs=[pl.BlockSpec((peers // 2, 1, 1, 2, own, wide), lambda s, place: (place[0] % 2, 1, s, 0, 0, 0))]
            + [pl.BlockSpec((1, wide, c4), lambda s, place: (s, 0, 0))] * 4,
            out_specs=pl.BlockSpec(shape, lambda s, place: (0, 0, 0)),
            scratch_shapes=[pltpu.VMEM((4 * wide, 3 * c4), BF16), pltpu.VMEM((3, c4 // 2, 3 * c4), F32)],
        ),
        out_shape=jax.ShapeDtypeStruct(shape, BF16),
        compiler_params=params(VMEM),
        cost_estimate=cost(0.7e9, 2e6),
        name="coarse_weight_level",
    )(place, received, *rows)


def coarse_input_kernel(chan_ref, weight_ref, first_ref, second_ref, third_ref, fourth_ref, *rest):
    *piece_refs, taps, stage = rest
    wide, c4 = first_ref.shape[1:]
    own = c4 // len(piece_refs)
    rows = (first_ref[0], second_ref[0], third_ref[0], fourth_ref[0])
    fill_coarse_taps(chan_ref[0] % 2 == 1, rows, taps)
    total = None
    for dy in range(3):
        for d in range(3):
            window = taps[dy * wide : (dy + 2) * wide, d * c4 : (d + 1) * c4]
            term = dott(weight_ref[2 - dy, 2 - d], window)
            total = term if total is None else total + term
    stage[...] = total.astype(BF16)
    for k, ref in enumerate(piece_refs):
        at = pl.multiple_of(jnp.bitwise_xor(chan_ref[0], k) * own, own)
        for i in range(2):
            ref[0, i] = stage[pl.ds(at, own), i * wide : (i + 1) * wide]


def coarse_input_level(chan, weight, rows, peers):
    samples, wide, c4 = rows[0].shape
    own = c4 // peers
    return pl.pallas_call(
        coarse_input_kernel,
        grid=(samples,),
        in_specs=[
            pl.BlockSpec(memory_space=pltpu.SMEM),
            pl.BlockSpec(weight.shape, lambda s: (0, 0, 0, 0)),
        ] + coarse_specs(wide, c4, 4),
        out_specs=[pl.BlockSpec((1, 2, own, wide), lambda s: (s, 0, 0, 0))] * peers,
        out_shape=[jax.ShapeDtypeStruct((samples, 2, own, wide), BF16)] * peers,
        scratch_shapes=[pltpu.VMEM((4 * wide, 3 * c4), BF16), pltpu.VMEM((c4, 2 * wide), BF16)],
        compiler_params=params(VMEM),
        cost_estimate=cost(1.3e9, 3e6),
        name="coarse_input_level",
    )(chan, weight, *rows)


def place_kernel(first, count, chan_ref, *refs):
    out_ref = refs[-1]
    if len(refs) > count + 1:
        out_ref[...] = refs[count][...]
    for k in range(count):
        at = jnp.bitwise_xor(chan_ref[0], first + k) * 2
        out_ref[:, pl.ds(at, 2)] = refs[k][...]


def placed(chan, pieces, first, peers, earlier=(), flops=1e6):
    samples, rows, own, wide = pieces[0].shape
    vmem = pl.BlockSpec(memory_space=pltpu.VMEM)
    return pl.pallas_call(
        functools.partial(place_kernel, first, len(pieces)),
        in_specs=[pl.BlockSpec(memory_space=pltpu.SMEM)] + [vmem] * (len(pieces) + len(earlier)),
        out_shape=jax.ShapeDtypeStruct((samples, rows * peers, own, wide), BF16),
        compiler_params=params(VMEM),
        cost_estimate=cost(flops, 1e6),
        name="place",
    )(chan, *pieces, *earlier)


def join_kernel(coarse_ref, coarse_more_ref, fine_ref, fine_more_ref, out_ref):
    count = coarse_ref.shape[0]
    out_ref[:count] = (coarse_ref[...].astype(F32) + coarse_more_ref[...].astype(F32)).astype(BF16)
    fines = fine_ref.shape[0]
    out_ref[count : count + fines] = (fine_ref[...].astype(F32) + fine_more_ref[...].astype(F32)).astype(BF16)
    rest = out_ref.shape[0] - count - fines
    if rest:
        out_ref[count + fines :] = jnp.zeros((rest,) + out_ref.shape[1:], BF16)


def sum_kernel(parts_ref, out_ref):
    total = parts_ref[0].astype(F32)
    for k in range(1, parts_ref.shape[0]):
        total = total + parts_ref[k].astype(F32)
    total = total.astype(BF16)
    for k in range(out_ref.shape[0]):
        out_ref[k] = total


def unpack_kernel(place_ref, parts_ref, *rest):
    fine_ref, coarse_ref, fine_stage, coarse_stage, sems = rest[-5:]
    c4 = coarse_ref.shape[-1]
    sides = c4 // 128
    lines, skips = c4 // 2, (fine_ref.shape[-2] - c4) // 2
    line_tiles, skip_tiles = lines // 16, skips // 16
    core = place_ref[0] % 2
    rows = pl.ds(pl.multiple_of(core * lines, lines), lines)
    skip_rows = pl.ds(pl.multiple_of(c4 + core * skips, skips), skips)

    def take(at, count):
        return parts_ref[at : at + count].astype(F32).reshape(count * 16, 128)

    copies = []

    def send(source, target):
        copies.append(pltpu.make_async_copy(source, target, sems.at[len(copies)]))
        copies[-1].start()

    for tap in range(9):
        for side in range(sides):
            at = (tap * sides + side) * line_tiles
            coarse_stage[tap, :, side * 128 : (side + 1) * 128] = take(at, line_tiles)
        send(coarse_stage.at[tap], coarse_ref.at[tap, rows])
        at = 9 * sides * line_tiles + tap * (line_tiles + skip_tiles)
        fine_stage[tap, :lines] = take(at, line_tiles)
        fine_stage[tap, lines:] = take(at + line_tiles, skip_tiles)
        send(fine_stage.at[tap, pl.ds(0, lines)], fine_ref.at[tap, rows])
        send(fine_stage.at[tap, pl.ds(lines, skips)], fine_ref.at[tap, skip_rows])
    for copy in copies:
        copy.wait()


SWAP = ((0, 1), (1, 0))


def grad_sums(fine_keep, fine_more, coarse_keep, coarse_more):
    chips = 1
    for axis in CHIPS:
        chips *= lax.axis_size(axis)
    fine_keep, fine_more = (a.reshape((-1, 16, 128)) for a in (fine_keep, fine_more))
    count = coarse_keep.shape[0] + fine_keep.shape[0]
    each = -(-count // chips)
    joined = pl.pallas_call(
        join_kernel,
        out_shape=jax.ShapeDtypeStruct((chips * each, 16, 128), BF16),
        compiler_params=params(VMEM),
        cost_estimate=cost(1e6, 3e6),
        name="join",
    )(coarse_keep, coarse_more, fine_keep, fine_more)
    parts = lax.all_to_all(joined.reshape(chips, each, 16, 128), CHIPS, 0, 0, tiled=True)
    summed = pl.pallas_call(
        sum_kernel,
        out_shape=jax.ShapeDtypeStruct((chips, each, 16, 128), BF16),
        compiler_params=params(VMEM),
        cost_estimate=cost(1e6, 1.3e6),
        name="sum_parts",
    )(parts)
    return lax.all_to_all(summed, CHIPS, 0, 0, tiled=True).reshape(chips * each, 16, 128)


def unpacked(place, half, fine_shape, coarse_shape, earlier=()):
    shapes = [jax.ShapeDtypeStruct((9,) + shape[2:], F32) for shape in (fine_shape, coarse_shape)]
    hbm = pl.BlockSpec(memory_space=pltpu.HBM)
    return pl.pallas_call(
        unpack_kernel,
        in_specs=[pl.BlockSpec(memory_space=pltpu.SMEM), pl.BlockSpec(memory_space=pltpu.VMEM)]
        + [hbm] * len(earlier),
        out_specs=[hbm, hbm],
        out_shape=shapes,
        input_output_aliases={2 + i: i for i in range(len(earlier))},
        scratch_shapes=[
            pltpu.VMEM((9, fine_shape[2] // 2, fine_shape[3]), F32),
            pltpu.VMEM((9, coarse_shape[2] // 2, coarse_shape[3]), F32),
            pltpu.SemaphoreType.DMA((27,)),
        ],
        compiler_params=params(VMEM),
        cost_estimate=cost(1, 1),
        name="unpack",
    )(place, half, *earlier)


def start_kernel(
    place_ref, pre_ref, input_ref, cot_ref, fine_pre_ref, pieces_ref, near_ref, far_ref, rows, row_sems, sems
):
    peers, _, samples, lines, _, _ = pieces_ref.shape
    odd = place_ref[0] >= 2
    last = cot_ref.shape[1] - 1
    row_copies = []
    for a, ref in enumerate((cot_ref, fine_pre_ref)):
        for e, line in enumerate((jnp.where(odd, 0, last), jnp.where(odd, last, 0))):
            for s in range(samples):
                row_copies.append(
                    pltpu.make_async_copy(ref.at[s, line], rows.at[a, e, s], row_sems.at[len(row_copies)])
                )
    copies = []
    for c in range(peers):
        for a, ref in enumerate((pre_ref, input_ref)):
            for s in range(samples):
                copies.append(
                    pltpu.make_async_copy(
                        ref.at[s, pl.ds(c * lines, lines)], pieces_ref.at[c, a, s], sems.at[len(copies)]
                    )
                )
    for copy in row_copies + copies:
        copy.start()
    for copy in row_copies:
        copy.wait()
    for e, out_ref in enumerate((near_ref, far_ref)):
        for s in range(samples):
            grad = rows[0, e, s].astype(F32) * silu_grad(rows[1, e, s].astype(F32))
            out_ref[s] = grad.astype(BF16)
    for copy in copies:
        copy.wait()


def start_level(place, pre, values, cot, fine_pre, peers):
    samples, lines, own, wide = pre.shape
    fine_wide, c3 = cot.shape[2:]
    hbm = pl.BlockSpec(memory_space=pltpu.HBM)
    vmem = pl.BlockSpec(memory_space=pltpu.VMEM)
    edge = jax.ShapeDtypeStruct((samples, fine_wide, c3), BF16)
    return pl.pallas_call(
        start_kernel,
        in_specs=[pl.BlockSpec(memory_space=pltpu.SMEM), hbm, hbm, hbm, hbm],
        out_specs=[vmem, vmem, vmem],
        out_shape=[jax.ShapeDtypeStruct((peers, 2, samples, lines // peers, own, wide), BF16), edge, edge],
        scratch_shapes=[
            pltpu.VMEM((2, 2, samples, fine_wide, c3), BF16),
            pltpu.SemaphoreType.DMA((4 * samples,)),
            pltpu.SemaphoreType.DMA((peers * 2 * samples,)),
        ],
        compiler_params=params(VMEM),
        cost_estimate=cost(1e7, 3e6),
        name="start",
    )(place, *(in_hbm(a) for a in (pre, values, cot, fine_pre)))


def swapped(near, far):
    count = 1
    for axis in ALL:
        count *= lax.axis_size(axis)
    inside = [(i, i ^ 1) for i in range(count)]
    outside = [(i, i + 1) for i in range(1, count - 1, 2)]
    outside += [(target, source) for source, target in outside]
    return lax.ppermute(near, ALL, inside), lax.ppermute(far, ALL, outside)


def shards(coarse_input, coarse_pre, skip_feats, fine_pre, fine_cotangent, fine_weight, coarse_weight):
    peers = 1
    for axis in CHAN:
        peers *= lax.axis_size(axis)
    devices = peers
    for axis in ROWS:
        devices *= lax.axis_size(axis)
    samples, lines, wide, own = coarse_input.shape
    core = lax.axis_index("core").astype(jnp.int32)
    chan = lax.axis_index(CHAN).astype(jnp.int32).reshape(1)
    place = (core + 2 * (lax.axis_index("xl").astype(jnp.int32))).reshape(1)
    other_place = (1 - core + 2 * (lax.axis_index("xl").astype(jnp.int32))).reshape(1)

    pieces, edge_near, edge_far = start_level(
        place, coarse_pre.transpose(0, 1, 3, 2), coarse_input.transpose(0, 1, 3, 2), fine_cotangent, fine_pre, peers
    )
    edge_near, edge_far = swapped(edge_near, edge_far)
    received = lax.all_to_all(pieces, CHAN, 0, 0, tiled=True)

    cs = skip_feats.shape[-1]
    fine_cells = fine_pre.shape[0] * fine_pre.shape[1] * fine_pre.shape[2] * devices
    edge_near, edge_far, cotangent = lax.optimization_barrier((edge_near, edge_far, fine_cotangent))
    fine_grad, pooled, box = box_level(place, cotangent, fine_pre, edge_near, edge_far, fine_weight, cs)
    near, far = coarse_grad(place, pooled, received)
    from_near, from_far = swapped(near, far)
    fine_grad, near = lax.optimization_barrier((fine_grad, near))
    grad_skip, skip_keep, skip_send = fine_level(place, fine_grad, skip_feats, fine_weight, fine_cells)
    fine_keep, fine_send = up_level(place, received, box, skip_keep, skip_send, fine_cells)
    fine_more = lax.ppermute(fine_send, "core", SWAP)
    from_near, from_far, fine_keep = lax.optimization_barrier((from_near, from_far, fine_keep))
    rows = (from_far, far, near, from_near)
    coarse_cells = samples * (lines // peers) * wide * devices
    coarse_send = coarse_weight_level(other_place, received, rows, coarse_cells)
    coarse_more = lax.ppermute(coarse_send, "core", SWAP)
    coarse_keep = coarse_weight_level(place, received, rows, coarse_cells)
    back = coarse_input_level(chan, coarse_weight, rows, peers)

    def home(k, piece):
        return lax.ppermute(piece, CHAN, [(i, i ^ k) for i in range(peers)])

    mine = grad_sums(fine_keep, fine_more, coarse_keep, coarse_more)
    early = [back[0]] + [home(k, back[k]) for k in range(1, EARLY)]
    grad_input = placed(chan, early, 0, peers, flops=LONG)
    grad_input, *late = lax.optimization_barrier((grad_input, *back[EARLY:]))
    late = [home(EARLY + k, piece) for k, piece in enumerate(late)]
    mine, grad_input = lax.optimization_barrier((mine, grad_input))
    grad_input = placed(chan, late, EARLY, peers, (grad_input,), flops=LONG)
    other = lax.ppermute(mine, "core", SWAP)
    sums = unpacked(place, mine, fine_weight.shape, coarse_weight.shape)
    grad_fine, grad_coarse = unpacked(other_place, other, fine_weight.shape, coarse_weight.shape, sums)
    return (
        grad_skip,
        grad_input.transpose(0, 1, 3, 2),
        grad_fine.reshape(fine_weight.shape),
        grad_coarse.reshape(coarse_weight.shape),
    )


def solution(mesh):
    split = Mesh(mesh.devices.reshape([size for _, size in SPLIT]), tuple(name for name, _ in SPLIT))
    coarse = P(None, ROWS, None, CHAN)
    fine = P(None, ALL, None, None)
    return jax.shard_map(
        shards,
        mesh=split,
        in_specs=(coarse, coarse, fine, fine, fine, P(), P()),
        out_specs=(fine, coarse, P(), P()),
        check_vma=False,
    )
```

time: 123 us -> 113 us (0.919)
  blocking collectives: 24.2 us -> 0 us
  Pallas kernels: 19.6 us -> 26.7 us
  local copies, waits for them, and re-layouts: 5.64 us -> 11.1 us
  starting transfers between devices: 42.7 us -> 46.6 us
  other arithmetic: 3.55 us -> 0 us
    all_to_all x1 -> x0, blocking collectives: 24.2 us -> none  [grad_sums(): lax.all_to_all(summed, CHIPS, 0, 0, tiled=True)]
    ppermute x11, waiting for transfers between devices: 22 us -> 6.61 us  [the longest x4 6.6 us: swapped(): return (lax.ppermute(near, ALL, inside), lax.ppermute(far, ALL, outside))]
    all_to_all x0 -> x1, waiting for transfers between devices: none -> 12.6 us  [grad_sums(): lax.all_to_all(summed, CHIPS, 0, 0, tiled=True)]
    all_to_all x1, waiting for transfers between devices: 0.37 us -> 7.05 us  [grad_sums(): lax.all_to_all(joined.reshape(chips, each, 16, 128), CHIPS, 0, 0, tiled=T...]
    all_to_all x0 -> x1, starting transfers between devices: none -> 5.61 us  [grad_sums(): lax.all_to_all(summed, CHIPS, 0, 0, tiled=True)]
    unnamed x34 -> x46, local copies, waits for them, and re-layouts: 5.64 us -> 11.1 us
    pallas_call x3 -> x5, Pallas kernels: 5.12 us -> 8.45 us  [the longest x1 3.32 us: start_level(): pl.pallas_call(start_kernel, in_specs=[pl.BlockSpec(memory_space=pltpu.SM...]
    transpose x1 -> x0, other arithmetic: 2.43 us -> none  [shards(): pieces = pieces.transpose(2, 0, 1, 3, 5, 4)]
  transfers between devices with their start and end apart: 16 -> 17, of which waited for: 11 -> 5; matrix products, arithmetic and copies ran while one was open for 1% -> 0% of each run, Pallas kernels for 10% -> 15%
where the time goes in v3:
time: 113 us; the launch traced here: 112 us
  starting transfers between devices  46.6 us (41%)
  Pallas kernels  26.7 us (24%)
  waiting for transfers between devices  26.5 us (23%)
  local copies, waits for them, and re-layouts  11.1 us (10%)
  between operations  1.15 us (1%)
    all_to_all x1, waiting for transfers between devices, grad_sums(): lax.all_to_all(summed, CHIPS, 0, 0, tiled=True)  12.6 us
    ppermute x4, starting transfers between devices, swapped(): return (lax.ppermute(near, ALL, inside), lax.ppermute(far, ALL, outside))  12.4 us
    unnamed x46, local copies, waits for them, and re-layouts  11.1 us
    all_to_all x1, starting transfers between devices, grad_sums(): lax.all_to_all(joined.reshape(chips, each, 16, 128), CHIPS, 0, 0, tiled=T...  10.6 us
    ppermute x7, starting transfers between devices, home(): return lax.ppermute(piece, CHAN, [(i, i ^ k) for i in range(peers)])  9.86 us
    all_to_all x1, waiting for transfers between devices, grad_sums(): lax.all_to_all(joined.reshape(chips, each, 16, 128), CHIPS, 0, 0, tiled=T...  7.05 us
    ppermute x4, waiting for transfers between devices, swapped(): return (lax.ppermute(near, ALL, inside), lax.ppermute(far, ALL, outside))  6.6 us
    all_to_all x1, starting transfers between devices, grad_sums(): lax.all_to_all(summed, CHIPS, 0, 0, tiled=True)  5.61 us
  transfers between devices with their start and end apart: 17, of which 5 were waited for; matrix products, arithmetic and copies ran while one was open for 0% of the time, Pallas kernels for 15%

profile of v3, /device:TPU:1, one launch (start us, length us, event | category | flops | bytes accessed | tf_op | source)
XLA Modules:
  0.0 112.0 jit_solution(2094276080441947842)
XLA Ops:
  0.6 3.3 %start.1 = (bf16[8,2,2,2,32,256]{5,4,3,2,1,0:T(8,128)(2,1)}, bf16[2,512,128]{2,1,0:T(8,128)(2,1)S(1)}, bf16[2,512,128]{2,1,0:T(8,128)(2,1)S(1)}) custom-call(s32[1]{0:T(128)} %bitcast.place_ref, bf16[2,16,32,256]{3,2,1,0:T(8,128)(2,1)} %bitcast.18, bf16[2,16,32,256]{3,2,1,0:T(8,128)(2,1)} %bitcast.19, bf16[2,4,512,128]{3,2,1,0:T(8,128)(2,1)} %cot_ref.2, ...), custom_call_target="tpu_custom_call" | custom-call | flops 10000000 | bytes 3000000 | tf_op jit(solution)/shard_map/start/pallas_call | solution.py:578
  4.0 2.1 %collective-permute-start = (bf16[2,512,128]{2,1,0:T(8,128)(2,1)S(1)}, bf16[2,512,128]{2,1,0:T(8,128)(2,1)S(1)}, u32[]{:S(2)}, u32[]{:S(2)}) collective-permute-start(bf16[2,512,128]{2,1,0:T(8,128)(2,1)S(1)} %get-tuple-element.42), channel_id=1, source_target_pairs={{0,1},{1,0},{2,3},{3,2},{4,5},{5,4},{6,7},{7,6},{8,9},{9,8},{10,11... | collective-permute-start | bytes 786440 | tf_op jit(solution)/shard_map/ppermute | solution.py:601
  6.1 5.4 %collective-permute-start.1 = (bf16[2,512,128]{2,1,0:T(8,128)(2,1)S(1)}, bf16[2,512,128]{2,1,0:T(8,128)(2,1)S(1)}, u32[]{:S(2)}, u32[]{:S(2)}) collective-permute-start(bf16[2,512,128]{2,1,0:T(8,128)(2,1)S(1)} %get-tuple-element.43), channel_id=1, source_target_pairs={{1,2},{3,4},{5,6},{7,8},{9,10},{11,12},{13,14},{15,16},{17,18},{19... | collective-permute-start | bytes 786440 | tf_op jit(solution)/shard_map/ppermute | solution.py:601
  11.5 3.6 %all-to-all-start = ((bf16[8,2,2,2,32,256]{5,4,3,2,1,0:T(8,128)(2,1)}), bf16[8,2,2,2,32,256]{5,4,3,2,1,0:T(8,128)(2,1)S(1)}, u32[]{:S(2)}, u32[]{:S(2)}) async-start(bf16[8,2,2,2,32,256]{5,4,3,2,1,0:T(8,128)(2,1)} %get-tuple-element.49), calls=%async_computation | async-start | bytes 2097152 | tf_op jit(solution)/shard_map/all_to_all | solution.py:621
  15.8 5.7 %collective-permute-done.1.far_ref = bf16[2,512,128]{2,1,0:T(8,128)(2,1)S(1)} collective-permute-done((bf16[2,512,128]{2,1,0:T(8,128)(2,1)S(1)}, bf16[2,512,128]{2,1,0:T(8,128)(2,1)S(1)}, u32[]{:S(2)}, u32[]{:S(2)}) %collective-permute-start.1) | collective-permute-done | bytes 262176 | tf_op jit(solution)/shard_map/ppermute | solution.py:601
  27.8 2.5 %box_level.1 = (bf16[2,6,512,128]{3,2,1,0:T(8,128)(2,1)S(1)}, f32[2,2,256,256]{3,2,1,0:T(8,128)S(1)}, bf16[2,512,1152]{2,1,0:T(8,128)(2,1)S(1)}) custom-call(s32[1]{0:T(128)} %bitcast.place_ref, bf16[2,4,512,128]{3,2,1,0:T(8,128)(2,1)S(1)} %copy-done.9, bf16[2,4,512,128]{3,2,1,0:T(8,128)(2,1)S(1)} %copy-done.10, bf16[2,512,128]{2,1,0:T(8,128)(2,1)S(1)} %copy-done.16, ...), custom_call_target="tpu_custom_call" | custom-call | flops 99999997952 | bytes 8000000 | tf_op jit(solution)/shard_map/box_level/pallas_call | solution.py:113
  32.5 1.7 %coarse_grad.1 = (bf16[2,256,256]{2,1,0:T(8,128)(2,1)S(1)}, bf16[2,256,256]{2,1,0:T(8,128)(2,1)S(1)}) custom-call(s32[1]{0:T(128)} %bitcast.place_ref, f32[2,2,256,256]{3,2,1,0:T(8,128)} %copy-done.8, bf16[8,2,2,2,32,256]{5,4,3,2,1,0:T(8,128)(2,1)S(1)} %all-to-all-done.pre_ref.input_ref), custom_call_target="tpu_custom_call" | custom-call | flops 20000000 | bytes 2000000 | tf_op jit(solution)/shard_map/coarse_grad/pallas_call | solution.py:234
  34.3 4.8 %collective-permute-start.3 = (bf16[2,256,256]{2,1,0:T(8,128)(2,1)S(1)}, bf16[2,256,256]{2,1,0:T(8,128)(2,1)S(1)}, u32[]{:S(2)}, u32[]{:S(2)}) collective-permute-start(bf16[2,256,256]{2,1,0:T(8,128)(2,1)S(1)} %get-tuple-element.53.second_ref), channel_id=1, source_target_pairs={{1,2},{3,4},{5,6},{7,8},{9,10},{11,12},{13,14},{15,16},{17,18},{19... | collective-permute-start | bytes 786440 | tf_op jit(solution)/shard_map/ppermute | solution.py:601
  39.1 1.4 %copy-done.22 = bf16[2,6,512,128]{3,2,1,0:T(8,128)(2,1)S(1)} copy-done((bf16[2,6,512,128]{3,2,1,0:T(8,128)(2,1)S(1)}, bf16[2,6,512,128]{3,2,1,0:T(8,128)(2,1)}, u32[]{:S(2)}) %copy-start.22) | copy-done | bytes 1572888
  40.5 4.9 %fine_level.1 = (bf16[2,4,512,128]{3,2,1,0:T(8,128)(2,1)}, bf16[9,4,16,128]{3,2,1,0:T(8,128)(2,1)S(1)}, bf16[9,4,16,128]{3,2,1,0:T(8,128)(2,1)S(1)}) custom-call(s32[1]{0:T(128)} %bitcast.place_ref, bf16[2,6,512,128]{3,2,1,0:T(8,128)(2,1)S(1)} %copy-done.22, bf16[2,4,512,128]{3,2,1,0:T(8,128)(2,1)S(1)} %copy-done.12, bf16[3,3,384,128]{3,2,1,0:T(8,128)(2,1)S(1)} %copy-done.14), custom_call_target="tpu_custom_call" | custom-call | flops 5000000000 | bytes 8000000 | tf_op jit(solution)/shard_map/fine_level/pallas_call | solution.py:196
  45.5 1.3 %up_level.1 = (bf16[9,12,16,128]{3,2,1,0:T(8,128)(2,1)S(1)}, bf16[9,12,16,128]{3,2,1,0:T(8,128)(2,1)S(1)}) custom-call(s32[1]{0:T(128)} %bitcast.place_ref, bf16[8,2,2,2,32,256]{5,4,3,2,1,0:T(8,128)(2,1)S(1)} %all-to-all-done.pre_ref.input_ref, bf16[2,512,1152]{2,1,0:T(8,128)(2,1)S(1)} %get-tuple-element.54.box_ref, ...), custom_call_target="tpu_custom_call" | custom-call | flops 1000000000 | bytes 5000000 | tf_op jit(solution)/shard_map/up_level/pallas_call | solution.py:290
  47.6 1.8 %coarse_weight_level.3 = bf16[144,16,128]{2,1,0:T(8,128)(2,1)S(1)} custom-call(s32[1]{0:T(128)} %bitcast.4.place_ref, bf16[8,2,2,2,32,256]{5,4,3,2,1,0:T(8,128)(2,1)S(1)} %all-to-all-done.pre_ref.input_ref, bf16[2,256,256]{2,1,0:T(8,128)(2,1)S(1)} %collective-permute-done.3.first_ref, bf16[2,256,256]{2,1,0:T(8,128)(2,1)S(1)} %get-tuple-element.53.second_ref, ...), custom_call_target="tpu_custom_call" | custom-call | flops 700000000 | bytes 2000000 | tf_op jit(solution)/shard_map/coarse_weight_level/pallas_call | solution.py:360
  50.0 1.8 %coarse_weight_level.2.coarse_ref = bf16[144,16,128]{2,1,0:T(8,128)(2,1)S(1)} custom-call(s32[1]{0:T(128)} %bitcast.place_ref, bf16[8,2,2,2,32,256]{5,4,3,2,1,0:T(8,128)(2,1)S(1)} %all-to-all-done.pre_ref.input_ref, bf16[2,256,256]{2,1,0:T(8,128)(2,1)S(1)} %collective-permute-done.3.first_ref, bf16[2,256,256]{2,1,0:T(8,128)(2,1)S(1)} %get-tuple-element.53.second_ref, ...), custom_call_target="tpu_custom_call" | custom-call | flops 700000000 | bytes 2000000 | tf_op jit(solution)/shard_map/coarse_weight_level/pallas_call | solution.py:360
  53.4 10.6 %all-to-all-start.1 = ((bf16[64,4,16,128]{3,2,1,0:T(8,128)(2,1)}), bf16[64,4,16,128]{3,2,1,0:T(8,128)(2,1)S(1)}, u32[]{:S(2)}, u32[]{:S(2)}) async-start(bf16[64,4,16,128]{3,2,1,0:T(8,128)(2,1)} %bitcast.7), calls=%async_computation.1 | async-start | bytes 2097152 | tf_op jit(solution)/shard_map/all_to_all | solution.py:506
  64.0 2.9 %coarse_input_level.1 = (bf16[2,2,32,256]{3,2,1,0:T(8,128)(2,1)S(1)}, bf16[2,2,32,256]{3,2,1,0:T(8,128)(2,1)}, bf16[2,2,32,256]{3,2,1,0:T(8,128)(2,1)}, bf16[2,2...) custom-call(s32[1]{0:T(128)} %bitcast.3.chan_ref, ...), custom_call_target="tpu_custom_call" | custom-call | flops 1300000000 | bytes 3000000 | tf_op jit(solution)/shard_map/coarse_input_level/pallas_call | solution.py:399
  70.2 2.5 %collective-permute-start.7 = (bf16[2,2,32,256]{3,2,1,0:T(8,128)(2,1)S(1)}, bf16[2,2,32,256]{3,2,1,0:T(8,128)(2,1)S(1)}, u32[]{:S(2)}, u32[]{:S(2)}) collective-permute-start(bf16[2,2,32,256]{3,2,1,0:T(8,128)(2,1)S(1)} %get-tuple-element.65), channel_id=1, source_target_pairs={{0,4},{1,5},{2,6},{3,7},{4,0},{5,1},{6,2},{7,3},{8,12},{9,13},{10,... | collective-permute-start | bytes 196616 | tf_op jit(solution)/shard_map/ppermute | solution.py:642
  73.9 7.1 %all-to-all-done.1.parts_ref = bf16[64,4,16,128]{3,2,1,0:T(8,128)(2,1)S(1)} async-done(((bf16[64,4,16,128]{3,2,1,0:T(8,128)(2,1)}), bf16[64,4,16,128]{3,2,1,0:T(8,128)(2,1)S(1)}, u32[]{:S(2)}, u32[]{:S(2)}) %all-to-all-start.1) | async-done | bytes 1048608 | tf_op jit(solution)/shard_map/all_to_all | solution.py:506
  81.0 1.2 %sum_parts.1 = bf16[64,4,16,128]{3,2,1,0:T(8,128)(2,1)} custom-call(bf16[64,4,16,128]{3,2,1,0:T(8,128)(2,1)S(1)} %all-to-all-done.1.parts_ref), custom_call_target="tpu_custom_call" | custom-call | flops 1000000 | bytes 1300000 | tf_op jit(solution)/shard_map/sum_parts/pallas_call | solution.py:507
  82.2 5.6 %all-to-all-start.2 = ((bf16[64,4,16,128]{3,2,1,0:T(8,128)(2,1)}), bf16[64,4,16,128]{3,2,1,0:T(8,128)(2,1)S(1)}, u32[]{:S(2)}, u32[]{:S(2)}) async-start(bf16[64,4,16,128]{3,2,1,0:T(8,128)(2,1)} %sum_parts.1), calls=%async_computation.2 | async-start | bytes 2097152 | tf_op jit(solution)/shard_map/all_to_all | solution.py:514
  87.9 2.3 %collective-permute-start.9 = (bf16[2,2,32,256]{3,2,1,0:T(8,128)(2,1)S(1)}, bf16[2,2,32,256]{3,2,1,0:T(8,128)(2,1)S(1)}, u32[]{:S(2)}, u32[]{:S(2)}) collective-permute-start(bf16[2,2,32,256]{3,2,1,0:T(8,128)(2,1)S(1)} %get-tuple-element.69), channel_id=1, source_target_pairs={{0,6},{1,7},{2,4},{3,5},{4,2},{5,3},{6,0},{7,1},{8,14},{9,15},{10,... | collective-permute-start | bytes 196616 | tf_op jit(solution)/shard_map/ppermute | solution.py:642
  91.4 12.6 %all-to-all-done.2 = bf16[64,4,16,128]{3,2,1,0:T(8,128)(2,1)S(1)} async-done(((bf16[64,4,16,128]{3,2,1,0:T(8,128)(2,1)}), bf16[64,4,16,128]{3,2,1,0:T(8,128)(2,1)S(1)}, u32[]{:S(2)}, u32[]{:S(2)}) %all-to-all-start.2) | async-done | bytes 1048608 | tf_op jit(solution)/shard_map/all_to_all | solution.py:514
  104.0 4.0 %collective-permute-start.13 = (bf16[256,16,128]{2,1,0:T(8,128)(2,1)S(1)}, bf16[256,16,128]{2,1,0:T(8,128)(2,1)S(1)}, u32[]{:S(2)}, u32[]{:S(2)}) collective-permute-start(bf16[256,16,128]{2,1,0:T(8,128)(2,1)S(1)} %bitcast.12), channel_id=1, source_target_pairs={{0,8},{8,0},{1,9},{9,1},{2,10},{10,2},{3,11},{11,3},{4,12},{12,4},... | collective-permute-start | bytes 3145736 | tf_op jit(solution)/shard_map/ppermute | solution.py:651
  108.8 1.5 %unpack.2 = (f32[9,384,128]{2,1,0:T(8,128)}, f32[9,256,256]{2,1,0:T(8,128)}) custom-call(s32[1]{0:T(128)} %bitcast.place_ref, bf16[256,16,128]{2,1,0:T(8,128)(2,1)S(1)} %bitcast.13), custom_call_target="tpu_custom_call" | custom-call | flops 1 | bytes 1 | tf_op jit(solution)/shard_map/unpack/pallas_call | solution.py:520
  110.3 1.5 %unpack.3 = (f32[9,384,128]{2,1,0:T(8,128)}, f32[9,256,256]{2,1,0:T(8,128)}) custom-call(s32[1]{0:T(128)} %bitcast.4.place_ref, bf16[256,16,128]{2,1,0:T(8,128)(2,1)S(1)} %collective-permute-done.13.parts_ref, f32[9,384,128]{2,1,0:T(8,128)} %get-tuple-element.76.rest_0_, ...), custom_call_target="tpu_custom_call", output_to_operand_aliasing={{0}: (2, {}), {1}: (3, {})} | custom-call | flops 1 | bytes 1 | tf_op jit(solution)/shard_map/unpack/pallas_call | solution.py:520
  (70 shorter events, 18.7 us)
Async XLA Ops:
  4.0 11.2 %collective-permute-start = (bf16[2,512,128]{2,1,0:T(8,128)(2,1)S(1)}, bf16[2,512,128]{2,1,0:T(8,128)(2,1)S(1)}, u32[]{:S(2)}, u32[]{:S(2)}) collective-permute-start(bf16[2,512,128]{2,1,0:T(8,128)(2,1)S(1)} %get-tuple-element.42), channel_id=1, source_target_pairs={{0,1},{1,0},{2,3},{3,2},{4,5},{5,4},{6,7},{7,6},{8,9},{9,8},{10,11... | collective-permute-start | bytes 786440 | tf_op jit(solution)/shard_map/ppermute | solution.py:601
  6.1 15.5 %collective-permute-start.1 = (bf16[2,512,128]{2,1,0:T(8,128)(2,1)S(1)}, bf16[2,512,128]{2,1,0:T(8,128)(2,1)S(1)}, u32[]{:S(2)}, u32[]{:S(2)}) collective-permute-start(bf16[2,512,128]{2,1,0:T(8,128)(2,1)S(1)} %get-tuple-element.43), channel_id=1, source_target_pairs={{1,2},{3,4},{5,6},{7,8},{9,10},{11,12},{13,14},{15,16},{17,18},{19... | collective-permute-start | bytes 786440 | tf_op jit(solution)/shard_map/ppermute | solution.py:601
  11.5 20.9 %all-to-all-start = ((bf16[8,2,2,2,32,256]{5,4,3,2,1,0:T(8,128)(2,1)}), bf16[8,2,2,2,32,256]{5,4,3,2,1,0:T(8,128)(2,1)S(1)}, u32[]{:S(2)}, u32[]{:S(2)}) async-start(bf16[8,2,2,2,32,256]{5,4,3,2,1,0:T(8,128)(2,1)} %get-tuple-element.49), calls=%async_computation | async-start | bytes 2097152 | tf_op jit(solution)/shard_map/all_to_all | solution.py:621
  34.2 15.8 %copy-start = (bf16[2,256,256]{2,1,0:T(8,128)(2,1)}, bf16[2,256,256]{2,1,0:T(8,128)(2,1)S(1)}, u32[]{:S(2)}) copy-start(bf16[2,256,256]{2,1,0:T(8,128)(2,1)S(1)} %get-tuple-element.59.third_ref) | copy-start | bytes 786436
  34.2 15.8 %copy-start.2 = (bf16[2,256,256]{2,1,0:T(8,128)(2,1)}, bf16[2,256,256]{2,1,0:T(8,128)(2,1)S(1)}, u32[]{:S(2)}) copy-start(bf16[2,256,256]{2,1,0:T(8,128)(2,1)S(1)} %get-tuple-element.53.second_ref) | copy-start | bytes 786436
  34.2 12.6 %collective-permute-start.2 = (bf16[2,256,256]{2,1,0:T(8,128)(2,1)S(1)}, bf16[2,256,256]{2,1,0:T(8,128)(2,1)S(1)}, u32[]{:S(2)}, u32[]{:S(2)}) collective-permute-start(bf16[2,256,256]{2,1,0:T(8,128)(2,1)S(1)} %get-tuple-element.59.third_ref), channel_id=1, source_target_pairs={{0,1},{1,0},{2,3},{3,2},{4,5},{5,4},{6,7},{7,6},{8,9},{9,8},{10,11... | collective-permute-start | bytes 786440 | tf_op jit(solution)/shard_map/ppermute | solution.py:601
  34.3 13.3 %collective-permute-start.3 = (bf16[2,256,256]{2,1,0:T(8,128)(2,1)S(1)}, bf16[2,256,256]{2,1,0:T(8,128)(2,1)S(1)}, u32[]{:S(2)}, u32[]{:S(2)}) collective-permute-start(bf16[2,256,256]{2,1,0:T(8,128)(2,1)S(1)} %get-tuple-element.53.second_ref), channel_id=1, source_target_pairs={{1,2},{3,4},{5,6},{7,8},{9,10},{11,12},{13,14},{15,16},{17,18},{19... | collective-permute-start | bytes 786440 | tf_op jit(solution)/shard_map/ppermute | solution.py:601
  49.4 2.7 %collective-permute-start.11 = (bf16[144,16,128]{2,1,0:T(8,128)(2,1)S(1)}, bf16[144,16,128]{2,1,0:T(8,128)(2,1)S(1)}, u32[]{:S(2)}, u32[]{:S(2)}) collective-permute-start(bf16[144,16,128]{2,1,0:T(8,128)(2,1)S(1)} %coarse_weight_level.3), channel_id=1, source_target_pairs={{0,8},{8,0},{1,9},{9,1},{2,10},{10,2},{3,11},{11,3},{4,12},{12,4},... | collective-permute-start | bytes 1769480 | tf_op jit(solution)/shard_map/ppermute | solution.py:637
  49.5 2.6 %collective-permute-start.12 = (bf16[9,12,16,128]{3,2,1,0:T(8,128)(2,1)S(1)}, bf16[9,12,16,128]{3,2,1,0:T(8,128)(2,1)S(1)}, u32[]{:S(2)}, u32[]{:S(2)}) collective-permute-start(bf16[9,12,16,128]{3,2,1,0:T(8,128)(2,1)S(1)} %get-tuple-element.72), channel_id=1, source_target_pairs={{0,8},{8,0},{1,9},{9,1},{2,10},{10,2},{3,11},{11,3},{4,12},{12,4},... | collective-permute-start | bytes 1327112 | tf_op jit(solution)/shard_map/ppermute | solution.py:632
  52.2 11.8 %copy-start.11 = (bf16[3,3,256,256]{3,2,1,0:T(8,128)(2,1)S(1)}, bf16[3,3,256,256]{3,2,1,0:T(8,128)(2,1)}, u32[]{:S(2)}) copy-start(bf16[3,3,256,256]{3,2,1,0:T(8,128)(2,1)} %weight_ref.5) | copy-start | bytes 3538948
  53.4 10.6 %copy-start.3 = (bf16[2,256,256]{2,1,0:T(8,128)(2,1)S(1)}, bf16[2,256,256]{2,1,0:T(8,128)(2,1)}, u32[]{:S(2)}) copy-start(bf16[2,256,256]{2,1,0:T(8,128)(2,1)} %copy-done.2) | copy-start | bytes 786436
  53.4 10.6 %copy-start.5 = (bf16[2,256,256]{2,1,0:T(8,128)(2,1)S(1)}, bf16[2,256,256]{2,1,0:T(8,128)(2,1)}, u32[]{:S(2)}) copy-start(bf16[2,256,256]{2,1,0:T(8,128)(2,1)} %copy-done.4) | copy-start | bytes 786436
  53.4 10.6 %copy-start.7 = (bf16[2,256,256]{2,1,0:T(8,128)(2,1)S(1)}, bf16[2,256,256]{2,1,0:T(8,128)(2,1)}, u32[]{:S(2)}) copy-start(bf16[2,256,256]{2,1,0:T(8,128)(2,1)} %copy-done.6) | copy-start | bytes 786436
  53.4 27.6 %all-to-all-start.1 = ((bf16[64,4,16,128]{3,2,1,0:T(8,128)(2,1)}), bf16[64,4,16,128]{3,2,1,0:T(8,128)(2,1)S(1)}, u32[]{:S(2)}, u32[]{:S(2)}) async-start(bf16[64,4,16,128]{3,2,1,0:T(8,128)(2,1)} %bitcast.7), calls=%async_computation.1 | async-start | bytes 2097152 | tf_op jit(solution)/shard_map/all_to_all | solution.py:506
  67.6 20.3 %collective-permute-start.4 = (bf16[2,2,32,256]{3,2,1,0:T(8,128)(2,1)}, bf16[2,2,32,256]{3,2,1,0:T(8,128)(2,1)S(1)}, u32[]{:S(2)}, u32[]{:S(2)}) collective-permute-start(bf16[2,2,32,256]{3,2,1,0:T(8,128)(2,1)} %get-tuple-element.62), channel_id=1, source_target_pairs={{0,1},{1,0},{2,3},{3,2},{4,5},{5,4},{6,7},{7,6},{8,9},{9,8},{10,11... | collective-permute-start | bytes 196616 | tf_op jit(solution)/shard_map/ppermute | solution.py:642
  68.6 19.2 %collective-permute-start.5 = (bf16[2,2,32,256]{3,2,1,0:T(8,128)(2,1)}, bf16[2,2,32,256]{3,2,1,0:T(8,128)(2,1)S(1)}, u32[]{:S(2)}, u32[]{:S(2)}) collective-permute-start(bf16[2,2,32,256]{3,2,1,0:T(8,128)(2,1)} %get-tuple-element.63), channel_id=1, source_target_pairs={{0,2},{1,3},{2,0},{3,1},{4,6},{5,7},{6,4},{7,5},{8,10},{9,11},{10,... | collective-permute-start | bytes 196616 | tf_op jit(solution)/shard_map/ppermute | solution.py:642
  69.8 18.1 %collective-permute-start.6 = (bf16[2,2,32,256]{3,2,1,0:T(8,128)(2,1)}, bf16[2,2,32,256]{3,2,1,0:T(8,128)(2,1)S(1)}, u32[]{:S(2)}, u32[]{:S(2)}) collective-permute-start(bf16[2,2,32,256]{3,2,1,0:T(8,128)(2,1)} %get-tuple-element.64), channel_id=1, source_target_pairs={{0,3},{1,2},{2,1},{3,0},{4,7},{5,6},{6,5},{7,4},{8,11},{9,10},{10,... | collective-permute-start | bytes 196616 | tf_op jit(solution)/shard_map/ppermute | solution.py:642
  70.2 17.7 %collective-permute-start.7 = (bf16[2,2,32,256]{3,2,1,0:T(8,128)(2,1)S(1)}, bf16[2,2,32,256]{3,2,1,0:T(8,128)(2,1)S(1)}, u32[]{:S(2)}, u32[]{:S(2)}) collective-permute-start(bf16[2,2,32,256]{3,2,1,0:T(8,128)(2,1)S(1)} %get-tuple-element.65), channel_id=1, source_target_pairs={{0,4},{1,5},{2,6},{3,7},{4,0},{5,1},{6,2},{7,3},{8,12},{9,13},{10,... | collective-permute-start | bytes 196616 | tf_op jit(solution)/shard_map/ppermute | solution.py:642
  72.7 15.2 %copy-start.20 = (bf16[2,2,32,256]{3,2,1,0:T(8,128)(2,1)S(1)}, bf16[2,2,32,256]{3,2,1,0:T(8,128)(2,1)}, u32[]{:S(2)}) copy-start(bf16[2,2,32,256]{3,2,1,0:T(8,128)(2,1)} %copy-done.19) | copy-start | bytes 196612
  72.7 15.1 %collective-permute-start.8 = (bf16[2,2,32,256]{3,2,1,0:T(8,128)(2,1)S(1)}, bf16[2,2,32,256]{3,2,1,0:T(8,128)(2,1)S(1)}, u32[]{:S(2)}, u32[]{:S(2)}) collective-permute-start(bf16[2,2,32,256]{3,2,1,0:T(8,128)(2,1)S(1)} %get-tuple-element.66), channel_id=1, source_target_pairs={{0,5},{1,4},{2,7},{3,6},{4,1},{5,0},{6,3},{7,2},{8,13},{9,12},{10,... | collective-permute-start | bytes 196616 | tf_op jit(solution)/shard_map/ppermute | solution.py:642
  82.2 21.8 %all-to-all-start.2 = ((bf16[64,4,16,128]{3,2,1,0:T(8,128)(2,1)}), bf16[64,4,16,128]{3,2,1,0:T(8,128)(2,1)S(1)}, u32[]{:S(2)}, u32[]{:S(2)}) async-start(bf16[64,4,16,128]{3,2,1,0:T(8,128)(2,1)} %sum_parts.1), calls=%async_computation.2 | async-start | bytes 2097152 | tf_op jit(solution)/shard_map/all_to_all | solution.py:514
  87.9 20.0 %collective-permute-start.9 = (bf16[2,2,32,256]{3,2,1,0:T(8,128)(2,1)S(1)}, bf16[2,2,32,256]{3,2,1,0:T(8,128)(2,1)S(1)}, u32[]{:S(2)}, u32[]{:S(2)}) collective-permute-start(bf16[2,2,32,256]{3,2,1,0:T(8,128)(2,1)S(1)} %get-tuple-element.69), channel_id=1, source_target_pairs={{0,6},{1,7},{2,4},{3,5},{4,2},{5,3},{6,0},{7,1},{8,14},{9,15},{10,... | collective-permute-start | bytes 196616 | tf_op jit(solution)/shard_map/ppermute | solution.py:642
  90.2 17.7 %collective-permute-start.10 = (bf16[2,2,32,256]{3,2,1,0:T(8,128)(2,1)S(1)}, bf16[2,2,32,256]{3,2,1,0:T(8,128)(2,1)S(1)}, u32[]{:S(2)}, u32[]{:S(2)}) collective-permute-start(bf16[2,2,32,256]{3,2,1,0:T(8,128)(2,1)S(1)} %get-tuple-element.70), channel_id=1, source_target_pairs={{0,7},{1,6},{2,5},{3,4},{4,3},{5,2},{6,1},{7,0},{8,15},{9,14},{10,... | collective-permute-start | bytes 196616 | tf_op jit(solution)/shard_map/ppermute | solution.py:642
  104.0 6.3 %collective-permute-start.13 = (bf16[256,16,128]{2,1,0:T(8,128)(2,1)S(1)}, bf16[256,16,128]{2,1,0:T(8,128)(2,1)S(1)}, u32[]{:S(2)}, u32[]{:S(2)}) collective-permute-start(bf16[256,16,128]{2,1,0:T(8,128)(2,1)S(1)} %bitcast.12), channel_id=1, source_target_pairs={{0,8},{8,0},{1,9},{9,1},{2,10},{10,2},{3,11},{11,3},{4,12},{12,4},... | collective-permute-start | bytes 3145736 | tf_op jit(solution)/shard_map/ppermute | solution.py:651
  (16 other events, 44.2 us)

commit v4 on v3

--- a/solution.py
+++ b/solution.py
@@ -20,7 +20,7 @@
 ROWS = ("xh", "z", "core")
 CHAN = ("y", "xl")
 ALL = ROWS + CHAN
-CHIPS = ("xh", "xl", "z", "y")
+CHIPS = ("xh", "z", "y", "xl")
 
 
 def params(limit):
@@ -68,76 +68,112 @@
     return (before + even).astype(BF16), (even + odd).astype(BF16), (odd + after).astype(BF16)
 
 
-def box_kernel(
-    place_ref, cot_ref, pre_ref, near_ref, far_ref, weight_ref, grad_ref, pooled_ref, box_ref, rows32, up_weight
-):
+def box_kernel(cot_ref, pre_ref, weight_ref, grad_ref, box_ref, edge_ref, pooled_ref, up_weight, rows32):
     c3 = cot_ref.shape[-1]
-    c4 = pooled_ref.shape[-1]
     half = pooled_ref.shape[-2]
-    odd = place_ref[0] >= 2
+    reach = 3 * c3
 
     @pl.when(pl.program_id(0) == 0)
     def _():
         for dy in range(3):
             for d in range(3):
                 at = (dy * 3 + d) * c3
-                up_weight[at : at + c3, :] = weight_ref[2 - dy, 2 - d, :c4, :].astype(F32).T.astype(BF16)
-
-    for v in range(6):
-        if v == 0:
-            grad = jnp.where(odd, near_ref[0], far_ref[0])
-        elif v == 5:
-            grad = jnp.where(odd, far_ref[0], near_ref[0])
-        else:
-            grad = (cot_ref[0, v - 1].astype(F32) * silu_grad(pre_ref[0, v - 1].astype(F32))).astype(BF16)
+                up_weight[at : at + c3, :] = weight_ref[2 - dy, 2 - d].astype(F32).T.astype(BF16)
+
+    for v in range(4):
+        grad = (cot_ref[0, v].astype(F32) * silu_grad(pre_ref[0, v].astype(F32))).astype(BF16)
         grad_ref[0, v] = grad
         rows32[v] = grad.astype(F32)
-    for v in range(5):
-        sums = box_sums(rows32.at[v], rows32.at[v + 1], half)
-        for i in range(2):
-            dy = v - 2 * i
-            if 0 <= dy <= 2:
-                for d in range(3):
-                    at = (dy * 3 + d) * c3
-                    box_ref[0, i * half : (i + 1) * half, at : at + c3] = sums[d]
-    pooled = jnp.dot(box_ref[0], up_weight[...], preferred_element_type=F32)
-    pooled_ref[0] = pooled.reshape(pooled_ref.shape[1:])
-
-
-def box_level(place, cot, pre, near, far, weight, cs):
+        if v % 3 == 0:
+            edge_ref[0, v // 3] = grad
+    for v in range(3):
+        for d, value in enumerate(box_sums(rows32.at[v], rows32.at[v + 1], half)):
+            at = v * reach + d * c3
+            box_ref[0, :, at : at + c3] = value
+    pooled_ref[0, 0] = jnp.dot(box_ref[0, :, : 2 * reach], up_weight[reach:, :], preferred_element_type=F32)
+    pooled_ref[0, 1] = jnp.dot(box_ref[0, :, reach:], up_weight[: 2 * reach, :], preferred_element_type=F32)
+
+
+def box_level(cot, pre, weight, cs):
     samples, height, wide, c3 = cot.shape
     c4 = weight.shape[2] - cs
     half = wide // 2
     block = pl.BlockSpec((1, height, wide, c3), lambda s: (s, 0, 0, 0))
-    edge = pl.BlockSpec((1, wide, c3), lambda s: (s, 0, 0))
     return pl.pallas_call(
         box_kernel,
         grid=(samples,),
+        in_specs=[block, block, pl.BlockSpec((3, 3, c4, c3), lambda s: (0, 0, 0, 0))],
+        out_specs=[
+            block,
+            pl.BlockSpec((1, half, 9 * c3), lambda s: (s, 0, 0)),
+            pl.BlockSpec((1, 2, wide, c3), lambda s: (s, 0, 0, 0)),
+            pl.BlockSpec((1, 2, half, c4), lambda s: (s, 0, 0, 0)),
+            pl.BlockSpec((9 * c3, c4), lambda s: (0, 0)),
+        ],
+        out_shape=[
+            pltpu.HBM((samples, height, wide, c3), BF16),
+            pltpu.HBM((samples, half, 9 * c3), BF16),
+            jax.ShapeDtypeStruct((samples, 2, wide, c3), BF16),
+            jax.ShapeDtypeStruct((samples, 2, half, c4), F32),
+            jax.ShapeDtypeStruct((9 * c3, c4), BF16),
+        ],
+        scratch_shapes=[pltpu.VMEM((height, wide, c3), F32)],
+        compiler_params=params(VMEM),
+        cost_estimate=cost(1.2e9, 8e6),
+        name="box_level",
+    )(in_hbm(cot), in_hbm(pre), in_hbm(weight))
+
+
+def edge_kernel(
+    place_ref, near_ref, far_ref, edge_ref, pooled_ref, low_weight_ref, high_weight_ref,
+    out_ref, box_low_ref, box_high_ref, rows32,
+):
+    half = pooled_ref.shape[-2]
+    c3 = edge_ref.shape[-1]
+    odd = place_ref[0] >= 2
+    near, far = near_ref[0].astype(F32), far_ref[0].astype(F32)
+    sides = (
+        (jnp.where(odd, near, far), edge_ref[0, 0].astype(F32), low_weight_ref, box_low_ref),
+        (edge_ref[0, 1].astype(F32), jnp.where(odd, far, near), high_weight_ref, box_high_ref),
+    )
+    for i, (upper, lower, weight_ref, box_ref) in enumerate(sides):
+        rows32[0] = upper
+        rows32[1] = lower
+        for d, value in enumerate(box_sums(rows32.at[0], rows32.at[1], half)):
+            box_ref[0, :, d * c3 : (d + 1) * c3] = value
+        out_ref[0, i] = pooled_ref[0, i] + jnp.dot(box_ref[0], weight_ref[...], preferred_element_type=F32)
+
+
+def edge_level(place, near, far, edge, pooled, up_weight):
+    samples, _, half, c4 = pooled.shape
+    _, _, wide, c3 = edge.shape
+    row = pl.BlockSpec((1, wide, c3), lambda s: (s, 0, 0))
+    whole = pl.BlockSpec((1, 2, half, c4), lambda s: (s, 0, 0, 0))
+    box_spec = pl.BlockSpec((1, half, 3 * c3), lambda s: (s, 0, 0))
+    box = pltpu.HBM((samples, half, 3 * c3), BF16)
+    return pl.pallas_call(
+        edge_kernel,
+        grid=(samples,),
         in_specs=[
-            pl.BlockSpec(memory_space=pltpu.SMEM), block, block, edge, edge,
-            pl.BlockSpec(weight.shape, lambda s: (0, 0, 0, 0)),
-        ],
-        out_specs=[
-            pl.BlockSpec((1, height + 2, wide, c3), lambda s: (s, 0, 0, 0)),
-            pl.BlockSpec((1, 2, half, c4), lambda s: (s, 0, 0, 0)),
-            pl.BlockSpec((1, 2 * half, 9 * c3), lambda s: (s, 0, 0)),
-        ],
-        out_shape=[
-            jax.ShapeDtypeStruct((samples, height + 2, wide, c3), BF16),
-            jax.ShapeDtypeStruct((samples, 2, half, c4), F32),
-            jax.ShapeDtypeStruct((samples, 2 * half, 9 * c3), BF16),
-        ],
-        scratch_shapes=[pltpu.VMEM((6, wide, c3), F32), pltpu.VMEM((9 * c3, c4), BF16)],
-        compiler_params=params(VMEM),
-        cost_estimate=cost(LONG, 8e6),
-        name="box_level",
-    )(place, cot, pre, near, far, weight)
+            pl.BlockSpec(memory_space=pltpu.SMEM), row, row,
+            pl.BlockSpec((1, 2, wide, c3), lambda s: (s, 0, 0, 0)), whole,
+            pl.BlockSpec((3 * c3, c4), lambda s: (0, 0)),
+            pl.BlockSpec((3 * c3, c4), lambda s: (2, 0)),
+        ],
+        out_specs=[whole, box_spec, box_spec],
+        out_shape=[pltpu.HBM((samples, 2, half, c4), F32), box, box],
+        scratch_shapes=[pltpu.VMEM((2, wide, c3), F32)],
+        compiler_params=params(VMEM),
+        cost_estimate=cost(LONG, 4e6),
+        name="edge_level",
+    )(place, in_hbm(near), in_hbm(far), edge, pooled, up_weight, up_weight)
 
 
 def fine_kernel(
-    place_ref, grad_ref, skip_ref, weight_ref, grad_skip_ref, keep_ref, send_ref, taps, skip_weight, total, *, scale
+    place_ref, grad_ref, near_ref, far_ref, skip_ref, weight_ref, grad_skip_ref, keep_ref, send_ref, taps, skip_weight, total, *, scale
 ):
     sample = pl.program_id(0)
+    odd = place_ref[0] >= 2
     c3 = grad_ref.shape[-1]
     cs = skip_ref.shape[-1]
     c4 = weight_ref.shape[2] - cs
@@ -157,7 +193,12 @@
                     skip_weight[at : at + c3, t * cs : (t + 1) * cs] = block
 
     for v in range(6):
-        grad = grad_ref[0, v]
+        if v == 0:
+            grad = jnp.where(odd, near_ref[0], far_ref[0])
+        elif v == 5:
+            grad = jnp.where(odd, far_ref[0], near_ref[0])
+        else:
+            grad = grad_ref[0, v - 1]
         before, after = shifted(grad.astype(F32))
         at = v * 3 * c3
         taps[:, at : at + c3] = before.astype(BF16)
@@ -188,7 +229,7 @@
                 send_ref[tap] = tiles(jnp.where(core == 0, high, low))
 
 
-def fine_level(place, grad, skip, weight, fine_cells):
+def fine_level(place, grad, near, far, skip, weight, fine_cells):
     samples, height, wide, cs = skip.shape
     c3 = grad.shape[-1]
     part = jax.ShapeDtypeStruct((9, cs // 32, 16, c3), BF16)
@@ -198,7 +239,9 @@
         grid=(samples,),
         in_specs=[
             pl.BlockSpec(memory_space=pltpu.SMEM),
-            pl.BlockSpec((1, height + 2, wide, c3), lambda s: (s, 0, 0, 0)),
+            pl.BlockSpec((1, height, wide, c3), lambda s: (s, 0, 0, 0)),
+            pl.BlockSpec((1, wide, c3), lambda s: (s, 0, 0)),
+            pl.BlockSpec((1, wide, c3), lambda s: (s, 0, 0)),
             pl.BlockSpec((1, height, wide, cs), lambda s: (s, 0, 0, 0)),
             pl.BlockSpec(weight.shape, lambda s: (0, 0, 0, 0)),
         ],
@@ -212,7 +255,7 @@
         compiler_params=params(VMEM),
         cost_estimate=cost(5e9, 8e6),
         name="fine_level",
-    )(place, grad, skip, weight)
+    )(place, *(in_hbm(a) for a in (grad, near, far, skip, weight)))
 
 
 def coarse_grad_kernel(place_ref, pooled_ref, pre_ref, near_ref, far_ref):
@@ -248,7 +291,8 @@
 
 
 def up_kernel(
-    place_ref, pre_ref, box_ref, skip_keep_ref, skip_send_ref, keep_ref, send_ref, total, *, scale
+    place_ref, pre_ref, box_ref, box_low_ref, box_high_ref, skip_keep_ref, skip_send_ref, keep_ref, send_ref, total,
+    *, scale
 ):
     sample = pl.program_id(0)
     wide = pre_ref.shape[-1]
@@ -259,9 +303,16 @@
     def _():
         total[...] = jnp.zeros_like(total)
 
-    value = jnp.concatenate([pre_ref[:, 0, 0, i].reshape(c4, wide) for i in range(2)], axis=1).astype(F32)
-    value = (value * jax.nn.sigmoid(value)).astype(BF16)
-    total[...] += jnp.dot(value, box_ref[0], preferred_element_type=F32)
+    reach = 3 * c3
+    windows = (
+        ((0, box_low_ref[0]), (reach, box_ref[0, :, : 2 * reach])),
+        ((0, box_ref[0, :, reach:]), (2 * reach, box_high_ref[0])),
+    )
+    for i in range(2):
+        value = pre_ref[:, 0, 0, i].reshape(c4, wide).astype(F32)
+        value = (value * jax.nn.sigmoid(value)).astype(BF16)
+        for at, window in windows[i]:
+            total[:, at : at + window.shape[1]] += jnp.dot(value, window, preferred_element_type=F32)
 
     @pl.when(sample == pl.num_programs(0) - 1)
     def _():
@@ -280,7 +331,7 @@
                 send_ref[tap, mine:] = skip_send_ref[tap]
 
 
-def up_level(place, received, box, skip_keep, skip_send, fine_cells):
+def up_level(place, received, box, box_low, box_high, skip_keep, skip_send, fine_cells):
     peers, _, samples, _, own, wide = received.shape
     c4 = peers * own
     c3 = box.shape[-1] // 9
@@ -293,7 +344,9 @@
         in_specs=[
             pl.BlockSpec(memory_space=pltpu.SMEM),
             pl.BlockSpec((peers, 1, 1, 2, own, wide), lambda s: (0, 0, s, 0, 0, 0)),
-            pl.BlockSpec((1, 2 * wide, 9 * c3), lambda s: (s, 0, 0)),
+            pl.BlockSpec((1, wide, 9 * c3), lambda s: (s, 0, 0)),
+            pl.BlockSpec((1, wide, 3 * c3), lambda s: (s, 0, 0)),
+            pl.BlockSpec((1, wide, 3 * c3), lambda s: (s, 0, 0)),
             skips, skips,
         ],
         out_specs=[whole, whole],
@@ -302,7 +355,7 @@
         compiler_params=params(VMEM),
         cost_estimate=cost(1e9, 5e6),
         name="up_level",
-    )(place, received, box, skip_keep, skip_send)
+    )(place, received, box, box_low, box_high, skip_keep, skip_send)
 
 
 def fill_coarse_taps(odd, rows, taps):
@@ -316,27 +369,69 @@
             taps[lines, c4 : 2 * c4] = row
             taps[lines, 2 * c4 :] = after.astype(BF16)
 
-    pl.when(odd)(lambda: fill((3, 2, 1, 0)))
-    pl.when(jnp.logical_not(odd))(lambda: fill((0, 1, 2, 3)))
-
-
-def coarse_weight_kernel(
-    place_ref, input_ref, first_ref, second_ref, third_ref, fourth_ref, out_ref, taps, total, *, scale
-):
+    count = len(rows)
+    pl.when(odd)(lambda: fill(range(count - 1, -1, -1)))
+    pl.when(jnp.logical_not(odd))(lambda: fill(range(count)))
+
+
+def dot32(left, right):
+    return jnp.dot(left, right, preferred_element_type=F32)
+
+
+def own_weight_kernel(place_ref, input_ref, far_ref, near_ref, out_ref, taps):
+    wide = input_ref.shape[-1]
+    c4 = far_ref.shape[-1]
+
+    @pl.when(pl.program_id(0) == 0)
+    def _():
+        out_ref[...] = jnp.zeros_like(out_ref)
+
+    fill_coarse_taps(place_ref[0] >= 2, (far_ref[0], near_ref[0]), taps)
+    first, second = (input_ref[:, 0, 0, i].reshape(c4, wide) for i in range(2))
+    out_ref[0] += dot32(second, taps[:wide, :])
+    out_ref[1] += dot32(jnp.concatenate([first, second], axis=1), taps[...])
+    out_ref[2] += dot32(first, taps[wide:, :])
+
+
+def own_weight_level(place, received, far, near):
+    peers, _, samples, _, own, wide = received.shape
+    c4 = peers * own
+    row = pl.BlockSpec((1, wide, c4), lambda s: (s, 0, 0))
+    return pl.pallas_call(
+        own_weight_kernel,
+        grid=(samples,),
+        in_specs=[
+            pl.BlockSpec(memory_space=pltpu.SMEM),
+            pl.BlockSpec((peers, 1, 1, 2, own, wide), lambda s: (0, 1, s, 0, 0, 0)),
+            row, row,
+        ],
+        out_specs=pl.BlockSpec((3, c4, 3 * c4), lambda s: (0, 0, 0)),
+        out_shape=jax.ShapeDtypeStruct((3, c4, 3 * c4), F32),
+        scratch_shapes=[pltpu.VMEM((2 * wide, 3 * c4), BF16)],
+        compiler_params=params(VMEM),
+        cost_estimate=cost(9e8, 4e6),
+        name="own_weight_level",
+    )(place, received, far, near)
+
+
+def coarse_weight_kernel(place_ref, input_ref, from_far_ref, from_near_ref, own_ref, out_ref, taps, total, *, scale):
     sample = pl.program_id(0)
     wide = input_ref.shape[-1]
     part = input_ref.shape[0] * input_ref.shape[-2]
-    c4 = first_ref.shape[-1]
+    c4 = from_far_ref.shape[-1]
+
+    fill_coarse_taps(place_ref[0] >= 2, (from_far_ref[0], from_near_ref[0]), taps)
+    terms = [dot32(input_ref[:, 0, 0, i].reshape(part, wide), taps[i * wide : (i + 1) * wide, :]) for i in range(2)]
 
     @pl.when(sample == 0)
     def _():
-        total[...] = jnp.zeros_like(total)
-
-    rows = (first_ref[0], second_ref[0], third_ref[0], fourth_ref[0])
-    fill_coarse_taps(place_ref[0] >= 2, rows, taps)
-    values = jnp.concatenate([input_ref[:, 0, 0, i].reshape(part, wide) for i in range(2)], axis=1)
-    for dy in range(3):
-        total[dy] += jnp.dot(values, taps[dy * wide : (dy + 2) * wide, :], preferred_element_type=F32)
+        for i, term in enumerate(terms):
+            total[i] = term
+
+    @pl.when(sample > 0)
+    def _():
+        for i, term in enumerate(terms):
+            total[i] += term
 
     @pl.when(sample == pl.num_programs(0) - 1)
     def _():
@@ -345,33 +440,40 @@
             for d in range(3):
                 for side in range(c4 // 128):
                     at = d * c4 + side * 128
+                    value = own_ref[dy, :, at : at + 128]
+                    if dy != 1:
+                        value = value + total[dy // 2, :, at : at + 128]
                     tap = ((2 - dy) * 3 + 2 - d) * (c4 // 128) + side
-                    out_ref[tap * count : (tap + 1) * count] = tiles(total[dy, :, at : at + 128] * scale)
-
-
-def coarse_specs(wide, c4, count):
-    return [pl.BlockSpec((1, wide, c4), lambda s: (s, 0, 0))] * count
-
-
-def coarse_weight_level(place, received, rows, coarse_cells):
+                    out_ref[tap * count : (tap + 1) * count] = tiles(value * scale)
+
+
+def coarse_weight_level(place, received, from_far, from_near, own_terms, coarse_cells):
     peers, _, samples, _, own, wide = received.shape
     c4 = peers * own
     shape = (9 * (c4 // 128) * (c4 // 32), 16, 128)
+    row = pl.BlockSpec((1, wide, c4), lambda s, place: (s, 0, 0))
     return pl.pallas_call(
         functools.partial(coarse_weight_kernel, scale=1.0 / math.sqrt(coarse_cells)),
         grid_spec=pltpu.PrefetchScalarGridSpec(
             num_scalar_prefetch=1,
             grid=(samples,),
-            in_specs=[pl.BlockSpec((peers // 2, 1, 1, 2, own, wide), lambda s, place: (place[0] % 2, 1, s, 0, 0, 0))]
-            + [pl.BlockSpec((1, wide, c4), lambda s, place: (s, 0, 0))] * 4,
+            in_specs=[
+                pl.BlockSpec((peers // 2, 1, 1, 2, own, wide), lambda s, place: (place[0] % 2, 1, s, 0, 0, 0)),
+                row, row,
+                pl.BlockSpec((3, c4 // 2, 3 * c4), lambda s, place: (0, place[0] % 2, 0)),
+            ],
             out_specs=pl.BlockSpec(shape, lambda s, place: (0, 0, 0)),
-            scratch_shapes=[pltpu.VMEM((4 * wide, 3 * c4), BF16), pltpu.VMEM((3, c4 // 2, 3 * c4), F32)],
+            scratch_shapes=[pltpu.VMEM((2 * wide, 3 * c4), BF16), pltpu.VMEM((2, c4 // 2, 3 * c4), F32)],
         ),
         out_shape=jax.ShapeDtypeStruct(shape, BF16),
         compiler_params=params(VMEM),
-        cost_estimate=cost(0.7e9, 2e6),
+        cost_estimate=cost(0.4e9, 2e6),
         name="coarse_weight_level",
-    )(place, received, *rows)
+    )(place, received, from_far, from_near, own_terms)
+
+
+def coarse_specs(wide, c4, count):
+    return [pl.BlockSpec((1, wide, c4), lambda s: (s, 0, 0))] * count
 
 
 def coarse_input_kernel(chan_ref, weight_ref, first_ref, second_ref, third_ref, fourth_ref, *rest):
@@ -622,20 +724,23 @@
 
     cs = skip_feats.shape[-1]
     fine_cells = fine_pre.shape[0] * fine_pre.shape[1] * fine_pre.shape[2] * devices
-    edge_near, edge_far, cotangent = lax.optimization_barrier((edge_near, edge_far, fine_cotangent))
-    fine_grad, pooled, box = box_level(place, cotangent, fine_pre, edge_near, edge_far, fine_weight, cs)
+    fine_grad, box, edge, pooled, up_weight = box_level(fine_cotangent, fine_pre, fine_weight, cs)
+    pooled, box_low, box_high = edge_level(place, edge_near, edge_far, edge, pooled, up_weight)
+    grad_skip, skip_keep, skip_send = fine_level(
+        place, fine_grad, edge_near, edge_far, skip_feats, fine_weight, fine_cells
+    )
+    received, skip_keep, skip_send = lax.optimization_barrier((received, skip_keep, skip_send))
     near, far = coarse_grad(place, pooled, received)
     from_near, from_far = swapped(near, far)
-    fine_grad, near = lax.optimization_barrier((fine_grad, near))
-    grad_skip, skip_keep, skip_send = fine_level(place, fine_grad, skip_feats, fine_weight, fine_cells)
-    fine_keep, fine_send = up_level(place, received, box, skip_keep, skip_send, fine_cells)
+    fine_keep, fine_send = up_level(place, received, box, box_low, box_high, skip_keep, skip_send, fine_cells)
     fine_more = lax.ppermute(fine_send, "core", SWAP)
-    from_near, from_far, fine_keep = lax.optimization_barrier((from_near, from_far, fine_keep))
+    own_terms = own_weight_level(place, received, far, near)
+    from_near, from_far, fine_keep, own_terms = lax.optimization_barrier((from_near, from_far, fine_keep, own_terms))
     rows = (from_far, far, near, from_near)
     coarse_cells = samples * (lines // peers) * wide * devices
-    coarse_send = coarse_weight_level(other_place, received, rows, coarse_cells)
+    coarse_send = coarse_weight_level(other_place, received, from_far, from_near, own_terms, coarse_cells)
     coarse_more = lax.ppermute(coarse_send, "core", SWAP)
-    coarse_keep = coarse_weight_level(place, received, rows, coarse_cells)
+    coarse_keep = coarse_weight_level(place, received, from_far, from_near, own_terms, coarse_cells)
     back = coarse_input_level(chan, coarse_weight, rows, peers)
 
     def home(k, piece):

time: 113 us -> 111 us (0.982)
  local copies, waits for them, and re-layouts: 11.1 us -> 1.35 us
  Pallas kernels: 26.7 us -> 33.3 us
  waiting for transfers between devices: 26.5 us -> 27.8 us
    unnamed x46 -> x16, local copies, waits for them, and re-layouts: 11.1 us -> 1.35 us
    pallas_call x1 -> x3, Pallas kernels: 2.54 us -> 8.71 us  [the longest x1 4.29 us: box_level(): pl.pallas_call(box_kernel, grid=(samples,), in_specs=[block, block, pl.Bl...]
    ppermute x4, waiting for transfers between devices: 6.6 us -> 8.5 us  [swapped(): return (lax.ppermute(near, ALL, inside), lax.ppermute(far, ALL, outside))]
    pallas_call x1, Pallas kernels: 4.93 us -> 6.59 us  [fine_level(): pl.pallas_call(functools.partial(fine_kernel, scale=1.0 / math.sqrt(fine_...]
  transfers between devices with their start and end apart: 17 -> 17, of which waited for: 5 -> 6; matrix products, arithmetic and copies ran while one was open for 0% -> 0% of each run, Pallas kernels for 15% -> 22%
where the time goes in v4:
time: 111 us
  starting transfers between devices  47.4 us (43%)
  Pallas kernels  33.3 us (30%)
  waiting for transfers between devices  27.8 us (25%)
  local copies, waits for them, and re-layouts  1.35 us (1%)
    ppermute x4, starting transfers between devices, swapped(): return (lax.ppermute(near, ALL, inside), lax.ppermute(far, ALL, outside))  12.6 us
    all_to_all x1, waiting for transfers between devices, grad_sums(): lax.all_to_all(summed, CHIPS, 0, 0, tiled=True)  11.4 us
    all_to_all x1, starting transfers between devices, grad_sums(): lax.all_to_all(joined.reshape(chips, each, 16, 128), CHIPS, 0, 0, tiled=T...  9.88 us
    ppermute x7, starting transfers between devices, home(): return lax.ppermute(piece, CHAN, [(i, i ^ k) for i in range(peers)])  9.85 us
    ppermute x4, waiting for transfers between devices, swapped(): return (lax.ppermute(near, ALL, inside), lax.ppermute(far, ALL, outside))  8.5 us
    pallas_call x1, Pallas kernels, fine_level(): pl.pallas_call(functools.partial(fine_kernel, scale=1.0 / math.sqrt(fine_...  6.59 us
    all_to_all x1, waiting for transfers between devices, grad_sums(): lax.all_to_all(joined.reshape(chips, each, 16, 128), CHIPS, 0, 0, tiled=T...  6.5 us
    all_to_all x1, starting transfers between devices, grad_sums(): lax.all_to_all(summed, CHIPS, 0, 0, tiled=True)  6.05 us
  transfers between devices with their start and end apart: 17, of which 6 were waited for; matrix products, arithmetic and copies ran while one was open for 0% of the time, Pallas kernels for 22%

profile of v4, /device:TPU:1, one launch (start us, length us, event | category | flops | bytes accessed | tf_op | source)
XLA Modules:
  0.0 110.9 jit_solution(5085211857005177952)
XLA Ops:
  0.6 3.3 %start.1 = (bf16[8,2,2,2,32,256]{5,4,3,2,1,0:T(8,128)(2,1)}, bf16[2,512,128]{2,1,0:T(8,128)(2,1)S(1)}, bf16[2,512,128]{2,1,0:T(8,128)(2,1)S(1)}) custom-call(s32[1]{0:T(128)} %bitcast.place_ref, bf16[2,16,32,256]{3,2,1,0:T(8,128)(2,1)} %bitcast.18, bf16[2,16,32,256]{3,2,1,0:T(8,128)(2,1)} %bitcast.19, bf16[2,4,512,128]{3,2,1,0:T(8,128)(2,1)} %cot_ref.3, ...), custom_call_target="tpu_custom_call" | custom-call | flops 10000000 | bytes 3000000 | tf_op jit(solution)/shard_map/start/pallas_call | solution.py:680
  4.0 2.1 %collective-permute-start = (bf16[2,512,128]{2,1,0:T(8,128)(2,1)S(1)}, bf16[2,512,128]{2,1,0:T(8,128)(2,1)S(1)}, u32[]{:S(2)}, u32[]{:S(2)}) collective-permute-start(bf16[2,512,128]{2,1,0:T(8,128)(2,1)S(1)} %get-tuple-element.47), channel_id=1, source_target_pairs={{0,1},{1,0},{2,3},{3,2},{4,5},{5,4},{6,7},{7,6},{8,9},{9,8},{10,11... | collective-permute-start | bytes 786440 | tf_op jit(solution)/shard_map/ppermute | solution.py:703
  6.1 5.4 %collective-permute-start.1 = (bf16[2,512,128]{2,1,0:T(8,128)(2,1)S(1)}, bf16[2,512,128]{2,1,0:T(8,128)(2,1)S(1)}, u32[]{:S(2)}, u32[]{:S(2)}) collective-permute-start(bf16[2,512,128]{2,1,0:T(8,128)(2,1)S(1)} %get-tuple-element.48), channel_id=1, source_target_pairs={{1,2},{3,4},{5,6},{7,8},{9,10},{11,12},{13,14},{15,16},{17,18},{19... | collective-permute-start | bytes 786440 | tf_op jit(solution)/shard_map/ppermute | solution.py:703
  11.5 3.6 %all-to-all-start = ((bf16[8,2,2,2,32,256]{5,4,3,2,1,0:T(8,128)(2,1)}), bf16[8,2,2,2,32,256]{5,4,3,2,1,0:T(8,128)(2,1)S(1)}, u32[]{:S(2)}, u32[]{:S(2)}) async-start(bf16[8,2,2,2,32,256]{5,4,3,2,1,0:T(8,128)(2,1)} %get-tuple-element.54), calls=%async_computation | async-start | bytes 2097152 | tf_op jit(solution)/shard_map/all_to_all | solution.py:723
  15.1 4.3 %box_level.1 = (bf16[2,4,512,128]{3,2,1,0:T(8,128)(2,1)}, bf16[2,256,1152]{2,1,0:T(8,128)(2,1)}, bf16[2,2,512,128]{3,2,1,0:T(8,128)(2,1)S(1)}, f32[2,2,256,256]{3,2,1,0:T(8,128)S(1)}, bf16[1152,256]{1,0:T(8,128)(2,1)S(1)}) custom-call(bf16[2,4,512,128]{3,2,1,0:T(8,128)(2,1)} %cot_ref.3, bf16[2,4,512,128]{3,2,1,0:T(8,128)(2,1)} %fine_pre_ref.1, ...), custom_call_target="tpu_custom_call" | custom-call | flops 1200000000 | bytes 8000000 | tf_op jit(solution)/shard_map/box_level/pallas_call | solution.py:102
  19.4 2.2 %collective-permute-done.1.far_ref = bf16[2,512,128]{2,1,0:T(8,128)(2,1)S(1)} collective-permute-done((bf16[2,512,128]{2,1,0:T(8,128)(2,1)S(1)}, bf16[2,512,128]{2,1,0:T(8,128)(2,1)S(1)}, u32[]{:S(2)}, u32[]{:S(2)}) %collective-permute-start.1) | collective-permute-done | bytes 262176 | tf_op jit(solution)/shard_map/ppermute | solution.py:703
  22.3 2.7 %edge_level.1 = (f32[2,2,256,256]{3,2,1,0:T(8,128)}, bf16[2,256,384]{2,1,0:T(8,128)(2,1)}, bf16[2,256,384]{2,1,0:T(8,128)(2,1)}) custom-call(s32[1]{0:T(128)} %bitcast.place_ref, bf16[2,512,128]{2,1,0:T(8,128)(2,1)} %copy-done.6, bf16[2,512,128]{2,1,0:T(8,128)(2,1)} %copy-done.7, bf16[2,2,512,128]{3,2,1,0:T(8,128)(2,1)S(1)} %get-tuple-element.50.edge_ref, ...), custom_call_target="tpu_custom_call" | custom-call | flops 99999997952 | bytes 4000000 | tf_op jit(solution)/shard_map/edge_level/pallas_call | solution.py:154
  24.9 6.6 %fine_level.1 = (bf16[2,4,512,128]{3,2,1,0:T(8,128)(2,1)}, bf16[9,4,16,128]{3,2,1,0:T(8,128)(2,1)S(1)}, bf16[9,4,16,128]{3,2,1,0:T(8,128)(2,1)S(1)}) custom-call(s32[1]{0:T(128)} %bitcast.place_ref, bf16[2,4,512,128]{3,2,1,0:T(8,128)(2,1)} %get-tuple-element.46.grad_ref, bf16[2,512,128]{2,1,0:T(8,128)(2,1)} %copy-done.6, bf16[2,512,128]{2,1,0:T(8,128)(2,1)} %copy-done.7, ...), custom_call_target="tpu_custom_call" | custom-call | flops 5000000000 | bytes 8000000 | tf_op jit(solution)/shard_map/fine_level/pallas_call | solution.py:237
  32.0 1.6 %coarse_grad.1 = (bf16[2,256,256]{2,1,0:T(8,128)(2,1)S(1)}, bf16[2,256,256]{2,1,0:T(8,128)(2,1)S(1)}) custom-call(s32[1]{0:T(128)} %bitcast.place_ref, f32[2,2,256,256]{3,2,1,0:T(8,128)} %get-tuple-element.53.pooled_ref, bf16[8,2,2,2,32,256]{5,4,3,2,1,0:T(8,128)(2,1)S(1)} %all-to-all-done.pre_ref.input_ref), custom_call_target="tpu_custom_call" | custom-call | flops 20000000 | bytes 2000000 | tf_op jit(solution)/shard_map/coarse_grad/pallas_call | solution.py:277
  33.7 5.0 %collective-permute-start.3 = (bf16[2,256,256]{2,1,0:T(8,128)(2,1)S(1)}, bf16[2,256,256]{2,1,0:T(8,128)(2,1)S(1)}, u32[]{:S(2)}, u32[]{:S(2)}) collective-permute-start(bf16[2,256,256]{2,1,0:T(8,128)(2,1)S(1)} %get-tuple-element.59.far_ref.second_ref), channel_id=1, source_target_pairs={{1,2},{3,4},{5,6},{7,8},{9,10},{11,12},{13,14},{15,16},{17,18},{19... | collective-permute-start | bytes 786440 | tf_op jit(solution)/shard_map/ppermute | solution.py:703
  38.7 1.8 %own_weight_level.1.own_ref = f32[3,256,768]{2,1,0:T(8,128)S(1)} custom-call(s32[1]{0:T(128)} %bitcast.place_ref, bf16[8,2,2,2,32,256]{5,4,3,2,1,0:T(8,128)(2,1)S(1)} %all-to-all-done.pre_ref.input_ref, bf16[2,256,256]{2,1,0:T(8,128)(2,1)S(1)} %get-tuple-element.59.far_ref.second_ref, bf16[2,256,256]{2,1,0:T(8,128)(2,1)S(1)} %get-tuple-element.58.near_ref.third_ref), custom_call_target="tpu_custom_call" | custom-call | flops 900000000 | bytes 4000000 | tf_op jit(solution)/shard_map/own_weight_level/pallas_call | solution.py:400
  40.5 1.3 %up_level.1 = (bf16[9,12,16,128]{3,2,1,0:T(8,128)(2,1)S(1)}, bf16[9,12,16,128]{3,2,1,0:T(8,128)(2,1)S(1)}) custom-call(s32[1]{0:T(128)} %bitcast.place_ref, bf16[8,2,2,2,32,256]{5,4,3,2,1,0:T(8,128)(2,1)S(1)} %all-to-all-done.pre_ref.input_ref, bf16[2,256,1152]{2,1,0:T(8,128)(2,1)S(1)} %copy-done.1, bf16[2,256,384]{2,1,0:T(8,128)(2,1)S(1)} %copy-done.2, ...), custom_call_target="tpu_custom_call" | custom-call | flops 1000000000 | bytes 5000000 | tf_op jit(solution)/shard_map/up_level/pallas_call | solution.py:341
  41.8 6.3 %collective-permute-done.3.first_ref.from_far_ref = bf16[2,256,256]{2,1,0:T(8,128)(2,1)S(1)} collective-permute-done((bf16[2,256,256]{2,1,0:T(8,128)(2,1)S(1)}, bf16[2,256,256]{2,1,0:T(8,128)(2,1)S(1)}, u32[]{:S(2)}, u32[]{:S(2)}) %collective-permute-start.3) | collective-permute-done | bytes 262176 | tf_op jit(solution)/shard_map/ppermute | solution.py:703
  50.0 1.2 %coarse_weight_level.2.coarse_ref = bf16[144,16,128]{2,1,0:T(8,128)(2,1)S(1)} custom-call(s32[1]{0:T(128)} %bitcast.place_ref, bf16[8,2,2,2,32,256]{5,4,3,2,1,0:T(8,128)(2,1)S(1)} %all-to-all-done.pre_ref.input_ref, bf16[2,256,256]{2,1,0:T(8,128)(2,1)S(1)} %collective-permute-done.3.first_ref.from_far_ref, ...), custom_call_target="tpu_custom_call" | custom-call | flops 400000000 | bytes 2000000 | tf_op jit(solution)/shard_map/coarse_weight_level/pallas_call | solution.py:455
  53.3 9.9 %all-to-all-start.1 = ((bf16[64,4,16,128]{3,2,1,0:T(8,128)(2,1)}), bf16[64,4,16,128]{3,2,1,0:T(8,128)(2,1)S(1)}, u32[]{:S(2)}, u32[]{:S(2)}) async-start(bf16[64,4,16,128]{3,2,1,0:T(8,128)(2,1)} %bitcast.7), calls=%async_computation.1 | async-start | bytes 2097152 | tf_op jit(solution)/shard_map/all_to_all | solution.py:608
  63.2 2.9 %coarse_input_level.1 = (bf16[2,2,32,256]{3,2,1,0:T(8,128)(2,1)S(1)}, bf16[2,2,32,256]{3,2,1,0:T(8,128)(2,1)}, bf16[2,2,32,256]{3,2,1,0:T(8,128)(2,1)}, bf16[2,2...) custom-call(s32[1]{0:T(128)} %bitcast.3.chan_ref, ...), custom_call_target="tpu_custom_call" | custom-call | flops 1300000000 | bytes 3000000 | tf_op jit(solution)/shard_map/coarse_input_level/pallas_call | solution.py:501
  69.4 2.5 %collective-permute-start.7 = (bf16[2,2,32,256]{3,2,1,0:T(8,128)(2,1)S(1)}, bf16[2,2,32,256]{3,2,1,0:T(8,128)(2,1)S(1)}, u32[]{:S(2)}, u32[]{:S(2)}) collective-permute-start(bf16[2,2,32,256]{3,2,1,0:T(8,128)(2,1)S(1)} %get-tuple-element.72), channel_id=1, source_target_pairs={{0,4},{1,5},{2,6},{3,7},{4,0},{5,1},{6,2},{7,3},{8,12},{9,13},{10,... | collective-permute-start | bytes 196616 | tf_op jit(solution)/shard_map/ppermute | solution.py:747
  73.2 6.5 %all-to-all-done.1.parts_ref = bf16[64,4,16,128]{3,2,1,0:T(8,128)(2,1)S(1)} async-done(((bf16[64,4,16,128]{3,2,1,0:T(8,128)(2,1)}), bf16[64,4,16,128]{3,2,1,0:T(8,128)(2,1)S(1)}, u32[]{:S(2)}, u32[]{:S(2)}) %all-to-all-start.1) | async-done | bytes 1048608 | tf_op jit(solution)/shard_map/all_to_all | solution.py:608
  80.9 6.0 %all-to-all-start.2 = ((bf16[64,4,16,128]{3,2,1,0:T(8,128)(2,1)}), bf16[64,4,16,128]{3,2,1,0:T(8,128)(2,1)S(1)}, u32[]{:S(2)}, u32[]{:S(2)}) async-start(bf16[64,4,16,128]{3,2,1,0:T(8,128)(2,1)} %sum_parts.1), calls=%async_computation.2 | async-start | bytes 2097152 | tf_op jit(solution)/shard_map/all_to_all | solution.py:616
  87.0 2.3 %collective-permute-start.9 = (bf16[2,2,32,256]{3,2,1,0:T(8,128)(2,1)S(1)}, bf16[2,2,32,256]{3,2,1,0:T(8,128)(2,1)S(1)}, u32[]{:S(2)}, u32[]{:S(2)}) collective-permute-start(bf16[2,2,32,256]{3,2,1,0:T(8,128)(2,1)S(1)} %get-tuple-element.76), channel_id=1, source_target_pairs={{0,6},{1,7},{2,4},{3,5},{4,2},{5,3},{6,0},{7,1},{8,14},{9,15},{10,... | collective-permute-start | bytes 196616 | tf_op jit(solution)/shard_map/ppermute | solution.py:747
  90.5 11.4 %all-to-all-done.2 = bf16[64,4,16,128]{3,2,1,0:T(8,128)(2,1)S(1)} async-done(((bf16[64,4,16,128]{3,2,1,0:T(8,128)(2,1)}), bf16[64,4,16,128]{3,2,1,0:T(8,128)(2,1)S(1)}, u32[]{:S(2)}, u32[]{:S(2)}) %all-to-all-start.2) | async-done | bytes 1048608 | tf_op jit(solution)/shard_map/all_to_all | solution.py:616
  102.0 4.9 %collective-permute-start.13 = (bf16[256,16,128]{2,1,0:T(8,128)(2,1)S(1)}, bf16[256,16,128]{2,1,0:T(8,128)(2,1)S(1)}, u32[]{:S(2)}, u32[]{:S(2)}) collective-permute-start(bf16[256,16,128]{2,1,0:T(8,128)(2,1)S(1)} %bitcast.12), channel_id=1, source_target_pairs={{0,8},{8,0},{1,9},{9,1},{2,10},{10,2},{3,11},{11,3},{4,12},{12,4},... | collective-permute-start | bytes 3145736 | tf_op jit(solution)/shard_map/ppermute | solution.py:756
  107.7 1.5 %unpack.2 = (f32[9,384,128]{2,1,0:T(8,128)}, f32[9,256,256]{2,1,0:T(8,128)}) custom-call(s32[1]{0:T(128)} %bitcast.place_ref, bf16[256,16,128]{2,1,0:T(8,128)(2,1)S(1)} %bitcast.13), custom_call_target="tpu_custom_call" | custom-call | flops 1 | bytes 1 | tf_op jit(solution)/shard_map/unpack/pallas_call | solution.py:622
  109.2 1.5 %unpack.3 = (f32[9,384,128]{2,1,0:T(8,128)}, f32[9,256,256]{2,1,0:T(8,128)}) custom-call(s32[1]{0:T(128)} %bitcast.4.place_ref, bf16[256,16,128]{2,1,0:T(8,128)(2,1)S(1)} %collective-permute-done.13.parts_ref, f32[9,384,128]{2,1,0:T(8,128)} %get-tuple-element.84.rest_0_, ...), custom_call_target="tpu_custom_call", output_to_operand_aliasing={{0}: (2, {}), {1}: (3, {})} | custom-call | flops 1 | bytes 1 | tf_op jit(solution)/shard_map/unpack/pallas_call | solution.py:622
  (42 shorter events, 13.0 us)
Async XLA Ops:
  4.0 15.4 %collective-permute-start = (bf16[2,512,128]{2,1,0:T(8,128)(2,1)S(1)}, bf16[2,512,128]{2,1,0:T(8,128)(2,1)S(1)}, u32[]{:S(2)}, u32[]{:S(2)}) collective-permute-start(bf16[2,512,128]{2,1,0:T(8,128)(2,1)S(1)} %get-tuple-element.47), channel_id=1, source_target_pairs={{0,1},{1,0},{2,3},{3,2},{4,5},{5,4},{6,7},{7,6},{8,9},{9,8},{10,11... | collective-permute-start | bytes 786440 | tf_op jit(solution)/shard_map/ppermute | solution.py:703
  6.1 15.5 %collective-permute-start.1 = (bf16[2,512,128]{2,1,0:T(8,128)(2,1)S(1)}, bf16[2,512,128]{2,1,0:T(8,128)(2,1)S(1)}, u32[]{:S(2)}, u32[]{:S(2)}) collective-permute-start(bf16[2,512,128]{2,1,0:T(8,128)(2,1)S(1)} %get-tuple-element.48), channel_id=1, source_target_pairs={{1,2},{3,4},{5,6},{7,8},{9,10},{11,12},{13,14},{15,16},{17,18},{19... | collective-permute-start | bytes 786440 | tf_op jit(solution)/shard_map/ppermute | solution.py:703
  11.5 20.5 %all-to-all-start = ((bf16[8,2,2,2,32,256]{5,4,3,2,1,0:T(8,128)(2,1)}), bf16[8,2,2,2,32,256]{5,4,3,2,1,0:T(8,128)(2,1)S(1)}, u32[]{:S(2)}, u32[]{:S(2)}) async-start(bf16[8,2,2,2,32,256]{5,4,3,2,1,0:T(8,128)(2,1)} %get-tuple-element.54), calls=%async_computation | async-start | bytes 2097152 | tf_op jit(solution)/shard_map/all_to_all | solution.py:723
  19.4 2.2 %copy-start.6 = (bf16[2,512,128]{2,1,0:T(8,128)(2,1)}, bf16[2,512,128]{2,1,0:T(8,128)(2,1)S(1)}, u32[]{:S(2)}) copy-start(bf16[2,512,128]{2,1,0:T(8,128)(2,1)S(1)} %collective-permute-done.near_ref) | copy-start | bytes 786436
  21.6 0.7 copy-start.7
  33.6 8.2 %collective-permute-start.2 = (bf16[2,256,256]{2,1,0:T(8,128)(2,1)S(1)}, bf16[2,256,256]{2,1,0:T(8,128)(2,1)S(1)}, u32[]{:S(2)}, u32[]{:S(2)}) collective-permute-start(bf16[2,256,256]{2,1,0:T(8,128)(2,1)S(1)} %get-tuple-element.58.near_ref.third_ref), channel_id=1, source_target_pairs={{0,1},{1,0},{2,3},{3,2},{4,5},{5,4},{6,7},{7,6},{8,9},{9,8},{10,11... | collective-permute-start | bytes 786440 | tf_op jit(solution)/shard_map/ppermute | solution.py:703
  33.7 14.4 %collective-permute-start.3 = (bf16[2,256,256]{2,1,0:T(8,128)(2,1)S(1)}, bf16[2,256,256]{2,1,0:T(8,128)(2,1)S(1)}, u32[]{:S(2)}, u32[]{:S(2)}) collective-permute-start(bf16[2,256,256]{2,1,0:T(8,128)(2,1)S(1)} %get-tuple-element.59.far_ref.second_ref), channel_id=1, source_target_pairs={{1,2},{3,4},{5,6},{7,8},{9,10},{11,12},{13,14},{15,16},{17,18},{19... | collective-permute-start | bytes 786440 | tf_op jit(solution)/shard_map/ppermute | solution.py:703
  38.7 1.8 %copy-start.1 = (bf16[2,256,1152]{2,1,0:T(8,128)(2,1)S(1)}, bf16[2,256,1152]{2,1,0:T(8,128)(2,1)}, u32[]{:S(2)}) copy-start(bf16[2,256,1152]{2,1,0:T(8,128)(2,1)} %get-tuple-element.60.box_ref) | copy-start | bytes 3538948
  38.7 1.8 %copy-start.2 = (bf16[2,256,384]{2,1,0:T(8,128)(2,1)S(1)}, bf16[2,256,384]{2,1,0:T(8,128)(2,1)}, u32[]{:S(2)}) copy-start(bf16[2,256,384]{2,1,0:T(8,128)(2,1)} %get-tuple-element.61.box_low_ref) | copy-start | bytes 1179652
  38.7 1.8 %copy-start.3 = (bf16[2,256,384]{2,1,0:T(8,128)(2,1)S(1)}, bf16[2,256,384]{2,1,0:T(8,128)(2,1)}, u32[]{:S(2)}) copy-start(bf16[2,256,384]{2,1,0:T(8,128)(2,1)} %get-tuple-element.62.box_high_ref) | copy-start | bytes 1179652
  49.4 2.7 %collective-permute-start.11 = (bf16[144,16,128]{2,1,0:T(8,128)(2,1)S(1)}, bf16[144,16,128]{2,1,0:T(8,128)(2,1)S(1)}, u32[]{:S(2)}, u32[]{:S(2)}) collective-permute-start(bf16[144,16,128]{2,1,0:T(8,128)(2,1)S(1)} %coarse_weight_level.3), channel_id=1, source_target_pairs={{0,8},{8,0},{1,9},{9,1},{2,10},{10,2},{3,11},{11,3},{4,12},{12,4},... | collective-permute-start | bytes 1769480 | tf_op jit(solution)/shard_map/ppermute | solution.py:742
  49.5 2.6 %collective-permute-start.12 = (bf16[9,12,16,128]{3,2,1,0:T(8,128)(2,1)S(1)}, bf16[9,12,16,128]{3,2,1,0:T(8,128)(2,1)S(1)}, u32[]{:S(2)}, u32[]{:S(2)}) collective-permute-start(bf16[9,12,16,128]{3,2,1,0:T(8,128)(2,1)S(1)} %get-tuple-element.80), channel_id=1, source_target_pairs={{0,8},{8,0},{1,9},{9,1},{2,10},{10,2},{3,11},{11,3},{4,12},{12,4},... | collective-permute-start | bytes 1327112 | tf_op jit(solution)/shard_map/ppermute | solution.py:736
  53.3 9.9 %copy-start = (bf16[3,3,256,256]{3,2,1,0:T(8,128)(2,1)S(1)}, bf16[3,3,256,256]{3,2,1,0:T(8,128)(2,1)}, u32[]{:S(2)}) copy-start(bf16[3,3,256,256]{3,2,1,0:T(8,128)(2,1)} %weight_ref.5) | copy-start | bytes 3538948
  53.3 26.3 %all-to-all-start.1 = ((bf16[64,4,16,128]{3,2,1,0:T(8,128)(2,1)}), bf16[64,4,16,128]{3,2,1,0:T(8,128)(2,1)S(1)}, u32[]{:S(2)}, u32[]{:S(2)}) async-start(bf16[64,4,16,128]{3,2,1,0:T(8,128)(2,1)} %bitcast.7), calls=%async_computation.1 | async-start | bytes 2097152 | tf_op jit(solution)/shard_map/all_to_all | solution.py:608
  66.8 20.1 %collective-permute-start.4 = (bf16[2,2,32,256]{3,2,1,0:T(8,128)(2,1)}, bf16[2,2,32,256]{3,2,1,0:T(8,128)(2,1)S(1)}, u32[]{:S(2)}, u32[]{:S(2)}) collective-permute-start(bf16[2,2,32,256]{3,2,1,0:T(8,128)(2,1)} %get-tuple-element.69), channel_id=1, source_target_pairs={{0,1},{1,0},{2,3},{3,2},{4,5},{5,4},{6,7},{7,6},{8,9},{9,8},{10,11... | collective-permute-start | bytes 196616 | tf_op jit(solution)/shard_map/ppermute | solution.py:747
  67.8 19.1 %collective-permute-start.5 = (bf16[2,2,32,256]{3,2,1,0:T(8,128)(2,1)}, bf16[2,2,32,256]{3,2,1,0:T(8,128)(2,1)S(1)}, u32[]{:S(2)}, u32[]{:S(2)}) collective-permute-start(bf16[2,2,32,256]{3,2,1,0:T(8,128)(2,1)} %get-tuple-element.70), channel_id=1, source_target_pairs={{0,2},{1,3},{2,0},{3,1},{4,6},{5,7},{6,4},{7,5},{8,10},{9,11},{10,... | collective-permute-start | bytes 196616 | tf_op jit(solution)/shard_map/ppermute | solution.py:747
  69.0 18.0 %collective-permute-start.6 = (bf16[2,2,32,256]{3,2,1,0:T(8,128)(2,1)}, bf16[2,2,32,256]{3,2,1,0:T(8,128)(2,1)S(1)}, u32[]{:S(2)}, u32[]{:S(2)}) collective-permute-start(bf16[2,2,32,256]{3,2,1,0:T(8,128)(2,1)} %get-tuple-element.71), channel_id=1, source_target_pairs={{0,3},{1,2},{2,1},{3,0},{4,7},{5,6},{6,5},{7,4},{8,11},{9,10},{10,... | collective-permute-start | bytes 196616 | tf_op jit(solution)/shard_map/ppermute | solution.py:747
  69.4 17.5 %collective-permute-start.7 = (bf16[2,2,32,256]{3,2,1,0:T(8,128)(2,1)S(1)}, bf16[2,2,32,256]{3,2,1,0:T(8,128)(2,1)S(1)}, u32[]{:S(2)}, u32[]{:S(2)}) collective-permute-start(bf16[2,2,32,256]{3,2,1,0:T(8,128)(2,1)S(1)} %get-tuple-element.72), channel_id=1, source_target_pairs={{0,4},{1,5},{2,6},{3,7},{4,0},{5,1},{6,2},{7,3},{8,12},{9,13},{10,... | collective-permute-start | bytes 196616 | tf_op jit(solution)/shard_map/ppermute | solution.py:747
  72.0 15.0 %copy-start.5 = (bf16[2,2,32,256]{3,2,1,0:T(8,128)(2,1)S(1)}, bf16[2,2,32,256]{3,2,1,0:T(8,128)(2,1)}, u32[]{:S(2)}) copy-start(bf16[2,2,32,256]{3,2,1,0:T(8,128)(2,1)} %copy-done.4) | copy-start | bytes 196612
  72.0 15.0 %collective-permute-start.8 = (bf16[2,2,32,256]{3,2,1,0:T(8,128)(2,1)S(1)}, bf16[2,2,32,256]{3,2,1,0:T(8,128)(2,1)S(1)}, u32[]{:S(2)}, u32[]{:S(2)}) collective-permute-start(bf16[2,2,32,256]{3,2,1,0:T(8,128)(2,1)S(1)} %get-tuple-element.73), channel_id=1, source_target_pairs={{0,5},{1,4},{2,7},{3,6},{4,1},{5,0},{6,3},{7,2},{8,13},{9,12},{10,... | collective-permute-start | bytes 196616 | tf_op jit(solution)/shard_map/ppermute | solution.py:747
  80.9 21.1 %all-to-all-start.2 = ((bf16[64,4,16,128]{3,2,1,0:T(8,128)(2,1)}), bf16[64,4,16,128]{3,2,1,0:T(8,128)(2,1)S(1)}, u32[]{:S(2)}, u32[]{:S(2)}) async-start(bf16[64,4,16,128]{3,2,1,0:T(8,128)(2,1)} %sum_parts.1), calls=%async_computation.2 | async-start | bytes 2097152 | tf_op jit(solution)/shard_map/all_to_all | solution.py:616
  87.0 19.8 %collective-permute-start.9 = (bf16[2,2,32,256]{3,2,1,0:T(8,128)(2,1)S(1)}, bf16[2,2,32,256]{3,2,1,0:T(8,128)(2,1)S(1)}, u32[]{:S(2)}, u32[]{:S(2)}) collective-permute-start(bf16[2,2,32,256]{3,2,1,0:T(8,128)(2,1)S(1)} %get-tuple-element.76), channel_id=1, source_target_pairs={{0,6},{1,7},{2,4},{3,5},{4,2},{5,3},{6,0},{7,1},{8,14},{9,15},{10,... | collective-permute-start | bytes 196616 | tf_op jit(solution)/shard_map/ppermute | solution.py:747
  89.3 17.5 %collective-permute-start.10 = (bf16[2,2,32,256]{3,2,1,0:T(8,128)(2,1)S(1)}, bf16[2,2,32,256]{3,2,1,0:T(8,128)(2,1)S(1)}, u32[]{:S(2)}, u32[]{:S(2)}) collective-permute-start(bf16[2,2,32,256]{3,2,1,0:T(8,128)(2,1)S(1)} %get-tuple-element.77), channel_id=1, source_target_pairs={{0,7},{1,6},{2,5},{3,4},{4,3},{5,2},{6,1},{7,0},{8,15},{9,14},{10,... | collective-permute-start | bytes 196616 | tf_op jit(solution)/shard_map/ppermute | solution.py:747
  102.0 7.3 %collective-permute-start.13 = (bf16[256,16,128]{2,1,0:T(8,128)(2,1)S(1)}, bf16[256,16,128]{2,1,0:T(8,128)(2,1)S(1)}, u32[]{:S(2)}, u32[]{:S(2)}) collective-permute-start(bf16[256,16,128]{2,1,0:T(8,128)(2,1)S(1)} %bitcast.12), channel_id=1, source_target_pairs={{0,8},{8,0},{1,9},{9,1},{2,10},{10,2},{3,11},{11,3},{4,12},{12,4},... | collective-permute-start | bytes 3145736 | tf_op jit(solution)/shard_map/ppermute | solution.py:756
  (1 other events, 0.6 us)

commit v5 on v4

--- a/solution.py
+++ b/solution.py
@@ -409,7 +409,7 @@
         out_shape=jax.ShapeDtypeStruct((3, c4, 3 * c4), F32),
         scratch_shapes=[pltpu.VMEM((2 * wide, 3 * c4), BF16)],
         compiler_params=params(VMEM),
-        cost_estimate=cost(9e8, 4e6),
+        cost_estimate=cost(LONG, 4e6),
         name="own_weight_level",
     )(place, received, far, near)
 
@@ -536,14 +536,43 @@
     )(chan, *pieces, *earlier)
 
 
-def join_kernel(coarse_ref, coarse_more_ref, fine_ref, fine_more_ref, out_ref):
-    count = coarse_ref.shape[0]
-    out_ref[:count] = (coarse_ref[...].astype(F32) + coarse_more_ref[...].astype(F32)).astype(BF16)
-    fines = fine_ref.shape[0]
-    out_ref[count : count + fines] = (fine_ref[...].astype(F32) + fine_more_ref[...].astype(F32)).astype(BF16)
-    rest = out_ref.shape[0] - count - fines
-    if rest:
-        out_ref[count + fines :] = jnp.zeros((rest,) + out_ref.shape[1:], BF16)
+def join_kernel(first, *refs):
+    *part_refs, out_ref, stage, sems = refs
+    one, more = part_refs[:2]
+    count = one.shape[0]
+    copies = []
+    for at in range(0, stage.shape[0], 36):
+        size = min(36, stage.shape[0] - at)
+        held = max(min(size, count - at), 0)
+        if held:
+            lines = slice(at, at + held)
+            stage[lines] = (one[lines].astype(F32) + more[lines].astype(F32)).astype(BF16)
+        if held < size:
+            stage[at + held : at + size] = jnp.zeros((size - held,) + stage.shape[1:], BF16)
+        copies.append(
+            pltpu.make_async_copy(
+                stage.at[pl.ds(at, size)], out_ref.at[pl.ds(first + at, size)], sems.at[len(copies)]
+            )
+        )
+        copies[-1].start()
+    for copy in copies:
+        copy.wait()
+
+
+def joined(one, more, first, size, total, earlier=()):
+    hbm = pl.BlockSpec(memory_space=pltpu.HBM)
+    vmem = pl.BlockSpec(memory_space=pltpu.VMEM)
+    return pl.pallas_call(
+        functools.partial(join_kernel, first),
+        in_specs=[vmem, vmem] + [hbm] * len(earlier),
+        out_specs=hbm,
+        out_shape=jax.ShapeDtypeStruct((total, 16, 128), BF16),
+        input_output_aliases={2: 0} if earlier else {},
+        scratch_shapes=[pltpu.VMEM((size, 16, 128), BF16), pltpu.SemaphoreType.DMA((-(-size // 36),))],
+        compiler_params=params(VMEM),
+        cost_estimate=cost(1e6, 2e6),
+        name="join",
+    )(one, more, *earlier)
 
 
 def sum_kernel(parts_ref, out_ref):
@@ -591,21 +620,9 @@
 SWAP = ((0, 1), (1, 0))
 
 
-def grad_sums(fine_keep, fine_more, coarse_keep, coarse_more):
-    chips = 1
-    for axis in CHIPS:
-        chips *= lax.axis_size(axis)
-    fine_keep, fine_more = (a.reshape((-1, 16, 128)) for a in (fine_keep, fine_more))
-    count = coarse_keep.shape[0] + fine_keep.shape[0]
-    each = -(-count // chips)
-    joined = pl.pallas_call(
-        join_kernel,
-        out_shape=jax.ShapeDtypeStruct((chips * each, 16, 128), BF16),
-        compiler_params=params(VMEM),
-        cost_estimate=cost(1e6, 3e6),
-        name="join",
-    )(coarse_keep, coarse_more, fine_keep, fine_more)
-    parts = lax.all_to_all(joined.reshape(chips, each, 16, 128), CHIPS, 0, 0, tiled=True)
+def grad_sums(parts, chips):
+    each = parts.shape[0] // chips
+    parts = lax.all_to_all(parts.reshape(chips, each, 16, 128), CHIPS, 0, 0, tiled=True)
     summed = pl.pallas_call(
         sum_kernel,
         out_shape=jax.ShapeDtypeStruct((chips, each, 16, 128), BF16),
@@ -735,7 +752,12 @@
     fine_keep, fine_send = up_level(place, received, box, box_low, box_high, skip_keep, skip_send, fine_cells)
     fine_more = lax.ppermute(fine_send, "core", SWAP)
     own_terms = own_weight_level(place, received, far, near)
-    from_near, from_far, fine_keep, own_terms = lax.optimization_barrier((from_near, from_far, fine_keep, own_terms))
+    chips = devices // lax.axis_size("core")
+    fine_keep, fine_more = (a.reshape((-1, 16, 128)) for a in (fine_keep, fine_more))
+    coarse_count = 9 * (fine_weight.shape[2] - cs) ** 2 // (2 * 16 * 128)
+    total = -(-(coarse_count + fine_keep.shape[0]) // chips) * chips
+    sums = joined(fine_keep, fine_more, coarse_count, total - coarse_count, total)
+    from_near, from_far, sums, own_terms = lax.optimization_barrier((from_near, from_far, sums, own_terms))
     rows = (from_far, far, near, from_near)
     coarse_cells = samples * (lines // peers) * wide * devices
     coarse_send = coarse_weight_level(other_place, received, from_far, from_near, own_terms, coarse_cells)
@@ -746,7 +768,8 @@
     def home(k, piece):
         return lax.ppermute(piece, CHAN, [(i, i ^ k) for i in range(peers)])
 
-    mine = grad_sums(fine_keep, fine_more, coarse_keep, coarse_more)
+    sums = joined(coarse_keep, coarse_more, 0, coarse_count, total, (sums,))
+    mine = grad_sums(sums, chips)
     early = [back[0]] + [home(k, back[k]) for k in range(1, EARLY)]
     grad_input = placed(chan, early, 0, peers, flops=LONG)
     grad_input, *late = lax.optimization_barrier((grad_input, *back[EARLY:]))

time: 111 us -> 111 us (level)
  waiting for transfers between devices: 27.8 us -> 25.9 us
    ppermute x4, waiting for transfers between devices: 8.5 us -> 6.69 us  [swapped(): return (lax.ppermute(near, ALL, inside), lax.ppermute(far, ALL, outside))]
    unnamed x16 -> x20, local copies, waits for them, and re-layouts: 1.35 us -> 2.25 us
  transfers between devices with their start and end apart: 17 -> 17, of which waited for: 6 -> 6; matrix products, arithmetic and copies ran while one was open for 0% -> 0% of each run, Pallas kernels for 22% -> 23%
where the time goes in v5:
time: 111 us; the launch traced here: 110 us
  starting transfers between devices  47 us (42%)
  Pallas kernels  33.8 us (30%)
  waiting for transfers between devices  25.9 us (23%)
  local copies, waits for them, and re-layouts  2.25 us (2%)
    ppermute x4, starting transfers between devices, swapped(): return (lax.ppermute(near, ALL, inside), lax.ppermute(far, ALL, outside))  12.6 us
    all_to_all x1, waiting for transfers between devices, grad_sums(): lax.all_to_all(summed, CHIPS, 0, 0, tiled=True)  11.4 us
    all_to_all x1, starting transfers between devices, grad_sums(): lax.all_to_all(parts.reshape(chips, each, 16, 128), CHIPS, 0, 0, tiled=True)  9.89 us
    ppermute x7, starting transfers between devices, home(): return lax.ppermute(piece, CHAN, [(i, i ^ k) for i in range(peers)])  9.84 us
    ppermute x4, waiting for transfers between devices, swapped(): return (lax.ppermute(near, ALL, inside), lax.ppermute(far, ALL, outside))  6.69 us
    pallas_call x1, Pallas kernels, fine_level(): pl.pallas_call(functools.partial(fine_kernel, scale=1.0 / math.sqrt(fine_...  6.59 us
    all_to_all x1, waiting for transfers between devices, grad_sums(): lax.all_to_all(parts.reshape(chips, each, 16, 128), CHIPS, 0, 0, tiled=True)  6.5 us
    all_to_all x1, starting transfers between devices, grad_sums(): lax.all_to_all(summed, CHIPS, 0, 0, tiled=True)  6.05 us
  transfers between devices with their start and end apart: 17, of which 6 were waited for; matrix products, arithmetic and copies ran while one was open for 0% of the time, Pallas kernels for 23%

profile of v5, /device:TPU:1, one launch (start us, length us, event | category | flops | bytes accessed | tf_op | source)
XLA Modules:
  0.0 110.0 jit_solution(13313254581913147307)
XLA Ops:
  0.6 3.3 %start.1 = (bf16[8,2,2,2,32,256]{5,4,3,2,1,0:T(8,128)(2,1)}, bf16[2,512,128]{2,1,0:T(8,128)(2,1)S(1)}, bf16[2,512,128]{2,1,0:T(8,128)(2,1)S(1)}) custom-call(s32[1]{0:T(128)} %bitcast.place_ref, bf16[2,16,32,256]{3,2,1,0:T(8,128)(2,1)} %bitcast.18, bf16[2,16,32,256]{3,2,1,0:T(8,128)(2,1)} %bitcast.19, bf16[2,4,512,128]{3,2,1,0:T(8,128)(2,1)} %cot_ref.3, ...), custom_call_target="tpu_custom_call" | custom-call | flops 10000000 | bytes 3000000 | tf_op jit(solution)/shard_map/start/pallas_call | solution.py:697
  4.0 2.1 %collective-permute-start = (bf16[2,512,128]{2,1,0:T(8,128)(2,1)S(1)}, bf16[2,512,128]{2,1,0:T(8,128)(2,1)S(1)}, u32[]{:S(2)}, u32[]{:S(2)}) collective-permute-start(bf16[2,512,128]{2,1,0:T(8,128)(2,1)S(1)} %get-tuple-element.47), channel_id=1, source_target_pairs={{0,1},{1,0},{2,3},{3,2},{4,5},{5,4},{6,7},{7,6},{8,9},{9,8},{10,11... | collective-permute-start | bytes 786440 | tf_op jit(solution)/shard_map/ppermute | solution.py:720
  6.1 5.4 %collective-permute-start.1 = (bf16[2,512,128]{2,1,0:T(8,128)(2,1)S(1)}, bf16[2,512,128]{2,1,0:T(8,128)(2,1)S(1)}, u32[]{:S(2)}, u32[]{:S(2)}) collective-permute-start(bf16[2,512,128]{2,1,0:T(8,128)(2,1)S(1)} %get-tuple-element.48), channel_id=1, source_target_pairs={{1,2},{3,4},{5,6},{7,8},{9,10},{11,12},{13,14},{15,16},{17,18},{19... | collective-permute-start | bytes 786440 | tf_op jit(solution)/shard_map/ppermute | solution.py:720
  11.5 3.6 %all-to-all-start = ((bf16[8,2,2,2,32,256]{5,4,3,2,1,0:T(8,128)(2,1)}), bf16[8,2,2,2,32,256]{5,4,3,2,1,0:T(8,128)(2,1)S(1)}, u32[]{:S(2)}, u32[]{:S(2)}) async-start(bf16[8,2,2,2,32,256]{5,4,3,2,1,0:T(8,128)(2,1)} %get-tuple-element.54), calls=%async_computation | async-start | bytes 2097152 | tf_op jit(solution)/shard_map/all_to_all | solution.py:740
  15.1 4.3 %box_level.1 = (bf16[2,4,512,128]{3,2,1,0:T(8,128)(2,1)}, bf16[2,256,1152]{2,1,0:T(8,128)(2,1)}, bf16[2,2,512,128]{3,2,1,0:T(8,128)(2,1)S(1)}, f32[2,2,256,256]{3,2,1,0:T(8,128)S(1)}, bf16[1152,256]{1,0:T(8,128)(2,1)S(1)}) custom-call(bf16[2,4,512,128]{3,2,1,0:T(8,128)(2,1)} %cot_ref.3, bf16[2,4,512,128]{3,2,1,0:T(8,128)(2,1)} %fine_pre_ref.1, ...), custom_call_target="tpu_custom_call" | custom-call | flops 1200000000 | bytes 8000000 | tf_op jit(solution)/shard_map/box_level/pallas_call | solution.py:102
  19.4 2.2 %collective-permute-done.1.far_ref = bf16[2,512,128]{2,1,0:T(8,128)(2,1)S(1)} collective-permute-done((bf16[2,512,128]{2,1,0:T(8,128)(2,1)S(1)}, bf16[2,512,128]{2,1,0:T(8,128)(2,1)S(1)}, u32[]{:S(2)}, u32[]{:S(2)}) %collective-permute-start.1) | collective-permute-done | bytes 262176 | tf_op jit(solution)/shard_map/ppermute | solution.py:720
  22.3 2.7 %edge_level.1 = (f32[2,2,256,256]{3,2,1,0:T(8,128)}, bf16[2,256,384]{2,1,0:T(8,128)(2,1)}, bf16[2,256,384]{2,1,0:T(8,128)(2,1)}) custom-call(s32[1]{0:T(128)} %bitcast.place_ref, bf16[2,512,128]{2,1,0:T(8,128)(2,1)} %copy-done.8, bf16[2,512,128]{2,1,0:T(8,128)(2,1)} %copy-done.9, bf16[2,2,512,128]{3,2,1,0:T(8,128)(2,1)S(1)} %get-tuple-element.50.edge_ref, ...), custom_call_target="tpu_custom_call" | custom-call | flops 99999997952 | bytes 4000000 | tf_op jit(solution)/shard_map/edge_level/pallas_call | solution.py:154
  24.9 6.6 %fine_level.1 = (bf16[2,4,512,128]{3,2,1,0:T(8,128)(2,1)}, bf16[9,4,16,128]{3,2,1,0:T(8,128)(2,1)S(1)}, bf16[9,4,16,128]{3,2,1,0:T(8,128)(2,1)S(1)}) custom-call(s32[1]{0:T(128)} %bitcast.place_ref, bf16[2,4,512,128]{3,2,1,0:T(8,128)(2,1)} %get-tuple-element.46.grad_ref, bf16[2,512,128]{2,1,0:T(8,128)(2,1)} %copy-done.8, bf16[2,512,128]{2,1,0:T(8,128)(2,1)} %copy-done.9, ...), custom_call_target="tpu_custom_call" | custom-call | flops 5000000000 | bytes 8000000 | tf_op jit(solution)/shard_map/fine_level/pallas_call | solution.py:237
  32.0 1.7 %coarse_grad.1 = (bf16[2,256,256]{2,1,0:T(8,128)(2,1)S(1)}, bf16[2,256,256]{2,1,0:T(8,128)(2,1)S(1)}) custom-call(s32[1]{0:T(128)} %bitcast.place_ref, f32[2,2,256,256]{3,2,1,0:T(8,128)} %get-tuple-element.53.pooled_ref, bf16[8,2,2,2,32,256]{5,4,3,2,1,0:T(8,128)(2,1)S(1)} %all-to-all-done.pre_ref.input_ref), custom_call_target="tpu_custom_call" | custom-call | flops 20000000 | bytes 2000000 | tf_op jit(solution)/shard_map/coarse_grad/pallas_call | solution.py:277
  33.8 5.0 %collective-permute-start.3 = (bf16[2,256,256]{2,1,0:T(8,128)(2,1)S(1)}, bf16[2,256,256]{2,1,0:T(8,128)(2,1)S(1)}, u32[]{:S(2)}, u32[]{:S(2)}) collective-permute-start(bf16[2,256,256]{2,1,0:T(8,128)(2,1)S(1)} %get-tuple-element.59.far_ref.second_ref), channel_id=1, source_target_pairs={{1,2},{3,4},{5,6},{7,8},{9,10},{11,12},{13,14},{15,16},{17,18},{19... | collective-permute-start | bytes 786440 | tf_op jit(solution)/shard_map/ppermute | solution.py:720
  39.7 1.3 %up_level.1 = (bf16[9,12,16,128]{3,2,1,0:T(8,128)(2,1)S(1)}, bf16[9,12,16,128]{3,2,1,0:T(8,128)(2,1)S(1)}) custom-call(s32[1]{0:T(128)} %bitcast.place_ref, bf16[8,2,2,2,32,256]{5,4,3,2,1,0:T(8,128)(2,1)S(1)} %all-to-all-done.pre_ref.input_ref, bf16[2,256,1152]{2,1,0:T(8,128)(2,1)S(1)} %copy-done.1, bf16[2,256,384]{2,1,0:T(8,128)(2,1)S(1)} %copy-done.2, ...), custom_call_target="tpu_custom_call" | custom-call | flops 1000000000 | bytes 5000000 | tf_op jit(solution)/shard_map/up_level/pallas_call | solution.py:341
  41.1 1.8 %own_weight_level.1.own_ref = f32[3,256,768]{2,1,0:T(8,128)S(1)} custom-call(s32[1]{0:T(128)} %bitcast.place_ref, bf16[8,2,2,2,32,256]{5,4,3,2,1,0:T(8,128)(2,1)S(1)} %all-to-all-done.pre_ref.input_ref, bf16[2,256,256]{2,1,0:T(8,128)(2,1)S(1)} %get-tuple-element.59.far_ref.second_ref, bf16[2,256,256]{2,1,0:T(8,128)(2,1)S(1)} %get-tuple-element.58.near_ref.third_ref), custom_call_target="tpu_custom_call" | custom-call | flops 99999997952 | bytes 4000000 | tf_op jit(solution)/shard_map/own_weight_level/pallas_call | solution.py:400
  43.7 4.5 %collective-permute-done.3.first_ref.from_far_ref = bf16[2,256,256]{2,1,0:T(8,128)(2,1)S(1)} collective-permute-done((bf16[2,256,256]{2,1,0:T(8,128)(2,1)S(1)}, bf16[2,256,256]{2,1,0:T(8,128)(2,1)S(1)}, u32[]{:S(2)}, u32[]{:S(2)}) %collective-permute-start.3) | collective-permute-done | bytes 262176 | tf_op jit(solution)/shard_map/ppermute | solution.py:720
  49.6 1.3 %coarse_weight_level.2.refs_0_ = bf16[144,16,128]{2,1,0:T(8,128)(2,1)S(1)} custom-call(s32[1]{0:T(128)} %bitcast.place_ref, bf16[8,2,2,2,32,256]{5,4,3,2,1,0:T(8,128)(2,1)S(1)} %all-to-all-done.pre_ref.input_ref, bf16[2,256,256]{2,1,0:T(8,128)(2,1)S(1)} %collective-permute-done.3.first_ref.from_far_ref, ...), custom_call_target="tpu_custom_call" | custom-call | flops 400000000 | bytes 2000000 | tf_op jit(solution)/shard_map/coarse_weight_level/pallas_call | solution.py:455
  52.4 9.9 %all-to-all-start.1 = ((bf16[64,4,16,128]{3,2,1,0:T(8,128)(2,1)}), bf16[64,4,16,128]{3,2,1,0:T(8,128)(2,1)S(1)}, u32[]{:S(2)}, u32[]{:S(2)}) async-start(bf16[64,4,16,128]{3,2,1,0:T(8,128)(2,1)} %bitcast.7), calls=%async_computation.1 | async-start | bytes 2097152 | tf_op jit(solution)/shard_map/all_to_all | solution.py:625
  62.4 2.9 %coarse_input_level.1 = (bf16[2,2,32,256]{3,2,1,0:T(8,128)(2,1)S(1)}, bf16[2,2,32,256]{3,2,1,0:T(8,128)(2,1)}, bf16[2,2,32,256]{3,2,1,0:T(8,128)(2,1)}, bf16[2,2...) custom-call(s32[1]{0:T(128)} %bitcast.3.chan_ref, ...), custom_call_target="tpu_custom_call" | custom-call | flops 1300000000 | bytes 3000000 | tf_op jit(solution)/shard_map/coarse_input_level/pallas_call | solution.py:501
  68.6 2.5 %collective-permute-start.8 = (bf16[2,2,32,256]{3,2,1,0:T(8,128)(2,1)S(1)}, bf16[2,2,32,256]{3,2,1,0:T(8,128)(2,1)S(1)}, u32[]{:S(2)}, u32[]{:S(2)}) collective-permute-start(bf16[2,2,32,256]{3,2,1,0:T(8,128)(2,1)S(1)} %get-tuple-element.73), channel_id=1, source_target_pairs={{0,4},{1,5},{2,6},{3,7},{4,0},{5,1},{6,2},{7,3},{8,12},{9,13},{10,... | collective-permute-start | bytes 196616 | tf_op jit(solution)/shard_map/ppermute | solution.py:769
  72.3 6.5 %all-to-all-done.1.parts_ref = bf16[64,4,16,128]{3,2,1,0:T(8,128)(2,1)S(1)} async-done(((bf16[64,4,16,128]{3,2,1,0:T(8,128)(2,1)}), bf16[64,4,16,128]{3,2,1,0:T(8,128)(2,1)S(1)}, u32[]{:S(2)}, u32[]{:S(2)}) %all-to-all-start.1) | async-done | bytes 1048608 | tf_op jit(solution)/shard_map/all_to_all | solution.py:625
  80.0 6.0 %all-to-all-start.2 = ((bf16[64,4,16,128]{3,2,1,0:T(8,128)(2,1)}), bf16[64,4,16,128]{3,2,1,0:T(8,128)(2,1)S(1)}, u32[]{:S(2)}, u32[]{:S(2)}) async-start(bf16[64,4,16,128]{3,2,1,0:T(8,128)(2,1)} %sum_parts.1), calls=%async_computation.2 | async-start | bytes 2097152 | tf_op jit(solution)/shard_map/all_to_all | solution.py:633
  86.2 2.3 %collective-permute-start.10 = (bf16[2,2,32,256]{3,2,1,0:T(8,128)(2,1)S(1)}, bf16[2,2,32,256]{3,2,1,0:T(8,128)(2,1)S(1)}, u32[]{:S(2)}, u32[]{:S(2)}) collective-permute-start(bf16[2,2,32,256]{3,2,1,0:T(8,128)(2,1)S(1)} %get-tuple-element.77), channel_id=1, source_target_pairs={{0,6},{1,7},{2,4},{3,5},{4,2},{5,3},{6,0},{7,1},{8,14},{9,15},{10,... | collective-permute-start | bytes 196616 | tf_op jit(solution)/shard_map/ppermute | solution.py:769
  89.6 11.4 %all-to-all-done.2 = bf16[64,4,16,128]{3,2,1,0:T(8,128)(2,1)S(1)} async-done(((bf16[64,4,16,128]{3,2,1,0:T(8,128)(2,1)}), bf16[64,4,16,128]{3,2,1,0:T(8,128)(2,1)S(1)}, u32[]{:S(2)}, u32[]{:S(2)}) %all-to-all-start.2) | async-done | bytes 1048608 | tf_op jit(solution)/shard_map/all_to_all | solution.py:633
  101.1 4.9 %collective-permute-start.13 = (bf16[256,16,128]{2,1,0:T(8,128)(2,1)S(1)}, bf16[256,16,128]{2,1,0:T(8,128)(2,1)S(1)}, u32[]{:S(2)}, u32[]{:S(2)}) collective-permute-start(bf16[256,16,128]{2,1,0:T(8,128)(2,1)S(1)} %bitcast.12), channel_id=1, source_target_pairs={{0,8},{8,0},{1,9},{9,1},{2,10},{10,2},{3,11},{11,3},{4,12},{12,4},... | collective-permute-start | bytes 3145736 | tf_op jit(solution)/shard_map/ppermute | solution.py:779
  106.8 1.5 %unpack.2 = (f32[9,384,128]{2,1,0:T(8,128)}, f32[9,256,256]{2,1,0:T(8,128)}) custom-call(s32[1]{0:T(128)} %bitcast.place_ref, bf16[256,16,128]{2,1,0:T(8,128)(2,1)S(1)} %bitcast.13), custom_call_target="tpu_custom_call" | custom-call | flops 1 | bytes 1 | tf_op jit(solution)/shard_map/unpack/pallas_call | solution.py:639
  108.3 1.5 %unpack.3 = (f32[9,384,128]{2,1,0:T(8,128)}, f32[9,256,256]{2,1,0:T(8,128)}) custom-call(s32[1]{0:T(128)} %bitcast.6.place_ref, bf16[256,16,128]{2,1,0:T(8,128)(2,1)S(1)} %collective-permute-done.13.parts_ref, f32[9,384,128]{2,1,0:T(8,128)} %get-tuple-element.84.rest_0_, ...), custom_call_target="tpu_custom_call", output_to_operand_aliasing={{0}: (2, {}), {1}: (3, {})} | custom-call | flops 1 | bytes 1 | tf_op jit(solution)/shard_map/unpack/pallas_call | solution.py:639
  (47 shorter events, 13.8 us)
Async XLA Ops:
  4.0 15.4 %collective-permute-start = (bf16[2,512,128]{2,1,0:T(8,128)(2,1)S(1)}, bf16[2,512,128]{2,1,0:T(8,128)(2,1)S(1)}, u32[]{:S(2)}, u32[]{:S(2)}) collective-permute-start(bf16[2,512,128]{2,1,0:T(8,128)(2,1)S(1)} %get-tuple-element.47), channel_id=1, source_target_pairs={{0,1},{1,0},{2,3},{3,2},{4,5},{5,4},{6,7},{7,6},{8,9},{9,8},{10,11... | collective-permute-start | bytes 786440 | tf_op jit(solution)/shard_map/ppermute | solution.py:720
  6.1 15.5 %collective-permute-start.1 = (bf16[2,512,128]{2,1,0:T(8,128)(2,1)S(1)}, bf16[2,512,128]{2,1,0:T(8,128)(2,1)S(1)}, u32[]{:S(2)}, u32[]{:S(2)}) collective-permute-start(bf16[2,512,128]{2,1,0:T(8,128)(2,1)S(1)} %get-tuple-element.48), channel_id=1, source_target_pairs={{1,2},{3,4},{5,6},{7,8},{9,10},{11,12},{13,14},{15,16},{17,18},{19... | collective-permute-start | bytes 786440 | tf_op jit(solution)/shard_map/ppermute | solution.py:720
  11.5 20.5 %all-to-all-start = ((bf16[8,2,2,2,32,256]{5,4,3,2,1,0:T(8,128)(2,1)}), bf16[8,2,2,2,32,256]{5,4,3,2,1,0:T(8,128)(2,1)S(1)}, u32[]{:S(2)}, u32[]{:S(2)}) async-start(bf16[8,2,2,2,32,256]{5,4,3,2,1,0:T(8,128)(2,1)} %get-tuple-element.54), calls=%async_computation | async-start | bytes 2097152 | tf_op jit(solution)/shard_map/all_to_all | solution.py:740
  19.4 2.2 %copy-start.8 = (bf16[2,512,128]{2,1,0:T(8,128)(2,1)}, bf16[2,512,128]{2,1,0:T(8,128)(2,1)S(1)}, u32[]{:S(2)}) copy-start(bf16[2,512,128]{2,1,0:T(8,128)(2,1)S(1)} %collective-permute-done.near_ref) | copy-start | bytes 786436
  31.5 2.2 %copy-start.4 = (bf16[9,4,16,128]{3,2,1,0:T(8,128)(2,1)}, bf16[9,4,16,128]{3,2,1,0:T(8,128)(2,1)S(1)}, u32[]{:S(2)}) copy-start(bf16[9,4,16,128]{3,2,1,0:T(8,128)(2,1)S(1)} %get-tuple-element.64.skip_send_ref) | copy-start | bytes 442372
  31.5 7.2 %copy-start.1 = (bf16[2,256,1152]{2,1,0:T(8,128)(2,1)S(1)}, bf16[2,256,1152]{2,1,0:T(8,128)(2,1)}, u32[]{:S(2)}) copy-start(bf16[2,256,1152]{2,1,0:T(8,128)(2,1)} %get-tuple-element.60.box_ref) | copy-start | bytes 3538948
  32.0 6.7 %copy-start.2 = (bf16[2,256,384]{2,1,0:T(8,128)(2,1)S(1)}, bf16[2,256,384]{2,1,0:T(8,128)(2,1)}, u32[]{:S(2)}) copy-start(bf16[2,256,384]{2,1,0:T(8,128)(2,1)} %get-tuple-element.61.box_low_ref) | copy-start | bytes 1179652
  32.0 6.7 %copy-start.3 = (bf16[2,256,384]{2,1,0:T(8,128)(2,1)S(1)}, bf16[2,256,384]{2,1,0:T(8,128)(2,1)}, u32[]{:S(2)}) copy-start(bf16[2,256,384]{2,1,0:T(8,128)(2,1)} %get-tuple-element.62.box_high_ref) | copy-start | bytes 1179652
  33.7 10.0 %collective-permute-start.2 = (bf16[2,256,256]{2,1,0:T(8,128)(2,1)S(1)}, bf16[2,256,256]{2,1,0:T(8,128)(2,1)S(1)}, u32[]{:S(2)}, u32[]{:S(2)}) collective-permute-start(bf16[2,256,256]{2,1,0:T(8,128)(2,1)S(1)} %get-tuple-element.58.near_ref.third_ref), channel_id=1, source_target_pairs={{0,1},{1,0},{2,3},{3,2},{4,5},{5,4},{6,7},{7,6},{8,9},{9,8},{10,11... | collective-permute-start | bytes 786440 | tf_op jit(solution)/shard_map/ppermute | solution.py:720
  33.8 14.4 %collective-permute-start.3 = (bf16[2,256,256]{2,1,0:T(8,128)(2,1)S(1)}, bf16[2,256,256]{2,1,0:T(8,128)(2,1)S(1)}, u32[]{:S(2)}, u32[]{:S(2)}) collective-permute-start(bf16[2,256,256]{2,1,0:T(8,128)(2,1)S(1)} %get-tuple-element.59.far_ref.second_ref), channel_id=1, source_target_pairs={{1,2},{3,4},{5,6},{7,8},{9,10},{11,12},{13,14},{15,16},{17,18},{19... | collective-permute-start | bytes 786440 | tf_op jit(solution)/shard_map/ppermute | solution.py:720
  41.0 1.9 %collective-permute-start.4 = (bf16[9,12,16,128]{3,2,1,0:T(8,128)(2,1)S(1)}, bf16[9,12,16,128]{3,2,1,0:T(8,128)(2,1)S(1)}, u32[]{:S(2)}, u32[]{:S(2)}) collective-permute-start(bf16[9,12,16,128]{3,2,1,0:T(8,128)(2,1)S(1)} %get-tuple-element.66), channel_id=1, source_target_pairs={{0,8},{8,0},{1,9},{9,1},{2,10},{10,2},{3,11},{11,3},{4,12},{12,4},... | collective-permute-start | bytes 1327112 | tf_op jit(solution)/shard_map/ppermute | solution.py:753
  49.5 2.1 %collective-permute-start.12 = (bf16[144,16,128]{2,1,0:T(8,128)(2,1)S(1)}, bf16[144,16,128]{2,1,0:T(8,128)(2,1)S(1)}, u32[]{:S(2)}, u32[]{:S(2)}) collective-permute-start(bf16[144,16,128]{2,1,0:T(8,128)(2,1)S(1)} %coarse_weight_level.3), channel_id=1, source_target_pairs={{0,8},{8,0},{1,9},{9,1},{2,10},{10,2},{3,11},{11,3},{4,12},{12,4},... | collective-permute-start | bytes 1769480 | tf_op jit(solution)/shard_map/ppermute | solution.py:764
  52.4 9.9 %copy-start = (bf16[3,3,256,256]{3,2,1,0:T(8,128)(2,1)S(1)}, bf16[3,3,256,256]{3,2,1,0:T(8,128)(2,1)}, u32[]{:S(2)}) copy-start(bf16[3,3,256,256]{3,2,1,0:T(8,128)(2,1)} %weight_ref.5) | copy-start | bytes 3538948
  52.4 26.3 %all-to-all-start.1 = ((bf16[64,4,16,128]{3,2,1,0:T(8,128)(2,1)}), bf16[64,4,16,128]{3,2,1,0:T(8,128)(2,1)S(1)}, u32[]{:S(2)}, u32[]{:S(2)}) async-start(bf16[64,4,16,128]{3,2,1,0:T(8,128)(2,1)} %bitcast.7), calls=%async_computation.1 | async-start | bytes 2097152 | tf_op jit(solution)/shard_map/all_to_all | solution.py:625
  65.9 20.1 %collective-permute-start.5 = (bf16[2,2,32,256]{3,2,1,0:T(8,128)(2,1)}, bf16[2,2,32,256]{3,2,1,0:T(8,128)(2,1)S(1)}, u32[]{:S(2)}, u32[]{:S(2)}) collective-permute-start(bf16[2,2,32,256]{3,2,1,0:T(8,128)(2,1)} %get-tuple-element.70), channel_id=1, source_target_pairs={{0,1},{1,0},{2,3},{3,2},{4,5},{5,4},{6,7},{7,6},{8,9},{9,8},{10,11... | collective-permute-start | bytes 196616 | tf_op jit(solution)/shard_map/ppermute | solution.py:769
  66.9 19.1 %collective-permute-start.6 = (bf16[2,2,32,256]{3,2,1,0:T(8,128)(2,1)}, bf16[2,2,32,256]{3,2,1,0:T(8,128)(2,1)S(1)}, u32[]{:S(2)}, u32[]{:S(2)}) collective-permute-start(bf16[2,2,32,256]{3,2,1,0:T(8,128)(2,1)} %get-tuple-element.71), channel_id=1, source_target_pairs={{0,2},{1,3},{2,0},{3,1},{4,6},{5,7},{6,4},{7,5},{8,10},{9,11},{10,... | collective-permute-start | bytes 196616 | tf_op jit(solution)/shard_map/ppermute | solution.py:769
  68.1 18.0 %collective-permute-start.7 = (bf16[2,2,32,256]{3,2,1,0:T(8,128)(2,1)}, bf16[2,2,32,256]{3,2,1,0:T(8,128)(2,1)S(1)}, u32[]{:S(2)}, u32[]{:S(2)}) collective-permute-start(bf16[2,2,32,256]{3,2,1,0:T(8,128)(2,1)} %get-tuple-element.72), channel_id=1, source_target_pairs={{0,3},{1,2},{2,1},{3,0},{4,7},{5,6},{6,5},{7,4},{8,11},{9,10},{10,... | collective-permute-start | bytes 196616 | tf_op jit(solution)/shard_map/ppermute | solution.py:769
  68.6 17.5 %collective-permute-start.8 = (bf16[2,2,32,256]{3,2,1,0:T(8,128)(2,1)S(1)}, bf16[2,2,32,256]{3,2,1,0:T(8,128)(2,1)S(1)}, u32[]{:S(2)}, u32[]{:S(2)}) collective-permute-start(bf16[2,2,32,256]{3,2,1,0:T(8,128)(2,1)S(1)} %get-tuple-element.73), channel_id=1, source_target_pairs={{0,4},{1,5},{2,6},{3,7},{4,0},{5,1},{6,2},{7,3},{8,12},{9,13},{10,... | collective-permute-start | bytes 196616 | tf_op jit(solution)/shard_map/ppermute | solution.py:769
  71.1 15.0 %copy-start.7 = (bf16[2,2,32,256]{3,2,1,0:T(8,128)(2,1)S(1)}, bf16[2,2,32,256]{3,2,1,0:T(8,128)(2,1)}, u32[]{:S(2)}) copy-start(bf16[2,2,32,256]{3,2,1,0:T(8,128)(2,1)} %copy-done.6) | copy-start | bytes 196612
  71.1 15.0 %collective-permute-start.9 = (bf16[2,2,32,256]{3,2,1,0:T(8,128)(2,1)S(1)}, bf16[2,2,32,256]{3,2,1,0:T(8,128)(2,1)S(1)}, u32[]{:S(2)}, u32[]{:S(2)}) collective-permute-start(bf16[2,2,32,256]{3,2,1,0:T(8,128)(2,1)S(1)} %get-tuple-element.74), channel_id=1, source_target_pairs={{0,5},{1,4},{2,7},{3,6},{4,1},{5,0},{6,3},{7,2},{8,13},{9,12},{10,... | collective-permute-start | bytes 196616 | tf_op jit(solution)/shard_map/ppermute | solution.py:769
  80.0 21.1 %all-to-all-start.2 = ((bf16[64,4,16,128]{3,2,1,0:T(8,128)(2,1)}), bf16[64,4,16,128]{3,2,1,0:T(8,128)(2,1)S(1)}, u32[]{:S(2)}, u32[]{:S(2)}) async-start(bf16[64,4,16,128]{3,2,1,0:T(8,128)(2,1)} %sum_parts.1), calls=%async_computation.2 | async-start | bytes 2097152 | tf_op jit(solution)/shard_map/all_to_all | solution.py:633
  86.2 19.8 %collective-permute-start.10 = (bf16[2,2,32,256]{3,2,1,0:T(8,128)(2,1)S(1)}, bf16[2,2,32,256]{3,2,1,0:T(8,128)(2,1)S(1)}, u32[]{:S(2)}, u32[]{:S(2)}) collective-permute-start(bf16[2,2,32,256]{3,2,1,0:T(8,128)(2,1)S(1)} %get-tuple-element.77), channel_id=1, source_target_pairs={{0,6},{1,7},{2,4},{3,5},{4,2},{5,3},{6,0},{7,1},{8,14},{9,15},{10,... | collective-permute-start | bytes 196616 | tf_op jit(solution)/shard_map/ppermute | solution.py:769
  88.5 17.5 %collective-permute-start.11 = (bf16[2,2,32,256]{3,2,1,0:T(8,128)(2,1)S(1)}, bf16[2,2,32,256]{3,2,1,0:T(8,128)(2,1)S(1)}, u32[]{:S(2)}, u32[]{:S(2)}) collective-permute-start(bf16[2,2,32,256]{3,2,1,0:T(8,128)(2,1)S(1)} %get-tuple-element.78), channel_id=1, source_target_pairs={{0,7},{1,6},{2,5},{3,4},{4,3},{5,2},{6,1},{7,0},{8,15},{9,14},{10,... | collective-permute-start | bytes 196616 | tf_op jit(solution)/shard_map/ppermute | solution.py:769
  101.1 7.3 %collective-permute-start.13 = (bf16[256,16,128]{2,1,0:T(8,128)(2,1)S(1)}, bf16[256,16,128]{2,1,0:T(8,128)(2,1)S(1)}, u32[]{:S(2)}, u32[]{:S(2)}) collective-permute-start(bf16[256,16,128]{2,1,0:T(8,128)(2,1)S(1)} %bitcast.12), channel_id=1, source_target_pairs={{0,8},{8,0},{1,9},{9,1},{2,10},{10,2},{3,11},{11,3},{4,12},{12,4},... | collective-permute-start | bytes 3145736 | tf_op jit(solution)/shard_map/ppermute | solution.py:779
  (3 other events, 2.2 us)

commit v6 on v5

--- a/solution.py
+++ b/solution.py
@@ -13,7 +13,7 @@
 BF16 = jnp.bfloat16
 MIB = 1 << 20
 VMEM = 18
-EARLY = 6
+LATE = (6, 7)
 LONG = 1e11
 
 SPLIT = (("xh", 2), ("z", 4), ("core", 2), ("y", 4), ("xl", 2))
@@ -161,12 +161,12 @@
             pl.BlockSpec((3 * c3, c4), lambda s: (2, 0)),
         ],
         out_specs=[whole, box_spec, box_spec],
-        out_shape=[pltpu.HBM((samples, 2, half, c4), F32), box, box],
+        out_shape=[jax.ShapeDtypeStruct((samples, 2, half, c4), F32), box, box],
         scratch_shapes=[pltpu.VMEM((2, wide, c3), F32)],
         compiler_params=params(VMEM),
         cost_estimate=cost(LONG, 4e6),
         name="edge_level",
-    )(place, in_hbm(near), in_hbm(far), edge, pooled, up_weight, up_weight)
+    )(place, near, far, edge, pooled, up_weight, up_weight)
 
 
 def fine_kernel(
@@ -255,7 +255,7 @@
         compiler_params=params(VMEM),
         cost_estimate=cost(5e9, 8e6),
         name="fine_level",
-    )(place, *(in_hbm(a) for a in (grad, near, far, skip, weight)))
+    )(place, in_hbm(grad), near, far, in_hbm(skip), in_hbm(weight))
 
 
 def coarse_grad_kernel(place_ref, pooled_ref, pre_ref, near_ref, far_ref):
@@ -287,7 +287,7 @@
         compiler_params=params(VMEM),
         cost_estimate=cost(2e7, 2e6),
         name="coarse_grad",
-    )(place, in_hbm(pooled), received)
+    )(place, pooled, received)
 
 
 def up_kernel(
@@ -514,20 +514,20 @@
     )(chan, weight, *rows)
 
 
-def place_kernel(first, count, chan_ref, *refs):
+def place_kernel(partners, chan_ref, *refs):
     out_ref = refs[-1]
-    if len(refs) > count + 1:
-        out_ref[...] = refs[count][...]
-    for k in range(count):
-        at = jnp.bitwise_xor(chan_ref[0], first + k) * 2
-        out_ref[:, pl.ds(at, 2)] = refs[k][...]
-
-
-def placed(chan, pieces, first, peers, earlier=(), flops=1e6):
+    if len(refs) > len(partners) + 1:
+        out_ref[...] = refs[len(partners)][...]
+    for k, ref in zip(partners, refs):
+        at = jnp.bitwise_xor(chan_ref[0], k) * 2
+        out_ref[:, pl.ds(at, 2)] = ref[...]
+
+
+def placed(chan, pieces, partners, peers, earlier=(), flops=1e6):
     samples, rows, own, wide = pieces[0].shape
     vmem = pl.BlockSpec(memory_space=pltpu.VMEM)
     return pl.pallas_call(
-        functools.partial(place_kernel, first, len(pieces)),
+        functools.partial(place_kernel, partners),
         in_specs=[pl.BlockSpec(memory_space=pltpu.SMEM)] + [vmem] * (len(pieces) + len(earlier)),
         out_shape=jax.ShapeDtypeStruct((samples, rows * peers, own, wide), BF16),
         compiler_params=params(VMEM),
@@ -770,12 +770,12 @@
 
     sums = joined(coarse_keep, coarse_more, 0, coarse_count, total, (sums,))
     mine = grad_sums(sums, chips)
-    early = [back[0]] + [home(k, back[k]) for k in range(1, EARLY)]
-    grad_input = placed(chan, early, 0, peers, flops=LONG)
-    grad_input, *late = lax.optimization_barrier((grad_input, *back[EARLY:]))
-    late = [home(EARLY + k, piece) for k, piece in enumerate(late)]
+    early = [k for k in range(peers) if k not in LATE]
+    grad_input = placed(chan, [home(k, back[k]) if k else back[k] for k in early], early, peers, flops=LONG)
+    grad_input, *late = lax.optimization_barrier((grad_input, *(back[k] for k in LATE)))
+    late = [home(k, piece) for k, piece in zip(LATE, late)]
     mine, grad_input = lax.optimization_barrier((mine, grad_input))
-    grad_input = placed(chan, late, EARLY, peers, (grad_input,), flops=LONG)
+    grad_input = placed(chan, late, LATE, peers, (grad_input,), flops=LONG)
     other = lax.ppermute(mine, "core", SWAP)
     sums = unpacked(place, mine, fine_weight.shape, coarse_weight.shape)
     grad_fine, grad_coarse = unpacked(other_place, other, fine_weight.shape, coarse_weight.shape, sums)

time: 111 us -> 109 us (0.982)
  Pallas kernels: 33.8 us -> 31.4 us
  waiting for transfers between devices: 25.9 us -> 27.3 us
    all_to_all x1, waiting for transfers between devices: 0.48 us -> 1.88 us  [shards(): received = lax.all_to_all(pieces, CHAN, 0, 0, tiled=True)]
    pallas_call x1, Pallas kernels: 2.66 us -> 1.47 us  [edge_level(): pl.pallas_call(edge_kernel, grid=(samples,), in_specs=[pl.BlockSpec(memor...]
    unnamed x20 -> x16, local copies, waits for them, and re-layouts: 2.25 us -> 2.2 us
  transfers between devices with their start and end apart: 17 -> 17, of which waited for: 6 -> 6; matrix products, arithmetic and copies ran while one was open for 0% -> 0% of each run, Pallas kernels for 23% -> 22%
where the time goes in v6:
time: 109 us
  starting transfers between devices  47 us (43%)
  Pallas kernels  31.4 us (29%)
  waiting for transfers between devices  27.3 us (25%)
  local copies, waits for them, and re-layouts  2.2 us (2%)
  between operations  1.09 us (1%)
    ppermute x4, starting transfers between devices, swapped(): return (lax.ppermute(near, ALL, inside), lax.ppermute(far, ALL, outside))  12.6 us
    all_to_all x1, waiting for transfers between devices, grad_sums(): lax.all_to_all(summed, CHIPS, 0, 0, tiled=True)  11.4 us
    all_to_all x1, starting transfers between devices, grad_sums(): lax.all_to_all(parts.reshape(chips, each, 16, 128), CHIPS, 0, 0, tiled=True)  9.89 us
    ppermute x7, starting transfers between devices, home(): return lax.ppermute(piece, CHAN, [(i, i ^ k) for i in range(peers)])  9.84 us
    ppermute x4, waiting for transfers between devices, swapped(): return (lax.ppermute(near, ALL, inside), lax.ppermute(far, ALL, outside))  6.7 us
    all_to_all x1, waiting for transfers between devices, grad_sums(): lax.all_to_all(parts.reshape(chips, each, 16, 128), CHIPS, 0, 0, tiled=True)  6.5 us
    pallas_call x1, Pallas kernels, fine_level(): pl.pallas_call(functools.partial(fine_kernel, scale=1.0 / math.sqrt(fine_...  6.43 us
    all_to_all x1, starting transfers between devices, grad_sums(): lax.all_to_all(summed, CHIPS, 0, 0, tiled=True)  6.05 us
  transfers between devices with their start and end apart: 17, of which 6 were waited for; matrix products, arithmetic and copies ran while one was open for 0% of the time, Pallas kernels for 22%

profile of v6, /device:TPU:1, one launch (start us, length us, event | category | flops | bytes accessed | tf_op | source)
XLA Modules:
  0.0 109.0 jit_solution(14742832653428974914)
XLA Ops:
  0.6 3.3 %start.1 = (bf16[8,2,2,2,32,256]{5,4,3,2,1,0:T(8,128)(2,1)}, bf16[2,512,128]{2,1,0:T(8,128)(2,1)S(1)}, bf16[2,512,128]{2,1,0:T(8,128)(2,1)S(1)}) custom-call(s32[1]{0:T(128)} %bitcast.place_ref, bf16[2,16,32,256]{3,2,1,0:T(8,128)(2,1)} %bitcast.18, bf16[2,16,32,256]{3,2,1,0:T(8,128)(2,1)} %bitcast.19, bf16[2,4,512,128]{3,2,1,0:T(8,128)(2,1)} %cot_ref.3, ...), custom_call_target="tpu_custom_call" | custom-call | flops 10000000 | bytes 3000000 | tf_op jit(solution)/shard_map/start/pallas_call | solution.py:697
  4.0 2.1 %collective-permute-start = (bf16[2,512,128]{2,1,0:T(8,128)(2,1)S(1)}, bf16[2,512,128]{2,1,0:T(8,128)(2,1)S(1)}, u32[]{:S(2)}, u32[]{:S(2)}) collective-permute-start(bf16[2,512,128]{2,1,0:T(8,128)(2,1)S(1)} %get-tuple-element.47), channel_id=1, source_target_pairs={{0,1},{1,0},{2,3},{3,2},{4,5},{5,4},{6,7},{7,6},{8,9},{9,8},{10,11... | collective-permute-start | bytes 786440 | tf_op jit(solution)/shard_map/ppermute | solution.py:720
  6.1 5.4 %collective-permute-start.1 = (bf16[2,512,128]{2,1,0:T(8,128)(2,1)S(1)}, bf16[2,512,128]{2,1,0:T(8,128)(2,1)S(1)}, u32[]{:S(2)}, u32[]{:S(2)}) collective-permute-start(bf16[2,512,128]{2,1,0:T(8,128)(2,1)S(1)} %get-tuple-element.48), channel_id=1, source_target_pairs={{1,2},{3,4},{5,6},{7,8},{9,10},{11,12},{13,14},{15,16},{17,18},{19... | collective-permute-start | bytes 786440 | tf_op jit(solution)/shard_map/ppermute | solution.py:720
  11.5 3.6 %all-to-all-start = ((bf16[8,2,2,2,32,256]{5,4,3,2,1,0:T(8,128)(2,1)}), bf16[8,2,2,2,32,256]{5,4,3,2,1,0:T(8,128)(2,1)S(1)}, u32[]{:S(2)}, u32[]{:S(2)}) async-start(bf16[8,2,2,2,32,256]{5,4,3,2,1,0:T(8,128)(2,1)} %get-tuple-element.54), calls=%async_computation | async-start | bytes 2097152 | tf_op jit(solution)/shard_map/all_to_all | solution.py:740
  15.1 4.3 %box_level.1 = (bf16[2,4,512,128]{3,2,1,0:T(8,128)(2,1)}, bf16[2,256,1152]{2,1,0:T(8,128)(2,1)}, bf16[2,2,512,128]{3,2,1,0:T(8,128)(2,1)S(1)}, f32[2,2,256,256]{3,2,1,0:T(8,128)S(1)}, bf16[1152,256]{1,0:T(8,128)(2,1)S(1)}) custom-call(bf16[2,4,512,128]{3,2,1,0:T(8,128)(2,1)} %cot_ref.3, bf16[2,4,512,128]{3,2,1,0:T(8,128)(2,1)} %fine_pre_ref.1, ...), custom_call_target="tpu_custom_call" | custom-call | flops 1200000000 | bytes 8000000 | tf_op jit(solution)/shard_map/box_level/pallas_call | solution.py:102
  19.4 2.2 %collective-permute-done.1.far_ref = bf16[2,512,128]{2,1,0:T(8,128)(2,1)S(1)} collective-permute-done((bf16[2,512,128]{2,1,0:T(8,128)(2,1)S(1)}, bf16[2,512,128]{2,1,0:T(8,128)(2,1)S(1)}, u32[]{:S(2)}, u32[]{:S(2)}) %collective-permute-start.1) | collective-permute-done | bytes 262176 | tf_op jit(solution)/shard_map/ppermute | solution.py:720
  21.6 1.5 %edge_level.1 = (f32[2,2,256,256]{3,2,1,0:T(8,128)S(1)}, bf16[2,256,384]{2,1,0:T(8,128)(2,1)}, bf16[2,256,384]{2,1,0:T(8,128)(2,1)}) custom-call(s32[1]{0:T(128)} %bitcast.place_ref, bf16[2,512,128]{2,1,0:T(8,128)(2,1)S(1)} %collective-permute-done.near_ref, bf16[2,512,128]{2,1,0:T(8,128)(2,1)S(1)} %collective-permute-done.1.far_ref, ...), custom_call_target="tpu_custom_call" | custom-call | flops 99999997952 | bytes 4000000 | tf_op jit(solution)/shard_map/edge_level/pallas_call | solution.py:154
  23.0 6.4 %fine_level.1 = (bf16[2,4,512,128]{3,2,1,0:T(8,128)(2,1)}, bf16[9,4,16,128]{3,2,1,0:T(8,128)(2,1)S(1)}, bf16[9,4,16,128]{3,2,1,0:T(8,128)(2,1)S(1)}) custom-call(s32[1]{0:T(128)} %bitcast.place_ref, bf16[2,4,512,128]{3,2,1,0:T(8,128)(2,1)} %get-tuple-element.46.grad_ref, bf16[2,512,128]{2,1,0:T(8,128)(2,1)S(1)} %collective-permute-done.near_ref, ...), custom_call_target="tpu_custom_call" | custom-call | flops 5000000000 | bytes 8000000 | tf_op jit(solution)/shard_map/fine_level/pallas_call | solution.py:237
  30.1 1.9 %all-to-all-done.pre_ref.input_ref = bf16[8,2,2,2,32,256]{5,4,3,2,1,0:T(8,128)(2,1)S(1)} async-done(((bf16[8,2,2,2,32,256]{5,4,3,2,1,0:T(8,128)(2,1)}), bf16[8,2,2,2,32,256]{5,4,3,2,1,0:T(8,128)(2,1)S(1)}, u32[]{:S(2)}, u32[]{:S(2)}) %all-to-all-start) | async-done | bytes 1048608 | tf_op jit(solution)/shard_map/all_to_all | solution.py:740
  32.7 5.0 %collective-permute-start.3 = (bf16[2,256,256]{2,1,0:T(8,128)(2,1)S(1)}, bf16[2,256,256]{2,1,0:T(8,128)(2,1)S(1)}, u32[]{:S(2)}, u32[]{:S(2)}) collective-permute-start(bf16[2,256,256]{2,1,0:T(8,128)(2,1)S(1)} %get-tuple-element.59.far_ref.second_ref), channel_id=1, source_target_pairs={{1,2},{3,4},{5,6},{7,8},{9,10},{11,12},{13,14},{15,16},{17,18},{19... | collective-permute-start | bytes 786440 | tf_op jit(solution)/shard_map/ppermute | solution.py:720
  38.6 1.3 %up_level.1 = (bf16[9,12,16,128]{3,2,1,0:T(8,128)(2,1)S(1)}, bf16[9,12,16,128]{3,2,1,0:T(8,128)(2,1)S(1)}) custom-call(s32[1]{0:T(128)} %bitcast.place_ref, bf16[8,2,2,2,32,256]{5,4,3,2,1,0:T(8,128)(2,1)S(1)} %all-to-all-done.pre_ref.input_ref, bf16[2,256,1152]{2,1,0:T(8,128)(2,1)S(1)} %copy-done.1, bf16[2,256,384]{2,1,0:T(8,128)(2,1)S(1)} %copy-done.2, ...), custom_call_target="tpu_custom_call" | custom-call | flops 1000000000 | bytes 5000000 | tf_op jit(solution)/shard_map/up_level/pallas_call | solution.py:341
  40.0 1.8 %own_weight_level.1.own_ref = f32[3,256,768]{2,1,0:T(8,128)S(1)} custom-call(s32[1]{0:T(128)} %bitcast.place_ref, bf16[8,2,2,2,32,256]{5,4,3,2,1,0:T(8,128)(2,1)S(1)} %all-to-all-done.pre_ref.input_ref, bf16[2,256,256]{2,1,0:T(8,128)(2,1)S(1)} %get-tuple-element.59.far_ref.second_ref, bf16[2,256,256]{2,1,0:T(8,128)(2,1)S(1)} %get-tuple-element.58.near_ref.third_ref), custom_call_target="tpu_custom_call" | custom-call | flops 99999997952 | bytes 4000000 | tf_op jit(solution)/shard_map/own_weight_level/pallas_call | solution.py:400
  42.6 4.5 %collective-permute-done.3.first_ref.from_far_ref = bf16[2,256,256]{2,1,0:T(8,128)(2,1)S(1)} collective-permute-done((bf16[2,256,256]{2,1,0:T(8,128)(2,1)S(1)}, bf16[2,256,256]{2,1,0:T(8,128)(2,1)S(1)}, u32[]{:S(2)}, u32[]{:S(2)}) %collective-permute-start.3) | collective-permute-done | bytes 262176 | tf_op jit(solution)/shard_map/ppermute | solution.py:720
  48.5 1.3 %coarse_weight_level.2.refs_0_ = bf16[144,16,128]{2,1,0:T(8,128)(2,1)S(1)} custom-call(s32[1]{0:T(128)} %bitcast.place_ref, bf16[8,2,2,2,32,256]{5,4,3,2,1,0:T(8,128)(2,1)S(1)} %all-to-all-done.pre_ref.input_ref, bf16[2,256,256]{2,1,0:T(8,128)(2,1)S(1)} %collective-permute-done.3.first_ref.from_far_ref, ...), custom_call_target="tpu_custom_call" | custom-call | flops 400000000 | bytes 2000000 | tf_op jit(solution)/shard_map/coarse_weight_level/pallas_call | solution.py:455
  51.4 9.9 %all-to-all-start.1 = ((bf16[64,4,16,128]{3,2,1,0:T(8,128)(2,1)}), bf16[64,4,16,128]{3,2,1,0:T(8,128)(2,1)S(1)}, u32[]{:S(2)}, u32[]{:S(2)}) async-start(bf16[64,4,16,128]{3,2,1,0:T(8,128)(2,1)} %bitcast.7), calls=%async_computation.1 | async-start | bytes 2097152 | tf_op jit(solution)/shard_map/all_to_all | solution.py:625
  61.3 2.9 %coarse_input_level.1 = (bf16[2,2,32,256]{3,2,1,0:T(8,128)(2,1)S(1)}, bf16[2,2,32,256]{3,2,1,0:T(8,128)(2,1)}, bf16[2,2,32,256]{3,2,1,0:T(8,128)(2,1)}, bf16[2,2...) custom-call(s32[1]{0:T(128)} %bitcast.3.chan_ref, ...), custom_call_target="tpu_custom_call" | custom-call | flops 1300000000 | bytes 3000000 | tf_op jit(solution)/shard_map/coarse_input_level/pallas_call | solution.py:501
  67.5 2.5 %collective-permute-start.8 = (bf16[2,2,32,256]{3,2,1,0:T(8,128)(2,1)S(1)}, bf16[2,2,32,256]{3,2,1,0:T(8,128)(2,1)S(1)}, u32[]{:S(2)}, u32[]{:S(2)}) collective-permute-start(bf16[2,2,32,256]{3,2,1,0:T(8,128)(2,1)S(1)} %get-tuple-element.73), channel_id=1, source_target_pairs={{0,4},{1,5},{2,6},{3,7},{4,0},{5,1},{6,2},{7,3},{8,12},{9,13},{10,... | collective-permute-start | bytes 196616 | tf_op jit(solution)/shard_map/ppermute | solution.py:769
  71.2 6.5 %all-to-all-done.1.parts_ref = bf16[64,4,16,128]{3,2,1,0:T(8,128)(2,1)S(1)} async-done(((bf16[64,4,16,128]{3,2,1,0:T(8,128)(2,1)}), bf16[64,4,16,128]{3,2,1,0:T(8,128)(2,1)S(1)}, u32[]{:S(2)}, u32[]{:S(2)}) %all-to-all-start.1) | async-done | bytes 1048608 | tf_op jit(solution)/shard_map/all_to_all | solution.py:625
  78.9 6.0 %all-to-all-start.2 = ((bf16[64,4,16,128]{3,2,1,0:T(8,128)(2,1)}), bf16[64,4,16,128]{3,2,1,0:T(8,128)(2,1)S(1)}, u32[]{:S(2)}, u32[]{:S(2)}) async-start(bf16[64,4,16,128]{3,2,1,0:T(8,128)(2,1)} %sum_parts.1), calls=%async_computation.2 | async-start | bytes 2097152 | tf_op jit(solution)/shard_map/all_to_all | solution.py:633
  85.1 2.3 %collective-permute-start.10 = (bf16[2,2,32,256]{3,2,1,0:T(8,128)(2,1)S(1)}, bf16[2,2,32,256]{3,2,1,0:T(8,128)(2,1)S(1)}, u32[]{:S(2)}, u32[]{:S(2)}) collective-permute-start(bf16[2,2,32,256]{3,2,1,0:T(8,128)(2,1)S(1)} %get-tuple-element.77), channel_id=1, source_target_pairs={{0,6},{1,7},{2,4},{3,5},{4,2},{5,3},{6,0},{7,1},{8,14},{9,15},{10,... | collective-permute-start | bytes 196616 | tf_op jit(solution)/shard_map/ppermute | solution.py:769
  88.6 11.4 %all-to-all-done.2 = bf16[64,4,16,128]{3,2,1,0:T(8,128)(2,1)S(1)} async-done(((bf16[64,4,16,128]{3,2,1,0:T(8,128)(2,1)}), bf16[64,4,16,128]{3,2,1,0:T(8,128)(2,1)S(1)}, u32[]{:S(2)}, u32[]{:S(2)}) %all-to-all-start.2) | async-done | bytes 1048608 | tf_op jit(solution)/shard_map/all_to_all | solution.py:633
  100.0 4.9 %collective-permute-start.13 = (bf16[256,16,128]{2,1,0:T(8,128)(2,1)S(1)}, bf16[256,16,128]{2,1,0:T(8,128)(2,1)S(1)}, u32[]{:S(2)}, u32[]{:S(2)}) collective-permute-start(bf16[256,16,128]{2,1,0:T(8,128)(2,1)S(1)} %bitcast.12), channel_id=1, source_target_pairs={{0,8},{8,0},{1,9},{9,1},{2,10},{10,2},{3,11},{11,3},{4,12},{12,4},... | collective-permute-start | bytes 3145736 | tf_op jit(solution)/shard_map/ppermute | solution.py:779
  105.7 1.5 %unpack.2 = (f32[9,384,128]{2,1,0:T(8,128)}, f32[9,256,256]{2,1,0:T(8,128)}) custom-call(s32[1]{0:T(128)} %bitcast.place_ref, bf16[256,16,128]{2,1,0:T(8,128)(2,1)S(1)} %bitcast.13), custom_call_target="tpu_custom_call" | custom-call | flops 1 | bytes 1 | tf_op jit(solution)/shard_map/unpack/pallas_call | solution.py:639
  107.3 1.5 %unpack.3 = (f32[9,384,128]{2,1,0:T(8,128)}, f32[9,256,256]{2,1,0:T(8,128)}) custom-call(s32[1]{0:T(128)} %bitcast.6.place_ref, bf16[256,16,128]{2,1,0:T(8,128)(2,1)S(1)} %collective-permute-done.13.parts_ref, f32[9,384,128]{2,1,0:T(8,128)} %get-tuple-element.84.rest_0_, ...), custom_call_target="tpu_custom_call", output_to_operand_aliasing={{0}: (2, {}), {1}: (3, {})} | custom-call | flops 1 | bytes 1 | tf_op jit(solution)/shard_map/unpack/pallas_call | solution.py:639
  (43 shorter events, 13.9 us)
Async XLA Ops:
  4.0 15.4 %collective-permute-start = (bf16[2,512,128]{2,1,0:T(8,128)(2,1)S(1)}, bf16[2,512,128]{2,1,0:T(8,128)(2,1)S(1)}, u32[]{:S(2)}, u32[]{:S(2)}) collective-permute-start(bf16[2,512,128]{2,1,0:T(8,128)(2,1)S(1)} %get-tuple-element.47), channel_id=1, source_target_pairs={{0,1},{1,0},{2,3},{3,2},{4,5},{5,4},{6,7},{7,6},{8,9},{9,8},{10,11... | collective-permute-start | bytes 786440 | tf_op jit(solution)/shard_map/ppermute | solution.py:720
  6.1 15.5 %collective-permute-start.1 = (bf16[2,512,128]{2,1,0:T(8,128)(2,1)S(1)}, bf16[2,512,128]{2,1,0:T(8,128)(2,1)S(1)}, u32[]{:S(2)}, u32[]{:S(2)}) collective-permute-start(bf16[2,512,128]{2,1,0:T(8,128)(2,1)S(1)} %get-tuple-element.48), channel_id=1, source_target_pairs={{1,2},{3,4},{5,6},{7,8},{9,10},{11,12},{13,14},{15,16},{17,18},{19... | collective-permute-start | bytes 786440 | tf_op jit(solution)/shard_map/ppermute | solution.py:720
  11.5 20.5 %all-to-all-start = ((bf16[8,2,2,2,32,256]{5,4,3,2,1,0:T(8,128)(2,1)}), bf16[8,2,2,2,32,256]{5,4,3,2,1,0:T(8,128)(2,1)S(1)}, u32[]{:S(2)}, u32[]{:S(2)}) async-start(bf16[8,2,2,2,32,256]{5,4,3,2,1,0:T(8,128)(2,1)} %get-tuple-element.54), calls=%async_computation | async-start | bytes 2097152 | tf_op jit(solution)/shard_map/all_to_all | solution.py:740
  29.5 0.7 copy-start.4
  30.1 7.5 %copy-start.2 = (bf16[2,256,384]{2,1,0:T(8,128)(2,1)S(1)}, bf16[2,256,384]{2,1,0:T(8,128)(2,1)}, u32[]{:S(2)}) copy-start(bf16[2,256,384]{2,1,0:T(8,128)(2,1)} %get-tuple-element.61.box_low_ref) | copy-start | bytes 1179652
  32.0 5.7 %copy-start.1 = (bf16[2,256,1152]{2,1,0:T(8,128)(2,1)S(1)}, bf16[2,256,1152]{2,1,0:T(8,128)(2,1)}, u32[]{:S(2)}) copy-start(bf16[2,256,1152]{2,1,0:T(8,128)(2,1)} %get-tuple-element.60.box_ref) | copy-start | bytes 3538948
  32.0 5.7 %copy-start.3 = (bf16[2,256,384]{2,1,0:T(8,128)(2,1)S(1)}, bf16[2,256,384]{2,1,0:T(8,128)(2,1)}, u32[]{:S(2)}) copy-start(bf16[2,256,384]{2,1,0:T(8,128)(2,1)} %get-tuple-element.62.box_high_ref) | copy-start | bytes 1179652
  32.6 10.0 %collective-permute-start.2 = (bf16[2,256,256]{2,1,0:T(8,128)(2,1)S(1)}, bf16[2,256,256]{2,1,0:T(8,128)(2,1)S(1)}, u32[]{:S(2)}, u32[]{:S(2)}) collective-permute-start(bf16[2,256,256]{2,1,0:T(8,128)(2,1)S(1)} %get-tuple-element.58.near_ref.third_ref), channel_id=1, source_target_pairs={{0,1},{1,0},{2,3},{3,2},{4,5},{5,4},{6,7},{7,6},{8,9},{9,8},{10,11... | collective-permute-start | bytes 786440 | tf_op jit(solution)/shard_map/ppermute | solution.py:720
  32.7 14.4 %collective-permute-start.3 = (bf16[2,256,256]{2,1,0:T(8,128)(2,1)S(1)}, bf16[2,256,256]{2,1,0:T(8,128)(2,1)S(1)}, u32[]{:S(2)}, u32[]{:S(2)}) collective-permute-start(bf16[2,256,256]{2,1,0:T(8,128)(2,1)S(1)} %get-tuple-element.59.far_ref.second_ref), channel_id=1, source_target_pairs={{1,2},{3,4},{5,6},{7,8},{9,10},{11,12},{13,14},{15,16},{17,18},{19... | collective-permute-start | bytes 786440 | tf_op jit(solution)/shard_map/ppermute | solution.py:720
  37.7 0.9 copy-start.5
  39.9 1.9 %collective-permute-start.4 = (bf16[9,12,16,128]{3,2,1,0:T(8,128)(2,1)S(1)}, bf16[9,12,16,128]{3,2,1,0:T(8,128)(2,1)S(1)}, u32[]{:S(2)}, u32[]{:S(2)}) collective-permute-start(bf16[9,12,16,128]{3,2,1,0:T(8,128)(2,1)S(1)} %get-tuple-element.66), channel_id=1, source_target_pairs={{0,8},{8,0},{1,9},{9,1},{2,10},{10,2},{3,11},{11,3},{4,12},{12,4},... | collective-permute-start | bytes 1327112 | tf_op jit(solution)/shard_map/ppermute | solution.py:753
  48.4 2.1 %collective-permute-start.12 = (bf16[144,16,128]{2,1,0:T(8,128)(2,1)S(1)}, bf16[144,16,128]{2,1,0:T(8,128)(2,1)S(1)}, u32[]{:S(2)}, u32[]{:S(2)}) collective-permute-start(bf16[144,16,128]{2,1,0:T(8,128)(2,1)S(1)} %coarse_weight_level.3), channel_id=1, source_target_pairs={{0,8},{8,0},{1,9},{9,1},{2,10},{10,2},{3,11},{11,3},{4,12},{12,4},... | collective-permute-start | bytes 1769480 | tf_op jit(solution)/shard_map/ppermute | solution.py:764
  51.4 9.9 %copy-start = (bf16[3,3,256,256]{3,2,1,0:T(8,128)(2,1)S(1)}, bf16[3,3,256,256]{3,2,1,0:T(8,128)(2,1)}, u32[]{:S(2)}) copy-start(bf16[3,3,256,256]{3,2,1,0:T(8,128)(2,1)} %weight_ref.5) | copy-start | bytes 3538948
  51.4 26.3 %all-to-all-start.1 = ((bf16[64,4,16,128]{3,2,1,0:T(8,128)(2,1)}), bf16[64,4,16,128]{3,2,1,0:T(8,128)(2,1)S(1)}, u32[]{:S(2)}, u32[]{:S(2)}) async-start(bf16[64,4,16,128]{3,2,1,0:T(8,128)(2,1)} %bitcast.7), calls=%async_computation.1 | async-start | bytes 2097152 | tf_op jit(solution)/shard_map/all_to_all | solution.py:625
  64.8 20.1 %collective-permute-start.5 = (bf16[2,2,32,256]{3,2,1,0:T(8,128)(2,1)}, bf16[2,2,32,256]{3,2,1,0:T(8,128)(2,1)S(1)}, u32[]{:S(2)}, u32[]{:S(2)}) collective-permute-start(bf16[2,2,32,256]{3,2,1,0:T(8,128)(2,1)} %get-tuple-element.70), channel_id=1, source_target_pairs={{0,1},{1,0},{2,3},{3,2},{4,5},{5,4},{6,7},{7,6},{8,9},{9,8},{10,11... | collective-permute-start | bytes 196616 | tf_op jit(solution)/shard_map/ppermute | solution.py:769
  65.9 19.1 %collective-permute-start.6 = (bf16[2,2,32,256]{3,2,1,0:T(8,128)(2,1)}, bf16[2,2,32,256]{3,2,1,0:T(8,128)(2,1)S(1)}, u32[]{:S(2)}, u32[]{:S(2)}) collective-permute-start(bf16[2,2,32,256]{3,2,1,0:T(8,128)(2,1)} %get-tuple-element.71), channel_id=1, source_target_pairs={{0,2},{1,3},{2,0},{3,1},{4,6},{5,7},{6,4},{7,5},{8,10},{9,11},{10,... | collective-permute-start | bytes 196616 | tf_op jit(solution)/shard_map/ppermute | solution.py:769
  67.1 18.0 %collective-permute-start.7 = (bf16[2,2,32,256]{3,2,1,0:T(8,128)(2,1)}, bf16[2,2,32,256]{3,2,1,0:T(8,128)(2,1)S(1)}, u32[]{:S(2)}, u32[]{:S(2)}) collective-permute-start(bf16[2,2,32,256]{3,2,1,0:T(8,128)(2,1)} %get-tuple-element.72), channel_id=1, source_target_pairs={{0,3},{1,2},{2,1},{3,0},{4,7},{5,6},{6,5},{7,4},{8,11},{9,10},{10,... | collective-permute-start | bytes 196616 | tf_op jit(solution)/shard_map/ppermute | solution.py:769
  67.5 17.5 %collective-permute-start.8 = (bf16[2,2,32,256]{3,2,1,0:T(8,128)(2,1)S(1)}, bf16[2,2,32,256]{3,2,1,0:T(8,128)(2,1)S(1)}, u32[]{:S(2)}, u32[]{:S(2)}) collective-permute-start(bf16[2,2,32,256]{3,2,1,0:T(8,128)(2,1)S(1)} %get-tuple-element.73), channel_id=1, source_target_pairs={{0,4},{1,5},{2,6},{3,7},{4,0},{5,1},{6,2},{7,3},{8,12},{9,13},{10,... | collective-permute-start | bytes 196616 | tf_op jit(solution)/shard_map/ppermute | solution.py:769
  70.0 15.0 %copy-start.7 = (bf16[2,2,32,256]{3,2,1,0:T(8,128)(2,1)S(1)}, bf16[2,2,32,256]{3,2,1,0:T(8,128)(2,1)}, u32[]{:S(2)}) copy-start(bf16[2,2,32,256]{3,2,1,0:T(8,128)(2,1)} %copy-done.6) | copy-start | bytes 196612
  70.0 15.0 %collective-permute-start.9 = (bf16[2,2,32,256]{3,2,1,0:T(8,128)(2,1)S(1)}, bf16[2,2,32,256]{3,2,1,0:T(8,128)(2,1)S(1)}, u32[]{:S(2)}, u32[]{:S(2)}) collective-permute-start(bf16[2,2,32,256]{3,2,1,0:T(8,128)(2,1)S(1)} %get-tuple-element.74), channel_id=1, source_target_pairs={{0,5},{1,4},{2,7},{3,6},{4,1},{5,0},{6,3},{7,2},{8,13},{9,12},{10,... | collective-permute-start | bytes 196616 | tf_op jit(solution)/shard_map/ppermute | solution.py:769
  78.9 21.1 %all-to-all-start.2 = ((bf16[64,4,16,128]{3,2,1,0:T(8,128)(2,1)}), bf16[64,4,16,128]{3,2,1,0:T(8,128)(2,1)S(1)}, u32[]{:S(2)}, u32[]{:S(2)}) async-start(bf16[64,4,16,128]{3,2,1,0:T(8,128)(2,1)} %sum_parts.1), calls=%async_computation.2 | async-start | bytes 2097152 | tf_op jit(solution)/shard_map/all_to_all | solution.py:633
  85.1 19.8 %collective-permute-start.10 = (bf16[2,2,32,256]{3,2,1,0:T(8,128)(2,1)S(1)}, bf16[2,2,32,256]{3,2,1,0:T(8,128)(2,1)S(1)}, u32[]{:S(2)}, u32[]{:S(2)}) collective-permute-start(bf16[2,2,32,256]{3,2,1,0:T(8,128)(2,1)S(1)} %get-tuple-element.77), channel_id=1, source_target_pairs={{0,6},{1,7},{2,4},{3,5},{4,2},{5,3},{6,0},{7,1},{8,14},{9,15},{10,... | collective-permute-start | bytes 196616 | tf_op jit(solution)/shard_map/ppermute | solution.py:769
  87.4 17.5 %collective-permute-start.11 = (bf16[2,2,32,256]{3,2,1,0:T(8,128)(2,1)S(1)}, bf16[2,2,32,256]{3,2,1,0:T(8,128)(2,1)S(1)}, u32[]{:S(2)}, u32[]{:S(2)}) collective-permute-start(bf16[2,2,32,256]{3,2,1,0:T(8,128)(2,1)S(1)} %get-tuple-element.78), channel_id=1, source_target_pairs={{0,7},{1,6},{2,5},{3,4},{4,3},{5,2},{6,1},{7,0},{8,15},{9,14},{10,... | collective-permute-start | bytes 196616 | tf_op jit(solution)/shard_map/ppermute | solution.py:769
  100.0 7.3 %collective-permute-start.13 = (bf16[256,16,128]{2,1,0:T(8,128)(2,1)S(1)}, bf16[256,16,128]{2,1,0:T(8,128)(2,1)S(1)}, u32[]{:S(2)}, u32[]{:S(2)}) collective-permute-start(bf16[256,16,128]{2,1,0:T(8,128)(2,1)S(1)} %bitcast.12), channel_id=1, source_target_pairs={{0,8},{8,0},{1,9},{9,1},{2,10},{10,2},{3,11},{11,3},{4,12},{12,4},... | collective-permute-start | bytes 3145736 | tf_op jit(solution)/shard_map/ppermute | solution.py:779
  (1 other events, 0.6 us)

commit v7 on v6

--- a/solution.py
+++ b/solution.py
@@ -654,60 +654,47 @@
     )(place, half, *earlier)
 
 
-def start_kernel(
-    place_ref, pre_ref, input_ref, cot_ref, fine_pre_ref, pieces_ref, near_ref, far_ref, rows, row_sems, sems
-):
-    peers, _, samples, lines, _, _ = pieces_ref.shape
+def start_kernel(place_ref, cot_ref, pre_ref, near_ref, far_ref, rows, sems):
+    samples = cot_ref.shape[0]
     odd = place_ref[0] >= 2
     last = cot_ref.shape[1] - 1
-    row_copies = []
-    for a, ref in enumerate((cot_ref, fine_pre_ref)):
-        for e, line in enumerate((jnp.where(odd, 0, last), jnp.where(odd, last, 0))):
-            for s in range(samples):
-                row_copies.append(
-                    pltpu.make_async_copy(ref.at[s, line], rows.at[a, e, s], row_sems.at[len(row_copies)])
-                )
-    copies = []
-    for c in range(peers):
-        for a, ref in enumerate((pre_ref, input_ref)):
-            for s in range(samples):
-                copies.append(
-                    pltpu.make_async_copy(
-                        ref.at[s, pl.ds(c * lines, lines)], pieces_ref.at[c, a, s], sems.at[len(copies)]
-                    )
-                )
-    for copy in row_copies + copies:
-        copy.start()
-    for copy in row_copies:
-        copy.wait()
-    for e, out_ref in enumerate((near_ref, far_ref)):
-        for s in range(samples):
-            grad = rows[0, e, s].astype(F32) * silu_grad(rows[1, e, s].astype(F32))
-            out_ref[s] = grad.astype(BF16)
-    for copy in copies:
-        copy.wait()
-
-
-def start_level(place, pre, values, cot, fine_pre, peers):
-    samples, lines, own, wide = pre.shape
-    fine_wide, c3 = cot.shape[2:]
+    ends = (jnp.where(odd, 0, last), jnp.where(odd, last, 0))
+    copies = [
+        [
+            pltpu.make_async_copy(ref.at[s, line], rows.at[a, e, s], sems.at[a, e, s])
+            for a, ref in enumerate((cot_ref, pre_ref))
+        ]
+        for e, line in enumerate(ends) for s in range(samples)
+    ]
+    for pair in copies:
+        for copy in pair:
+            copy.start()
+    for k, pair in enumerate(copies):
+        for copy in pair:
+            copy.wait()
+        e, s = divmod(k, samples)
+        grad = rows[0, e, s].astype(F32) * silu_grad(rows[1, e, s].astype(F32))
+        (near_ref, far_ref)[e][s] = grad.astype(BF16)
+
+
+def start_level(place, cot, fine_pre):
+    samples, _, wide, c3 = cot.shape
     hbm = pl.BlockSpec(memory_space=pltpu.HBM)
     vmem = pl.BlockSpec(memory_space=pltpu.VMEM)
-    edge = jax.ShapeDtypeStruct((samples, fine_wide, c3), BF16)
+    edge = jax.ShapeDtypeStruct((samples, wide, c3), BF16)
     return pl.pallas_call(
         start_kernel,
-        in_specs=[pl.BlockSpec(memory_space=pltpu.SMEM), hbm, hbm, hbm, hbm],
-        out_specs=[vmem, vmem, vmem],
-        out_shape=[jax.ShapeDtypeStruct((peers, 2, samples, lines // peers, own, wide), BF16), edge, edge],
+        in_specs=[pl.BlockSpec(memory_space=pltpu.SMEM), hbm, hbm],
+        out_specs=[vmem, vmem],
+        out_shape=[edge, edge],
         scratch_shapes=[
-            pltpu.VMEM((2, 2, samples, fine_wide, c3), BF16),
-            pltpu.SemaphoreType.DMA((4 * samples,)),
-            pltpu.SemaphoreType.DMA((peers * 2 * samples,)),
-        ],
-        compiler_params=params(VMEM),
-        cost_estimate=cost(1e7, 3e6),
+            pltpu.VMEM((2, 2, samples, wide, c3), BF16),
+            pltpu.SemaphoreType.DMA((2, 2, samples)),
+        ],
+        compiler_params=params(VMEM),
+        cost_estimate=cost(1e7, 2e6),
         name="start",
-    )(place, *(in_hbm(a) for a in (pre, values, cot, fine_pre)))
+    )(place, in_hbm(cot), in_hbm(fine_pre))
 
 
 def swapped(near, far):
@@ -733,9 +720,9 @@
     place = (core + 2 * (lax.axis_index("xl").astype(jnp.int32))).reshape(1)
     other_place = (1 - core + 2 * (lax.axis_index("xl").astype(jnp.int32))).reshape(1)
 
-    pieces, edge_near, edge_far = start_level(
-        place, coarse_pre.transpose(0, 1, 3, 2), coarse_input.transpose(0, 1, 3, 2), fine_cotangent, fine_pre, peers
-    )
+    edge_near, edge_far = start_level(place, fine_cotangent, fine_pre)
+    pieces = jnp.stack([coarse_pre, coarse_input]).reshape(2, samples, peers, lines // peers, wide, own)
+    pieces = pieces.transpose(2, 0, 1, 3, 5, 4)
     edge_near, edge_far = swapped(edge_near, edge_far)
     received = lax.all_to_all(pieces, CHAN, 0, 0, tiled=True)
 

time: 109 us -> 108 us (level)
  Pallas kernels: 31.4 us -> 29.6 us
  waiting for transfers between devices: 27.3 us -> 25.6 us
    ppermute x4, waiting for transfers between devices: 6.7 us -> 4.76 us  [swapped(): return (lax.ppermute(near, ALL, inside), lax.ppermute(far, ALL, outside))]
    pallas_call x1, Pallas kernels: 3.32 us -> 1.53 us  [start_level(): pl.pallas_call(start_kernel, in_specs=[pl.BlockSpec(memory_space=pltpu.SM...]
    unnamed x16 -> x20, local copies, waits for them, and re-layouts: 2.2 us -> 2.22 us
  transfers between devices with their start and end apart: 17 -> 17, of which waited for: 6 -> 6; matrix products, arithmetic and copies ran while one was open for 0% -> 1% of each run, Pallas kernels for 22% -> 22%
where the time goes in v7:
time: 108 us; the launch traced here: 107 us
  starting transfers between devices  47.6 us (44%)
  Pallas kernels  29.6 us (27%)
  waiting for transfers between devices  25.6 us (24%)
  local copies, waits for them, and re-layouts  2.22 us (2%)
  between operations  1.12 us (1%)
    ppermute x4, starting transfers between devices, swapped(): return (lax.ppermute(near, ALL, inside), lax.ppermute(far, ALL, outside))  12.8 us
    all_to_all x1, waiting for transfers between devices, grad_sums(): lax.all_to_all(summed, CHIPS, 0, 0, tiled=True)  11.4 us
    all_to_all x1, starting transfers between devices, grad_sums(): lax.all_to_all(parts.reshape(chips, each, 16, 128), CHIPS, 0, 0, tiled=True)  10.4 us
    ppermute x7, starting transfers between devices, home(): return lax.ppermute(piece, CHAN, [(i, i ^ k) for i in range(peers)])  9.84 us
    all_to_all x1, waiting for transfers between devices, grad_sums(): lax.all_to_all(parts.reshape(chips, each, 16, 128), CHIPS, 0, 0, tiled=True)  6.5 us
    pallas_call x1, Pallas kernels, fine_level(): pl.pallas_call(functools.partial(fine_kernel, scale=1.0 / math.sqrt(fine_...  6.43 us
    all_to_all x1, starting transfers between devices, grad_sums(): lax.all_to_all(summed, CHIPS, 0, 0, tiled=True)  6.05 us
    ppermute x1, starting transfers between devices, shards(): other = lax.ppermute(mine, 'core', SWAP)  4.88 us
  transfers between devices with their start and end apart: 17, of which 6 were waited for; matrix products, arithmetic and copies ran while one was open for 1% of the time, Pallas kernels for 22%

profile of v7, /device:TPU:1, one launch (start us, length us, event | category | flops | bytes accessed | tf_op | source)
XLA Modules:
  0.0 107.2 jit_solution(10968639168419426842)
XLA Ops:
  0.7 1.5 %start.1 = (bf16[2,512,128]{2,1,0:T(8,128)(2,1)S(1)}, bf16[2,512,128]{2,1,0:T(8,128)(2,1)S(1)}) custom-call(s32[1]{0:T(128)} %bitcast.place_ref, bf16[2,4,512,128]{3,2,1,0:T(8,128)(2,1)} %cot_ref.3, bf16[2,4,512,128]{3,2,1,0:T(8,128)(2,1)} %pre_ref.3), custom_call_target="tpu_custom_call" | custom-call | flops 10000000 | bytes 2000000 | tf_op jit(solution)/shard_map/start/pallas_call | solution.py:685
  2.2 2.1 %collective-permute-start = (bf16[2,512,128]{2,1,0:T(8,128)(2,1)S(1)}, bf16[2,512,128]{2,1,0:T(8,128)(2,1)S(1)}, u32[]{:S(2)}, u32[]{:S(2)}) collective-permute-start(bf16[2,512,128]{2,1,0:T(8,128)(2,1)S(1)} %get-tuple-element.46), channel_id=1, source_target_pairs={{0,1},{1,0},{2,3},{3,2},{4,5},{5,4},{6,7},{7,6},{8,9},{9,8},{10,11... | collective-permute-start | bytes 786440 | tf_op jit(solution)/shard_map/ppermute | solution.py:707
  4.3 5.4 %collective-permute-start.1 = (bf16[2,512,128]{2,1,0:T(8,128)(2,1)S(1)}, bf16[2,512,128]{2,1,0:T(8,128)(2,1)S(1)}, u32[]{:S(2)}, u32[]{:S(2)}) collective-permute-start(bf16[2,512,128]{2,1,0:T(8,128)(2,1)S(1)} %get-tuple-element.47), channel_id=1, source_target_pairs={{1,2},{3,4},{5,6},{7,8},{9,10},{11,12},{13,14},{15,16},{17,18},{19... | collective-permute-start | bytes 786440 | tf_op jit(solution)/shard_map/ppermute | solution.py:707
  10.8 3.6 %all-to-all-start = ((bf16[8,2,2,2,32,256]{5,4,3,2,1,0:T(8,128)(2,1)}), bf16[8,2,2,2,32,256]{5,4,3,2,1,0:T(8,128)(2,1)S(1)}, u32[]{:S(2)}, u32[]{:S(2)}) async-start(bf16[8,2,2,2,32,256]{5,4,3,2,1,0:T(8,128)(2,1)} %copy_bitcast_fusion), calls=%async_computation | async-start | bytes 2097152 | tf_op jit(solution)/shard_map/all_to_all | solution.py:727
  14.4 4.3 %box_level.1 = (bf16[2,4,512,128]{3,2,1,0:T(8,128)(2,1)}, bf16[2,256,1152]{2,1,0:T(8,128)(2,1)}, bf16[2,2,512,128]{3,2,1,0:T(8,128)(2,1)S(1)}, f32[2,2,256,256]{3,2,1,0:T(8,128)S(1)}, bf16[1152,256]{1,0:T(8,128)(2,1)S(1)}) custom-call(bf16[2,4,512,128]{3,2,1,0:T(8,128)(2,1)} %cot_ref.3, bf16[2,4,512,128]{3,2,1,0:T(8,128)(2,1)} %pre_ref.3, ...), custom_call_target="tpu_custom_call" | custom-call | flops 1200000000 | bytes 8000000 | tf_op jit(solution)/shard_map/box_level/pallas_call | solution.py:102
  19.3 1.5 %edge_level.1 = (f32[2,2,256,256]{3,2,1,0:T(8,128)S(1)}, bf16[2,256,384]{2,1,0:T(8,128)(2,1)}, bf16[2,256,384]{2,1,0:T(8,128)(2,1)}) custom-call(s32[1]{0:T(128)} %bitcast.place_ref, bf16[2,512,128]{2,1,0:T(8,128)(2,1)S(1)} %collective-permute-done.near_ref, bf16[2,512,128]{2,1,0:T(8,128)(2,1)S(1)} %collective-permute-done.1.far_ref, ...), custom_call_target="tpu_custom_call" | custom-call | flops 99999997952 | bytes 4000000 | tf_op jit(solution)/shard_map/edge_level/pallas_call | solution.py:154
  20.8 6.4 %fine_level.1 = (bf16[2,4,512,128]{3,2,1,0:T(8,128)(2,1)}, bf16[9,4,16,128]{3,2,1,0:T(8,128)(2,1)S(1)}, bf16[9,4,16,128]{3,2,1,0:T(8,128)(2,1)S(1)}) custom-call(s32[1]{0:T(128)} %bitcast.place_ref, bf16[2,4,512,128]{3,2,1,0:T(8,128)(2,1)} %get-tuple-element.45.grad_ref, bf16[2,512,128]{2,1,0:T(8,128)(2,1)S(1)} %collective-permute-done.near_ref, ...), custom_call_target="tpu_custom_call" | custom-call | flops 5000000000 | bytes 8000000 | tf_op jit(solution)/shard_map/fine_level/pallas_call | solution.py:237
  27.9 2.1 %all-to-all-done.pre_ref.input_ref = bf16[8,2,2,2,32,256]{5,4,3,2,1,0:T(8,128)(2,1)S(1)} async-done(((bf16[8,2,2,2,32,256]{5,4,3,2,1,0:T(8,128)(2,1)}), bf16[8,2,2,2,32,256]{5,4,3,2,1,0:T(8,128)(2,1)S(1)}, u32[]{:S(2)}, u32[]{:S(2)}) %all-to-all-start) | async-done | bytes 1048608 | tf_op jit(solution)/shard_map/all_to_all | solution.py:727
  30.7 5.1 %collective-permute-start.3 = (bf16[2,256,256]{2,1,0:T(8,128)(2,1)S(1)}, bf16[2,256,256]{2,1,0:T(8,128)(2,1)S(1)}, u32[]{:S(2)}, u32[]{:S(2)}) collective-permute-start(bf16[2,256,256]{2,1,0:T(8,128)(2,1)S(1)} %get-tuple-element.57.far_ref.second_ref), channel_id=1, source_target_pairs={{1,2},{3,4},{5,6},{7,8},{9,10},{11,12},{13,14},{15,16},{17,18},{19... | collective-permute-start | bytes 786440 | tf_op jit(solution)/shard_map/ppermute | solution.py:707
  36.8 1.3 %up_level.1 = (bf16[9,12,16,128]{3,2,1,0:T(8,128)(2,1)S(1)}, bf16[9,12,16,128]{3,2,1,0:T(8,128)(2,1)S(1)}) custom-call(s32[1]{0:T(128)} %bitcast.place_ref, bf16[8,2,2,2,32,256]{5,4,3,2,1,0:T(8,128)(2,1)S(1)} %all-to-all-done.pre_ref.input_ref, bf16[2,256,1152]{2,1,0:T(8,128)(2,1)S(1)} %copy-done.1, bf16[2,256,384]{2,1,0:T(8,128)(2,1)S(1)} %copy-done.2, ...), custom_call_target="tpu_custom_call" | custom-call | flops 1000000000 | bytes 5000000 | tf_op jit(solution)/shard_map/up_level/pallas_call | solution.py:341
  38.1 1.8 %own_weight_level.1.own_ref = f32[3,256,768]{2,1,0:T(8,128)S(1)} custom-call(s32[1]{0:T(128)} %bitcast.place_ref, bf16[8,2,2,2,32,256]{5,4,3,2,1,0:T(8,128)(2,1)S(1)} %all-to-all-done.pre_ref.input_ref, bf16[2,256,256]{2,1,0:T(8,128)(2,1)S(1)} %get-tuple-element.57.far_ref.second_ref, bf16[2,256,256]{2,1,0:T(8,128)(2,1)S(1)} %get-tuple-element.56.near_ref.third_ref), custom_call_target="tpu_custom_call" | custom-call | flops 99999997952 | bytes 4000000 | tf_op jit(solution)/shard_map/own_weight_level/pallas_call | solution.py:400
  40.8 4.1 %collective-permute-done.3.first_ref.from_far_ref = bf16[2,256,256]{2,1,0:T(8,128)(2,1)S(1)} collective-permute-done((bf16[2,256,256]{2,1,0:T(8,128)(2,1)S(1)}, bf16[2,256,256]{2,1,0:T(8,128)(2,1)S(1)}, u32[]{:S(2)}, u32[]{:S(2)}) %collective-permute-start.3) | collective-permute-done | bytes 262176 | tf_op jit(solution)/shard_map/ppermute | solution.py:707
  46.2 1.3 %coarse_weight_level.2.refs_0_ = bf16[144,16,128]{2,1,0:T(8,128)(2,1)S(1)} custom-call(s32[1]{0:T(128)} %bitcast.place_ref, bf16[8,2,2,2,32,256]{5,4,3,2,1,0:T(8,128)(2,1)S(1)} %all-to-all-done.pre_ref.input_ref, bf16[2,256,256]{2,1,0:T(8,128)(2,1)S(1)} %collective-permute-done.3.first_ref.from_far_ref, ...), custom_call_target="tpu_custom_call" | custom-call | flops 400000000 | bytes 2000000 | tf_op jit(solution)/shard_map/coarse_weight_level/pallas_call | solution.py:455
  49.1 10.4 %all-to-all-start.1 = ((bf16[64,4,16,128]{3,2,1,0:T(8,128)(2,1)}), bf16[64,4,16,128]{3,2,1,0:T(8,128)(2,1)S(1)}, u32[]{:S(2)}, u32[]{:S(2)}) async-start(bf16[64,4,16,128]{3,2,1,0:T(8,128)(2,1)} %bitcast.8), calls=%async_computation.1 | async-start | bytes 2097152 | tf_op jit(solution)/shard_map/all_to_all | solution.py:625
  59.5 2.9 %coarse_input_level.1 = (bf16[2,2,32,256]{3,2,1,0:T(8,128)(2,1)S(1)}, bf16[2,2,32,256]{3,2,1,0:T(8,128)(2,1)}, bf16[2,2,32,256]{3,2,1,0:T(8,128)(2,1)}, bf16[2,2...) custom-call(s32[1]{0:T(128)} %bitcast.1.chan_ref, ...), custom_call_target="tpu_custom_call" | custom-call | flops 1300000000 | bytes 3000000 | tf_op jit(solution)/shard_map/coarse_input_level/pallas_call | solution.py:501
  65.7 2.5 %collective-permute-start.8 = (bf16[2,2,32,256]{3,2,1,0:T(8,128)(2,1)S(1)}, bf16[2,2,32,256]{3,2,1,0:T(8,128)(2,1)S(1)}, u32[]{:S(2)}, u32[]{:S(2)}) collective-permute-start(bf16[2,2,32,256]{3,2,1,0:T(8,128)(2,1)S(1)} %get-tuple-element.71), channel_id=1, source_target_pairs={{0,4},{1,5},{2,6},{3,7},{4,0},{5,1},{6,2},{7,3},{8,12},{9,13},{10,... | collective-permute-start | bytes 196616 | tf_op jit(solution)/shard_map/ppermute | solution.py:756
  69.4 6.5 %all-to-all-done.1.parts_ref = bf16[64,4,16,128]{3,2,1,0:T(8,128)(2,1)S(1)} async-done(((bf16[64,4,16,128]{3,2,1,0:T(8,128)(2,1)}), bf16[64,4,16,128]{3,2,1,0:T(8,128)(2,1)S(1)}, u32[]{:S(2)}, u32[]{:S(2)}) %all-to-all-start.1) | async-done | bytes 1048608 | tf_op jit(solution)/shard_map/all_to_all | solution.py:625
  75.9 1.2 %sum_parts.1 = bf16[64,4,16,128]{3,2,1,0:T(8,128)(2,1)} custom-call(bf16[64,4,16,128]{3,2,1,0:T(8,128)(2,1)S(1)} %all-to-all-done.1.parts_ref), custom_call_target="tpu_custom_call" | custom-call | flops 1000000 | bytes 1300000 | tf_op jit(solution)/shard_map/sum_parts/pallas_call | solution.py:626
  77.2 6.0 %all-to-all-start.2 = ((bf16[64,4,16,128]{3,2,1,0:T(8,128)(2,1)}), bf16[64,4,16,128]{3,2,1,0:T(8,128)(2,1)S(1)}, u32[]{:S(2)}, u32[]{:S(2)}) async-start(bf16[64,4,16,128]{3,2,1,0:T(8,128)(2,1)} %sum_parts.1), calls=%async_computation.2 | async-start | bytes 2097152 | tf_op jit(solution)/shard_map/all_to_all | solution.py:633
  83.3 2.3 %collective-permute-start.10 = (bf16[2,2,32,256]{3,2,1,0:T(8,128)(2,1)S(1)}, bf16[2,2,32,256]{3,2,1,0:T(8,128)(2,1)S(1)}, u32[]{:S(2)}, u32[]{:S(2)}) collective-permute-start(bf16[2,2,32,256]{3,2,1,0:T(8,128)(2,1)S(1)} %get-tuple-element.75), channel_id=1, source_target_pairs={{0,6},{1,7},{2,4},{3,5},{4,2},{5,3},{6,0},{7,1},{8,14},{9,15},{10,... | collective-permute-start | bytes 196616 | tf_op jit(solution)/shard_map/ppermute | solution.py:756
  86.8 11.4 %all-to-all-done.2 = bf16[64,4,16,128]{3,2,1,0:T(8,128)(2,1)S(1)} async-done(((bf16[64,4,16,128]{3,2,1,0:T(8,128)(2,1)}), bf16[64,4,16,128]{3,2,1,0:T(8,128)(2,1)S(1)}, u32[]{:S(2)}, u32[]{:S(2)}) %all-to-all-start.2) | async-done | bytes 1048608 | tf_op jit(solution)/shard_map/all_to_all | solution.py:633
  98.2 4.9 %collective-permute-start.13 = (bf16[256,16,128]{2,1,0:T(8,128)(2,1)S(1)}, bf16[256,16,128]{2,1,0:T(8,128)(2,1)S(1)}, u32[]{:S(2)}, u32[]{:S(2)}) collective-permute-start(bf16[256,16,128]{2,1,0:T(8,128)(2,1)S(1)} %bitcast.14), channel_id=1, source_target_pairs={{0,8},{8,0},{1,9},{9,1},{2,10},{10,2},{3,11},{11,3},{4,12},{12,4},... | collective-permute-start | bytes 3145736 | tf_op jit(solution)/shard_map/ppermute | solution.py:766
  104.0 1.5 %unpack.2 = (f32[9,384,128]{2,1,0:T(8,128)}, f32[9,256,256]{2,1,0:T(8,128)}) custom-call(s32[1]{0:T(128)} %bitcast.place_ref, bf16[256,16,128]{2,1,0:T(8,128)(2,1)S(1)} %bitcast.15), custom_call_target="tpu_custom_call" | custom-call | flops 1 | bytes 1 | tf_op jit(solution)/shard_map/unpack/pallas_call | solution.py:639
  105.5 1.5 %unpack.3 = (f32[9,384,128]{2,1,0:T(8,128)}, f32[9,256,256]{2,1,0:T(8,128)}) custom-call(s32[1]{0:T(128)} %bitcast.7.place_ref, bf16[256,16,128]{2,1,0:T(8,128)(2,1)S(1)} %collective-permute-done.13.parts_ref, f32[9,384,128]{2,1,0:T(8,128)} %get-tuple-element.82.rest_0_, ...), custom_call_target="tpu_custom_call", output_to_operand_aliasing={{0}: (2, {}), {1}: (3, {})} | custom-call | flops 1 | bytes 1 | tf_op jit(solution)/shard_map/unpack/pallas_call | solution.py:639
  (48 shorter events, 14.3 us)
Async XLA Ops:
  0.6 9.1 %copy-start.9 = (bf16[2,16,256,32]{2,3,1,0:T(8,128)(2,1)S(1)}, bf16[2,16,256,32]{2,3,1,0:T(8,128)(2,1)}, u32[]{:S(2)}) copy-start(bf16[2,16,256,32]{2,3,1,0:T(8,128)(2,1)} %param.8) | copy-start | bytes 1572868
  0.6 9.1 %copy-start.8 = (bf16[2,16,256,32]{2,3,1,0:T(8,128)(2,1)S(1)}, bf16[2,16,256,32]{2,3,1,0:T(8,128)(2,1)}, u32[]{:S(2)}) copy-start(bf16[2,16,256,32]{2,3,1,0:T(8,128)(2,1)} %param.7) | copy-start | bytes 1572868
  2.2 16.5 %collective-permute-start = (bf16[2,512,128]{2,1,0:T(8,128)(2,1)S(1)}, bf16[2,512,128]{2,1,0:T(8,128)(2,1)S(1)}, u32[]{:S(2)}, u32[]{:S(2)}) collective-permute-start(bf16[2,512,128]{2,1,0:T(8,128)(2,1)S(1)} %get-tuple-element.46), channel_id=1, source_target_pairs={{0,1},{1,0},{2,3},{3,2},{4,5},{5,4},{6,7},{7,6},{8,9},{9,8},{10,11... | collective-permute-start | bytes 786440 | tf_op jit(solution)/shard_map/ppermute | solution.py:707
  4.3 15.0 %collective-permute-start.1 = (bf16[2,512,128]{2,1,0:T(8,128)(2,1)S(1)}, bf16[2,512,128]{2,1,0:T(8,128)(2,1)S(1)}, u32[]{:S(2)}, u32[]{:S(2)}) collective-permute-start(bf16[2,512,128]{2,1,0:T(8,128)(2,1)S(1)} %get-tuple-element.47), channel_id=1, source_target_pairs={{1,2},{3,4},{5,6},{7,8},{9,10},{11,12},{13,14},{15,16},{17,18},{19... | collective-permute-start | bytes 786440 | tf_op jit(solution)/shard_map/ppermute | solution.py:707
  10.8 19.1 %all-to-all-start = ((bf16[8,2,2,2,32,256]{5,4,3,2,1,0:T(8,128)(2,1)}), bf16[8,2,2,2,32,256]{5,4,3,2,1,0:T(8,128)(2,1)S(1)}, u32[]{:S(2)}, u32[]{:S(2)}) async-start(bf16[8,2,2,2,32,256]{5,4,3,2,1,0:T(8,128)(2,1)} %copy_bitcast_fusion), calls=%async_computation | async-start | bytes 2097152 | tf_op jit(solution)/shard_map/all_to_all | solution.py:727
  27.9 7.9 %copy-start.2 = (bf16[2,256,384]{2,1,0:T(8,128)(2,1)S(1)}, bf16[2,256,384]{2,1,0:T(8,128)(2,1)}, u32[]{:S(2)}) copy-start(bf16[2,256,384]{2,1,0:T(8,128)(2,1)} %get-tuple-element.59.box_low_ref) | copy-start | bytes 1179652
  30.0 5.9 %copy-start.1 = (bf16[2,256,1152]{2,1,0:T(8,128)(2,1)S(1)}, bf16[2,256,1152]{2,1,0:T(8,128)(2,1)}, u32[]{:S(2)}) copy-start(bf16[2,256,1152]{2,1,0:T(8,128)(2,1)} %get-tuple-element.58.box_ref) | copy-start | bytes 3538948
  30.0 5.9 %copy-start.3 = (bf16[2,256,384]{2,1,0:T(8,128)(2,1)S(1)}, bf16[2,256,384]{2,1,0:T(8,128)(2,1)}, u32[]{:S(2)}) copy-start(bf16[2,256,384]{2,1,0:T(8,128)(2,1)} %get-tuple-element.60.box_high_ref) | copy-start | bytes 1179652
  30.6 10.2 %collective-permute-start.2 = (bf16[2,256,256]{2,1,0:T(8,128)(2,1)S(1)}, bf16[2,256,256]{2,1,0:T(8,128)(2,1)S(1)}, u32[]{:S(2)}, u32[]{:S(2)}) collective-permute-start(bf16[2,256,256]{2,1,0:T(8,128)(2,1)S(1)} %get-tuple-element.56.near_ref.third_ref), channel_id=1, source_target_pairs={{0,1},{1,0},{2,3},{3,2},{4,5},{5,4},{6,7},{7,6},{8,9},{9,8},{10,11... | collective-permute-start | bytes 786440 | tf_op jit(solution)/shard_map/ppermute | solution.py:707
  30.7 14.3 %collective-permute-start.3 = (bf16[2,256,256]{2,1,0:T(8,128)(2,1)S(1)}, bf16[2,256,256]{2,1,0:T(8,128)(2,1)S(1)}, u32[]{:S(2)}, u32[]{:S(2)}) collective-permute-start(bf16[2,256,256]{2,1,0:T(8,128)(2,1)S(1)} %get-tuple-element.57.far_ref.second_ref), channel_id=1, source_target_pairs={{1,2},{3,4},{5,6},{7,8},{9,10},{11,12},{13,14},{15,16},{17,18},{19... | collective-permute-start | bytes 786440 | tf_op jit(solution)/shard_map/ppermute | solution.py:707
  38.0 1.9 %collective-permute-start.4 = (bf16[9,12,16,128]{3,2,1,0:T(8,128)(2,1)S(1)}, bf16[9,12,16,128]{3,2,1,0:T(8,128)(2,1)S(1)}, u32[]{:S(2)}, u32[]{:S(2)}) collective-permute-start(bf16[9,12,16,128]{3,2,1,0:T(8,128)(2,1)S(1)} %get-tuple-element.64), channel_id=1, source_target_pairs={{0,8},{8,0},{1,9},{9,1},{2,10},{10,2},{3,11},{11,3},{4,12},{12,4},... | collective-permute-start | bytes 1327112 | tf_op jit(solution)/shard_map/ppermute | solution.py:740
  46.2 2.1 %collective-permute-start.12 = (bf16[144,16,128]{2,1,0:T(8,128)(2,1)S(1)}, bf16[144,16,128]{2,1,0:T(8,128)(2,1)S(1)}, u32[]{:S(2)}, u32[]{:S(2)}) collective-permute-start(bf16[144,16,128]{2,1,0:T(8,128)(2,1)S(1)} %coarse_weight_level.3), channel_id=1, source_target_pairs={{0,8},{8,0},{1,9},{9,1},{2,10},{10,2},{3,11},{11,3},{4,12},{12,4},... | collective-permute-start | bytes 1769480 | tf_op jit(solution)/shard_map/ppermute | solution.py:751
  49.1 10.4 %copy-start = (bf16[3,3,256,256]{3,2,1,0:T(8,128)(2,1)S(1)}, bf16[3,3,256,256]{3,2,1,0:T(8,128)(2,1)}, u32[]{:S(2)}) copy-start(bf16[3,3,256,256]{3,2,1,0:T(8,128)(2,1)} %weight_ref.5) | copy-start | bytes 3538948
  49.1 26.8 %all-to-all-start.1 = ((bf16[64,4,16,128]{3,2,1,0:T(8,128)(2,1)}), bf16[64,4,16,128]{3,2,1,0:T(8,128)(2,1)S(1)}, u32[]{:S(2)}, u32[]{:S(2)}) async-start(bf16[64,4,16,128]{3,2,1,0:T(8,128)(2,1)} %bitcast.8), calls=%async_computation.1 | async-start | bytes 2097152 | tf_op jit(solution)/shard_map/all_to_all | solution.py:625
  63.1 20.1 %collective-permute-start.5 = (bf16[2,2,32,256]{3,2,1,0:T(8,128)(2,1)}, bf16[2,2,32,256]{3,2,1,0:T(8,128)(2,1)S(1)}, u32[]{:S(2)}, u32[]{:S(2)}) collective-permute-start(bf16[2,2,32,256]{3,2,1,0:T(8,128)(2,1)} %get-tuple-element.68), channel_id=1, source_target_pairs={{0,1},{1,0},{2,3},{3,2},{4,5},{5,4},{6,7},{7,6},{8,9},{9,8},{10,11... | collective-permute-start | bytes 196616 | tf_op jit(solution)/shard_map/ppermute | solution.py:756
  64.1 19.1 %collective-permute-start.6 = (bf16[2,2,32,256]{3,2,1,0:T(8,128)(2,1)}, bf16[2,2,32,256]{3,2,1,0:T(8,128)(2,1)S(1)}, u32[]{:S(2)}, u32[]{:S(2)}) collective-permute-start(bf16[2,2,32,256]{3,2,1,0:T(8,128)(2,1)} %get-tuple-element.69), channel_id=1, source_target_pairs={{0,2},{1,3},{2,0},{3,1},{4,6},{5,7},{6,4},{7,5},{8,10},{9,11},{10,... | collective-permute-start | bytes 196616 | tf_op jit(solution)/shard_map/ppermute | solution.py:756
  65.3 18.0 %collective-permute-start.7 = (bf16[2,2,32,256]{3,2,1,0:T(8,128)(2,1)}, bf16[2,2,32,256]{3,2,1,0:T(8,128)(2,1)S(1)}, u32[]{:S(2)}, u32[]{:S(2)}) collective-permute-start(bf16[2,2,32,256]{3,2,1,0:T(8,128)(2,1)} %get-tuple-element.70), channel_id=1, source_target_pairs={{0,3},{1,2},{2,1},{3,0},{4,7},{5,6},{6,5},{7,4},{8,11},{9,10},{10,... | collective-permute-start | bytes 196616 | tf_op jit(solution)/shard_map/ppermute | solution.py:756
  65.7 17.5 %collective-permute-start.8 = (bf16[2,2,32,256]{3,2,1,0:T(8,128)(2,1)S(1)}, bf16[2,2,32,256]{3,2,1,0:T(8,128)(2,1)S(1)}, u32[]{:S(2)}, u32[]{:S(2)}) collective-permute-start(bf16[2,2,32,256]{3,2,1,0:T(8,128)(2,1)S(1)} %get-tuple-element.71), channel_id=1, source_target_pairs={{0,4},{1,5},{2,6},{3,7},{4,0},{5,1},{6,2},{7,3},{8,12},{9,13},{10,... | collective-permute-start | bytes 196616 | tf_op jit(solution)/shard_map/ppermute | solution.py:756
  68.2 15.0 %copy-start.7 = (bf16[2,2,32,256]{3,2,1,0:T(8,128)(2,1)S(1)}, bf16[2,2,32,256]{3,2,1,0:T(8,128)(2,1)}, u32[]{:S(2)}) copy-start(bf16[2,2,32,256]{3,2,1,0:T(8,128)(2,1)} %copy-done.6) | copy-start | bytes 196612
  68.2 15.0 %collective-permute-start.9 = (bf16[2,2,32,256]{3,2,1,0:T(8,128)(2,1)S(1)}, bf16[2,2,32,256]{3,2,1,0:T(8,128)(2,1)S(1)}, u32[]{:S(2)}, u32[]{:S(2)}) collective-permute-start(bf16[2,2,32,256]{3,2,1,0:T(8,128)(2,1)S(1)} %get-tuple-element.72), channel_id=1, source_target_pairs={{0,5},{1,4},{2,7},{3,6},{4,1},{5,0},{6,3},{7,2},{8,13},{9,12},{10,... | collective-permute-start | bytes 196616 | tf_op jit(solution)/shard_map/ppermute | solution.py:756
  77.2 21.1 %all-to-all-start.2 = ((bf16[64,4,16,128]{3,2,1,0:T(8,128)(2,1)}), bf16[64,4,16,128]{3,2,1,0:T(8,128)(2,1)S(1)}, u32[]{:S(2)}, u32[]{:S(2)}) async-start(bf16[64,4,16,128]{3,2,1,0:T(8,128)(2,1)} %sum_parts.1), calls=%async_computation.2 | async-start | bytes 2097152 | tf_op jit(solution)/shard_map/all_to_all | solution.py:633
  83.3 19.8 %collective-permute-start.10 = (bf16[2,2,32,256]{3,2,1,0:T(8,128)(2,1)S(1)}, bf16[2,2,32,256]{3,2,1,0:T(8,128)(2,1)S(1)}, u32[]{:S(2)}, u32[]{:S(2)}) collective-permute-start(bf16[2,2,32,256]{3,2,1,0:T(8,128)(2,1)S(1)} %get-tuple-element.75), channel_id=1, source_target_pairs={{0,6},{1,7},{2,4},{3,5},{4,2},{5,3},{6,0},{7,1},{8,14},{9,15},{10,... | collective-permute-start | bytes 196616 | tf_op jit(solution)/shard_map/ppermute | solution.py:756
  85.6 17.5 %collective-permute-start.11 = (bf16[2,2,32,256]{3,2,1,0:T(8,128)(2,1)S(1)}, bf16[2,2,32,256]{3,2,1,0:T(8,128)(2,1)S(1)}, u32[]{:S(2)}, u32[]{:S(2)}) collective-permute-start(bf16[2,2,32,256]{3,2,1,0:T(8,128)(2,1)S(1)} %get-tuple-element.76), channel_id=1, source_target_pairs={{0,7},{1,6},{2,5},{3,4},{4,3},{5,2},{6,1},{7,0},{8,15},{9,14},{10,... | collective-permute-start | bytes 196616 | tf_op jit(solution)/shard_map/ppermute | solution.py:756
  98.2 7.3 %collective-permute-start.13 = (bf16[256,16,128]{2,1,0:T(8,128)(2,1)S(1)}, bf16[256,16,128]{2,1,0:T(8,128)(2,1)S(1)}, u32[]{:S(2)}, u32[]{:S(2)}) collective-permute-start(bf16[256,16,128]{2,1,0:T(8,128)(2,1)S(1)} %bitcast.14), channel_id=1, source_target_pairs={{0,8},{8,0},{1,9},{9,1},{2,10},{10,2},{3,11},{11,3},{4,12},{12,4},... | collective-permute-start | bytes 3145736 | tf_op jit(solution)/shard_map/ppermute | solution.py:766
  (3 other events, 2.2 us)

commit v8 on v7

--- a/solution.py
+++ b/solution.py
@@ -723,6 +723,7 @@
     edge_near, edge_far = start_level(place, fine_cotangent, fine_pre)
     pieces = jnp.stack([coarse_pre, coarse_input]).reshape(2, samples, peers, lines // peers, wide, own)
     pieces = pieces.transpose(2, 0, 1, 3, 5, 4)
+    pieces, edge_far = lax.optimization_barrier((pieces, edge_far))
     edge_near, edge_far = swapped(edge_near, edge_far)
     received = lax.all_to_all(pieces, CHAN, 0, 0, tiled=True)
 

time: 108 us -> 108 us (level)
  no operation moved by 1% of the time
where the time goes in v8:
time: 108 us; the launch traced here: 107 us
  starting transfers between devices  47.2 us (44%)
  Pallas kernels  29.6 us (27%)
  waiting for transfers between devices  26 us (24%)
  local copies, waits for them, and re-layouts  2.22 us (2%)
  between operations  1.1 us (1%)
    ppermute x4, starting transfers between devices, swapped(): return (lax.ppermute(near, ALL, inside), lax.ppermute(far, ALL, outside))  12.8 us
    all_to_all x1, waiting for transfers between devices, grad_sums(): lax.all_to_all(summed, CHIPS, 0, 0, tiled=True)  11.4 us
    all_to_all x1, starting transfers between devices, grad_sums(): lax.all_to_all(parts.reshape(chips, each, 16, 128), CHIPS, 0, 0, tiled=True)  9.86 us
    ppermute x7, starting transfers between devices, home(): return lax.ppermute(piece, CHAN, [(i, i ^ k) for i in range(peers)])  9.84 us
    all_to_all x1, waiting for transfers between devices, grad_sums(): lax.all_to_all(parts.reshape(chips, each, 16, 128), CHIPS, 0, 0, tiled=True)  6.49 us
    pallas_call x1, Pallas kernels, fine_level(): pl.pallas_call(functools.partial(fine_kernel, scale=1.0 / math.sqrt(fine_...  6.43 us
    all_to_all x1, starting transfers between devices, grad_sums(): lax.all_to_all(summed, CHIPS, 0, 0, tiled=True)  6.05 us
    ppermute x1, starting transfers between devices, shards(): other = lax.ppermute(mine, 'core', SWAP)  4.88 us
  transfers between devices with their start and end apart: 17, of which 6 were waited for; matrix products, arithmetic and copies ran while one was open for 1% of the time, Pallas kernels for 22%

profile of v8, /device:TPU:1, one launch (start us, length us, event | category | flops | bytes accessed | tf_op | source)
XLA Modules:
  0.0 107.2 jit_solution(14532924240854454072)
XLA Ops:
  0.7 1.5 %start.1 = (bf16[2,512,128]{2,1,0:T(8,128)(2,1)S(1)}, bf16[2,512,128]{2,1,0:T(8,128)(2,1)S(1)}) custom-call(s32[1]{0:T(128)} %bitcast.place_ref, bf16[2,4,512,128]{3,2,1,0:T(8,128)(2,1)} %cot_ref.3, bf16[2,4,512,128]{3,2,1,0:T(8,128)(2,1)} %pre_ref.3), custom_call_target="tpu_custom_call" | custom-call | flops 10000000 | bytes 2000000 | tf_op jit(solution)/shard_map/start/pallas_call | solution.py:685
  2.2 2.1 %collective-permute-start = (bf16[2,512,128]{2,1,0:T(8,128)(2,1)S(1)}, bf16[2,512,128]{2,1,0:T(8,128)(2,1)S(1)}, u32[]{:S(2)}, u32[]{:S(2)}) collective-permute-start(bf16[2,512,128]{2,1,0:T(8,128)(2,1)S(1)} %get-tuple-element.48), channel_id=1, source_target_pairs={{0,1},{1,0},{2,3},{3,2},{4,5},{5,4},{6,7},{7,6},{8,9},{9,8},{10,11... | collective-permute-start | bytes 786440 | tf_op jit(solution)/shard_map/ppermute | solution.py:707
  5.4 5.4 %collective-permute-start.1 = (bf16[2,512,128]{2,1,0:T(8,128)(2,1)S(1)}, bf16[2,512,128]{2,1,0:T(8,128)(2,1)S(1)}, u32[]{:S(2)}, u32[]{:S(2)}) collective-permute-start(bf16[2,512,128]{2,1,0:T(8,128)(2,1)S(1)} %get-tuple-element.50), channel_id=1, source_target_pairs={{1,2},{3,4},{5,6},{7,8},{9,10},{11,12},{13,14},{15,16},{17,18},{19... | collective-permute-start | bytes 786440 | tf_op jit(solution)/shard_map/ppermute | solution.py:707
  10.8 3.6 %all-to-all-start = ((bf16[8,2,2,2,32,256]{5,4,3,2,1,0:T(8,128)(2,1)}), bf16[8,2,2,2,32,256]{5,4,3,2,1,0:T(8,128)(2,1)S(1)}, u32[]{:S(2)}, u32[]{:S(2)}) async-start(bf16[8,2,2,2,32,256]{5,4,3,2,1,0:T(8,128)(2,1)} %copy_bitcast_fusion), calls=%async_computation | async-start | bytes 2097152 | tf_op jit(solution)/shard_map/all_to_all | solution.py:728
  14.4 4.3 %box_level.1 = (bf16[2,4,512,128]{3,2,1,0:T(8,128)(2,1)}, bf16[2,256,1152]{2,1,0:T(8,128)(2,1)}, bf16[2,2,512,128]{3,2,1,0:T(8,128)(2,1)S(1)}, f32[2,2,256,256]{3,2,1,0:T(8,128)S(1)}, bf16[1152,256]{1,0:T(8,128)(2,1)S(1)}) custom-call(bf16[2,4,512,128]{3,2,1,0:T(8,128)(2,1)} %cot_ref.3, bf16[2,4,512,128]{3,2,1,0:T(8,128)(2,1)} %pre_ref.3, ...), custom_call_target="tpu_custom_call" | custom-call | flops 1200000000 | bytes 8000000 | tf_op jit(solution)/shard_map/box_level/pallas_call | solution.py:102
  18.8 1.5 %edge_level.1 = (f32[2,2,256,256]{3,2,1,0:T(8,128)S(1)}, bf16[2,256,384]{2,1,0:T(8,128)(2,1)}, bf16[2,256,384]{2,1,0:T(8,128)(2,1)}) custom-call(s32[1]{0:T(128)} %bitcast.place_ref, bf16[2,512,128]{2,1,0:T(8,128)(2,1)S(1)} %collective-permute-done.near_ref, bf16[2,512,128]{2,1,0:T(8,128)(2,1)S(1)} %collective-permute-done.1.far_ref, ...), custom_call_target="tpu_custom_call" | custom-call | flops 99999997952 | bytes 4000000 | tf_op jit(solution)/shard_map/edge_level/pallas_call | solution.py:154
  20.3 6.4 %fine_level.1 = (bf16[2,4,512,128]{3,2,1,0:T(8,128)(2,1)}, bf16[9,4,16,128]{3,2,1,0:T(8,128)(2,1)S(1)}, bf16[9,4,16,128]{3,2,1,0:T(8,128)(2,1)S(1)}) custom-call(s32[1]{0:T(128)} %bitcast.place_ref, bf16[2,4,512,128]{3,2,1,0:T(8,128)(2,1)} %get-tuple-element.47.grad_ref, bf16[2,512,128]{2,1,0:T(8,128)(2,1)S(1)} %collective-permute-done.near_ref, ...), custom_call_target="tpu_custom_call" | custom-call | flops 5000000000 | bytes 8000000 | tf_op jit(solution)/shard_map/fine_level/pallas_call | solution.py:237
  27.4 2.5 %all-to-all-done.pre_ref.input_ref = bf16[8,2,2,2,32,256]{5,4,3,2,1,0:T(8,128)(2,1)S(1)} async-done(((bf16[8,2,2,2,32,256]{5,4,3,2,1,0:T(8,128)(2,1)}), bf16[8,2,2,2,32,256]{5,4,3,2,1,0:T(8,128)(2,1)S(1)}, u32[]{:S(2)}, u32[]{:S(2)}) %all-to-all-start) | async-done | bytes 1048608 | tf_op jit(solution)/shard_map/all_to_all | solution.py:728
  30.7 5.1 %collective-permute-start.3 = (bf16[2,256,256]{2,1,0:T(8,128)(2,1)S(1)}, bf16[2,256,256]{2,1,0:T(8,128)(2,1)S(1)}, u32[]{:S(2)}, u32[]{:S(2)}) collective-permute-start(bf16[2,256,256]{2,1,0:T(8,128)(2,1)S(1)} %get-tuple-element.61.far_ref.second_ref), channel_id=1, source_target_pairs={{1,2},{3,4},{5,6},{7,8},{9,10},{11,12},{13,14},{15,16},{17,18},{19... | collective-permute-start | bytes 786440 | tf_op jit(solution)/shard_map/ppermute | solution.py:707
  36.7 1.3 %up_level.1 = (bf16[9,12,16,128]{3,2,1,0:T(8,128)(2,1)S(1)}, bf16[9,12,16,128]{3,2,1,0:T(8,128)(2,1)S(1)}) custom-call(s32[1]{0:T(128)} %bitcast.place_ref, bf16[8,2,2,2,32,256]{5,4,3,2,1,0:T(8,128)(2,1)S(1)} %all-to-all-done.pre_ref.input_ref, bf16[2,256,1152]{2,1,0:T(8,128)(2,1)S(1)} %copy-done.1, bf16[2,256,384]{2,1,0:T(8,128)(2,1)S(1)} %copy-done.2, ...), custom_call_target="tpu_custom_call" | custom-call | flops 1000000000 | bytes 5000000 | tf_op jit(solution)/shard_map/up_level/pallas_call | solution.py:341
  38.1 1.8 %own_weight_level.1.own_ref = f32[3,256,768]{2,1,0:T(8,128)S(1)} custom-call(s32[1]{0:T(128)} %bitcast.place_ref, bf16[8,2,2,2,32,256]{5,4,3,2,1,0:T(8,128)(2,1)S(1)} %all-to-all-done.pre_ref.input_ref, bf16[2,256,256]{2,1,0:T(8,128)(2,1)S(1)} %get-tuple-element.61.far_ref.second_ref, bf16[2,256,256]{2,1,0:T(8,128)(2,1)S(1)} %get-tuple-element.60.near_ref.third_ref), custom_call_target="tpu_custom_call" | custom-call | flops 99999997952 | bytes 4000000 | tf_op jit(solution)/shard_map/own_weight_level/pallas_call | solution.py:400
  40.7 4.7 %collective-permute-done.3.first_ref.from_far_ref = bf16[2,256,256]{2,1,0:T(8,128)(2,1)S(1)} collective-permute-done((bf16[2,256,256]{2,1,0:T(8,128)(2,1)S(1)}, bf16[2,256,256]{2,1,0:T(8,128)(2,1)S(1)}, u32[]{:S(2)}, u32[]{:S(2)}) %collective-permute-start.3) | collective-permute-done | bytes 262176 | tf_op jit(solution)/shard_map/ppermute | solution.py:707
  45.4 1.2 %coarse_weight_level.3 = bf16[144,16,128]{2,1,0:T(8,128)(2,1)S(1)} custom-call(s32[1]{0:T(128)} %bitcast.7.place_ref, bf16[8,2,2,2,32,256]{5,4,3,2,1,0:T(8,128)(2,1)S(1)} %all-to-all-done.pre_ref.input_ref, bf16[2,256,256]{2,1,0:T(8,128)(2,1)S(1)} %collective-permute-done.3.first_ref.from_far_ref, ...), custom_call_target="tpu_custom_call" | custom-call | flops 400000000 | bytes 2000000 | tf_op jit(solution)/shard_map/coarse_weight_level/pallas_call | solution.py:455
  46.7 1.3 %coarse_weight_level.2.refs_0_ = bf16[144,16,128]{2,1,0:T(8,128)(2,1)S(1)} custom-call(s32[1]{0:T(128)} %bitcast.place_ref, bf16[8,2,2,2,32,256]{5,4,3,2,1,0:T(8,128)(2,1)S(1)} %all-to-all-done.pre_ref.input_ref, bf16[2,256,256]{2,1,0:T(8,128)(2,1)S(1)} %collective-permute-done.3.first_ref.from_far_ref, ...), custom_call_target="tpu_custom_call" | custom-call | flops 400000000 | bytes 2000000 | tf_op jit(solution)/shard_map/coarse_weight_level/pallas_call | solution.py:455
  49.6 9.9 %all-to-all-start.1 = ((bf16[64,4,16,128]{3,2,1,0:T(8,128)(2,1)}), bf16[64,4,16,128]{3,2,1,0:T(8,128)(2,1)S(1)}, u32[]{:S(2)}, u32[]{:S(2)}) async-start(bf16[64,4,16,128]{3,2,1,0:T(8,128)(2,1)} %bitcast.8), calls=%async_computation.1 | async-start | bytes 2097152 | tf_op jit(solution)/shard_map/all_to_all | solution.py:625
  59.5 2.9 %coarse_input_level.1 = (bf16[2,2,32,256]{3,2,1,0:T(8,128)(2,1)S(1)}, bf16[2,2,32,256]{3,2,1,0:T(8,128)(2,1)}, bf16[2,2,32,256]{3,2,1,0:T(8,128)(2,1)}, bf16[2,2...) custom-call(s32[1]{0:T(128)} %bitcast.4.chan_ref, ...), custom_call_target="tpu_custom_call" | custom-call | flops 1300000000 | bytes 3000000 | tf_op jit(solution)/shard_map/coarse_input_level/pallas_call | solution.py:501
  65.7 2.5 %collective-permute-start.8 = (bf16[2,2,32,256]{3,2,1,0:T(8,128)(2,1)S(1)}, bf16[2,2,32,256]{3,2,1,0:T(8,128)(2,1)S(1)}, u32[]{:S(2)}, u32[]{:S(2)}) collective-permute-start(bf16[2,2,32,256]{3,2,1,0:T(8,128)(2,1)S(1)} %get-tuple-element.75), channel_id=1, source_target_pairs={{0,4},{1,5},{2,6},{3,7},{4,0},{5,1},{6,2},{7,3},{8,12},{9,13},{10,... | collective-permute-start | bytes 196616 | tf_op jit(solution)/shard_map/ppermute | solution.py:757
  69.4 6.5 %all-to-all-done.1.parts_ref = bf16[64,4,16,128]{3,2,1,0:T(8,128)(2,1)S(1)} async-done(((bf16[64,4,16,128]{3,2,1,0:T(8,128)(2,1)}), bf16[64,4,16,128]{3,2,1,0:T(8,128)(2,1)S(1)}, u32[]{:S(2)}, u32[]{:S(2)}) %all-to-all-start.1) | async-done | bytes 1048608 | tf_op jit(solution)/shard_map/all_to_all | solution.py:625
  77.2 6.0 %all-to-all-start.2 = ((bf16[64,4,16,128]{3,2,1,0:T(8,128)(2,1)}), bf16[64,4,16,128]{3,2,1,0:T(8,128)(2,1)S(1)}, u32[]{:S(2)}, u32[]{:S(2)}) async-start(bf16[64,4,16,128]{3,2,1,0:T(8,128)(2,1)} %sum_parts.1), calls=%async_computation.2 | async-start | bytes 2097152 | tf_op jit(solution)/shard_map/all_to_all | solution.py:633
  83.3 2.3 %collective-permute-start.10 = (bf16[2,2,32,256]{3,2,1,0:T(8,128)(2,1)S(1)}, bf16[2,2,32,256]{3,2,1,0:T(8,128)(2,1)S(1)}, u32[]{:S(2)}, u32[]{:S(2)}) collective-permute-start(bf16[2,2,32,256]{3,2,1,0:T(8,128)(2,1)S(1)} %get-tuple-element.79), channel_id=1, source_target_pairs={{0,6},{1,7},{2,4},{3,5},{4,2},{5,3},{6,0},{7,1},{8,14},{9,15},{10,... | collective-permute-start | bytes 196616 | tf_op jit(solution)/shard_map/ppermute | solution.py:757
  86.8 11.4 %all-to-all-done.2 = bf16[64,4,16,128]{3,2,1,0:T(8,128)(2,1)S(1)} async-done(((bf16[64,4,16,128]{3,2,1,0:T(8,128)(2,1)}), bf16[64,4,16,128]{3,2,1,0:T(8,128)(2,1)S(1)}, u32[]{:S(2)}, u32[]{:S(2)}) %all-to-all-start.2) | async-done | bytes 1048608 | tf_op jit(solution)/shard_map/all_to_all | solution.py:633
  98.2 4.9 %collective-permute-start.13 = (bf16[256,16,128]{2,1,0:T(8,128)(2,1)S(1)}, bf16[256,16,128]{2,1,0:T(8,128)(2,1)S(1)}, u32[]{:S(2)}, u32[]{:S(2)}) collective-permute-start(bf16[256,16,128]{2,1,0:T(8,128)(2,1)S(1)} %bitcast.14), channel_id=1, source_target_pairs={{0,8},{8,0},{1,9},{9,1},{2,10},{10,2},{3,11},{11,3},{4,12},{12,4},... | collective-permute-start | bytes 3145736 | tf_op jit(solution)/shard_map/ppermute | solution.py:767
  104.0 1.5 %unpack.2 = (f32[9,384,128]{2,1,0:T(8,128)}, f32[9,256,256]{2,1,0:T(8,128)}) custom-call(s32[1]{0:T(128)} %bitcast.place_ref, bf16[256,16,128]{2,1,0:T(8,128)(2,1)S(1)} %bitcast.15), custom_call_target="tpu_custom_call" | custom-call | flops 1 | bytes 1 | tf_op jit(solution)/shard_map/unpack/pallas_call | solution.py:639
  105.5 1.5 %unpack.3 = (f32[9,384,128]{2,1,0:T(8,128)}, f32[9,256,256]{2,1,0:T(8,128)}) custom-call(s32[1]{0:T(128)} %bitcast.7.place_ref, bf16[256,16,128]{2,1,0:T(8,128)(2,1)S(1)} %collective-permute-done.13.parts_ref, f32[9,384,128]{2,1,0:T(8,128)} %get-tuple-element.86.rest_0_, ...), custom_call_target="tpu_custom_call", output_to_operand_aliasing={{0}: (2, {}), {1}: (3, {})} | custom-call | flops 1 | bytes 1 | tf_op jit(solution)/shard_map/unpack/pallas_call | solution.py:639
  (48 shorter events, 13.9 us)
Async XLA Ops:
  0.6 3.7 %copy-start.9 = (bf16[2,16,256,32]{2,3,1,0:T(8,128)(2,1)S(1)}, bf16[2,16,256,32]{2,3,1,0:T(8,128)(2,1)}, u32[]{:S(2)}) copy-start(bf16[2,16,256,32]{2,3,1,0:T(8,128)(2,1)} %param.8) | copy-start | bytes 1572868
  0.6 3.7 %copy-start.8 = (bf16[2,16,256,32]{2,3,1,0:T(8,128)(2,1)S(1)}, bf16[2,16,256,32]{2,3,1,0:T(8,128)(2,1)}, u32[]{:S(2)}) copy-start(bf16[2,16,256,32]{2,3,1,0:T(8,128)(2,1)} %param.7) | copy-start | bytes 1572868
  2.2 16.5 %collective-permute-start = (bf16[2,512,128]{2,1,0:T(8,128)(2,1)S(1)}, bf16[2,512,128]{2,1,0:T(8,128)(2,1)S(1)}, u32[]{:S(2)}, u32[]{:S(2)}) collective-permute-start(bf16[2,512,128]{2,1,0:T(8,128)(2,1)S(1)} %get-tuple-element.48), channel_id=1, source_target_pairs={{0,1},{1,0},{2,3},{3,2},{4,5},{5,4},{6,7},{7,6},{8,9},{9,8},{10,11... | collective-permute-start | bytes 786440 | tf_op jit(solution)/shard_map/ppermute | solution.py:707
  5.4 13.4 %collective-permute-start.1 = (bf16[2,512,128]{2,1,0:T(8,128)(2,1)S(1)}, bf16[2,512,128]{2,1,0:T(8,128)(2,1)S(1)}, u32[]{:S(2)}, u32[]{:S(2)}) collective-permute-start(bf16[2,512,128]{2,1,0:T(8,128)(2,1)S(1)} %get-tuple-element.50), channel_id=1, source_target_pairs={{1,2},{3,4},{5,6},{7,8},{9,10},{11,12},{13,14},{15,16},{17,18},{19... | collective-permute-start | bytes 786440 | tf_op jit(solution)/shard_map/ppermute | solution.py:707
  10.8 19.1 %all-to-all-start = ((bf16[8,2,2,2,32,256]{5,4,3,2,1,0:T(8,128)(2,1)}), bf16[8,2,2,2,32,256]{5,4,3,2,1,0:T(8,128)(2,1)S(1)}, u32[]{:S(2)}, u32[]{:S(2)}) async-start(bf16[8,2,2,2,32,256]{5,4,3,2,1,0:T(8,128)(2,1)} %copy_bitcast_fusion), calls=%async_computation | async-start | bytes 2097152 | tf_op jit(solution)/shard_map/all_to_all | solution.py:728
  27.4 8.4 %copy-start.2 = (bf16[2,256,384]{2,1,0:T(8,128)(2,1)S(1)}, bf16[2,256,384]{2,1,0:T(8,128)(2,1)}, u32[]{:S(2)}) copy-start(bf16[2,256,384]{2,1,0:T(8,128)(2,1)} %get-tuple-element.63.box_low_ref) | copy-start | bytes 1179652
  29.9 5.9 %copy-start.1 = (bf16[2,256,1152]{2,1,0:T(8,128)(2,1)S(1)}, bf16[2,256,1152]{2,1,0:T(8,128)(2,1)}, u32[]{:S(2)}) copy-start(bf16[2,256,1152]{2,1,0:T(8,128)(2,1)} %get-tuple-element.62.box_ref) | copy-start | bytes 3538948
  29.9 5.9 %copy-start.3 = (bf16[2,256,384]{2,1,0:T(8,128)(2,1)S(1)}, bf16[2,256,384]{2,1,0:T(8,128)(2,1)}, u32[]{:S(2)}) copy-start(bf16[2,256,384]{2,1,0:T(8,128)(2,1)} %get-tuple-element.64.box_high_ref) | copy-start | bytes 1179652
  30.5 10.2 %collective-permute-start.2 = (bf16[2,256,256]{2,1,0:T(8,128)(2,1)S(1)}, bf16[2,256,256]{2,1,0:T(8,128)(2,1)S(1)}, u32[]{:S(2)}, u32[]{:S(2)}) collective-permute-start(bf16[2,256,256]{2,1,0:T(8,128)(2,1)S(1)} %get-tuple-element.60.near_ref.third_ref), channel_id=1, source_target_pairs={{0,1},{1,0},{2,3},{3,2},{4,5},{5,4},{6,7},{7,6},{8,9},{9,8},{10,11... | collective-permute-start | bytes 786440 | tf_op jit(solution)/shard_map/ppermute | solution.py:707
  30.7 14.8 %collective-permute-start.3 = (bf16[2,256,256]{2,1,0:T(8,128)(2,1)S(1)}, bf16[2,256,256]{2,1,0:T(8,128)(2,1)S(1)}, u32[]{:S(2)}, u32[]{:S(2)}) collective-permute-start(bf16[2,256,256]{2,1,0:T(8,128)(2,1)S(1)} %get-tuple-element.61.far_ref.second_ref), channel_id=1, source_target_pairs={{1,2},{3,4},{5,6},{7,8},{9,10},{11,12},{13,14},{15,16},{17,18},{19... | collective-permute-start | bytes 786440 | tf_op jit(solution)/shard_map/ppermute | solution.py:707
  38.0 1.9 %collective-permute-start.4 = (bf16[9,12,16,128]{3,2,1,0:T(8,128)(2,1)S(1)}, bf16[9,12,16,128]{3,2,1,0:T(8,128)(2,1)S(1)}, u32[]{:S(2)}, u32[]{:S(2)}) collective-permute-start(bf16[9,12,16,128]{3,2,1,0:T(8,128)(2,1)S(1)} %get-tuple-element.68), channel_id=1, source_target_pairs={{0,8},{8,0},{1,9},{9,1},{2,10},{10,2},{3,11},{11,3},{4,12},{12,4},... | collective-permute-start | bytes 1327112 | tf_op jit(solution)/shard_map/ppermute | solution.py:741
  46.6 2.1 %collective-permute-start.12 = (bf16[144,16,128]{2,1,0:T(8,128)(2,1)S(1)}, bf16[144,16,128]{2,1,0:T(8,128)(2,1)S(1)}, u32[]{:S(2)}, u32[]{:S(2)}) collective-permute-start(bf16[144,16,128]{2,1,0:T(8,128)(2,1)S(1)} %coarse_weight_level.3), channel_id=1, source_target_pairs={{0,8},{8,0},{1,9},{9,1},{2,10},{10,2},{3,11},{11,3},{4,12},{12,4},... | collective-permute-start | bytes 1769480 | tf_op jit(solution)/shard_map/ppermute | solution.py:752
  49.6 9.9 %copy-start = (bf16[3,3,256,256]{3,2,1,0:T(8,128)(2,1)S(1)}, bf16[3,3,256,256]{3,2,1,0:T(8,128)(2,1)}, u32[]{:S(2)}) copy-start(bf16[3,3,256,256]{3,2,1,0:T(8,128)(2,1)} %weight_ref.5) | copy-start | bytes 3538948
  49.6 26.3 %all-to-all-start.1 = ((bf16[64,4,16,128]{3,2,1,0:T(8,128)(2,1)}), bf16[64,4,16,128]{3,2,1,0:T(8,128)(2,1)S(1)}, u32[]{:S(2)}, u32[]{:S(2)}) async-start(bf16[64,4,16,128]{3,2,1,0:T(8,128)(2,1)} %bitcast.8), calls=%async_computation.1 | async-start | bytes 2097152 | tf_op jit(solution)/shard_map/all_to_all | solution.py:625
  63.1 20.1 %collective-permute-start.5 = (bf16[2,2,32,256]{3,2,1,0:T(8,128)(2,1)}, bf16[2,2,32,256]{3,2,1,0:T(8,128)(2,1)S(1)}, u32[]{:S(2)}, u32[]{:S(2)}) collective-permute-start(bf16[2,2,32,256]{3,2,1,0:T(8,128)(2,1)} %get-tuple-element.72), channel_id=1, source_target_pairs={{0,1},{1,0},{2,3},{3,2},{4,5},{5,4},{6,7},{7,6},{8,9},{9,8},{10,11... | collective-permute-start | bytes 196616 | tf_op jit(solution)/shard_map/ppermute | solution.py:757
  64.1 19.1 %collective-permute-start.6 = (bf16[2,2,32,256]{3,2,1,0:T(8,128)(2,1)}, bf16[2,2,32,256]{3,2,1,0:T(8,128)(2,1)S(1)}, u32[]{:S(2)}, u32[]{:S(2)}) collective-permute-start(bf16[2,2,32,256]{3,2,1,0:T(8,128)(2,1)} %get-tuple-element.73), channel_id=1, source_target_pairs={{0,2},{1,3},{2,0},{3,1},{4,6},{5,7},{6,4},{7,5},{8,10},{9,11},{10,... | collective-permute-start | bytes 196616 | tf_op jit(solution)/shard_map/ppermute | solution.py:757
  65.3 18.0 %collective-permute-start.7 = (bf16[2,2,32,256]{3,2,1,0:T(8,128)(2,1)}, bf16[2,2,32,256]{3,2,1,0:T(8,128)(2,1)S(1)}, u32[]{:S(2)}, u32[]{:S(2)}) collective-permute-start(bf16[2,2,32,256]{3,2,1,0:T(8,128)(2,1)} %get-tuple-element.74), channel_id=1, source_target_pairs={{0,3},{1,2},{2,1},{3,0},{4,7},{5,6},{6,5},{7,4},{8,11},{9,10},{10,... | collective-permute-start | bytes 196616 | tf_op jit(solution)/shard_map/ppermute | solution.py:757
  65.7 17.5 %collective-permute-start.8 = (bf16[2,2,32,256]{3,2,1,0:T(8,128)(2,1)S(1)}, bf16[2,2,32,256]{3,2,1,0:T(8,128)(2,1)S(1)}, u32[]{:S(2)}, u32[]{:S(2)}) collective-permute-start(bf16[2,2,32,256]{3,2,1,0:T(8,128)(2,1)S(1)} %get-tuple-element.75), channel_id=1, source_target_pairs={{0,4},{1,5},{2,6},{3,7},{4,0},{5,1},{6,2},{7,3},{8,12},{9,13},{10,... | collective-permute-start | bytes 196616 | tf_op jit(solution)/shard_map/ppermute | solution.py:757
  68.2 15.0 %copy-start.7 = (bf16[2,2,32,256]{3,2,1,0:T(8,128)(2,1)S(1)}, bf16[2,2,32,256]{3,2,1,0:T(8,128)(2,1)}, u32[]{:S(2)}) copy-start(bf16[2,2,32,256]{3,2,1,0:T(8,128)(2,1)} %copy-done.6) | copy-start | bytes 196612
  68.2 15.0 %collective-permute-start.9 = (bf16[2,2,32,256]{3,2,1,0:T(8,128)(2,1)S(1)}, bf16[2,2,32,256]{3,2,1,0:T(8,128)(2,1)S(1)}, u32[]{:S(2)}, u32[]{:S(2)}) collective-permute-start(bf16[2,2,32,256]{3,2,1,0:T(8,128)(2,1)S(1)} %get-tuple-element.76), channel_id=1, source_target_pairs={{0,5},{1,4},{2,7},{3,6},{4,1},{5,0},{6,3},{7,2},{8,13},{9,12},{10,... | collective-permute-start | bytes 196616 | tf_op jit(solution)/shard_map/ppermute | solution.py:757
  77.2 21.1 %all-to-all-start.2 = ((bf16[64,4,16,128]{3,2,1,0:T(8,128)(2,1)}), bf16[64,4,16,128]{3,2,1,0:T(8,128)(2,1)S(1)}, u32[]{:S(2)}, u32[]{:S(2)}) async-start(bf16[64,4,16,128]{3,2,1,0:T(8,128)(2,1)} %sum_parts.1), calls=%async_computation.2 | async-start | bytes 2097152 | tf_op jit(solution)/shard_map/all_to_all | solution.py:633
  83.3 19.8 %collective-permute-start.10 = (bf16[2,2,32,256]{3,2,1,0:T(8,128)(2,1)S(1)}, bf16[2,2,32,256]{3,2,1,0:T(8,128)(2,1)S(1)}, u32[]{:S(2)}, u32[]{:S(2)}) collective-permute-start(bf16[2,2,32,256]{3,2,1,0:T(8,128)(2,1)S(1)} %get-tuple-element.79), channel_id=1, source_target_pairs={{0,6},{1,7},{2,4},{3,5},{4,2},{5,3},{6,0},{7,1},{8,14},{9,15},{10,... | collective-permute-start | bytes 196616 | tf_op jit(solution)/shard_map/ppermute | solution.py:757
  85.6 17.5 %collective-permute-start.11 = (bf16[2,2,32,256]{3,2,1,0:T(8,128)(2,1)S(1)}, bf16[2,2,32,256]{3,2,1,0:T(8,128)(2,1)S(1)}, u32[]{:S(2)}, u32[]{:S(2)}) collective-permute-start(bf16[2,2,32,256]{3,2,1,0:T(8,128)(2,1)S(1)} %get-tuple-element.80), channel_id=1, source_target_pairs={{0,7},{1,6},{2,5},{3,4},{4,3},{5,2},{6,1},{7,0},{8,15},{9,14},{10,... | collective-permute-start | bytes 196616 | tf_op jit(solution)/shard_map/ppermute | solution.py:757
  98.2 7.3 %collective-permute-start.13 = (bf16[256,16,128]{2,1,0:T(8,128)(2,1)S(1)}, bf16[256,16,128]{2,1,0:T(8,128)(2,1)S(1)}, u32[]{:S(2)}, u32[]{:S(2)}) collective-permute-start(bf16[256,16,128]{2,1,0:T(8,128)(2,1)S(1)} %bitcast.14), channel_id=1, source_target_pairs={{0,8},{8,0},{1,9},{9,1},{2,10},{10,2},{3,11},{11,3},{4,12},{12,4},... | collective-permute-start | bytes 3145736 | tf_op jit(solution)/shard_map/ppermute | solution.py:767
  (3 other events, 2.2 us)

commit v9 on v7

--- a/solution.py
+++ b/solution.py
@@ -13,7 +13,7 @@
 BF16 = jnp.bfloat16
 MIB = 1 << 20
 VMEM = 18
-LATE = (6, 7)
+LATE = (2, 6)
 LONG = 1e11
 
 SPLIT = (("xh", 2), ("z", 4), ("core", 2), ("y", 4), ("xl", 2))

time: 108 us -> 107 us (level)
    all_to_all x1, waiting for transfers between devices: 6.5 us -> 5.06 us  [grad_sums(): lax.all_to_all(parts.reshape(chips, each, 16, 128), CHIPS, 0, 0, tiled=True)]
where the time goes in v9:
time: 107 us; the launch traced here: 106 us
  starting transfers between devices  47.4 us (44%)
  Pallas kernels  29.6 us (28%)
  waiting for transfers between devices  24.7 us (23%)
  local copies, waits for them, and re-layouts  2.22 us (2%)
  between operations  1.12 us (1%)
    ppermute x4, starting transfers between devices, swapped(): return (lax.ppermute(near, ALL, inside), lax.ppermute(far, ALL, outside))  12.8 us
    all_to_all x1, waiting for transfers between devices, grad_sums(): lax.all_to_all(summed, CHIPS, 0, 0, tiled=True)  12 us
    ppermute x7, starting transfers between devices, home(): return lax.ppermute(piece, CHAN, [(i, i ^ k) for i in range(peers)])  10.7 us
    all_to_all x1, starting transfers between devices, grad_sums(): lax.all_to_all(parts.reshape(chips, each, 16, 128), CHIPS, 0, 0, tiled=True)  10.4 us
    pallas_call x1, Pallas kernels, fine_level(): pl.pallas_call(functools.partial(fine_kernel, scale=1.0 / math.sqrt(fine_...  6.43 us
    all_to_all x1, starting transfers between devices, grad_sums(): lax.all_to_all(summed, CHIPS, 0, 0, tiled=True)  6.02 us
    all_to_all x1, waiting for transfers between devices, grad_sums(): lax.all_to_all(parts.reshape(chips, each, 16, 128), CHIPS, 0, 0, tiled=True)  5.06 us
    ppermute x4, waiting for transfers between devices, swapped(): return (lax.ppermute(near, ALL, inside), lax.ppermute(far, ALL, outside))  4.76 us
  transfers between devices with their start and end apart: 17, of which 6 were waited for; matrix products, arithmetic and copies ran while one was open for 1% of the time, Pallas kernels for 22%

profile of v9, /device:TPU:1, one launch (start us, length us, event | category | flops | bytes accessed | tf_op | source)
XLA Modules:
  0.0 106.2 jit_solution(8031476540435581134)
XLA Ops:
  0.7 1.5 %start.1 = (bf16[2,512,128]{2,1,0:T(8,128)(2,1)S(1)}, bf16[2,512,128]{2,1,0:T(8,128)(2,1)S(1)}) custom-call(s32[1]{0:T(128)} %bitcast.place_ref, bf16[2,4,512,128]{3,2,1,0:T(8,128)(2,1)} %cot_ref.3, bf16[2,4,512,128]{3,2,1,0:T(8,128)(2,1)} %pre_ref.3), custom_call_target="tpu_custom_call" | custom-call | flops 10000000 | bytes 2000000 | tf_op jit(solution)/shard_map/start/pallas_call | solution.py:685
  2.2 2.1 %collective-permute-start = (bf16[2,512,128]{2,1,0:T(8,128)(2,1)S(1)}, bf16[2,512,128]{2,1,0:T(8,128)(2,1)S(1)}, u32[]{:S(2)}, u32[]{:S(2)}) collective-permute-start(bf16[2,512,128]{2,1,0:T(8,128)(2,1)S(1)} %get-tuple-element.46), channel_id=1, source_target_pairs={{0,1},{1,0},{2,3},{3,2},{4,5},{5,4},{6,7},{7,6},{8,9},{9,8},{10,11... | collective-permute-start | bytes 786440 | tf_op jit(solution)/shard_map/ppermute | solution.py:707
  4.3 5.4 %collective-permute-start.1 = (bf16[2,512,128]{2,1,0:T(8,128)(2,1)S(1)}, bf16[2,512,128]{2,1,0:T(8,128)(2,1)S(1)}, u32[]{:S(2)}, u32[]{:S(2)}) collective-permute-start(bf16[2,512,128]{2,1,0:T(8,128)(2,1)S(1)} %get-tuple-element.47), channel_id=1, source_target_pairs={{1,2},{3,4},{5,6},{7,8},{9,10},{11,12},{13,14},{15,16},{17,18},{19... | collective-permute-start | bytes 786440 | tf_op jit(solution)/shard_map/ppermute | solution.py:707
  10.8 3.6 %all-to-all-start = ((bf16[8,2,2,2,32,256]{5,4,3,2,1,0:T(8,128)(2,1)}), bf16[8,2,2,2,32,256]{5,4,3,2,1,0:T(8,128)(2,1)S(1)}, u32[]{:S(2)}, u32[]{:S(2)}) async-start(bf16[8,2,2,2,32,256]{5,4,3,2,1,0:T(8,128)(2,1)} %copy_bitcast_fusion), calls=%async_computation | async-start | bytes 2097152 | tf_op jit(solution)/shard_map/all_to_all | solution.py:727
  14.4 4.3 %box_level.1 = (bf16[2,4,512,128]{3,2,1,0:T(8,128)(2,1)}, bf16[2,256,1152]{2,1,0:T(8,128)(2,1)}, bf16[2,2,512,128]{3,2,1,0:T(8,128)(2,1)S(1)}, f32[2,2,256,256]{3,2,1,0:T(8,128)S(1)}, bf16[1152,256]{1,0:T(8,128)(2,1)S(1)}) custom-call(bf16[2,4,512,128]{3,2,1,0:T(8,128)(2,1)} %cot_ref.3, bf16[2,4,512,128]{3,2,1,0:T(8,128)(2,1)} %pre_ref.3, ...), custom_call_target="tpu_custom_call" | custom-call | flops 1200000000 | bytes 8000000 | tf_op jit(solution)/shard_map/box_level/pallas_call | solution.py:102
  19.3 1.5 %edge_level.1 = (f32[2,2,256,256]{3,2,1,0:T(8,128)S(1)}, bf16[2,256,384]{2,1,0:T(8,128)(2,1)}, bf16[2,256,384]{2,1,0:T(8,128)(2,1)}) custom-call(s32[1]{0:T(128)} %bitcast.place_ref, bf16[2,512,128]{2,1,0:T(8,128)(2,1)S(1)} %collective-permute-done.near_ref, bf16[2,512,128]{2,1,0:T(8,128)(2,1)S(1)} %collective-permute-done.1.far_ref, ...), custom_call_target="tpu_custom_call" | custom-call | flops 99999997952 | bytes 4000000 | tf_op jit(solution)/shard_map/edge_level/pallas_call | solution.py:154
  20.8 6.4 %fine_level.1 = (bf16[2,4,512,128]{3,2,1,0:T(8,128)(2,1)}, bf16[9,4,16,128]{3,2,1,0:T(8,128)(2,1)S(1)}, bf16[9,4,16,128]{3,2,1,0:T(8,128)(2,1)S(1)}) custom-call(s32[1]{0:T(128)} %bitcast.place_ref, bf16[2,4,512,128]{3,2,1,0:T(8,128)(2,1)} %get-tuple-element.45.grad_ref, bf16[2,512,128]{2,1,0:T(8,128)(2,1)S(1)} %collective-permute-done.near_ref, ...), custom_call_target="tpu_custom_call" | custom-call | flops 5000000000 | bytes 8000000 | tf_op jit(solution)/shard_map/fine_level/pallas_call | solution.py:237
  27.9 2.1 %all-to-all-done.pre_ref.input_ref = bf16[8,2,2,2,32,256]{5,4,3,2,1,0:T(8,128)(2,1)S(1)} async-done(((bf16[8,2,2,2,32,256]{5,4,3,2,1,0:T(8,128)(2,1)}), bf16[8,2,2,2,32,256]{5,4,3,2,1,0:T(8,128)(2,1)S(1)}, u32[]{:S(2)}, u32[]{:S(2)}) %all-to-all-start) | async-done | bytes 1048608 | tf_op jit(solution)/shard_map/all_to_all | solution.py:727
  30.7 5.1 %collective-permute-start.3 = (bf16[2,256,256]{2,1,0:T(8,128)(2,1)S(1)}, bf16[2,256,256]{2,1,0:T(8,128)(2,1)S(1)}, u32[]{:S(2)}, u32[]{:S(2)}) collective-permute-start(bf16[2,256,256]{2,1,0:T(8,128)(2,1)S(1)} %get-tuple-element.57.far_ref.second_ref), channel_id=1, source_target_pairs={{1,2},{3,4},{5,6},{7,8},{9,10},{11,12},{13,14},{15,16},{17,18},{19... | collective-permute-start | bytes 786440 | tf_op jit(solution)/shard_map/ppermute | solution.py:707
  36.8 1.3 %up_level.1 = (bf16[9,12,16,128]{3,2,1,0:T(8,128)(2,1)S(1)}, bf16[9,12,16,128]{3,2,1,0:T(8,128)(2,1)S(1)}) custom-call(s32[1]{0:T(128)} %bitcast.place_ref, bf16[8,2,2,2,32,256]{5,4,3,2,1,0:T(8,128)(2,1)S(1)} %all-to-all-done.pre_ref.input_ref, bf16[2,256,1152]{2,1,0:T(8,128)(2,1)S(1)} %copy-done.1, bf16[2,256,384]{2,1,0:T(8,128)(2,1)S(1)} %copy-done.2, ...), custom_call_target="tpu_custom_call" | custom-call | flops 1000000000 | bytes 5000000 | tf_op jit(solution)/shard_map/up_level/pallas_call | solution.py:341
  38.1 1.8 %own_weight_level.1.own_ref = f32[3,256,768]{2,1,0:T(8,128)S(1)} custom-call(s32[1]{0:T(128)} %bitcast.place_ref, bf16[8,2,2,2,32,256]{5,4,3,2,1,0:T(8,128)(2,1)S(1)} %all-to-all-done.pre_ref.input_ref, bf16[2,256,256]{2,1,0:T(8,128)(2,1)S(1)} %get-tuple-element.57.far_ref.second_ref, bf16[2,256,256]{2,1,0:T(8,128)(2,1)S(1)} %get-tuple-element.56.near_ref.third_ref), custom_call_target="tpu_custom_call" | custom-call | flops 99999997952 | bytes 4000000 | tf_op jit(solution)/shard_map/own_weight_level/pallas_call | solution.py:400
  40.8 4.1 %collective-permute-done.3.first_ref.from_far_ref = bf16[2,256,256]{2,1,0:T(8,128)(2,1)S(1)} collective-permute-done((bf16[2,256,256]{2,1,0:T(8,128)(2,1)S(1)}, bf16[2,256,256]{2,1,0:T(8,128)(2,1)S(1)}, u32[]{:S(2)}, u32[]{:S(2)}) %collective-permute-start.3) | collective-permute-done | bytes 262176 | tf_op jit(solution)/shard_map/ppermute | solution.py:707
  49.1 10.4 %all-to-all-start.1 = ((bf16[64,4,16,128]{3,2,1,0:T(8,128)(2,1)}), bf16[64,4,16,128]{3,2,1,0:T(8,128)(2,1)S(1)}, u32[]{:S(2)}, u32[]{:S(2)}) async-start(bf16[64,4,16,128]{3,2,1,0:T(8,128)(2,1)} %bitcast.8), calls=%async_computation.1 | async-start | bytes 2097152 | tf_op jit(solution)/shard_map/all_to_all | solution.py:625
  59.5 2.9 %coarse_input_level.1 = (bf16[2,2,32,256]{3,2,1,0:T(8,128)(2,1)S(1)}, bf16[2,2,32,256]{3,2,1,0:T(8,128)(2,1)}, bf16[2,2,32,256]{3,2,1,0:T(8,128)(2,1)S(1)}, bf16...) custom-call(s32[1]{0:T(128)} %bitcast.1.chan_ref, ...), custom_call_target="tpu_custom_call" | custom-call | flops 1300000000 | bytes 3000000 | tf_op jit(solution)/shard_map/coarse_input_level/pallas_call | solution.py:501
  65.3 2.4 %collective-permute-start.7 = (bf16[2,2,32,256]{3,2,1,0:T(8,128)(2,1)}, bf16[2,2,32,256]{3,2,1,0:T(8,128)(2,1)S(1)}, u32[]{:S(2)}, u32[]{:S(2)}) collective-permute-start(bf16[2,2,32,256]{3,2,1,0:T(8,128)(2,1)} %get-tuple-element.70), channel_id=1, source_target_pairs={{0,4},{1,5},{2,6},{3,7},{4,0},{5,1},{6,2},{7,3},{8,12},{9,13},{10,... | collective-permute-start | bytes 196616 | tf_op jit(solution)/shard_map/ppermute | solution.py:756
  67.7 1.5 %collective-permute-start.8 = (bf16[2,2,32,256]{3,2,1,0:T(8,128)(2,1)S(1)}, bf16[2,2,32,256]{3,2,1,0:T(8,128)(2,1)S(1)}, u32[]{:S(2)}, u32[]{:S(2)}) collective-permute-start(bf16[2,2,32,256]{3,2,1,0:T(8,128)(2,1)S(1)} %get-tuple-element.71), channel_id=1, source_target_pairs={{0,5},{1,4},{2,7},{3,6},{4,1},{5,0},{6,3},{7,2},{8,13},{9,12},{10,... | collective-permute-start | bytes 196616 | tf_op jit(solution)/shard_map/ppermute | solution.py:756
  69.2 1.8 %collective-permute-start.9 = (bf16[2,2,32,256]{3,2,1,0:T(8,128)(2,1)S(1)}, bf16[2,2,32,256]{3,2,1,0:T(8,128)(2,1)S(1)}, u32[]{:S(2)}, u32[]{:S(2)}) collective-permute-start(bf16[2,2,32,256]{3,2,1,0:T(8,128)(2,1)S(1)} %get-tuple-element.72), channel_id=1, source_target_pairs={{0,7},{1,6},{2,5},{3,4},{4,3},{5,2},{6,1},{7,0},{8,15},{9,14},{10,... | collective-permute-start | bytes 196616 | tf_op jit(solution)/shard_map/ppermute | solution.py:756
  70.9 5.1 %all-to-all-done.1.parts_ref = bf16[64,4,16,128]{3,2,1,0:T(8,128)(2,1)S(1)} async-done(((bf16[64,4,16,128]{3,2,1,0:T(8,128)(2,1)}), bf16[64,4,16,128]{3,2,1,0:T(8,128)(2,1)S(1)}, u32[]{:S(2)}, u32[]{:S(2)}) %all-to-all-start.1) | async-done | bytes 1048608 | tf_op jit(solution)/shard_map/all_to_all | solution.py:625
  77.2 6.0 %all-to-all-start.2 = ((bf16[64,4,16,128]{3,2,1,0:T(8,128)(2,1)}), bf16[64,4,16,128]{3,2,1,0:T(8,128)(2,1)S(1)}, u32[]{:S(2)}, u32[]{:S(2)}) async-start(bf16[64,4,16,128]{3,2,1,0:T(8,128)(2,1)} %sum_parts.1), calls=%async_computation.2 | async-start | bytes 2097152 | tf_op jit(solution)/shard_map/all_to_all | solution.py:633
  84.4 1.8 %collective-permute-start.11 = (bf16[2,2,32,256]{3,2,1,0:T(8,128)(2,1)S(1)}, bf16[2,2,32,256]{3,2,1,0:T(8,128)(2,1)S(1)}, u32[]{:S(2)}, u32[]{:S(2)}) collective-permute-start(bf16[2,2,32,256]{3,2,1,0:T(8,128)(2,1)S(1)} %get-tuple-element.76), channel_id=1, source_target_pairs={{0,6},{1,7},{2,4},{3,5},{4,2},{5,3},{6,0},{7,1},{8,14},{9,15},{10,... | collective-permute-start | bytes 196616 | tf_op jit(solution)/shard_map/ppermute | solution.py:756
  86.2 12.0 %all-to-all-done.2 = bf16[64,4,16,128]{3,2,1,0:T(8,128)(2,1)S(1)} async-done(((bf16[64,4,16,128]{3,2,1,0:T(8,128)(2,1)}), bf16[64,4,16,128]{3,2,1,0:T(8,128)(2,1)S(1)}, u32[]{:S(2)}, u32[]{:S(2)}) %all-to-all-start.2) | async-done | bytes 1048608 | tf_op jit(solution)/shard_map/all_to_all | solution.py:633
  98.3 3.8 %collective-permute-start.13 = (bf16[256,16,128]{2,1,0:T(8,128)(2,1)S(1)}, bf16[256,16,128]{2,1,0:T(8,128)(2,1)S(1)}, u32[]{:S(2)}, u32[]{:S(2)}) collective-permute-start(bf16[256,16,128]{2,1,0:T(8,128)(2,1)S(1)} %bitcast.14), channel_id=1, source_target_pairs={{0,8},{8,0},{1,9},{9,1},{2,10},{10,2},{3,11},{11,3},{4,12},{12,4},... | collective-permute-start | bytes 3145736 | tf_op jit(solution)/shard_map/ppermute | solution.py:766
  102.9 1.5 %unpack.2 = (f32[9,384,128]{2,1,0:T(8,128)}, f32[9,256,256]{2,1,0:T(8,128)}) custom-call(s32[1]{0:T(128)} %bitcast.place_ref, bf16[256,16,128]{2,1,0:T(8,128)(2,1)S(1)} %bitcast.15), custom_call_target="tpu_custom_call" | custom-call | flops 1 | bytes 1 | tf_op jit(solution)/shard_map/unpack/pallas_call | solution.py:639
  104.5 1.5 %unpack.3 = (f32[9,384,128]{2,1,0:T(8,128)}, f32[9,256,256]{2,1,0:T(8,128)}) custom-call(s32[1]{0:T(128)} %bitcast.7.place_ref, bf16[256,16,128]{2,1,0:T(8,128)(2,1)S(1)} %collective-permute-done.13.parts_ref, f32[9,384,128]{2,1,0:T(8,128)} %get-tuple-element.82.rest_0_, ...), custom_call_target="tpu_custom_call", output_to_operand_aliasing={{0}: (2, {}), {1}: (3, {})} | custom-call | flops 1 | bytes 1 | tf_op jit(solution)/shard_map/unpack/pallas_call | solution.py:639
  (48 shorter events, 15.0 us)
Async XLA Ops:
  0.6 9.1 %copy-start.9 = (bf16[2,16,256,32]{2,3,1,0:T(8,128)(2,1)S(1)}, bf16[2,16,256,32]{2,3,1,0:T(8,128)(2,1)}, u32[]{:S(2)}) copy-start(bf16[2,16,256,32]{2,3,1,0:T(8,128)(2,1)} %param.8) | copy-start | bytes 1572868
  0.6 9.1 %copy-start.8 = (bf16[2,16,256,32]{2,3,1,0:T(8,128)(2,1)S(1)}, bf16[2,16,256,32]{2,3,1,0:T(8,128)(2,1)}, u32[]{:S(2)}) copy-start(bf16[2,16,256,32]{2,3,1,0:T(8,128)(2,1)} %param.7) | copy-start | bytes 1572868
  2.2 16.5 %collective-permute-start = (bf16[2,512,128]{2,1,0:T(8,128)(2,1)S(1)}, bf16[2,512,128]{2,1,0:T(8,128)(2,1)S(1)}, u32[]{:S(2)}, u32[]{:S(2)}) collective-permute-start(bf16[2,512,128]{2,1,0:T(8,128)(2,1)S(1)} %get-tuple-element.46), channel_id=1, source_target_pairs={{0,1},{1,0},{2,3},{3,2},{4,5},{5,4},{6,7},{7,6},{8,9},{9,8},{10,11... | collective-permute-start | bytes 786440 | tf_op jit(solution)/shard_map/ppermute | solution.py:707
  4.3 15.0 %collective-permute-start.1 = (bf16[2,512,128]{2,1,0:T(8,128)(2,1)S(1)}, bf16[2,512,128]{2,1,0:T(8,128)(2,1)S(1)}, u32[]{:S(2)}, u32[]{:S(2)}) collective-permute-start(bf16[2,512,128]{2,1,0:T(8,128)(2,1)S(1)} %get-tuple-element.47), channel_id=1, source_target_pairs={{1,2},{3,4},{5,6},{7,8},{9,10},{11,12},{13,14},{15,16},{17,18},{19... | collective-permute-start | bytes 786440 | tf_op jit(solution)/shard_map/ppermute | solution.py:707
  10.8 19.1 %all-to-all-start = ((bf16[8,2,2,2,32,256]{5,4,3,2,1,0:T(8,128)(2,1)}), bf16[8,2,2,2,32,256]{5,4,3,2,1,0:T(8,128)(2,1)S(1)}, u32[]{:S(2)}, u32[]{:S(2)}) async-start(bf16[8,2,2,2,32,256]{5,4,3,2,1,0:T(8,128)(2,1)} %copy_bitcast_fusion), calls=%async_computation | async-start | bytes 2097152 | tf_op jit(solution)/shard_map/all_to_all | solution.py:727
  27.9 7.9 %copy-start.2 = (bf16[2,256,384]{2,1,0:T(8,128)(2,1)S(1)}, bf16[2,256,384]{2,1,0:T(8,128)(2,1)}, u32[]{:S(2)}) copy-start(bf16[2,256,384]{2,1,0:T(8,128)(2,1)} %get-tuple-element.59.box_low_ref) | copy-start | bytes 1179652
  30.0 5.9 %copy-start.1 = (bf16[2,256,1152]{2,1,0:T(8,128)(2,1)S(1)}, bf16[2,256,1152]{2,1,0:T(8,128)(2,1)}, u32[]{:S(2)}) copy-start(bf16[2,256,1152]{2,1,0:T(8,128)(2,1)} %get-tuple-element.58.box_ref) | copy-start | bytes 3538948
  30.0 5.9 %copy-start.3 = (bf16[2,256,384]{2,1,0:T(8,128)(2,1)S(1)}, bf16[2,256,384]{2,1,0:T(8,128)(2,1)}, u32[]{:S(2)}) copy-start(bf16[2,256,384]{2,1,0:T(8,128)(2,1)} %get-tuple-element.60.box_high_ref) | copy-start | bytes 1179652
  30.6 10.2 %collective-permute-start.2 = (bf16[2,256,256]{2,1,0:T(8,128)(2,1)S(1)}, bf16[2,256,256]{2,1,0:T(8,128)(2,1)S(1)}, u32[]{:S(2)}, u32[]{:S(2)}) collective-permute-start(bf16[2,256,256]{2,1,0:T(8,128)(2,1)S(1)} %get-tuple-element.56.near_ref.third_ref), channel_id=1, source_target_pairs={{0,1},{1,0},{2,3},{3,2},{4,5},{5,4},{6,7},{7,6},{8,9},{9,8},{10,11... | collective-permute-start | bytes 786440 | tf_op jit(solution)/shard_map/ppermute | solution.py:707
  30.7 14.3 %collective-permute-start.3 = (bf16[2,256,256]{2,1,0:T(8,128)(2,1)S(1)}, bf16[2,256,256]{2,1,0:T(8,128)(2,1)S(1)}, u32[]{:S(2)}, u32[]{:S(2)}) collective-permute-start(bf16[2,256,256]{2,1,0:T(8,128)(2,1)S(1)} %get-tuple-element.57.far_ref.second_ref), channel_id=1, source_target_pairs={{1,2},{3,4},{5,6},{7,8},{9,10},{11,12},{13,14},{15,16},{17,18},{19... | collective-permute-start | bytes 786440 | tf_op jit(solution)/shard_map/ppermute | solution.py:707
  38.0 1.9 %collective-permute-start.4 = (bf16[9,12,16,128]{3,2,1,0:T(8,128)(2,1)S(1)}, bf16[9,12,16,128]{3,2,1,0:T(8,128)(2,1)S(1)}, u32[]{:S(2)}, u32[]{:S(2)}) collective-permute-start(bf16[9,12,16,128]{3,2,1,0:T(8,128)(2,1)S(1)} %get-tuple-element.64), channel_id=1, source_target_pairs={{0,8},{8,0},{1,9},{9,1},{2,10},{10,2},{3,11},{11,3},{4,12},{12,4},... | collective-permute-start | bytes 1327112 | tf_op jit(solution)/shard_map/ppermute | solution.py:740
  46.2 2.1 %collective-permute-start.12 = (bf16[144,16,128]{2,1,0:T(8,128)(2,1)S(1)}, bf16[144,16,128]{2,1,0:T(8,128)(2,1)S(1)}, u32[]{:S(2)}, u32[]{:S(2)}) collective-permute-start(bf16[144,16,128]{2,1,0:T(8,128)(2,1)S(1)} %coarse_weight_level.3), channel_id=1, source_target_pairs={{0,8},{8,0},{1,9},{9,1},{2,10},{10,2},{3,11},{11,3},{4,12},{12,4},... | collective-permute-start | bytes 1769480 | tf_op jit(solution)/shard_map/ppermute | solution.py:751
  49.1 10.4 %copy-start = (bf16[3,3,256,256]{3,2,1,0:T(8,128)(2,1)S(1)}, bf16[3,3,256,256]{3,2,1,0:T(8,128)(2,1)}, u32[]{:S(2)}) copy-start(bf16[3,3,256,256]{3,2,1,0:T(8,128)(2,1)} %weight_ref.5) | copy-start | bytes 3538948
  49.1 26.9 %all-to-all-start.1 = ((bf16[64,4,16,128]{3,2,1,0:T(8,128)(2,1)}), bf16[64,4,16,128]{3,2,1,0:T(8,128)(2,1)S(1)}, u32[]{:S(2)}, u32[]{:S(2)}) async-start(bf16[64,4,16,128]{3,2,1,0:T(8,128)(2,1)} %bitcast.8), calls=%async_computation.1 | async-start | bytes 2097152 | tf_op jit(solution)/shard_map/all_to_all | solution.py:625
  63.1 20.2 %collective-permute-start.5 = (bf16[2,2,32,256]{3,2,1,0:T(8,128)(2,1)}, bf16[2,2,32,256]{3,2,1,0:T(8,128)(2,1)S(1)}, u32[]{:S(2)}, u32[]{:S(2)}) collective-permute-start(bf16[2,2,32,256]{3,2,1,0:T(8,128)(2,1)} %get-tuple-element.68), channel_id=1, source_target_pairs={{0,1},{1,0},{2,3},{3,2},{4,5},{5,4},{6,7},{7,6},{8,9},{9,8},{10,11... | collective-permute-start | bytes 196616 | tf_op jit(solution)/shard_map/ppermute | solution.py:756
  64.1 19.2 %collective-permute-start.6 = (bf16[2,2,32,256]{3,2,1,0:T(8,128)(2,1)}, bf16[2,2,32,256]{3,2,1,0:T(8,128)(2,1)S(1)}, u32[]{:S(2)}, u32[]{:S(2)}) collective-permute-start(bf16[2,2,32,256]{3,2,1,0:T(8,128)(2,1)} %get-tuple-element.69), channel_id=1, source_target_pairs={{0,3},{1,2},{2,1},{3,0},{4,7},{5,6},{6,5},{7,4},{8,11},{9,10},{10,... | collective-permute-start | bytes 196616 | tf_op jit(solution)/shard_map/ppermute | solution.py:756
  65.3 18.0 %collective-permute-start.7 = (bf16[2,2,32,256]{3,2,1,0:T(8,128)(2,1)}, bf16[2,2,32,256]{3,2,1,0:T(8,128)(2,1)S(1)}, u32[]{:S(2)}, u32[]{:S(2)}) collective-permute-start(bf16[2,2,32,256]{3,2,1,0:T(8,128)(2,1)} %get-tuple-element.70), channel_id=1, source_target_pairs={{0,4},{1,5},{2,6},{3,7},{4,0},{5,1},{6,2},{7,3},{8,12},{9,13},{10,... | collective-permute-start | bytes 196616 | tf_op jit(solution)/shard_map/ppermute | solution.py:756
  67.7 15.6 %collective-permute-start.8 = (bf16[2,2,32,256]{3,2,1,0:T(8,128)(2,1)S(1)}, bf16[2,2,32,256]{3,2,1,0:T(8,128)(2,1)S(1)}, u32[]{:S(2)}, u32[]{:S(2)}) collective-permute-start(bf16[2,2,32,256]{3,2,1,0:T(8,128)(2,1)S(1)} %get-tuple-element.71), channel_id=1, source_target_pairs={{0,5},{1,4},{2,7},{3,6},{4,1},{5,0},{6,3},{7,2},{8,13},{9,12},{10,... | collective-permute-start | bytes 196616 | tf_op jit(solution)/shard_map/ppermute | solution.py:756
  69.2 14.1 %copy-start.7 = (bf16[2,2,32,256]{3,2,1,0:T(8,128)(2,1)S(1)}, bf16[2,2,32,256]{3,2,1,0:T(8,128)(2,1)}, u32[]{:S(2)}) copy-start(bf16[2,2,32,256]{3,2,1,0:T(8,128)(2,1)} %copy-done.6) | copy-start | bytes 196612
  69.2 14.1 %collective-permute-start.9 = (bf16[2,2,32,256]{3,2,1,0:T(8,128)(2,1)S(1)}, bf16[2,2,32,256]{3,2,1,0:T(8,128)(2,1)S(1)}, u32[]{:S(2)}, u32[]{:S(2)}) collective-permute-start(bf16[2,2,32,256]{3,2,1,0:T(8,128)(2,1)S(1)} %get-tuple-element.72), channel_id=1, source_target_pairs={{0,7},{1,6},{2,5},{3,4},{4,3},{5,2},{6,1},{7,0},{8,15},{9,14},{10,... | collective-permute-start | bytes 196616 | tf_op jit(solution)/shard_map/ppermute | solution.py:756
  77.2 21.1 %all-to-all-start.2 = ((bf16[64,4,16,128]{3,2,1,0:T(8,128)(2,1)}), bf16[64,4,16,128]{3,2,1,0:T(8,128)(2,1)S(1)}, u32[]{:S(2)}, u32[]{:S(2)}) async-start(bf16[64,4,16,128]{3,2,1,0:T(8,128)(2,1)} %sum_parts.1), calls=%async_computation.2 | async-start | bytes 2097152 | tf_op jit(solution)/shard_map/all_to_all | solution.py:633
  83.3 18.7 %collective-permute-start.10 = (bf16[2,2,32,256]{3,2,1,0:T(8,128)(2,1)S(1)}, bf16[2,2,32,256]{3,2,1,0:T(8,128)(2,1)S(1)}, u32[]{:S(2)}, u32[]{:S(2)}) collective-permute-start(bf16[2,2,32,256]{3,2,1,0:T(8,128)(2,1)S(1)} %get-tuple-element.75), channel_id=1, source_target_pairs={{0,2},{1,3},{2,0},{3,1},{4,6},{5,7},{6,4},{7,5},{8,10},{9,11},{10,... | collective-permute-start | bytes 196616 | tf_op jit(solution)/shard_map/ppermute | solution.py:756
  84.4 17.7 %collective-permute-start.11 = (bf16[2,2,32,256]{3,2,1,0:T(8,128)(2,1)S(1)}, bf16[2,2,32,256]{3,2,1,0:T(8,128)(2,1)S(1)}, u32[]{:S(2)}, u32[]{:S(2)}) collective-permute-start(bf16[2,2,32,256]{3,2,1,0:T(8,128)(2,1)S(1)} %get-tuple-element.76), channel_id=1, source_target_pairs={{0,6},{1,7},{2,4},{3,5},{4,2},{5,3},{6,0},{7,1},{8,14},{9,15},{10,... | collective-permute-start | bytes 196616 | tf_op jit(solution)/shard_map/ppermute | solution.py:756
  98.3 6.2 %collective-permute-start.13 = (bf16[256,16,128]{2,1,0:T(8,128)(2,1)S(1)}, bf16[256,16,128]{2,1,0:T(8,128)(2,1)S(1)}, u32[]{:S(2)}, u32[]{:S(2)}) collective-permute-start(bf16[256,16,128]{2,1,0:T(8,128)(2,1)S(1)} %bitcast.14), channel_id=1, source_target_pairs={{0,8},{8,0},{1,9},{9,1},{2,10},{10,2},{3,11},{11,3},{4,12},{12,4},... | collective-permute-start | bytes 3145736 | tf_op jit(solution)/shard_map/ppermute | solution.py:766
  (3 other events, 2.2 us)
